TPU v7x, 32 devices: a whole 2x2x4 slice. The times are simulated.
32 devices in a mesh: groups: 2 (over y), blk: 8 (over z, x), fsdp: 2 (over core).
Axes of the slice: x: 2, y: 2, z: 4, core: 2. Of those that a mesh axis runs over, the one named last changes fastest.
Arguments:
- query_out: bfloat16 [28672, 64], P('blk'), may hold values from -6 to 6
- query_act: bfloat16 [8192, 64], P('blk'), may hold values from -6 to 6
- out_basis: bfloat16 [28672, 512], P('blk', 'fsdp'), may hold values from -0.03125 to 0.03125
- act_basis: bfloat16 [8192, 256], P('blk', 'fsdp'), may hold values from -0.0625 to 0.0625
- eigenvalues: float32 [512, 256], P('fsdp'), may hold values from 0.05 to 5
- train_out: bfloat16 [32, 32, 512], P(('groups', 'blk', 'fsdp')), parts along dimension 0, may hold values from -0.078125 to 0.078125
- train_act: bfloat16 [32, 32, 256], P(('groups', 'blk', 'fsdp')), parts along dimension 0, may hold values from -0.078125 to 0.078125
- train_tokens: int32 [32], P(('groups', 'blk', 'fsdp')), parts along dimension 0, may hold values from 1 to 32, 256 in all
- train_ids: int32 [32], P(('groups', 'blk', 'fsdp')), parts along dimension 0, may hold values from 0 to 15, each once
Outputs:
- scores: float32 [16, 32], P('blk', 'groups'), parts along dimension 1
There are 2 independent parts, one for each index of `groups`. A program takes and returns all parts, laid end to end along the dimension named above; an argument that names none is the same for every part. Nothing has to cross between parts.
Inputs may be any that keep to these rules, and one draw needn't show every extreme that they name: `train_tokens`: number of tokens of each training example; its factor rows from this number on are padding and hold stale values. Some example has exactly 32. `train_ids`: A permutation of the score columns: every column is named by exactly one stored training example.
All inputs are finite; a program needn't handle non-finite values. No bound on the sum of `train_tokens` on one device may be relied on, other than what follows from the above.
Results may differ from a plain program's by a relative error of at most 0.0029.
Values may be sent and summed in bfloat16 or wider, within the bound.
No kernel may reach another device: no remote copies, remote signals or barrier semaphores. Data moves between devices by JAX's collectives and lax.ppermute only.
A program may use at most 64 MiB of HBM per device.

v0:
```python
import jax
import jax.numpy as jnp
from jax import lax
from jax.sharding import PartitionSpec as P

RQ = 4


damping = 0.1


def score_block(precond, out_rows, act_rows, token_counts):
    factor_rows = out_rows.shape[1]
    valid = (
        lax.broadcasted_iota(jnp.int32, (out_rows.shape[0], factor_rows), 1) < token_counts[:, None]
    ).astype(jnp.float32)
    projected = jnp.einsum("nri,qij->nrqj", out_rows, precond, preferred_element_type=jnp.float32)
    weights = act_rows.astype(jnp.float32) * valid[:, :, None]
    return jnp.einsum("nrqj,nrj->qn", projected, weights, precision=lax.Precision.HIGHEST)


def on_device(
    query_out,
    query_act,
    out_basis,
    act_basis,
    eigenvalues,
    train_out,
    train_act,
    train_tokens,
    train_ids,
):
    half_ks = out_basis.shape[1]
    local_rows = query_out.shape[1] // lax.axis_size("blk")
    out_part = lax.dot_general(
        query_out, out_basis, (((0,), (0,)), ((), ())), preferred_element_type=jnp.float32
    )
    act_part = lax.dot_general(
        query_act, act_basis, (((0,), (0,)), ((), ())), preferred_element_type=jnp.float32
    )
    rotated = lax.psum_scatter(
        jnp.concatenate([out_part, act_part], axis=1), "blk", scatter_dimension=0, tiled=True
    )
    out_coords = rotated[:, :half_ks]
    act_half = rotated[:, half_ks:]
    act_coords = lax.all_gather(act_half, "fsdp", axis=1, tiled=True)
    queries = local_rows // RQ
    out_three = out_coords.reshape(queries, RQ, half_ks)
    act_three = act_coords.reshape(queries, RQ, act_coords.shape[1])
    numer = jnp.einsum("qri,qrj->qij", out_three, act_three, precision=lax.Precision.HIGHEST)
    precond = (numer / (eigenvalues + damping)).astype(jnp.bfloat16)
    train_total = train_out.shape[0] * lax.axis_size("blk") * lax.axis_size("fsdp")
    empty = jnp.zeros((queries, train_total), jnp.float32)
    full_precond = lax.all_gather(precond, "fsdp", axis=1, tiled=True)
    out_rows = lax.all_gather(train_out, "blk", axis=0, tiled=True)
    act_rows = lax.all_gather(train_act, "blk", axis=0, tiled=True)
    token_counts = lax.all_gather(train_tokens, "blk", axis=0, tiled=True)
    column_ids = lax.all_gather(train_ids, "blk", axis=0, tiled=True)
    gathered = empty.at[:, column_ids].add(
        score_block(full_precond, out_rows, act_rows, token_counts)
    )
    return lax.psum(gathered, "fsdp")


def solution(mesh):
    return jax.shard_map(
        on_device,
        mesh=mesh,
        in_specs=(
            P("blk", None),
            P("blk", None),
            P("blk", "fsdp"),
            P("blk", "fsdp"),
            P("fsdp", None),
            P(("groups", "blk", "fsdp"), None, None),
            P(("groups", "blk", "fsdp"), None, None),
            P(("groups", "blk", "fsdp")),
            P(("groups", "blk", "fsdp")),
        ),
        out_specs=P("blk", "groups"),
        check_vma=False,
    )
```

profile of v0, /device:TPU:0, one launch (start us, length us, event | category | flops | bytes accessed | tf_op | source)
XLA Modules:
  0.0 111.3 jit_solution(1010473310939424396)
XLA Ops:
  6.6 0.0 all-reduce.6.cloned.1.call-start
  6.6 1.6 %copy-done = bf16[3584,256]{1,0:T(8,128)(2,1)S(1)} copy-done((bf16[3584,256]{1,0:T(8,128)(2,1)S(1)}, bf16[3584,256]{1,0:T(8,128)(2,1)}, u32[]{:S(2)}) %copy-start) | copy-done | bytes 1835032
  8.3 1.5 %fusion.10 = f32[64,256]{1,0:T(8,128)S(1)} fusion(bf16[3584,64]{0,1:T(8,128)(2,1)} %param.9, bf16[3584,256]{1,0:T(8,128)(2,1)S(1)} %copy-done), kind=kOutput, calls=%fused_computation.19 | convolution fusion | flops 117440512 | bytes 2359296 | tf_op jit(solution)/shard_map/dot_general | solution.py:35
  9.7 0.2 fusion.11
  9.9 0.6 pad_maximum_fusion
  10.6 0.0 all-reduce.6.cloned.1.call-update
  12.0 0.6 fusion.9
  12.6 0.7 dynamic-update-slice
  13.3 0.7 dynamic-update-slice.1
  14.1 13.1 %all-reduce.3 = (s32[8]{0:T(128)S(1)}, s32[8]{0:T(128)S(1)}) all-reduce(s32[8]{0:T(128)S(1)} %dynamic-update-slice, s32[8]{0:T(128)S(1)} %dynamic-update-slice.1), channel_id=1, replica_groups=mesh['groups'=2,'blk'=8,'fsdp'=2] {'blk'}, use_global_device_ids=true, to_apply=%add | all-reduce | flops 16 | bytes 128
  27.1 0.1 fusion.8
  27.2 30.5 %all_gather.19 = bf16[8,32,256]{2,1,0:T(8,128)(2,1)S(1)} all-gather(bf16[1,32,256]{2,1,0:T(8,128)(2,1)S(1)} %copy-done.5), channel_id=1, replica_groups=mesh['groups'=2,'blk'=8,'fsdp'=2] {'blk'}, dimensions={0}, use_global_device_ids=true | all-gather | bytes 147456 | tf_op jit(solution)/shard_map/all_gather | solution.py:56
  58.4 0.1 multiply_bitcast_fusion
  58.5 30.8 %all_gather.23 = bf16[8,32,512]{2,1,0:T(8,128)(2,1)S(1)} all-gather(bf16[1,32,512]{2,1,0:T(8,128)(2,1)S(1)} %copy-done.4), channel_id=1, replica_groups=mesh['groups'=2,'blk'=8,'fsdp'=2] {'blk'}, dimensions={0}, use_global_device_ids=true | all-gather | bytes 294912 | tf_op jit(solution)/shard_map/all_gather | solution.py:55
  89.3 0.8 dynamic-slice.5
  90.1 1.8 %all_gather.21 = f32[8,256]{1,0:T(8,128)S(1)} all-gather(f32[8,128]{1,0:T(8,128)S(1)} %dynamic-slice.5), channel_id=1, replica_groups=mesh['groups'=2,'blk'=8,'fsdp'=2] {'fsdp'}, dimensions={1}, use_global_device_ids=true | all-gather | bytes 12288 | tf_op jit(solution)/shard_map/all_gather | solution.py:46
  91.8 0.7 constant_dynamic-slice_fusion
  92.6 0.6 fusion
  93.2 2.2 %all_gather.22 = bf16[2,512,256]{2,1,0:T(8,128)(2,1)S(1)} all-gather(bf16[2,256,256]{2,1,0:T(8,128)(2,1)S(1)} %fusion), channel_id=1, replica_groups=mesh['groups'=2,'blk'=8,'fsdp'=2] {'fsdp'}, dimensions={1}, use_global_device_ids=true | all-gather | bytes 786432 | tf_op jit(solution)/shard_map/all_gather | solution.py:54
  95.4 0.3 convolution_bitcast_fusion
  95.7 5.0 %fusion.2 = f32[8,1,2,1]{2,1,3,0:T(1,128)S(1)} fusion(f32[8,32,2,256]{3,1,0,2:T(8,128)S(1)} %convolution_bitcast_fusion, f32[8,32,256,1]{2,1,0,3:T(8,128)S(1)} %multiply_bitcast_fusion), kind=kOutput, calls=%fused_computation.5 | convolution fusion | flops 1572864 | bytes 786496 | tf_op jit(solution)/shard_map/nrqj,nrj->qn/dot_general | solution.py:19
  100.7 0.6 scatter_custom_fusion
  101.3 2.5 %psum.7 = f32[2,16]{0,1:T(8,128)S(1)} all-reduce(f32[2,16]{0,1:T(8,128)S(1)} %scatter_custom_fusion), channel_id=1, replica_groups=mesh['groups'=2,'blk'=8,'fsdp'=2] {'fsdp'}, use_global_device_ids=true, to_apply=%region_2.0 | all-reduce | flops 32 | bytes 256 | tf_op jit(solution)/shard_map/psum | solution.py:62
  103.8 0.6 copy.12
  (20 shorter events, 0.1 us)
Async XLA Ops:
  6.5 1.7 %copy-start = (bf16[3584,256]{1,0:T(8,128)(2,1)S(1)}, bf16[3584,256]{1,0:T(8,128)(2,1)}, u32[]{:S(2)}) copy-start(bf16[3584,256]{1,0:T(8,128)(2,1)} %param.11) | copy-start | bytes 5505028
  6.5 5.4 %copy-start.6 = (u32[32]{0:T(128)S(1)}, u32[32]{0:T(128)}, u32[]{:S(2)}) copy-start(u32[32]{0:T(128)} %constant.14) | copy-start | bytes 388
  6.5 3.2 %copy-start.3 = (bf16[1024,64]{0,1:T(8,128)(2,1)S(1)}, bf16[1024,64]{0,1:T(8,128)(2,1)}, u32[]{:S(2)}) copy-start(bf16[1024,64]{0,1:T(8,128)(2,1)} %param.10) | copy-start | bytes 393220
  6.5 3.2 %copy-start.2 = (bf16[1024,128]{1,0:T(8,128)(2,1)S(1)}, bf16[1024,128]{1,0:T(8,128)(2,1)}, u32[]{:S(2)}) copy-start(bf16[1024,128]{1,0:T(8,128)(2,1)} %param.12) | copy-start | bytes 786436
  6.5 4.1 %copy-start.1 = (f32[256,256]{1,0:T(8,128)S(1)}, f32[256,256]{1,0:T(8,128)}, u32[]{:S(2)}) copy-start(f32[256,256]{1,0:T(8,128)} %param.13) | copy-start | bytes 786436
  6.5 20.7 %copy-start.5 = (bf16[1,32,256]{2,1,0:T(8,128)(2,1)S(1)}, bf16[1,32,256]{2,1,0:T(8,128)(2,1)}, u32[]{:S(2)}) copy-start(bf16[1,32,256]{2,1,0:T(8,128)(2,1)} %param.15) | copy-start | bytes 49156
  6.6 51.9 %copy-start.4 = (bf16[1,32,512]{2,1,0:T(8,128)(2,1)S(1)}, bf16[1,32,512]{2,1,0:T(8,128)(2,1)}, u32[]{:S(2)}) copy-start(bf16[1,32,512]{2,1,0:T(8,128)(2,1)} %param.14) | copy-start | bytes 98308
  6.6 82.7 %all-reduce.6.cloned.1.call-start = ((), (), s32[]{:S(2)}) async-start(), calls=%async_computation | async-start | bytes 196608
Sparse Core Ops, SparseCore 0:
  10.8 72.1 all-reduce.5
where the time goes:
time: 112 us; the launch traced here: 111 us
  blocking collectives  80.8 us (72%)
  between operations  15.5 us (14%)
  matrix products  7.52 us (7%)
  local copies, waits for them, and re-layouts  5.88 us (5%)
  other arithmetic  1.48 us (1%)
    all_gather x1, blocking collectives, on_device(): out_rows = lax.all_gather(train_out, 'blk', axis=0, tiled=True)  30.8 us
    all_gather x1, blocking collectives, on_device(): act_rows = lax.all_gather(train_act, 'blk', axis=0, tiled=True)  30.5 us
    unnamed x1, blocking collectives  13.1 us
    dot_general x1, matrix products, score_block(): jnp.einsum('nrqj,nrj->qn', projected, weights, precision=lax.Precision.HI...  4.96 us
    unnamed x19, local copies, waits for them, and re-layouts  3.77 us
    psum x1, blocking collectives, on_device(): return lax.psum(gathered, 'fsdp')  2.5 us
  transfers between devices with their start and end apart: 1, of which 0 were waited for; matrix products, arithmetic and copies ran while one was open for 2% of the time, Pallas kernels for 0%

commit v1 on v0

--- a/solution.py
+++ b/solution.py
@@ -1,12 +1,203 @@
+import functools
+
 import jax
 import jax.numpy as jnp
 from jax import lax
+from jax.experimental import pallas as pl
+from jax.experimental.pallas import tpu as pltpu
 from jax.sharding import PartitionSpec as P
 
 RQ = 4
+LANES = 128
+MOST_DIRECT = 16
 
 
 damping = 0.1
+
+
+def chunk_count(rows):
+    for chunks in (4, 2):
+        if rows % (chunks * LANES) == 0:
+            return chunks
+    return 1
+
+
+def project_kernel(
+    chunks,
+    parts,
+    place_ref,
+    query_out,
+    query_act,
+    out_basis,
+    act_basis,
+    *rest,
+):
+    pieces = rest[:parts]
+    q_out, q_act, b_out, b_act, total, sems = rest[parts:]
+    rows = query_out.shape[1] // chunks
+    copies = []
+    for c in range(chunks):
+        cut = pl.ds(c * rows, rows)
+        copies.append(
+            (
+                pltpu.make_async_copy(query_out.at[:, cut], q_out.at[:, cut], sems.at[2 * c]),
+                pltpu.make_async_copy(out_basis.at[cut, :], b_out.at[cut, :], sems.at[2 * c + 1]),
+            )
+        )
+    copies.append(
+        (
+            pltpu.make_async_copy(query_act, q_act, sems.at[2 * chunks]),
+            pltpu.make_async_copy(act_basis, b_act, sems.at[2 * chunks + 1]),
+        )
+    )
+    for pair in copies:
+        for copy in pair:
+            copy.start()
+    out_part = None
+    for c in range(chunks):
+        for copy in copies[c]:
+            copy.wait()
+        cut = pl.ds(c * rows, rows)
+        term = jnp.dot(q_out[:, cut], b_out[cut, :], preferred_element_type=jnp.float32)
+        out_part = term if out_part is None else out_part + term
+    for copy in copies[chunks]:
+        copy.wait()
+    half_ks = b_out.shape[1]
+    total[:, :half_ks] = out_part
+    total[:, half_ks:] = jnp.dot(q_act[...], b_act[...], preferred_element_type=jnp.float32)
+    place = place_ref[0]
+    local_rows = total.shape[0] // parts
+    for k in range(parts):
+        target = lax.rem(place + k, parts)
+        start = pl.multiple_of(target * local_rows, local_rows)
+        pieces[k][...] = total[pl.ds(start, local_rows), :]
+
+
+def project(place, query_out, query_act, out_basis, act_basis, parts):
+    columns = query_out.shape[0]
+    width = out_basis.shape[1] + act_basis.shape[1]
+    chunks = chunk_count(query_out.shape[1])
+    anywhere = pl.BlockSpec(memory_space=pl.ANY)
+    return pl.pallas_call(
+        functools.partial(project_kernel, chunks, parts),
+        out_shape=[jax.ShapeDtypeStruct((columns // parts, width), jnp.float32)] * parts,
+        in_specs=[pl.BlockSpec(memory_space=pltpu.SMEM)] + [anywhere] * 4,
+        out_specs=[pl.BlockSpec(memory_space=pltpu.VMEM)] * parts,
+        scratch_shapes=[
+            pltpu.VMEM(query_out.shape, query_out.dtype),
+            pltpu.VMEM(query_act.shape, query_act.dtype),
+            pltpu.VMEM(out_basis.shape, out_basis.dtype),
+            pltpu.VMEM(act_basis.shape, act_basis.dtype),
+            pltpu.VMEM((columns, width), jnp.float32),
+            pltpu.SemaphoreType.DMA((2 * chunks + 2,)),
+        ],
+        compiler_params=pltpu.CompilerParams(vmem_limit_bytes=24 * 2**20),
+    )(place, query_out, query_act, out_basis, act_basis)
+
+
+def pack_kernel(meta_ref, train_out, train_act, packed):
+    rows, ks = train_out.shape[1:]
+    ka = train_act.shape[2]
+    keep = lax.broadcasted_iota(jnp.int32, (rows, ka), 0) < meta_ref[0]
+    act = jnp.where(keep, train_act[0].astype(jnp.float32), 0.0)
+    packed[:, :ks] = train_out[0]
+    packed[:, ks : ks + ka] = act.astype(packed.dtype)
+    ident = jnp.full((rows, LANES), meta_ref[1], jnp.int32).astype(jnp.float32)
+    packed[:, ks + ka :] = ident.astype(packed.dtype)
+
+
+def pack(train_out, train_act, train_tokens, train_ids):
+    rows, ks = train_out.shape[1:]
+    width = ks + train_act.shape[2] + LANES
+    return pl.pallas_call(
+        pack_kernel,
+        out_shape=jax.ShapeDtypeStruct((rows, width), train_out.dtype),
+        in_specs=[pl.BlockSpec(memory_space=pltpu.SMEM)] + [pl.BlockSpec(memory_space=pltpu.VMEM)] * 2,
+        out_specs=pl.BlockSpec(memory_space=pltpu.VMEM),
+    )(jnp.concatenate([train_tokens, train_ids]), train_out, train_act)
+
+
+def score_kernel(ks, ka, place_ref, coords, other_coords, eigen, other_eigen, *rest):
+    blocks, out = rest[:-1], rest[-1]
+    first = place_ref[0] == 0
+    half = ks // 2
+    low, high = (
+        jnp.where(first, coords[...], other_coords[...]),
+        jnp.where(first, other_coords[...], coords[...]),
+    )
+    low_eigen, high_eigen = (
+        jnp.where(first, eigen[...], other_eigen[...]),
+        jnp.where(first, other_eigen[...], eigen[...]),
+    )
+    act = jnp.concatenate([low[:, half:], high[:, half:]], axis=1)
+    rows = jnp.concatenate([b[...].reshape(-1, b.shape[-1]) for b in blocks], axis=0)
+    weights = rows[:, ks : ks + ka].astype(jnp.float32)
+    column = lax.broadcasted_iota(jnp.int32, (rows.shape[0], LANES), 1).astype(jnp.float32)
+    hot = rows[:, ks + ka :].astype(jnp.float32) == column
+    for q in range(low.shape[0] // RQ):
+        cut = slice(q * RQ, (q + 1) * RQ)
+        projected = None
+        for part, values, part_eigen in ((0, low, low_eigen), (1, high, high_eigen)):
+            numer = lax.dot_general(
+                values[cut, :half],
+                act[cut],
+                (((0,), (0,)), ((), ())),
+                precision=lax.Precision.HIGHEST,
+                preferred_element_type=jnp.float32,
+            )
+            precond = (numer / (part_eigen + damping)).astype(jnp.bfloat16)
+            term = jnp.dot(
+                rows[:, part * half : (part + 1) * half], precond, preferred_element_type=jnp.float32
+            )
+            projected = term if projected is None else projected + term
+        per_row = jnp.sum(projected * weights, axis=1, keepdims=True)
+        scores = jnp.sum(jnp.where(hot, per_row, 0.0), axis=0, keepdims=True)
+        out[q : q + 1, :] = scores[:, : out.shape[1]]
+
+
+def score(place, coords, other_coords, eigen, other_eigen, blocks, ks, ka, total):
+    return pl.pallas_call(
+        functools.partial(score_kernel, ks, ka),
+        out_shape=jax.ShapeDtypeStruct((coords.shape[0] // RQ, total), jnp.float32),
+        in_specs=[pl.BlockSpec(memory_space=pltpu.SMEM)]
+        + [pl.BlockSpec(memory_space=pltpu.VMEM)] * (4 + len(blocks)),
+        out_specs=pl.BlockSpec(memory_space=pltpu.VMEM),
+        compiler_params=pltpu.CompilerParams(vmem_limit_bytes=32 * 2**20),
+    )(place, coords, other_coords, eigen, other_eigen, *blocks)
+
+
+def direct(
+    query_out,
+    query_act,
+    out_basis,
+    act_basis,
+    eigenvalues,
+    train_out,
+    train_act,
+    train_tokens,
+    train_ids,
+):
+    parts = lax.axis_size("blk")
+    ks, ka = train_out.shape[2], train_act.shape[2]
+    swap = [(0, 1), (1, 0)]
+    packed = pack(train_out, train_act, train_tokens, train_ids)
+    other_eigen = lax.ppermute(eigenvalues, "fsdp", swap)
+    blocks = [packed]
+    for k in range(1, parts):
+        blocks.append(lax.ppermute(packed, "blk", [(s, (s + k) % parts) for s in range(parts)]))
+    stacked = jnp.stack(blocks)
+    other = lax.ppermute(stacked, "fsdp", swap)
+    place = lax.axis_index("blk").reshape(1)
+    pieces = project(place, query_out.T, query_act.T, out_basis, act_basis, parts)
+    coords = pieces[0]
+    for k in range(1, parts):
+        coords = coords + lax.ppermute(pieces[k], "blk", [(s, (s + k) % parts) for s in range(parts)])
+    other_coords = lax.ppermute(coords, "fsdp", swap)
+    core = lax.axis_index("fsdp").reshape(1)
+    total = parts * 2 * train_out.shape[0]
+    return score(
+        core, coords, other_coords, eigenvalues, other_eigen, [stacked, other], ks, ka, total
+    )
 
 
 def score_block(precond, out_rows, act_rows, token_counts):
@@ -19,7 +210,7 @@
     return jnp.einsum("nrqj,nrj->qn", projected, weights, precision=lax.Precision.HIGHEST)
 
 
-def on_device(
+def gathered(
     query_out,
     query_act,
     out_basis,
@@ -56,15 +247,16 @@
     act_rows = lax.all_gather(train_act, "blk", axis=0, tiled=True)
     token_counts = lax.all_gather(train_tokens, "blk", axis=0, tiled=True)
     column_ids = lax.all_gather(train_ids, "blk", axis=0, tiled=True)
-    gathered = empty.at[:, column_ids].add(
+    scores = empty.at[:, column_ids].add(
         score_block(full_precond, out_rows, act_rows, token_counts)
     )
-    return lax.psum(gathered, "fsdp")
+    return lax.psum(scores, "fsdp")
 
 
 def solution(mesh):
+    few = mesh.shape["blk"] <= MOST_DIRECT and mesh.shape["fsdp"] == 2
     return jax.shard_map(
-        on_device,
+        direct if few else gathered,
         mesh=mesh,
         in_specs=(
             P("blk", None),

time: 112 us -> 46.5 us (0.42)
  blocking collectives: 80.8 us -> 0 us
  starting transfers between devices: 0.04 us -> 24.3 us
  between operations: 15.5 us -> 1.38 us
  waiting for transfers between devices: 0.02 us -> 8.36 us
  matrix products: 7.52 us -> 0 us
  Pallas kernels: 0 us -> 6.27 us
    all_gather x4 -> x0, blocking collectives: 65.3 us -> none  [the longest x1 30.8 us: on_device(): out_rows = lax.all_gather(train_out, 'blk', axis=0, tiled=True)]
    ppermute x0 -> x17, starting transfers between devices: none -> 24.3 us  [the longest x7 13.8 us: direct(): lax.ppermute(packed, 'blk', [(s, (s + k) % parts) for s in range(parts)])]
    unnamed x1 -> x0, blocking collectives: 13.1 us -> none
    ppermute x0 -> x17, waiting for transfers between devices: none -> 8.36 us  [the longest x7 4.31 us: direct(): lax.ppermute(pieces[k], 'blk', [(s, (s + k) % parts) for s in range(parts)])]
    dot_general x5 -> x0, matrix products: 7.52 us -> none  [the longest x1 4.96 us: score_block(): jnp.einsum('nrqj,nrj->qn', projected, weights, precision=lax.Precision.HI...]
    pallas_call x0 -> x3, Pallas kernels: none -> 6.27 us  [the longest x1 2.46 us: score(): pl.pallas_call(functools.partial(score_kernel, ks, ka), out_shape=jax.Sha...]
    psum x1 -> x0, blocking collectives: 2.5 us -> none  [on_device(): return lax.psum(gathered, 'fsdp')]
    unnamed x19 -> x17, local copies, waits for them, and re-layouts: 3.77 us -> 5.3 us
  transfers between devices with their start and end apart: 1 -> 17, of which waited for: 0 -> 9; matrix products, arithmetic and copies ran while one was open for 2% -> 2% of each run, Pallas kernels for 0% -> 5%
where the time goes in v1:
time: 46.5 us; the launch traced here: 46.2 us
  starting transfers between devices  24.3 us (52%)
  waiting for transfers between devices  8.36 us (18%)
  Pallas kernels  6.27 us (13%)
  local copies, waits for them, and re-layouts  5.31 us (11%)
  between operations  1.38 us (3%)
  other arithmetic  0.6 us (1%)
    ppermute x7, starting transfers between devices, direct(): lax.ppermute(packed, 'blk', [(s, (s + k) % parts) for s in range(parts)])  13.8 us
    ppermute x7, starting transfers between devices, direct(): lax.ppermute(pieces[k], 'blk', [(s, (s + k) % parts) for s in range(parts)])  10.3 us
    unnamed x17, local copies, waits for them, and re-layouts  5.3 us
    ppermute x7, waiting for transfers between devices, direct(): lax.ppermute(pieces[k], 'blk', [(s, (s + k) % parts) for s in range(parts)])  4.31 us
    ppermute x7, waiting for transfers between devices, direct(): lax.ppermute(packed, 'blk', [(s, (s + k) % parts) for s in range(parts)])  2.88 us
    pallas_call x1, Pallas kernels, score(): pl.pallas_call(functools.partial(score_kernel, ks, ka), out_shape=jax.Sha...  2.46 us
    pallas_call x1, Pallas kernels, project(): pl.pallas_call(functools.partial(project_kernel, chunks, parts), out_shap...  2.41 us
    pallas_call x1, Pallas kernels, pack(): pl.pallas_call(pack_kernel, out_shape=jax.ShapeDtypeStruct((rows, width),...  1.4 us
  transfers between devices with their start and end apart: 17, of which 9 were waited for; matrix products, arithmetic and copies ran while one was open for 2% of the time, Pallas kernels for 5%

profile of v1, /device:TPU:0, one launch (start us, length us, event | category | flops | bytes accessed | tf_op | source)
XLA Modules:
  0.0 46.2 jit_solution(14295823122805305541)
XLA Ops:
  1.9 1.4 %shard_map.92 = bf16[32,896]{1,0:T(8,128)(2,1)} custom-call(s32[2]{0:T(128)} %pad_add_fusion.meta_ref, bf16[1,32,512]{2,1,0:T(8,128)(2,1)} %train_out.1, bf16[1,32,256]{2,1,0:T(8,128)(2,1)} %train_act.1), custom_call_target="tpu_custom_call" | custom-call | tf_op jit(solution)/shard_map/pallas_call | solution.py:112
  3.3 2.9 %collective-permute-start.9 = (bf16[32,896]{1,0:T(8,128)(2,1)}, bf16[32,896]{1,0:T(8,128)(2,1)S(1)}, u32[]{:S(2)}, u32[]{:S(2)}) collective-permute-start(bf16[32,896]{1,0:T(8,128)(2,1)} %shard_map.92), channel_id=1, source_target_pairs={{0,2},{2,4},{4,6},{6,8},{8,10},{10,12},{12,14},{14,0},{1,3},{3,5},... | collective-permute-start | bytes 172040 | tf_op jit(solution)/shard_map/ppermute | solution.py:187
  6.2 1.6 %collective-permute-start.10 = (bf16[32,896]{1,0:T(8,128)(2,1)}, bf16[32,896]{1,0:T(8,128)(2,1)S(1)}, u32[]{:S(2)}, u32[]{:S(2)}) collective-permute-start(bf16[32,896]{1,0:T(8,128)(2,1)} %shard_map.92), channel_id=1, source_target_pairs={{0,4},{2,6},{4,8},{6,10},{8,12},{10,14},{12,0},{14,2},{1,5},{3,7},... | collective-permute-start | bytes 172040 | tf_op jit(solution)/shard_map/ppermute | solution.py:187
  7.8 2.6 %collective-permute-start.11 = (bf16[32,896]{1,0:T(8,128)(2,1)}, bf16[32,896]{1,0:T(8,128)(2,1)S(1)}, u32[]{:S(2)}, u32[]{:S(2)}) collective-permute-start(bf16[32,896]{1,0:T(8,128)(2,1)} %shard_map.92), channel_id=1, source_target_pairs={{0,6},{2,8},{4,10},{6,12},{8,14},{10,0},{12,2},{14,4},{1,7},{3,9},... | collective-permute-start | bytes 172040 | tf_op jit(solution)/shard_map/ppermute | solution.py:187
  10.4 1.2 %collective-permute-start.12 = (bf16[32,896]{1,0:T(8,128)(2,1)}, bf16[32,896]{1,0:T(8,128)(2,1)S(1)}, u32[]{:S(2)}, u32[]{:S(2)}) collective-permute-start(bf16[32,896]{1,0:T(8,128)(2,1)} %shard_map.92), channel_id=1, source_target_pairs={{0,8},{2,10},{4,12},{6,14},{8,0},{10,2},{12,4},{14,6},{1,9},{3,11}... | collective-permute-start | bytes 172040 | tf_op jit(solution)/shard_map/ppermute | solution.py:187
  11.6 2.6 %collective-permute-start.13 = (bf16[32,896]{1,0:T(8,128)(2,1)}, bf16[32,896]{1,0:T(8,128)(2,1)S(1)}, u32[]{:S(2)}, u32[]{:S(2)}) collective-permute-start(bf16[32,896]{1,0:T(8,128)(2,1)} %shard_map.92), channel_id=1, source_target_pairs={{0,10},{2,12},{4,14},{6,0},{8,2},{10,4},{12,6},{14,8},{1,11},{3,13... | collective-permute-start | bytes 172040 | tf_op jit(solution)/shard_map/ppermute | solution.py:187
  15.1 1.4 %collective-permute-start.14 = (bf16[32,896]{1,0:T(8,128)(2,1)}, bf16[32,896]{1,0:T(8,128)(2,1)S(1)}, u32[]{:S(2)}, u32[]{:S(2)}) collective-permute-start(bf16[32,896]{1,0:T(8,128)(2,1)} %shard_map.92), channel_id=1, source_target_pairs={{0,12},{2,14},{4,0},{6,2},{8,4},{10,6},{12,8},{14,10},{1,13},{3,15... | collective-permute-start | bytes 172040 | tf_op jit(solution)/shard_map/ppermute | solution.py:187
  16.5 1.5 %collective-permute-start.15 = (bf16[32,896]{1,0:T(8,128)(2,1)}, bf16[32,896]{1,0:T(8,128)(2,1)S(1)}, u32[]{:S(2)}, u32[]{:S(2)}) collective-permute-start(bf16[32,896]{1,0:T(8,128)(2,1)} %shard_map.92), channel_id=1, source_target_pairs={{0,14},{2,0},{4,2},{6,4},{8,6},{10,8},{12,10},{14,12},{1,15},{3,1}... | collective-permute-start | bytes 172040 | tf_op jit(solution)/shard_map/ppermute | solution.py:187
  18.7 1.3 %collective-permute-done.14 = bf16[32,896]{1,0:T(8,128)(2,1)S(1)} collective-permute-done((bf16[32,896]{1,0:T(8,128)(2,1)}, bf16[32,896]{1,0:T(8,128)(2,1)S(1)}, u32[]{:S(2)}, u32[]{:S(2)}) %collective-permute-start.14) | collective-permute-done | bytes 57376 | tf_op jit(solution)/shard_map/ppermute | solution.py:187
  20.0 0.9 %collective-permute-done.15 = bf16[32,896]{1,0:T(8,128)(2,1)S(1)} collective-permute-done((bf16[32,896]{1,0:T(8,128)(2,1)}, bf16[32,896]{1,0:T(8,128)(2,1)S(1)}, u32[]{:S(2)}, u32[]{:S(2)}) %collective-permute-start.15) | collective-permute-done | bytes 57376 | tf_op jit(solution)/shard_map/ppermute | solution.py:187
  21.0 1.5 %copy-done = bf16[3584,256]{1,0:T(8,128)(2,1)S(1)} copy-done((bf16[3584,256]{1,0:T(8,128)(2,1)S(1)}, bf16[3584,256]{1,0:T(8,128)(2,1)}, u32[]{:S(2)}) %copy-start) | copy-done | bytes 1835032
  22.5 1.0 %copy-done.1 = bf16[3584,64]{0,1:T(8,128)(2,1)S(1)} copy-done((bf16[3584,64]{0,1:T(8,128)(2,1)S(1)}, bf16[3584,64]{0,1:T(8,128)(2,1)}, u32[]{:S(2)}) %copy-start.1) | copy-done | bytes 458776
  23.5 0.9 %copy-done.2 = bf16[1024,128]{1,0:T(8,128)(2,1)S(1)} copy-done((bf16[1024,128]{1,0:T(8,128)(2,1)S(1)}, bf16[1024,128]{1,0:T(8,128)(2,1)}, u32[]{:S(2)}) %copy-start.2) | copy-done | bytes 262168
  24.5 0.9 %copy-done.4 = bf16[1024,64]{0,1:T(8,128)(2,1)S(1)} copy-done((bf16[1024,64]{0,1:T(8,128)(2,1)S(1)}, bf16[1024,64]{0,1:T(8,128)(2,1)}, u32[]{:S(2)}) %copy-start.4) | copy-done | bytes 131096
  25.4 2.4 %shard_map.91 = (f32[8,384]{1,0:T(8,128)S(1)}, f32[8,384]{1,0:T(8,128)S(1)}, f32[8,384]{1,0:T(8,128)S(1)}, f32[8,384]{1,0:T(8,128)S(1)}, f32[8,384]{1,0:T(8,128)...) custom-call(s32[1]{0:T(128)} %bitcast.1.place_ref, bf16[64,3584]{1,0:T(8,128)(2,1)S(1)} %bitcast.20, ...), custom_call_target="tpu_custom_call" | custom-call | tf_op jit(solution)/shard_map/pallas_call | solution.py:81
  27.8 1.6 %collective-permute-start = (f32[8,384]{1,0:T(8,128)S(1)}, f32[8,384]{1,0:T(8,128)S(1)}, u32[]{:S(2)}, u32[]{:S(2)}) collective-permute-start(f32[8,384]{1,0:T(8,128)S(1)} %get-tuple-element.14), channel_id=1, source_target_pairs={{0,2},{2,4},{4,6},{6,8},{8,10},{10,12},{12,14},{14,0},{1,3},{3,5},... | collective-permute-start | bytes 36872 | tf_op jit(solution)/shard_map/ppermute | solution.py:194
  30.2 1.4 %collective-permute-start.2 = (f32[8,384]{1,0:T(8,128)S(1)}, f32[8,384]{1,0:T(8,128)S(1)}, u32[]{:S(2)}, u32[]{:S(2)}) collective-permute-start(f32[8,384]{1,0:T(8,128)S(1)} %get-tuple-element.16), channel_id=1, source_target_pairs={{0,6},{2,8},{4,10},{6,12},{8,14},{10,0},{12,2},{14,4},{1,7},{3,9},... | collective-permute-start | bytes 36872 | tf_op jit(solution)/shard_map/ppermute | solution.py:194
  31.7 2.2 %collective-permute-start.3 = (f32[8,384]{1,0:T(8,128)S(1)}, f32[8,384]{1,0:T(8,128)S(1)}, u32[]{:S(2)}, u32[]{:S(2)}) collective-permute-start(f32[8,384]{1,0:T(8,128)S(1)} %get-tuple-element.17), channel_id=1, source_target_pairs={{0,8},{2,10},{4,12},{6,14},{8,0},{10,2},{12,4},{14,6},{1,9},{3,11}... | collective-permute-start | bytes 36872 | tf_op jit(solution)/shard_map/ppermute | solution.py:194
  34.9 2.1 %collective-permute-start.4 = (f32[8,384]{1,0:T(8,128)S(1)}, f32[8,384]{1,0:T(8,128)S(1)}, u32[]{:S(2)}, u32[]{:S(2)}) collective-permute-start(f32[8,384]{1,0:T(8,128)S(1)} %get-tuple-element.18), channel_id=1, source_target_pairs={{0,10},{2,12},{4,14},{6,0},{8,2},{10,4},{12,6},{14,8},{1,11},{3,13... | collective-permute-start | bytes 36872 | tf_op jit(solution)/shard_map/ppermute | solution.py:194
  37.0 1.7 %collective-permute-start.5 = (f32[8,384]{1,0:T(8,128)S(1)}, f32[8,384]{1,0:T(8,128)S(1)}, u32[]{:S(2)}, u32[]{:S(2)}) collective-permute-start(f32[8,384]{1,0:T(8,128)S(1)} %get-tuple-element.19), channel_id=1, source_target_pairs={{0,12},{2,14},{4,0},{6,2},{8,4},{10,6},{12,8},{14,10},{1,13},{3,15... | collective-permute-start | bytes 36872 | tf_op jit(solution)/shard_map/ppermute | solution.py:194
  39.5 1.2 %collective-permute-done.5 = f32[8,384]{1,0:T(8,128)S(1)} collective-permute-done((f32[8,384]{1,0:T(8,128)S(1)}, f32[8,384]{1,0:T(8,128)S(1)}, u32[]{:S(2)}, u32[]{:S(2)}) %collective-permute-start.5) | collective-permute-done | bytes 12320 | tf_op jit(solution)/shard_map/ppermute | solution.py:194
  40.7 1.7 %collective-permute-done.6 = f32[8,384]{1,0:T(8,128)S(1)} collective-permute-done((f32[8,384]{1,0:T(8,128)S(1)}, f32[8,384]{1,0:T(8,128)S(1)}, u32[]{:S(2)}, u32[]{:S(2)}) %collective-permute-start.6) | collective-permute-done | bytes 12320 | tf_op jit(solution)/shard_map/ppermute | solution.py:194
  42.5 1.2 %collective-permute-done.7.other_coords = f32[8,384]{1,0:T(8,128)S(1)} collective-permute-done((f32[8,384]{1,0:T(8,128)S(1)}, f32[8,384]{1,0:T(8,128)S(1)}, u32[]{:S(2)}, u32[]{:S(2)}) %collective-permute-start.7) | collective-permute-done | bytes 12320 | tf_op jit(solution)/shard_map/ppermute | solution.py:195
  43.7 2.5 %shard_map.93 = f32[2,16]{1,0:T(2,128)} custom-call(s32[1]{0:T(128)} %bitcast.place_ref, f32[8,384]{1,0:T(8,128)S(1)} %add_add_fusion.coords, f32[8,384]{1,0:T(8,128)S(1)} %collective-permute-done.7.other_coords, f32[256,256]{1,0:T(8,128)S(1)} %copy-done.3, f32[256,256]{1,0:T(8,128)S(1)} %collective-permute-done.8.other_eigen, ...), custom_call_target="tpu_custom_call" | custom-call | tf_op jit(solution)/shard_map/pallas_call | solution.py:159
  (33 shorter events, 5.0 us)
Async XLA Ops:
  3.3 31.1 %copy-start.3 = (f32[256,256]{1,0:T(8,128)S(1)}, f32[256,256]{1,0:T(8,128)}, u32[]{:S(2)}) copy-start(f32[256,256]{1,0:T(8,128)} %eigen.1) | copy-start | bytes 786436
  3.3 11.8 %collective-permute-start.9 = (bf16[32,896]{1,0:T(8,128)(2,1)}, bf16[32,896]{1,0:T(8,128)(2,1)S(1)}, u32[]{:S(2)}, u32[]{:S(2)}) collective-permute-start(bf16[32,896]{1,0:T(8,128)(2,1)} %shard_map.92), channel_id=1, source_target_pairs={{0,2},{2,4},{4,6},{6,8},{8,10},{10,12},{12,14},{14,0},{1,3},{3,5},... | collective-permute-start | bytes 172040 | tf_op jit(solution)/shard_map/ppermute | solution.py:187
  6.2 10.3 %collective-permute-start.10 = (bf16[32,896]{1,0:T(8,128)(2,1)}, bf16[32,896]{1,0:T(8,128)(2,1)S(1)}, u32[]{:S(2)}, u32[]{:S(2)}) collective-permute-start(bf16[32,896]{1,0:T(8,128)(2,1)} %shard_map.92), channel_id=1, source_target_pairs={{0,4},{2,6},{4,8},{6,10},{8,12},{10,14},{12,0},{14,2},{1,5},{3,7},... | collective-permute-start | bytes 172040 | tf_op jit(solution)/shard_map/ppermute | solution.py:187
  7.8 10.2 %collective-permute-start.11 = (bf16[32,896]{1,0:T(8,128)(2,1)}, bf16[32,896]{1,0:T(8,128)(2,1)S(1)}, u32[]{:S(2)}, u32[]{:S(2)}) collective-permute-start(bf16[32,896]{1,0:T(8,128)(2,1)} %shard_map.92), channel_id=1, source_target_pairs={{0,6},{2,8},{4,10},{6,12},{8,14},{10,0},{12,2},{14,4},{1,7},{3,9},... | collective-permute-start | bytes 172040 | tf_op jit(solution)/shard_map/ppermute | solution.py:187
  10.4 7.6 %collective-permute-start.12 = (bf16[32,896]{1,0:T(8,128)(2,1)}, bf16[32,896]{1,0:T(8,128)(2,1)S(1)}, u32[]{:S(2)}, u32[]{:S(2)}) collective-permute-start(bf16[32,896]{1,0:T(8,128)(2,1)} %shard_map.92), channel_id=1, source_target_pairs={{0,8},{2,10},{4,12},{6,14},{8,0},{10,2},{12,4},{14,6},{1,9},{3,11}... | collective-permute-start | bytes 172040 | tf_op jit(solution)/shard_map/ppermute | solution.py:187
  11.6 7.1 %collective-permute-start.13 = (bf16[32,896]{1,0:T(8,128)(2,1)}, bf16[32,896]{1,0:T(8,128)(2,1)S(1)}, u32[]{:S(2)}, u32[]{:S(2)}) collective-permute-start(bf16[32,896]{1,0:T(8,128)(2,1)} %shard_map.92), channel_id=1, source_target_pairs={{0,10},{2,12},{4,14},{6,0},{8,2},{10,4},{12,6},{14,8},{1,11},{3,13... | collective-permute-start | bytes 172040 | tf_op jit(solution)/shard_map/ppermute | solution.py:187
  15.1 5.0 %collective-permute-start.14 = (bf16[32,896]{1,0:T(8,128)(2,1)}, bf16[32,896]{1,0:T(8,128)(2,1)S(1)}, u32[]{:S(2)}, u32[]{:S(2)}) collective-permute-start(bf16[32,896]{1,0:T(8,128)(2,1)} %shard_map.92), channel_id=1, source_target_pairs={{0,12},{2,14},{4,0},{6,2},{8,4},{10,6},{12,8},{14,10},{1,13},{3,15... | collective-permute-start | bytes 172040 | tf_op jit(solution)/shard_map/ppermute | solution.py:187
  16.5 4.4 %collective-permute-start.15 = (bf16[32,896]{1,0:T(8,128)(2,1)}, bf16[32,896]{1,0:T(8,128)(2,1)S(1)}, u32[]{:S(2)}, u32[]{:S(2)}) collective-permute-start(bf16[32,896]{1,0:T(8,128)(2,1)} %shard_map.92), channel_id=1, source_target_pairs={{0,14},{2,0},{4,2},{6,4},{8,6},{10,8},{12,10},{14,12},{1,15},{3,1}... | collective-permute-start | bytes 172040 | tf_op jit(solution)/shard_map/ppermute | solution.py:187
  20.9 22.8 %collective-permute-start.16 = (bf16[8,32,896]{2,1,0:T(8,128)(2,1)S(1)}, bf16[8,32,896]{2,1,0:T(8,128)(2,1)S(1)}, u32[]{:S(2)}, u32[]{:S(2)}) collective-permute-start(bf16[8,32,896]{2,1,0:T(8,128)(2,1)S(1)} %bitcast_dynamic-update-slice_fusion.rest_0_), channel_id=1, source_target_pairs={{0,1},{1,0},{2,3},{3,2},{4,5},{5,4},{6,7},{7,6},{8,9},{9,8},{10,11... | collective-permute-start | bytes 1376264 | tf_op jit(solution)/shard_map/ppermute | solution.py:189
  21.0 1.5 %copy-start = (bf16[3584,256]{1,0:T(8,128)(2,1)S(1)}, bf16[3584,256]{1,0:T(8,128)(2,1)}, u32[]{:S(2)}) copy-start(bf16[3584,256]{1,0:T(8,128)(2,1)} %out_basis.1) | copy-start | bytes 5505028
  22.5 1.0 %copy-start.1 = (bf16[3584,64]{0,1:T(8,128)(2,1)S(1)}, bf16[3584,64]{0,1:T(8,128)(2,1)}, u32[]{:S(2)}) copy-start(bf16[3584,64]{0,1:T(8,128)(2,1)} %param.9) | copy-start | bytes 1376260
  23.5 0.9 %copy-start.2 = (bf16[1024,128]{1,0:T(8,128)(2,1)S(1)}, bf16[1024,128]{1,0:T(8,128)(2,1)}, u32[]{:S(2)}) copy-start(bf16[1024,128]{1,0:T(8,128)(2,1)} %act_basis.1) | copy-start | bytes 786436
  24.5 0.9 %copy-start.4 = (bf16[1024,64]{0,1:T(8,128)(2,1)S(1)}, bf16[1024,64]{0,1:T(8,128)(2,1)}, u32[]{:S(2)}) copy-start(bf16[1024,64]{0,1:T(8,128)(2,1)} %param.10) | copy-start | bytes 393220
  27.8 6.5 %collective-permute-start = (f32[8,384]{1,0:T(8,128)S(1)}, f32[8,384]{1,0:T(8,128)S(1)}, u32[]{:S(2)}, u32[]{:S(2)}) collective-permute-start(f32[8,384]{1,0:T(8,128)S(1)} %get-tuple-element.14), channel_id=1, source_target_pairs={{0,2},{2,4},{4,6},{6,8},{8,10},{10,12},{12,14},{14,0},{1,3},{3,5},... | collective-permute-start | bytes 36872 | tf_op jit(solution)/shard_map/ppermute | solution.py:194
  29.4 5.5 %collective-permute-start.1 = (f32[8,384]{1,0:T(8,128)S(1)}, f32[8,384]{1,0:T(8,128)S(1)}, u32[]{:S(2)}, u32[]{:S(2)}) collective-permute-start(f32[8,384]{1,0:T(8,128)S(1)} %get-tuple-element.15), channel_id=1, source_target_pairs={{0,4},{2,6},{4,8},{6,10},{8,12},{10,14},{12,0},{14,2},{1,5},{3,7},... | collective-permute-start | bytes 36872 | tf_op jit(solution)/shard_map/ppermute | solution.py:194
  30.2 6.8 %collective-permute-start.2 = (f32[8,384]{1,0:T(8,128)S(1)}, f32[8,384]{1,0:T(8,128)S(1)}, u32[]{:S(2)}, u32[]{:S(2)}) collective-permute-start(f32[8,384]{1,0:T(8,128)S(1)} %get-tuple-element.16), channel_id=1, source_target_pairs={{0,6},{2,8},{4,10},{6,12},{8,14},{10,0},{12,2},{14,4},{1,7},{3,9},... | collective-permute-start | bytes 36872 | tf_op jit(solution)/shard_map/ppermute | solution.py:194
  31.7 7.1 %collective-permute-start.3 = (f32[8,384]{1,0:T(8,128)S(1)}, f32[8,384]{1,0:T(8,128)S(1)}, u32[]{:S(2)}, u32[]{:S(2)}) collective-permute-start(f32[8,384]{1,0:T(8,128)S(1)} %get-tuple-element.17), channel_id=1, source_target_pairs={{0,8},{2,10},{4,12},{6,14},{8,0},{10,2},{12,4},{14,6},{1,9},{3,11}... | collective-permute-start | bytes 36872 | tf_op jit(solution)/shard_map/ppermute | solution.py:194
  34.4 9.4 %collective-permute-start.8 = (f32[256,256]{1,0:T(8,128)S(1)}, f32[256,256]{1,0:T(8,128)S(1)}, u32[]{:S(2)}, u32[]{:S(2)}) collective-permute-start(f32[256,256]{1,0:T(8,128)S(1)} %copy-done.3), channel_id=1, source_target_pairs={{0,1},{1,0},{2,3},{3,2},{4,5},{5,4},{6,7},{7,6},{8,9},{9,8},{10,11... | collective-permute-start | bytes 786440 | tf_op jit(solution)/shard_map/ppermute | solution.py:184
  34.9 4.6 %collective-permute-start.4 = (f32[8,384]{1,0:T(8,128)S(1)}, f32[8,384]{1,0:T(8,128)S(1)}, u32[]{:S(2)}, u32[]{:S(2)}) collective-permute-start(f32[8,384]{1,0:T(8,128)S(1)} %get-tuple-element.18), channel_id=1, source_target_pairs={{0,10},{2,12},{4,14},{6,0},{8,2},{10,4},{12,6},{14,8},{1,11},{3,13... | collective-permute-start | bytes 36872 | tf_op jit(solution)/shard_map/ppermute | solution.py:194
  37.0 3.7 %collective-permute-start.5 = (f32[8,384]{1,0:T(8,128)S(1)}, f32[8,384]{1,0:T(8,128)S(1)}, u32[]{:S(2)}, u32[]{:S(2)}) collective-permute-start(f32[8,384]{1,0:T(8,128)S(1)} %get-tuple-element.19), channel_id=1, source_target_pairs={{0,12},{2,14},{4,0},{6,2},{8,4},{10,6},{12,8},{14,10},{1,13},{3,15... | collective-permute-start | bytes 36872 | tf_op jit(solution)/shard_map/ppermute | solution.py:194
  38.8 3.7 %collective-permute-start.6 = (f32[8,384]{1,0:T(8,128)S(1)}, f32[8,384]{1,0:T(8,128)S(1)}, u32[]{:S(2)}, u32[]{:S(2)}) collective-permute-start(f32[8,384]{1,0:T(8,128)S(1)} %get-tuple-element.20), channel_id=1, source_target_pairs={{0,14},{2,0},{4,2},{6,4},{8,6},{10,8},{12,10},{14,12},{1,15},{3,1}... | collective-permute-start | bytes 36872 | tf_op jit(solution)/shard_map/ppermute | solution.py:194
  42.5 1.2 %collective-permute-start.7 = (f32[8,384]{1,0:T(8,128)S(1)}, f32[8,384]{1,0:T(8,128)S(1)}, u32[]{:S(2)}, u32[]{:S(2)}) collective-permute-start(f32[8,384]{1,0:T(8,128)S(1)} %add_add_fusion.coords), channel_id=1, source_target_pairs={{0,1},{1,0},{2,3},{3,2},{4,5},{5,4},{6,7},{7,6},{8,9},{9,8},{10,11... | collective-permute-start | bytes 36872 | tf_op jit(solution)/shard_map/ppermute | solution.py:195

commit v2 on v1

--- a/solution.py
+++ b/solution.py
@@ -23,17 +23,8 @@
 
 
 def project_kernel(
-    chunks,
-    parts,
-    place_ref,
-    query_out,
-    query_act,
-    out_basis,
-    act_basis,
-    *rest,
+    chunks, query_out, query_act, out_basis, act_basis, pieces, q_out, q_act, b_out, b_act, sems
 ):
-    pieces = rest[:parts]
-    q_out, q_act, b_out, b_act, total, sems = rest[parts:]
     rows = query_out.shape[1] // chunks
     copies = []
     for c in range(chunks):
@@ -62,90 +53,87 @@
         out_part = term if out_part is None else out_part + term
     for copy in copies[chunks]:
         copy.wait()
+    act_part = jnp.dot(q_act[...], b_act[...], preferred_element_type=jnp.float32)
+    parts, cores, local_rows, _ = pieces.shape
     half_ks = b_out.shape[1]
-    total[:, :half_ks] = out_part
-    total[:, half_ks:] = jnp.dot(q_act[...], b_act[...], preferred_element_type=jnp.float32)
-    place = place_ref[0]
-    local_rows = total.shape[0] // parts
-    for k in range(parts):
-        target = lax.rem(place + k, parts)
-        start = pl.multiple_of(target * local_rows, local_rows)
-        pieces[k][...] = total[pl.ds(start, local_rows), :]
-
-
-def project(place, query_out, query_act, out_basis, act_basis, parts):
+    for part in range(parts):
+        cut = slice(part * local_rows, (part + 1) * local_rows)
+        for core in range(cores):
+            pieces[part, core, :, :half_ks] = out_part[cut]
+            pieces[part, core, :, half_ks:] = act_part[cut]
+
+
+def project(query_out, query_act, out_basis, act_basis, parts, cores):
     columns = query_out.shape[0]
     width = out_basis.shape[1] + act_basis.shape[1]
     chunks = chunk_count(query_out.shape[1])
-    anywhere = pl.BlockSpec(memory_space=pl.ANY)
     return pl.pallas_call(
-        functools.partial(project_kernel, chunks, parts),
-        out_shape=[jax.ShapeDtypeStruct((columns // parts, width), jnp.float32)] * parts,
-        in_specs=[pl.BlockSpec(memory_space=pltpu.SMEM)] + [anywhere] * 4,
-        out_specs=[pl.BlockSpec(memory_space=pltpu.VMEM)] * parts,
+        functools.partial(project_kernel, chunks),
+        out_shape=jax.ShapeDtypeStruct((parts, cores, columns // parts, width), jnp.float32),
+        in_specs=[pl.BlockSpec(memory_space=pltpu.HBM)] * 4,
+        out_specs=pl.BlockSpec(memory_space=pltpu.VMEM),
         scratch_shapes=[
             pltpu.VMEM(query_out.shape, query_out.dtype),
             pltpu.VMEM(query_act.shape, query_act.dtype),
             pltpu.VMEM(out_basis.shape, out_basis.dtype),
             pltpu.VMEM(act_basis.shape, act_basis.dtype),
-            pltpu.VMEM((columns, width), jnp.float32),
             pltpu.SemaphoreType.DMA((2 * chunks + 2,)),
         ],
-        compiler_params=pltpu.CompilerParams(vmem_limit_bytes=24 * 2**20),
-    )(place, query_out, query_act, out_basis, act_basis)
-
-
-def pack_kernel(meta_ref, train_out, train_act, packed):
+        compiler_params=pltpu.CompilerParams(vmem_limit_bytes=60 * 2**20),
+    )(query_out, query_act, out_basis, act_basis)
+
+
+def pack_kernel(tokens_ref, ids_ref, train_out, train_act, packed):
     rows, ks = train_out.shape[1:]
     ka = train_act.shape[2]
-    keep = lax.broadcasted_iota(jnp.int32, (rows, ka), 0) < meta_ref[0]
-    act = jnp.where(keep, train_act[0].astype(jnp.float32), 0.0)
-    packed[:, :ks] = train_out[0]
-    packed[:, ks : ks + ka] = act.astype(packed.dtype)
-    ident = jnp.full((rows, LANES), meta_ref[1], jnp.int32).astype(jnp.float32)
-    packed[:, ks + ka :] = ident.astype(packed.dtype)
-
-
-def pack(train_out, train_act, train_tokens, train_ids):
+    keep = lax.broadcasted_iota(jnp.int32, (rows, ka), 0) < tokens_ref[0]
+    act = jnp.where(keep, train_act[0].astype(jnp.float32), 0.0).astype(packed.dtype)
+    ident = jnp.full((rows, LANES), ids_ref[0], jnp.int32).astype(jnp.float32).astype(packed.dtype)
+    for part in range(packed.shape[0]):
+        packed[part, :, :ks] = train_out[0]
+        packed[part, :, ks : ks + ka] = act
+        packed[part, :, ks + ka :] = ident
+
+
+def pack(train_out, train_act, train_tokens, train_ids, parts):
     rows, ks = train_out.shape[1:]
     width = ks + train_act.shape[2] + LANES
     return pl.pallas_call(
         pack_kernel,
-        out_shape=jax.ShapeDtypeStruct((rows, width), train_out.dtype),
-        in_specs=[pl.BlockSpec(memory_space=pltpu.SMEM)] + [pl.BlockSpec(memory_space=pltpu.VMEM)] * 2,
+        out_shape=jax.ShapeDtypeStruct((parts, rows, width), train_out.dtype),
+        in_specs=[pl.BlockSpec(memory_space=pltpu.SMEM)] * 2
+        + [pl.BlockSpec(memory_space=pltpu.VMEM)] * 2,
         out_specs=pl.BlockSpec(memory_space=pltpu.VMEM),
-    )(jnp.concatenate([train_tokens, train_ids]), train_out, train_act)
-
-
-def score_kernel(ks, ka, place_ref, coords, other_coords, eigen, other_eigen, *rest):
+    )(train_tokens, train_ids, train_out, train_act)
+
+
+def score_kernel(ks, ka, place_ref, pieces, eigen, other_eigen, *rest):
     blocks, out = rest[:-1], rest[-1]
     first = place_ref[0] == 0
     half = ks // 2
-    low, high = (
-        jnp.where(first, coords[...], other_coords[...]),
-        jnp.where(first, other_coords[...], coords[...]),
-    )
-    low_eigen, high_eigen = (
+    values = jnp.sum(pieces[...], axis=0)
+    coords = (values[0], values[1])
+    eigens = (
         jnp.where(first, eigen[...], other_eigen[...]),
         jnp.where(first, other_eigen[...], eigen[...]),
     )
-    act = jnp.concatenate([low[:, half:], high[:, half:]], axis=1)
+    act = jnp.concatenate([v[:, half:] for v in coords], axis=1)
     rows = jnp.concatenate([b[...].reshape(-1, b.shape[-1]) for b in blocks], axis=0)
     weights = rows[:, ks : ks + ka].astype(jnp.float32)
     column = lax.broadcasted_iota(jnp.int32, (rows.shape[0], LANES), 1).astype(jnp.float32)
     hot = rows[:, ks + ka :].astype(jnp.float32) == column
-    for q in range(low.shape[0] // RQ):
+    for q in range(act.shape[0] // RQ):
         cut = slice(q * RQ, (q + 1) * RQ)
         projected = None
-        for part, values, part_eigen in ((0, low, low_eigen), (1, high, high_eigen)):
+        for part in range(2):
             numer = lax.dot_general(
-                values[cut, :half],
+                coords[part][cut, :half],
                 act[cut],
                 (((0,), (0,)), ((), ())),
                 precision=lax.Precision.HIGHEST,
                 preferred_element_type=jnp.float32,
             )
-            precond = (numer / (part_eigen + damping)).astype(jnp.bfloat16)
+            precond = (numer / (eigens[part] + damping)).astype(jnp.bfloat16)
             term = jnp.dot(
                 rows[:, part * half : (part + 1) * half], precond, preferred_element_type=jnp.float32
             )
@@ -155,15 +143,15 @@
         out[q : q + 1, :] = scores[:, : out.shape[1]]
 
 
-def score(place, coords, other_coords, eigen, other_eigen, blocks, ks, ka, total):
+def score(core, pieces, eigen, other_eigen, blocks, ks, ka, total):
     return pl.pallas_call(
         functools.partial(score_kernel, ks, ka),
-        out_shape=jax.ShapeDtypeStruct((coords.shape[0] // RQ, total), jnp.float32),
+        out_shape=jax.ShapeDtypeStruct((pieces.shape[2] // RQ, total), jnp.float32),
         in_specs=[pl.BlockSpec(memory_space=pltpu.SMEM)]
-        + [pl.BlockSpec(memory_space=pltpu.VMEM)] * (4 + len(blocks)),
+        + [pl.BlockSpec(memory_space=pltpu.VMEM)] * (3 + len(blocks)),
         out_specs=pl.BlockSpec(memory_space=pltpu.VMEM),
         compiler_params=pltpu.CompilerParams(vmem_limit_bytes=32 * 2**20),
-    )(place, coords, other_coords, eigen, other_eigen, *blocks)
+    )(core, pieces, eigen, other_eigen, *blocks)
 
 
 def direct(
@@ -177,27 +165,20 @@
     train_tokens,
     train_ids,
 ):
-    parts = lax.axis_size("blk")
+    parts, cores = lax.axis_size("blk"), lax.axis_size("fsdp")
     ks, ka = train_out.shape[2], train_act.shape[2]
     swap = [(0, 1), (1, 0)]
-    packed = pack(train_out, train_act, train_tokens, train_ids)
+    pieces = project(query_out.T, query_act.T, out_basis, act_basis, parts, cores)
+    pieces = lax.all_to_all(
+        pieces.reshape(parts * cores, *pieces.shape[2:]), ("blk", "fsdp"), 0, 0, tiled=True
+    ).reshape(pieces.shape)
+    packed = pack(train_out, train_act, train_tokens, train_ids, parts)
+    stacked = lax.all_to_all(packed, "blk", 0, 0, tiled=True)
+    other = lax.ppermute(stacked, "fsdp", swap)
     other_eigen = lax.ppermute(eigenvalues, "fsdp", swap)
-    blocks = [packed]
-    for k in range(1, parts):
-        blocks.append(lax.ppermute(packed, "blk", [(s, (s + k) % parts) for s in range(parts)]))
-    stacked = jnp.stack(blocks)
-    other = lax.ppermute(stacked, "fsdp", swap)
-    place = lax.axis_index("blk").reshape(1)
-    pieces = project(place, query_out.T, query_act.T, out_basis, act_basis, parts)
-    coords = pieces[0]
-    for k in range(1, parts):
-        coords = coords + lax.ppermute(pieces[k], "blk", [(s, (s + k) % parts) for s in range(parts)])
-    other_coords = lax.ppermute(coords, "fsdp", swap)
     core = lax.axis_index("fsdp").reshape(1)
-    total = parts * 2 * train_out.shape[0]
-    return score(
-        core, coords, other_coords, eigenvalues, other_eigen, [stacked, other], ks, ka, total
-    )
+    total = parts * cores * train_out.shape[0]
+    return score(core, pieces, eigenvalues, other_eigen, [stacked, other], ks, ka, total)
 
 
 def score_block(precond, out_rows, act_rows, token_counts):

time: 46.5 us -> 41.9 us (0.901)
  blocking collectives: 0 us -> 20.5 us
  starting transfers between devices: 24.3 us -> 4.15 us
  local copies, waits for them, and re-layouts: 5.31 us -> 0.01 us
  Pallas kernels: 6.27 us -> 7.01 us
  other arithmetic: 0.6 us -> 0 us
    ppermute x15 -> x0, starting transfers between devices: 24.2 us -> none  [the longest x7 13.8 us: direct(): lax.ppermute(packed, 'blk', [(s, (s + k) % parts) for s in range(parts)])]
    all_to_all x0 -> x1, blocking collectives: none -> 20.5 us  [direct(): stacked = lax.all_to_all(packed, 'blk', 0, 0, tiled=True)]
    ppermute x15 -> x0, waiting for transfers between devices: 8.36 us -> none  [the longest x7 4.31 us: direct(): lax.ppermute(pieces[k], 'blk', [(s, (s + k) % parts) for s in range(parts)])]
    all_to_all x0 -> x1, waiting for transfers between devices: none -> 7.35 us  [direct(): lax.all_to_all(pieces.reshape(parts * cores, *pieces.shape[2:]), ('blk',...]
    unnamed x17 -> x2, local copies, waits for them, and re-layouts: 5.3 us -> 0.01 us
    all_to_all x0 -> x1, starting transfers between devices: none -> 3.68 us  [direct(): lax.all_to_all(pieces.reshape(parts * cores, *pieces.shape[2:]), ('blk',...]
    ppermute x1, waiting for transfers between devices: 0.01 us -> 1.16 us  [direct(): other_eigen = lax.ppermute(eigenvalues, 'fsdp', swap)]
    pallas_call x2, Pallas kernels: 3.81 us -> 4.56 us  [the longest x1 3 us: project(): pl.pallas_call(functools.partial(project_kernel, chunks), out_shape=jax.S...]
  transfers between devices with their start and end apart: 17 -> 3, of which waited for: 9 -> 2; matrix products, arithmetic and copies ran while one was open for 2% -> 0% of each run, Pallas kernels for 5% -> 7%
where the time goes in v2:
time: 41.9 us; the launch traced here: 41.5 us
  blocking collectives  20.5 us (49%)
  waiting for transfers between devices  8.51 us (20%)
  Pallas kernels  7.01 us (17%)
  starting transfers between devices  4.15 us (10%)
  between operations  1.32 us (3%)
    all_to_all x1, blocking collectives, direct(): stacked = lax.all_to_all(packed, 'blk', 0, 0, tiled=True)  20.5 us
    all_to_all x1, waiting for transfers between devices, direct(): lax.all_to_all(pieces.reshape(parts * cores, *pieces.shape[2:]), ('blk',...  7.35 us
    all_to_all x1, starting transfers between devices, direct(): lax.all_to_all(pieces.reshape(parts * cores, *pieces.shape[2:]), ('blk',...  3.68 us
    pallas_call x1, Pallas kernels, project(): pl.pallas_call(functools.partial(project_kernel, chunks), out_shape=jax.S...  3 us
    pallas_call x1, Pallas kernels, score(): pl.pallas_call(functools.partial(score_kernel, ks, ka), out_shape=jax.Sha...  2.45 us
    pallas_call x1, Pallas kernels, pack(): pl.pallas_call(pack_kernel, out_shape=jax.ShapeDtypeStruct((parts, rows,...  1.56 us
    ppermute x1, waiting for transfers between devices, direct(): other_eigen = lax.ppermute(eigenvalues, 'fsdp', swap)  1.16 us
  transfers between devices with their start and end apart: 3, of which 2 were waited for; matrix products, arithmetic and copies ran while one was open for 0% of the time, Pallas kernels for 7%

profile of v2, /device:TPU:0, one launch (start us, length us, event | category | flops | bytes accessed | tf_op | source)
XLA Modules:
  0.0 41.5 jit_solution(17507555715478590493)
XLA Ops:
  1.3 1.6 %shard_map.92 = bf16[8,32,896]{2,1,0:T(8,128)(2,1)} custom-call(s32[1]{0:T(128)S(6)} %copy.10.tokens_ref, s32[1]{0:T(128)S(6)} %copy.11.ids_ref, bf16[1,32,512]{2,1,0:T(8,128)(2,1)} %train_out.1, bf16[1,32,256]{2,1,0:T(8,128)(2,1)} %train_act.1), custom_call_target="tpu_custom_call" | custom-call | tf_op jit(solution)/shard_map/pallas_call | solution.py:101
  2.9 20.5 %all_to_all.10.rest_0_ = bf16[8,32,896]{2,1,0:T(8,128)(2,1)S(1)} all-to-all(bf16[8,32,896]{2,1,0:T(8,128)(2,1)} %shard_map.92), channel_id=1, replica_groups=mesh['groups'=2,'blk'=8,'fsdp'=2] {'blk'}, dimensions={0} | all-to-all | bytes 917504 | tf_op jit(solution)/shard_map/all_to_all | solution.py:176
  23.3 0.0 copy-start
  23.3 0.0 collective-permute-start.1
  23.3 3.0 %shard_map.91 = f32[8,2,8,384]{3,2,1,0:T(8,128)} custom-call(bf16[64,3584]{1,0:T(8,128)(2,1)} %bitcast.7, bf16[64,1024]{1,0:T(8,128)(2,1)} %bitcast.8, bf16[3584,256]{1,0:T(8,128)(2,1)} %out_basis.1, bf16[1024,128]{1,0:T(8,128)(2,1)} %act_basis.1), custom_call_target="tpu_custom_call" | custom-call | tf_op jit(solution)/shard_map/pallas_call | solution.py:70
  26.4 3.7 %all-to-all-start = ((f32[16,8,384]{2,1,0:T(8,128)}), f32[16,8,384]{2,1,0:T(8,128)S(1)}, u32[]{:S(2)}, u32[]{:S(2)}) async-start(f32[16,8,384]{2,1,0:T(8,128)} %bitcast.6), calls=%async_computation | async-start | bytes 393216 | tf_op jit(solution)/shard_map/all_to_all | solution.py:172
  30.0 0.0 copy-done
  30.1 0.5 %collective-permute-start = (f32[256,256]{1,0:T(8,128)S(1)}, f32[256,256]{1,0:T(8,128)S(1)}, u32[]{:S(2)}, u32[]{:S(2)}) collective-permute-start(f32[256,256]{1,0:T(8,128)S(1)} %copy-done), channel_id=1, source_target_pairs={{0,1},{1,0},{2,3},{3,2},{4,5},{5,4},{6,7},{7,6},{8,9},{9,8},{10,11... | collective-permute-start | bytes 786440 | tf_op jit(solution)/shard_map/ppermute | solution.py:178
  30.5 1.2 %collective-permute-done.other_eigen = f32[256,256]{1,0:T(8,128)S(1)} collective-permute-done((f32[256,256]{1,0:T(8,128)S(1)}, f32[256,256]{1,0:T(8,128)S(1)}, u32[]{:S(2)}, u32[]{:S(2)}) %collective-permute-start) | collective-permute-done | bytes 262176 | tf_op jit(solution)/shard_map/ppermute | solution.py:178
  31.7 7.3 %all-to-all-done = f32[16,8,384]{2,1,0:T(8,128)S(1)} async-done(((f32[16,8,384]{2,1,0:T(8,128)}), f32[16,8,384]{2,1,0:T(8,128)S(1)}, u32[]{:S(2)}, u32[]{:S(2)}) %all-to-all-start) | async-done | bytes 196640 | tf_op jit(solution)/shard_map/all_to_all | solution.py:172
  39.0 0.0 collective-permute-done.1.rest_1_
  39.0 2.5 %shard_map.93 = f32[2,16]{1,0:T(2,128)} custom-call(s32[1]{0:T(128)} %bitcast.place_ref, f32[8,2,8,384]{3,2,1,0:T(8,128)S(1)} %bitcast.5, f32[256,256]{1,0:T(8,128)S(1)} %copy-done, f32[256,256]{1,0:T(8,128)S(1)} %collective-permute-done.other_eigen, bf16[8,32,896]{2,1,0:T(8,128)(2,1)S(1)} %all_to_all.10.rest_0_, ...), custom_call_target="tpu_custom_call" | custom-call | tf_op jit(solution)/shard_map/pallas_call | solution.py:147
Async XLA Ops:
  23.3 6.7 %copy-start = (f32[256,256]{1,0:T(8,128)S(1)}, f32[256,256]{1,0:T(8,128)}, u32[]{:S(2)}) copy-start(f32[256,256]{1,0:T(8,128)} %eigen.1) | copy-start | bytes 786436
  23.3 15.7 %collective-permute-start.1 = (bf16[8,32,896]{2,1,0:T(8,128)(2,1)S(1)}, bf16[8,32,896]{2,1,0:T(8,128)(2,1)S(1)}, u32[]{:S(2)}, u32[]{:S(2)}) collective-permute-start(bf16[8,32,896]{2,1,0:T(8,128)(2,1)S(1)} %all_to_all.10.rest_0_), channel_id=1, source_target_pairs={{0,1},{1,0},{2,3},{3,2},{4,5},{5,4},{6,7},{7,6},{8,9},{9,8},{10,11... | collective-permute-start | bytes 1376264 | tf_op jit(solution)/shard_map/ppermute | solution.py:177
  26.4 12.7 %all-to-all-start = ((f32[16,8,384]{2,1,0:T(8,128)}), f32[16,8,384]{2,1,0:T(8,128)S(1)}, u32[]{:S(2)}, u32[]{:S(2)}) async-start(f32[16,8,384]{2,1,0:T(8,128)} %bitcast.6), calls=%async_computation | async-start | bytes 393216 | tf_op jit(solution)/shard_map/all_to_all | solution.py:172
  30.1 1.6 %collective-permute-start = (f32[256,256]{1,0:T(8,128)S(1)}, f32[256,256]{1,0:T(8,128)S(1)}, u32[]{:S(2)}, u32[]{:S(2)}) collective-permute-start(f32[256,256]{1,0:T(8,128)S(1)} %copy-done), channel_id=1, source_target_pairs={{0,1},{1,0},{2,3},{3,2},{4,5},{5,4},{6,7},{7,6},{8,9},{9,8},{10,11... | collective-permute-start | bytes 786440 | tf_op jit(solution)/shard_map/ppermute | solution.py:178

commit v3 on v2

--- a/solution.py
+++ b/solution.py
@@ -23,7 +23,19 @@
 
 
 def project_kernel(
-    chunks, query_out, query_act, out_basis, act_basis, pieces, q_out, q_act, b_out, b_act, sems
+    chunks,
+    place_ref,
+    query_out,
+    query_act,
+    out_basis,
+    act_basis,
+    pieces,
+    q_out,
+    q_act,
+    b_out,
+    b_act,
+    total,
+    sems,
 ):
     rows = query_out.shape[1] // chunks
     copies = []
@@ -54,33 +66,35 @@
     for copy in copies[chunks]:
         copy.wait()
     act_part = jnp.dot(q_act[...], b_act[...], preferred_element_type=jnp.float32)
-    parts, cores, local_rows, _ = pieces.shape
     half_ks = b_out.shape[1]
+    total[:, :half_ks] = out_part
+    total[:, half_ks:] = act_part
+    parts, local_rows, _ = pieces.shape
     for part in range(parts):
-        cut = slice(part * local_rows, (part + 1) * local_rows)
-        for core in range(cores):
-            pieces[part, core, :, :half_ks] = out_part[cut]
-            pieces[part, core, :, half_ks:] = act_part[cut]
-
-
-def project(query_out, query_act, out_basis, act_basis, parts, cores):
+        start = pl.multiple_of((place_ref[0] ^ part) * local_rows, local_rows)
+        pieces[part] = total[pl.ds(start, local_rows), :]
+
+
+def project(place, query_out, query_act, out_basis, act_basis, parts):
     columns = query_out.shape[0]
     width = out_basis.shape[1] + act_basis.shape[1]
     chunks = chunk_count(query_out.shape[1])
     return pl.pallas_call(
         functools.partial(project_kernel, chunks),
-        out_shape=jax.ShapeDtypeStruct((parts, cores, columns // parts, width), jnp.float32),
-        in_specs=[pl.BlockSpec(memory_space=pltpu.HBM)] * 4,
+        out_shape=jax.ShapeDtypeStruct((parts, columns // parts, width), jnp.float32),
+        in_specs=[pl.BlockSpec(memory_space=pltpu.SMEM)]
+        + [pl.BlockSpec(memory_space=pltpu.HBM)] * 4,
         out_specs=pl.BlockSpec(memory_space=pltpu.VMEM),
         scratch_shapes=[
             pltpu.VMEM(query_out.shape, query_out.dtype),
             pltpu.VMEM(query_act.shape, query_act.dtype),
             pltpu.VMEM(out_basis.shape, out_basis.dtype),
             pltpu.VMEM(act_basis.shape, act_basis.dtype),
+            pltpu.VMEM((columns, width), jnp.float32),
             pltpu.SemaphoreType.DMA((2 * chunks + 2,)),
         ],
         compiler_params=pltpu.CompilerParams(vmem_limit_bytes=60 * 2**20),
-    )(query_out, query_act, out_basis, act_basis)
+    )(place, query_out, query_act, out_basis, act_basis)
 
 
 def pack_kernel(tokens_ref, ids_ref, train_out, train_act, packed):
@@ -89,30 +103,31 @@
     keep = lax.broadcasted_iota(jnp.int32, (rows, ka), 0) < tokens_ref[0]
     act = jnp.where(keep, train_act[0].astype(jnp.float32), 0.0).astype(packed.dtype)
     ident = jnp.full((rows, LANES), ids_ref[0], jnp.int32).astype(jnp.float32).astype(packed.dtype)
-    for part in range(packed.shape[0]):
-        packed[part, :, :ks] = train_out[0]
-        packed[part, :, ks : ks + ka] = act
-        packed[part, :, ks + ka :] = ident
-
-
-def pack(train_out, train_act, train_tokens, train_ids, parts):
+    packed[0, :, :ks] = train_out[0]
+    packed[0, :, ks : ks + ka] = act
+    packed[0, :, ks + ka :] = ident
+
+
+def pack(train_out, train_act, train_tokens, train_ids):
     rows, ks = train_out.shape[1:]
     width = ks + train_act.shape[2] + LANES
     return pl.pallas_call(
         pack_kernel,
-        out_shape=jax.ShapeDtypeStruct((parts, rows, width), train_out.dtype),
+        out_shape=jax.ShapeDtypeStruct((1, rows, width), train_out.dtype),
         in_specs=[pl.BlockSpec(memory_space=pltpu.SMEM)] * 2
         + [pl.BlockSpec(memory_space=pltpu.VMEM)] * 2,
         out_specs=pl.BlockSpec(memory_space=pltpu.VMEM),
     )(train_tokens, train_ids, train_out, train_act)
 
 
-def score_kernel(ks, ka, place_ref, pieces, eigen, other_eigen, *rest):
+def score_kernel(ks, ka, place_ref, own, other, eigen, other_eigen, *rest):
     blocks, out = rest[:-1], rest[-1]
     first = place_ref[0] == 0
     half = ks // 2
-    values = jnp.sum(pieces[...], axis=0)
-    coords = (values[0], values[1])
+    coords = (
+        jnp.where(first, own[...], other[...]),
+        jnp.where(first, other[...], own[...]),
+    )
     eigens = (
         jnp.where(first, eigen[...], other_eigen[...]),
         jnp.where(first, other_eigen[...], eigen[...]),
@@ -143,15 +158,15 @@
         out[q : q + 1, :] = scores[:, : out.shape[1]]
 
 
-def score(core, pieces, eigen, other_eigen, blocks, ks, ka, total):
+def score(core, own, other, eigen, other_eigen, blocks, ks, ka, total):
     return pl.pallas_call(
         functools.partial(score_kernel, ks, ka),
-        out_shape=jax.ShapeDtypeStruct((pieces.shape[2] // RQ, total), jnp.float32),
+        out_shape=jax.ShapeDtypeStruct((own.shape[0] // RQ, total), jnp.float32),
         in_specs=[pl.BlockSpec(memory_space=pltpu.SMEM)]
-        + [pl.BlockSpec(memory_space=pltpu.VMEM)] * (3 + len(blocks)),
+        + [pl.BlockSpec(memory_space=pltpu.VMEM)] * (4 + len(blocks)),
         out_specs=pl.BlockSpec(memory_space=pltpu.VMEM),
         compiler_params=pltpu.CompilerParams(vmem_limit_bytes=32 * 2**20),
-    )(core, pieces, eigen, other_eigen, *blocks)
+    )(core, own, other, eigen, other_eigen, *blocks)
 
 
 def direct(
@@ -168,17 +183,30 @@
     parts, cores = lax.axis_size("blk"), lax.axis_size("fsdp")
     ks, ka = train_out.shape[2], train_act.shape[2]
     swap = [(0, 1), (1, 0)]
-    pieces = project(query_out.T, query_act.T, out_basis, act_basis, parts, cores)
-    pieces = lax.all_to_all(
-        pieces.reshape(parts * cores, *pieces.shape[2:]), ("blk", "fsdp"), 0, 0, tiled=True
-    ).reshape(pieces.shape)
-    packed = pack(train_out, train_act, train_tokens, train_ids, parts)
-    stacked = lax.all_to_all(packed, "blk", 0, 0, tiled=True)
-    other = lax.ppermute(stacked, "fsdp", swap)
+
+    def across(x, bit):
+        return lax.ppermute(x, "blk", [(s, s ^ bit) for s in range(parts)])
+
+    bits = [1 << i for i in range(parts.bit_length() - 1)]
+    place = lax.axis_index("blk").reshape(1)
+    core = lax.axis_index("fsdp").reshape(1)
+    block = pack(train_out, train_act, train_tokens, train_ids)
+    for bit in reversed(bits):
+        block = jnp.concatenate([block, across(block, bit)], axis=0)
+    other_block = lax.ppermute(block, "fsdp", swap)
     other_eigen = lax.ppermute(eigenvalues, "fsdp", swap)
-    core = lax.axis_index("fsdp").reshape(1)
+    pieces = project(place, query_out.T, query_act.T, out_basis, act_basis, parts)
+    pieces = pieces.reshape((2,) * len(bits) + pieces.shape[1:])
+    for bit in bits:
+        moved = lax.index_in_dim(pieces, 1, len(bits) - bit.bit_length(), keepdims=True)
+        kept = lax.index_in_dim(pieces, 0, len(bits) - bit.bit_length(), keepdims=True)
+        pieces = kept + across(moved, bit)
+    coords = pieces.reshape(pieces.shape[-2:])
+    other = lax.ppermute(coords, "fsdp", swap)
     total = parts * cores * train_out.shape[0]
-    return score(core, pieces, eigenvalues, other_eigen, [stacked, other], ks, ka, total)
+    return score(
+        core, coords, other, eigenvalues, other_eigen, [block, other_block], ks, ka, total
+    )
 
 
 def score_block(precond, out_rows, act_rows, token_counts):
@@ -235,7 +263,8 @@
 
 
 def solution(mesh):
-    few = mesh.shape["blk"] <= MOST_DIRECT and mesh.shape["fsdp"] == 2
+    parts = mesh.shape["blk"]
+    few = parts <= MOST_DIRECT and parts & (parts - 1) == 0 and mesh.shape["fsdp"] == 2
     return jax.shard_map(
         direct if few else gathered,
         mesh=mesh,

time: 41.9 us -> 34 us (0.81)
  blocking collectives: 20.5 us -> 0 us
  starting transfers between devices: 4.15 us -> 12 us
  waiting for transfers between devices: 8.51 us -> 10.9 us
  other arithmetic: 0 us -> 1.74 us
  local copies, waits for them, and re-layouts: 0.01 us -> 0.82 us
    all_to_all x1 -> x0, blocking collectives: 20.5 us -> none  [direct(): stacked = lax.all_to_all(packed, 'blk', 0, 0, tiled=True)]
    ppermute x1 -> x8, starting transfers between devices: 0.01 us -> 12 us  [the longest x6 11.9 us: across(): return lax.ppermute(x, 'blk', [(s, s ^ bit) for s in range(parts)])]
    ppermute x1 -> x8, waiting for transfers between devices: 0.01 us -> 10.9 us  [the longest x6 9.75 us: across(): return lax.ppermute(x, 'blk', [(s, s ^ bit) for s in range(parts)])]
    all_to_all x1 -> x0, waiting for transfers between devices: 7.35 us -> none  [direct(): lax.all_to_all(pieces.reshape(parts * cores, *pieces.shape[2:]), ('blk',...]
    all_to_all x1 -> x0, starting transfers between devices: 3.68 us -> none  [direct(): lax.all_to_all(pieces.reshape(parts * cores, *pieces.shape[2:]), ('blk',...]
    ppermute x1, waiting for transfers between devices: 1.16 us -> 0.01 us  [direct(): other_eigen = lax.ppermute(eigenvalues, 'fsdp', swap)]
    concatenate x0 -> x3, other arithmetic: none -> 0.93 us  [direct(): block = jnp.concatenate([block, across(block, bit)], axis=0)]
    slice x0 -> x3, local copies, waits for them, and re-layouts: none -> 0.81 us  [direct(): lax.index_in_dim(pieces, 1, len(bits) - bit.bit_length(), keepdims=True)]
  transfers between devices with their start and end apart: 3 -> 9, of which waited for: 2 -> 6; matrix products, arithmetic and copies ran while one was open for 0% -> 5% of each run, Pallas kernels for 7% -> 9%
where the time goes in v3:
time: 34 us; the launch traced here: 33.6 us
  starting transfers between devices  12 us (35%)
  waiting for transfers between devices  10.9 us (32%)
  Pallas kernels  6.83 us (20%)
  other arithmetic  1.74 us (5%)
  between operations  1.35 us (4%)
  local copies, waits for them, and re-layouts  0.82 us (2%)
    ppermute x6, starting transfers between devices, across(): return lax.ppermute(x, 'blk', [(s, s ^ bit) for s in range(parts)])  11.9 us
    ppermute x6, waiting for transfers between devices, across(): return lax.ppermute(x, 'blk', [(s, s ^ bit) for s in range(parts)])  9.75 us
    pallas_call x1, Pallas kernels, project(): pl.pallas_call(functools.partial(project_kernel, chunks), out_shape=jax.S...  2.94 us
    pallas_call x1, Pallas kernels, score(): pl.pallas_call(functools.partial(score_kernel, ks, ka), out_shape=jax.Sha...  2.46 us
    pallas_call x1, Pallas kernels, pack(): pl.pallas_call(pack_kernel, out_shape=jax.ShapeDtypeStruct((1, rows, widt...  1.43 us
    ppermute x1, waiting for transfers between devices, direct(): other = lax.ppermute(coords, 'fsdp', swap)  1.18 us
    concatenate x3, other arithmetic, direct(): block = jnp.concatenate([block, across(block, bit)], axis=0)  0.93 us
    slice x3, local copies, waits for them, and re-layouts, direct(): lax.index_in_dim(pieces, 1, len(bits) - bit.bit_length(), keepdims=True)  0.81 us
  transfers between devices with their start and end apart: 9, of which 6 were waited for; matrix products, arithmetic and copies ran while one was open for 5% of the time, Pallas kernels for 9%

profile of v3, /device:TPU:0, one launch (start us, length us, event | category | flops | bytes accessed | tf_op | source)
XLA Modules:
  0.0 33.6 jit_solution(3669255148467455637)
XLA Ops:
  1.3 1.4 %shard_map.92 = bf16[1,32,896]{2,1,0:T(8,128)(2,1)} custom-call(s32[1]{0:T(128)S(6)} %copy.10.tokens_ref, s32[1]{0:T(128)S(6)} %copy.11.ids_ref, bf16[1,32,512]{2,1,0:T(8,128)(2,1)} %train_out.1, bf16[1,32,256]{2,1,0:T(8,128)(2,1)} %train_act.1), custom_call_target="tpu_custom_call" | custom-call | tf_op jit(solution)/shard_map/pallas_call | solution.py:114
  2.7 4.0 %collective-permute-start.5 = (bf16[1,32,896]{2,1,0:T(8,128)(2,1)}, bf16[1,32,896]{2,1,0:T(8,128)(2,1)S(1)}, u32[]{:S(2)}, u32[]{:S(2)}) collective-permute-start(bf16[1,32,896]{2,1,0:T(8,128)(2,1)} %shard_map.92), channel_id=1, source_target_pairs={{0,8},{2,10},{4,12},{6,14},{8,0},{10,2},{12,4},{14,6},{1,9},{3,11}... | collective-permute-start | bytes 172040 | tf_op jit(solution)/shard_map/ppermute | solution.py:188
  6.8 3.0 %collective-permute-done.5 = bf16[1,32,896]{2,1,0:T(8,128)(2,1)S(1)} collective-permute-done((bf16[1,32,896]{2,1,0:T(8,128)(2,1)}, bf16[1,32,896]{2,1,0:T(8,128)(2,1)S(1)}, u32[]{:S(2)}, u32[]{:S(2)}) %collective-permute-start.5) | collective-permute-done | bytes 57376 | tf_op jit(solution)/shard_map/ppermute | solution.py:188
  9.8 0.8 %pad_maximum_fusion.2 = bf16[2,32,896]{2,1,0:T(8,128)(2,1)S(1)} fusion(bf16[1,32,896]{2,1,0:T(8,128)(2,1)S(1)} %collective-permute-done.5, bf16[1,32,896]{2,1,0:T(8,128)(2,1)} %shard_map.92), kind=kLoop, calls=%fused_computation.2 | loop fusion | flops 57344 | bytes 229376 | tf_op jit(solution)/shard_map/concatenate | solution.py:195
  10.7 1.3 %collective-permute-start.6 = (bf16[2,32,896]{2,1,0:T(8,128)(2,1)S(1)}, bf16[2,32,896]{2,1,0:T(8,128)(2,1)S(1)}, u32[]{:S(2)}, u32[]{:S(2)}) collective-permute-start(bf16[2,32,896]{2,1,0:T(8,128)(2,1)S(1)} %pad_maximum_fusion.2), channel_id=1, source_target_pairs={{0,4},{2,6},{4,0},{6,2},{8,12},{10,14},{12,8},{14,10},{1,5},{3,7},... | collective-permute-start | bytes 344072 | tf_op jit(solution)/shard_map/ppermute | solution.py:188
  12.0 2.9 %shard_map.91 = f32[8,8,384]{2,1,0:T(8,128)} custom-call(s32[1]{0:T(128)} %bitcast.1.place_ref, bf16[64,3584]{1,0:T(8,128)(2,1)} %bitcast.7, bf16[64,1024]{1,0:T(8,128)(2,1)} %bitcast.10, bf16[3584,256]{1,0:T(8,128)(2,1)} %out_basis.1, bf16[1024,128]{1,0:T(8,128)(2,1)} %act_basis.1), custom_call_target="tpu_custom_call" | custom-call | tf_op jit(solution)/shard_map/pallas_call | solution.py:82
  14.9 0.8 %slice.25 = f32[2,2,1,8,384]{4,3,2,1,0:T(8,128)S(1)} slice(f32[2,2,2,8,384]{4,3,2,1,0:T(8,128)} %bitcast.8), slice={[0:2], [0:2], [1:2], [0:8], [0:384]} | slice | bytes 98304 | tf_op jit(solution)/shard_map/slice | solution.py:201
  15.7 1.6 %collective-permute-start = (f32[2,2,1,8,384]{4,3,2,1,0:T(8,128)S(1)}, f32[2,2,1,8,384]{4,3,2,1,0:T(8,128)S(1)}, u32[]{:S(2)}, u32[]{:S(2)}) collective-permute-start(f32[2,2,1,8,384]{4,3,2,1,0:T(8,128)S(1)} %slice.25), channel_id=1, source_target_pairs={{0,2},{2,0},{4,6},{6,4},{8,10},{10,8},{12,14},{14,12},{1,3},{3,1},... | collective-permute-start | bytes 147464 | tf_op jit(solution)/shard_map/ppermute | solution.py:188
  17.3 0.0 collective-permute-done.6
  17.3 0.6 %collective-permute-start.7 = (bf16[4,32,896]{2,1,0:T(8,128)(2,1)S(1)}, bf16[4,32,896]{2,1,0:T(8,128)(2,1)S(1)}, u32[]{:S(2)}, u32[]{:S(2)}) collective-permute-start(bf16[4,32,896]{2,1,0:T(8,128)(2,1)S(1)} %pad_maximum_fusion.1), channel_id=1, source_target_pairs={{0,2},{2,0},{4,6},{6,4},{8,10},{10,8},{12,14},{14,12},{1,3},{3,1},... | collective-permute-start | bytes 688136 | tf_op jit(solution)/shard_map/ppermute | solution.py:188
  17.9 2.4 %collective-permute-done = f32[2,2,1,8,384]{4,3,2,1,0:T(8,128)S(1)} collective-permute-done((f32[2,2,1,8,384]{4,3,2,1,0:T(8,128)S(1)}, f32[2,2,1,8,384]{4,3,2,1,0:T(8,128)S(1)}, u32[]{:S(2)}, u32[]{:S(2)}) %collective-permute-start) | collective-permute-done | bytes 49184 | tf_op jit(solution)/shard_map/ppermute | solution.py:188
  20.3 0.8 %slice_add_fusion = f32[2,2,1,8,384]{4,3,2,1,0:T(8,128)S(1)} fusion(f32[2,2,1,8,384]{4,3,2,1,0:T(8,128)S(1)} %collective-permute-done, f32[2,2,2,8,384]{4,3,2,1,0:T(8,128)} %bitcast.9), kind=kLoop, calls=%fused_computation.3 | loop fusion | flops 12288 | bytes 147456 | tf_op jit(solution)/shard_map/add | solution.py:203
  21.1 1.2 %collective-permute-start.1 = (f32[2,1,1,8,384]{4,3,2,1,0:T(8,128)S(1)}, f32[2,1,1,8,384]{4,3,2,1,0:T(8,128)S(1)}, u32[]{:S(2)}, u32[]{:S(2)}) collective-permute-start(f32[2,1,1,8,384]{4,3,2,1,0:T(8,128)S(1)} %slice.27), channel_id=1, source_target_pairs={{0,4},{2,6},{4,0},{6,2},{8,12},{10,14},{12,8},{14,10},{1,5},{3,7},... | collective-permute-start | bytes 73736 | tf_op jit(solution)/shard_map/ppermute | solution.py:188
  22.3 1.3 %collective-permute-done.7 = bf16[4,32,896]{2,1,0:T(8,128)(2,1)S(1)} collective-permute-done((bf16[4,32,896]{2,1,0:T(8,128)(2,1)S(1)}, bf16[4,32,896]{2,1,0:T(8,128)(2,1)S(1)}, u32[]{:S(2)}, u32[]{:S(2)}) %collective-permute-start.7) | collective-permute-done | bytes 229408 | tf_op jit(solution)/shard_map/ppermute | solution.py:188
  23.6 0.1 pad_maximum_fusion.rest_0_
  23.7 0.1 collective-permute-start.8
  23.7 1.3 %collective-permute-done.1 = f32[2,1,1,8,384]{4,3,2,1,0:T(8,128)S(1)} collective-permute-done((f32[2,1,1,8,384]{4,3,2,1,0:T(8,128)S(1)}, f32[2,1,1,8,384]{4,3,2,1,0:T(8,128)S(1)}, u32[]{:S(2)}, u32[]{:S(2)}) %collective-permute-start.1) | collective-permute-done | bytes 24608 | tf_op jit(solution)/shard_map/ppermute | solution.py:188
  25.0 3.3 %collective-permute-start.2 = (f32[1,1,1,8,384]{4,3,2,1,0:T(8,128)S(1)}, f32[1,1,1,8,384]{4,3,2,1,0:T(8,128)S(1)}, u32[]{:S(2)}, u32[]{:S(2)}) collective-permute-start(f32[1,1,1,8,384]{4,3,2,1,0:T(8,128)S(1)} %slice.29), channel_id=1, source_target_pairs={{0,8},{2,10},{4,12},{6,14},{8,0},{10,2},{12,4},{14,6},{1,9},{3,11}... | collective-permute-start | bytes 36872 | tf_op jit(solution)/shard_map/ppermute | solution.py:188
  28.3 1.7 %collective-permute-done.2 = f32[1,1,1,8,384]{4,3,2,1,0:T(8,128)S(1)} collective-permute-done((f32[1,1,1,8,384]{4,3,2,1,0:T(8,128)S(1)}, f32[1,1,1,8,384]{4,3,2,1,0:T(8,128)S(1)}, u32[]{:S(2)}, u32[]{:S(2)}) %collective-permute-start.2) | collective-permute-done | bytes 12320 | tf_op jit(solution)/shard_map/ppermute | solution.py:188
  30.0 0.0 collective-permute-start.3
  30.0 1.2 %collective-permute-done.3.other = f32[8,384]{1,0:T(8,128)S(1)} collective-permute-done((f32[8,384]{1,0:T(8,128)S(1)}, f32[8,384]{1,0:T(8,128)S(1)}, u32[]{:S(2)}, u32[]{:S(2)}) %collective-permute-start.3) | collective-permute-done | bytes 12320 | tf_op jit(solution)/shard_map/ppermute | solution.py:205
  31.2 0.0 collective-permute-done.4.other_eigen
  31.2 0.0 collective-permute-done.8.rest_1_
  31.2 2.5 %shard_map.93 = f32[2,16]{1,0:T(2,128)} custom-call(s32[1]{0:T(128)} %bitcast.place_ref, f32[8,384]{1,0:T(8,128)S(1)} %fusion.own, f32[8,384]{1,0:T(8,128)S(1)} %collective-permute-done.3.other, f32[256,256]{1,0:T(8,128)S(1)} %copy-done, f32[256,256]{1,0:T(8,128)S(1)} %collective-permute-done.4.other_eigen, bf16[8,32,896]{2,1,0:T(8,128)(2,1)S(1)} %pad_maximum_fusion.rest_0_, ...), custom_call_target="tpu_custom_call" | custom-call | tf_op jit(solution)/shard_map/pallas_call | solution.py:162
  (10 shorter events, 0.1 us)
Async XLA Ops:
  1.3 16.6 %copy-start = (f32[256,256]{1,0:T(8,128)S(1)}, f32[256,256]{1,0:T(8,128)}, u32[]{:S(2)}) copy-start(f32[256,256]{1,0:T(8,128)} %eigen.1) | copy-start | bytes 786436
  2.7 14.6 %copy-start.1 = (bf16[1,32,896]{2,1,0:T(8,128)(2,1)S(1)}, bf16[1,32,896]{2,1,0:T(8,128)(2,1)}, u32[]{:S(2)}) copy-start(bf16[1,32,896]{2,1,0:T(8,128)(2,1)} %shard_map.92) | copy-start | bytes 172036
  2.7 7.1 %collective-permute-start.5 = (bf16[1,32,896]{2,1,0:T(8,128)(2,1)}, bf16[1,32,896]{2,1,0:T(8,128)(2,1)S(1)}, u32[]{:S(2)}, u32[]{:S(2)}) collective-permute-start(bf16[1,32,896]{2,1,0:T(8,128)(2,1)} %shard_map.92), channel_id=1, source_target_pairs={{0,8},{2,10},{4,12},{6,14},{8,0},{10,2},{12,4},{14,6},{1,9},{3,11}... | collective-permute-start | bytes 172040 | tf_op jit(solution)/shard_map/ppermute | solution.py:188
  10.7 6.6 %collective-permute-start.6 = (bf16[2,32,896]{2,1,0:T(8,128)(2,1)S(1)}, bf16[2,32,896]{2,1,0:T(8,128)(2,1)S(1)}, u32[]{:S(2)}, u32[]{:S(2)}) collective-permute-start(bf16[2,32,896]{2,1,0:T(8,128)(2,1)S(1)} %pad_maximum_fusion.2), channel_id=1, source_target_pairs={{0,4},{2,6},{4,0},{6,2},{8,12},{10,14},{12,8},{14,10},{1,5},{3,7},... | collective-permute-start | bytes 344072 | tf_op jit(solution)/shard_map/ppermute | solution.py:188
  15.7 4.6 %collective-permute-start = (f32[2,2,1,8,384]{4,3,2,1,0:T(8,128)S(1)}, f32[2,2,1,8,384]{4,3,2,1,0:T(8,128)S(1)}, u32[]{:S(2)}, u32[]{:S(2)}) collective-permute-start(f32[2,2,1,8,384]{4,3,2,1,0:T(8,128)S(1)} %slice.25), channel_id=1, source_target_pairs={{0,2},{2,0},{4,6},{6,4},{8,10},{10,8},{12,14},{14,12},{1,3},{3,1},... | collective-permute-start | bytes 147464 | tf_op jit(solution)/shard_map/ppermute | solution.py:188
  17.3 6.3 %collective-permute-start.7 = (bf16[4,32,896]{2,1,0:T(8,128)(2,1)S(1)}, bf16[4,32,896]{2,1,0:T(8,128)(2,1)S(1)}, u32[]{:S(2)}, u32[]{:S(2)}) collective-permute-start(bf16[4,32,896]{2,1,0:T(8,128)(2,1)S(1)} %pad_maximum_fusion.1), channel_id=1, source_target_pairs={{0,2},{2,0},{4,6},{6,4},{8,10},{10,8},{12,14},{14,12},{1,3},{3,1},... | collective-permute-start | bytes 688136 | tf_op jit(solution)/shard_map/ppermute | solution.py:188
  17.9 13.3 %collective-permute-start.4 = (f32[256,256]{1,0:T(8,128)S(1)}, f32[256,256]{1,0:T(8,128)S(1)}, u32[]{:S(2)}, u32[]{:S(2)}) collective-permute-start(f32[256,256]{1,0:T(8,128)S(1)} %copy-done), channel_id=1, source_target_pairs={{0,1},{1,0},{2,3},{3,2},{4,5},{5,4},{6,7},{7,6},{8,9},{9,8},{10,11... | collective-permute-start | bytes 786440 | tf_op jit(solution)/shard_map/ppermute | solution.py:197
  21.1 3.9 %collective-permute-start.1 = (f32[2,1,1,8,384]{4,3,2,1,0:T(8,128)S(1)}, f32[2,1,1,8,384]{4,3,2,1,0:T(8,128)S(1)}, u32[]{:S(2)}, u32[]{:S(2)}) collective-permute-start(f32[2,1,1,8,384]{4,3,2,1,0:T(8,128)S(1)} %slice.27), channel_id=1, source_target_pairs={{0,4},{2,6},{4,0},{6,2},{8,12},{10,14},{12,8},{14,10},{1,5},{3,7},... | collective-permute-start | bytes 73736 | tf_op jit(solution)/shard_map/ppermute | solution.py:188
  23.7 7.5 %collective-permute-start.8 = (bf16[8,32,896]{2,1,0:T(8,128)(2,1)S(1)}, bf16[8,32,896]{2,1,0:T(8,128)(2,1)S(1)}, u32[]{:S(2)}, u32[]{:S(2)}) collective-permute-start(bf16[8,32,896]{2,1,0:T(8,128)(2,1)S(1)} %pad_maximum_fusion.rest_0_), channel_id=1, source_target_pairs={{0,1},{1,0},{2,3},{3,2},{4,5},{5,4},{6,7},{7,6},{8,9},{9,8},{10,11... | collective-permute-start | bytes 1376264 | tf_op jit(solution)/shard_map/ppermute | solution.py:196
  25.0 4.9 %collective-permute-start.2 = (f32[1,1,1,8,384]{4,3,2,1,0:T(8,128)S(1)}, f32[1,1,1,8,384]{4,3,2,1,0:T(8,128)S(1)}, u32[]{:S(2)}, u32[]{:S(2)}) collective-permute-start(f32[1,1,1,8,384]{4,3,2,1,0:T(8,128)S(1)} %slice.29), channel_id=1, source_target_pairs={{0,8},{2,10},{4,12},{6,14},{8,0},{10,2},{12,4},{14,6},{1,9},{3,11}... | collective-permute-start | bytes 36872 | tf_op jit(solution)/shard_map/ppermute | solution.py:188
  30.0 1.2 %collective-permute-start.3 = (f32[8,384]{1,0:T(8,128)S(1)}, f32[8,384]{1,0:T(8,128)S(1)}, u32[]{:S(2)}, u32[]{:S(2)}) collective-permute-start(f32[8,384]{1,0:T(8,128)S(1)} %fusion.own), channel_id=1, source_target_pairs={{0,1},{1,0},{2,3},{3,2},{4,5},{5,4},{6,7},{7,6},{8,9},{9,8},{10,11... | collective-permute-start | bytes 36872 | tf_op jit(solution)/shard_map/ppermute | solution.py:205

commit v4 on v3

v4 whole, which is shorter than its diff:
```python
import functools

import jax
import jax.numpy as jnp
from jax import lax
from jax.experimental import pallas as pl
from jax.experimental.pallas import tpu as pltpu
from jax.sharding import PartitionSpec as P

RQ = 4
LANES = 128
MOST_DIRECT = 16


damping = 0.1


def chunk_count(rows):
    for chunks in (4, 2):
        if rows % (chunks * LANES) == 0:
            return chunks
    return 1


def project_kernel(
    chunks,
    place_ref,
    tokens_ref,
    ids_ref,
    query_out,
    query_act,
    out_basis,
    act_basis,
    pieces,
    q_out,
    q_act,
    b_out,
    b_act,
    sems,
):
    rows = query_out.shape[1] // chunks
    copies = []
    for c in range(chunks):
        cut = pl.ds(c * rows, rows)
        copies.append(
            (
                pltpu.make_async_copy(query_out.at[:, cut], q_out.at[:, cut], sems.at[2 * c]),
                pltpu.make_async_copy(out_basis.at[cut, :], b_out.at[cut, :], sems.at[2 * c + 1]),
            )
        )
    copies.append(
        (
            pltpu.make_async_copy(query_act, q_act, sems.at[2 * chunks]),
            pltpu.make_async_copy(act_basis, b_act, sems.at[2 * chunks + 1]),
        )
    )
    for pair in copies:
        for copy in pair:
            copy.start()
    parts, local_rows, _ = pieces.shape
    half_ks, half_ka = b_out.shape[1], b_act.shape[1]
    row = lax.broadcasted_iota(jnp.int32, (local_rows, LANES), 0)
    lane = lax.broadcasted_iota(jnp.int32, (local_rows, LANES), 1)
    facts = jnp.where(lane < LANES // 2, ids_ref[0], tokens_ref[0]).astype(jnp.float32)
    for part in range(parts):
        slot = doubling_slot(part, parts)
        pieces[place_ref[0] ^ part, :, half_ks + half_ka :] = jnp.where(row == slot, facts, 0.0)
    out_part = None
    for c in range(chunks):
        for copy in copies[c]:
            copy.wait()
        cut = pl.ds(c * rows, rows)
        term = jnp.dot(q_out[:, cut], b_out[cut, :], preferred_element_type=jnp.float32)
        out_part = term if out_part is None else out_part + term
    pieces[:, :, :half_ks] = out_part.reshape(parts, local_rows, half_ks)
    for copy in copies[chunks]:
        copy.wait()
    act_part = jnp.dot(q_act[...], b_act[...], preferred_element_type=jnp.float32)
    pieces[:, :, half_ks : half_ks + half_ka] = act_part.reshape(parts, local_rows, half_ka)


def doubling_slot(distance, parts):
    bits = parts.bit_length() - 1
    return sum(1 << (bits - 1 - i) for i in range(bits) if distance >> i & 1)


def project(place, tokens, ids, query_out, query_act, out_basis, act_basis, parts):
    columns = query_out.shape[0]
    width = out_basis.shape[1] + act_basis.shape[1] + LANES
    chunks = chunk_count(query_out.shape[1])
    return pl.pallas_call(
        functools.partial(project_kernel, chunks),
        out_shape=jax.ShapeDtypeStruct((parts, columns // parts, width), jnp.float32),
        in_specs=[pl.BlockSpec(memory_space=pltpu.SMEM)] * 3
        + [pl.BlockSpec(memory_space=pltpu.HBM)] * 4,
        out_specs=pl.BlockSpec(memory_space=pltpu.VMEM),
        scratch_shapes=[
            pltpu.VMEM(query_out.shape, query_out.dtype),
            pltpu.VMEM(query_act.shape, query_act.dtype),
            pltpu.VMEM(out_basis.shape, out_basis.dtype),
            pltpu.VMEM(act_basis.shape, act_basis.dtype),
            pltpu.SemaphoreType.DMA((2 * chunks + 2,)),
        ],
        compiler_params=pltpu.CompilerParams(vmem_limit_bytes=60 * 2**20),
        cost_estimate=pl.CostEstimate(
            flops=2 * columns * (out_basis.size + act_basis.size),
            bytes_accessed=2 * (out_basis.size + act_basis.size + query_out.size + query_act.size),
            transcendentals=0,
        ),
    )(place, tokens, ids, query_out, query_act, out_basis, act_basis)


def precondition_kernel(core_ref, own, other, eigen, other_eigen, precond):
    first = core_ref[0] == 0
    half = eigen.shape[0]
    ka = eigen.shape[1]
    coords = (
        jnp.where(first, own[...], other[...]),
        jnp.where(first, other[...], own[...]),
    )
    eigens = (
        jnp.where(first, eigen[...], other_eigen[...]),
        jnp.where(first, other_eigen[...], eigen[...]),
    )
    act = jnp.concatenate([v[:, half : half + ka // 2] for v in coords], axis=1)
    for part in range(2):
        scale = eigens[part] + damping
        for q in range(precond.shape[0]):
            cut = slice(q * RQ, (q + 1) * RQ)
            numer = lax.dot_general(
                coords[part][cut, :half],
                act[cut],
                (((0,), (0,)), ((), ())),
                precision=lax.Precision.HIGHEST,
                preferred_element_type=jnp.float32,
            )
            precond[q, part * half : (part + 1) * half, :] = (numer / scale).astype(jnp.bfloat16)


def precondition(core, own, other, eigen, other_eigen):
    half, ka = eigen.shape
    return pl.pallas_call(
        precondition_kernel,
        out_shape=jax.ShapeDtypeStruct((own.shape[0] // RQ, 2 * half, ka), jnp.bfloat16),
        in_specs=[pl.BlockSpec(memory_space=pltpu.SMEM)]
        + [pl.BlockSpec(memory_space=pltpu.VMEM)] * 4,
        out_specs=pl.BlockSpec(memory_space=pltpu.VMEM),
        cost_estimate=pl.CostEstimate(
            flops=16 * own.shape[0] * half * ka, bytes_accessed=16 * half * ka, transcendentals=0
        ),
    )(core, own, other, eigen, other_eigen)


def score_kernel(precond, own, other, block, other_block, out):
    ks, ka = precond.shape[1:]
    examples, factor_rows, _ = block.shape
    scores = [0.0] * precond.shape[0]
    for coords, rows in ((own, block), (other, other_block)):
        facts = coords[:, coords.shape[1] - LANES :]
        ids, tokens = facts[:, :1], facts[:, LANES // 2 : LANES // 2 + 1]
        lane = lax.broadcasted_iota(jnp.int32, (examples, LANES), 1).astype(jnp.float32)
        hot = lane == ids
        row = lax.broadcasted_iota(jnp.int32, (examples, factor_rows, ka), 1).astype(jnp.float32)
        weights = jnp.where(row < tokens[:, :, None], rows[:, :, ks:].astype(jnp.float32), 0.0)
        flat = rows[:, :, :ks].reshape(examples * factor_rows, ks)
        for q in range(precond.shape[0]):
            projected = jnp.dot(flat, precond[q], preferred_element_type=jnp.float32)
            terms = projected.reshape(examples, factor_rows, ka) * weights
            per_example = jnp.sum(jnp.sum(terms, axis=1), axis=1, keepdims=True)
            scores[q] += jnp.sum(jnp.where(hot, per_example, 0.0), axis=0, keepdims=True)
    for q, value in enumerate(scores):
        out[q : q + 1, :] = value[:, : out.shape[1]]


def score(precond, own, other, block, other_block):
    return pl.pallas_call(
        score_kernel,
        out_shape=jax.ShapeDtypeStruct(
            (precond.shape[0], block.shape[0] + other_block.shape[0]), jnp.float32
        ),
        in_specs=[pl.BlockSpec(memory_space=pltpu.VMEM)] * 5,
        out_specs=pl.BlockSpec(memory_space=pltpu.VMEM),
    )(precond, own, other, block, other_block)


def direct(
    query_out,
    query_act,
    out_basis,
    act_basis,
    eigenvalues,
    train_out,
    train_act,
    train_tokens,
    train_ids,
):
    parts = lax.axis_size("blk")
    swap = [(0, 1), (1, 0)]
    place = lax.axis_index("blk").reshape(1)
    core = lax.axis_index("fsdp").reshape(1)
    block = jnp.concatenate([train_out, train_act], axis=2)
    for i in reversed(range(parts.bit_length() - 1)):
        pairs = [(s, s ^ (1 << i)) for s in range(parts)]
        block = jnp.concatenate([block, lax.ppermute(block, "blk", pairs)], axis=0)
    other_block = lax.ppermute(block, "fsdp", swap)
    other_eigen = lax.ppermute(eigenvalues, "fsdp", swap)
    pieces = project(
        place, train_tokens, train_ids, query_out.T, query_act.T, out_basis, act_basis, parts
    )
    own = jnp.sum(lax.all_to_all(pieces, "blk", 0, 0, tiled=True), axis=0)
    other = lax.ppermute(own, "fsdp", swap)
    precond = precondition(core, own, other, eigenvalues, other_eigen)
    return score(precond, own, other, block, other_block)


def score_block(precond, out_rows, act_rows, token_counts):
    factor_rows = out_rows.shape[1]
    valid = (
        lax.broadcasted_iota(jnp.int32, (out_rows.shape[0], factor_rows), 1) < token_counts[:, None]
    ).astype(jnp.float32)
    projected = jnp.einsum("nri,qij->nrqj", out_rows, precond, preferred_element_type=jnp.float32)
    weights = act_rows.astype(jnp.float32) * valid[:, :, None]
    return jnp.einsum("nrqj,nrj->qn", projected, weights, precision=lax.Precision.HIGHEST)


def gathered(
    query_out,
    query_act,
    out_basis,
    act_basis,
    eigenvalues,
    train_out,
    train_act,
    train_tokens,
    train_ids,
):
    half_ks = out_basis.shape[1]
    local_rows = query_out.shape[1] // lax.axis_size("blk")
    out_part = lax.dot_general(
        query_out, out_basis, (((0,), (0,)), ((), ())), preferred_element_type=jnp.float32
    )
    act_part = lax.dot_general(
        query_act, act_basis, (((0,), (0,)), ((), ())), preferred_element_type=jnp.float32
    )
    rotated = lax.psum_scatter(
        jnp.concatenate([out_part, act_part], axis=1), "blk", scatter_dimension=0, tiled=True
    )
    out_coords = rotated[:, :half_ks]
    act_half = rotated[:, half_ks:]
    act_coords = lax.all_gather(act_half, "fsdp", axis=1, tiled=True)
    queries = local_rows // RQ
    out_three = out_coords.reshape(queries, RQ, half_ks)
    act_three = act_coords.reshape(queries, RQ, act_coords.shape[1])
    numer = jnp.einsum("qri,qrj->qij", out_three, act_three, precision=lax.Precision.HIGHEST)
    precond = (numer / (eigenvalues + damping)).astype(jnp.bfloat16)
    train_total = train_out.shape[0] * lax.axis_size("blk") * lax.axis_size("fsdp")
    empty = jnp.zeros((queries, train_total), jnp.float32)
    full_precond = lax.all_gather(precond, "fsdp", axis=1, tiled=True)
    out_rows = lax.all_gather(train_out, "blk", axis=0, tiled=True)
    act_rows = lax.all_gather(train_act, "blk", axis=0, tiled=True)
    token_counts = lax.all_gather(train_tokens, "blk", axis=0, tiled=True)
    column_ids = lax.all_gather(train_ids, "blk", axis=0, tiled=True)
    scores = empty.at[:, column_ids].add(
        score_block(full_precond, out_rows, act_rows, token_counts)
    )
    return lax.psum(scores, "fsdp")


def solution(mesh):
    parts = mesh.shape["blk"]
    few = parts <= MOST_DIRECT and parts & (parts - 1) == 0 and mesh.shape["fsdp"] == 2
    return jax.shard_map(
        direct if few else gathered,
        mesh=mesh,
        in_specs=(
            P("blk", None),
            P("blk", None),
            P("blk", "fsdp"),
            P("blk", "fsdp"),
            P("fsdp", None),
            P(("groups", "blk", "fsdp"), None, None),
            P(("groups", "blk", "fsdp"), None, None),
            P(("groups", "blk", "fsdp")),
            P(("groups", "blk", "fsdp")),
        ),
        out_specs=P("blk", "groups"),
        check_vma=False,
    )
```

time: 34 us -> 45.3 us (1.33)
  blocking collectives: 0 us -> 13.4 us
  starting transfers between devices: 12 us -> 7.89 us
  local copies, waits for them, and re-layouts: 0.82 us -> 2.95 us
  other arithmetic: 1.74 us -> 0.09 us
  Pallas kernels: 6.83 us -> 8.26 us
    all_to_all x0 -> x1, blocking collectives: none -> 13.4 us  [direct(): own = jnp.sum(lax.all_to_all(pieces, 'blk', 0, 0, tiled=True), axis=0)]
    ppermute x7 -> x4, starting transfers between devices: 11.9 us -> 7.32 us  [the longest x3 7.25 us: direct(): block = jnp.concatenate([block, lax.ppermute(block, 'blk', pairs)], axis=0)]
    unnamed x4 -> x11, local copies, waits for them, and re-layouts: 0.01 us -> 2.23 us
    pallas_call x2, Pallas kernels: 3.89 us -> 5.31 us  [the longest x1 2.91 us: precondition(): pl.pallas_call(precondition_kernel, out_shape=jax.ShapeDtypeStruct((own.s...]
    concatenate x3, other arithmetic: 0.93 us -> 0.07 us  [direct(): block = jnp.concatenate([block, lax.ppermute(block, 'blk', pairs)], axis=0)]
    slice x3 -> x0, local copies, waits for them, and re-layouts: 0.81 us -> none  [direct(): lax.index_in_dim(pieces, 1, len(bits) - bit.bit_length(), keepdims=True)]
    add x2 -> x0, other arithmetic: 0.81 us -> none  [direct(): pieces = kept + across(moved, bit)]
    concatenate x0 -> x1, local copies, waits for them, and re-layouts: none -> 0.72 us  [direct(): block = jnp.concatenate([train_out, train_act], axis=2)]
  transfers between devices with their start and end apart: 9 -> 6, of which waited for: 6 -> 4; matrix products, arithmetic and copies ran while one was open for 5% -> 0% of each run, Pallas kernels for 9% -> 13%
where the time goes in v4:
time: 45.3 us; the launch traced here: 44.9 us
  blocking collectives  13.4 us (30%)
  waiting for transfers between devices  11 us (24%)
  Pallas kernels  8.26 us (18%)
  starting transfers between devices  7.89 us (17%)
  local copies, waits for them, and re-layouts  2.95 us (7%)
  between operations  1.37 us (3%)
    all_to_all x1, blocking collectives, direct(): own = jnp.sum(lax.all_to_all(pieces, 'blk', 0, 0, tiled=True), axis=0)  13.4 us
    ppermute x3, waiting for transfers between devices, direct(): block = jnp.concatenate([block, lax.ppermute(block, 'blk', pairs)], axis=0)  9.79 us
    ppermute x3, starting transfers between devices, direct(): block = jnp.concatenate([block, lax.ppermute(block, 'blk', pairs)], axis=0)  7.25 us
    pallas_call x1, Pallas kernels, project(): pl.pallas_call(functools.partial(project_kernel, chunks), out_shape=jax.S...  2.95 us
    pallas_call x1, Pallas kernels, precondition(): pl.pallas_call(precondition_kernel, out_shape=jax.ShapeDtypeStruct((own.s...  2.91 us
    pallas_call x1, Pallas kernels, score(): pl.pallas_call(score_kernel, out_shape=jax.ShapeDtypeStruct((precond.shap...  2.41 us
    unnamed x11, local copies, waits for them, and re-layouts  2.23 us
    ppermute x1, waiting for transfers between devices, direct(): other = lax.ppermute(own, 'fsdp', swap)  1.17 us
  transfers between devices with their start and end apart: 6, of which 4 were waited for; matrix products, arithmetic and copies ran while one was open for 0% of the time, Pallas kernels for 13%

profile of v4, /device:TPU:0, one launch (start us, length us, event | category | flops | bytes accessed | tf_op | source)
XLA Modules:
  0.0 44.9 jit_solution(778219444261795281)
XLA Ops:
  0.0 0.8 %constant_dynamic-update-slice_fusion.1 = bf16[1,32,768]{2,1,0:T(8,128)(2,1)S(1)} fusion(bf16[1,32,512]{2,1,0:T(8,128)(2,1)} %param.14), kind=kLoop, calls=%fused_computation.4 | loop fusion | bytes 65536
  0.8 0.7 %constant_dynamic-update-slice_fusion = bf16[1,32,768]{2,1,0:T(8,128)(2,1)S(1)} fusion(bf16[1,32,768]{2,1,0:T(8,128)(2,1)S(1)} %constant_dynamic-update-slice_fusion.1, bf16[1,32,256]{2,1,0:T(8,128)(2,1)} %param.15), kind=kLoop, calls=%fused_computation.3 | loop fusion | bytes 32768 | tf_op jit(solution)/shard_map/concatenate | solution.py:201
  1.5 4.0 %collective-permute-start.2 = (bf16[1,32,768]{2,1,0:T(8,128)(2,1)S(1)}, bf16[1,32,768]{2,1,0:T(8,128)(2,1)S(1)}, u32[]{:S(2)}, u32[]{:S(2)}) collective-permute-start(bf16[1,32,768]{2,1,0:T(8,128)(2,1)S(1)} %constant_dynamic-update-slice_fusion), channel_id=1, source_target_pairs={{0,8},{2,10},{4,12},{6,14},{8,0},{10,2},{12,4},{14,6},{1,9},{3,11}... | collective-permute-start | bytes 147464 | tf_op jit(solution)/shard_map/ppermute | solution.py:204
  5.5 2.6 %collective-permute-done.2 = bf16[1,32,768]{2,1,0:T(8,128)(2,1)S(1)} collective-permute-done((bf16[1,32,768]{2,1,0:T(8,128)(2,1)S(1)}, bf16[1,32,768]{2,1,0:T(8,128)(2,1)S(1)}, u32[]{:S(2)}, u32[]{:S(2)}) %collective-permute-start.2) | collective-permute-done | bytes 49184 | tf_op jit(solution)/shard_map/ppermute | solution.py:204
  8.1 1.4 %collective-permute-start.3 = (bf16[2,32,768]{2,1,0:T(8,128)(2,1)S(1)}, bf16[2,32,768]{2,1,0:T(8,128)(2,1)S(1)}, u32[]{:S(2)}, u32[]{:S(2)}) collective-permute-start(bf16[2,32,768]{2,1,0:T(8,128)(2,1)S(1)} %pad_maximum_fusion.2), channel_id=1, source_target_pairs={{0,4},{2,6},{4,0},{6,2},{8,12},{10,14},{12,8},{14,10},{1,5},{3,7},... | collective-permute-start | bytes 294920 | tf_op jit(solution)/shard_map/ppermute | solution.py:204
  9.6 3.2 %collective-permute-done.3 = bf16[2,32,768]{2,1,0:T(8,128)(2,1)S(1)} collective-permute-done((bf16[2,32,768]{2,1,0:T(8,128)(2,1)S(1)}, bf16[2,32,768]{2,1,0:T(8,128)(2,1)S(1)}, u32[]{:S(2)}, u32[]{:S(2)}) %collective-permute-start.3) | collective-permute-done | bytes 98336 | tf_op jit(solution)/shard_map/ppermute | solution.py:204
  12.8 1.8 %collective-permute-start.4 = (bf16[4,32,768]{2,1,0:T(8,128)(2,1)S(1)}, bf16[4,32,768]{2,1,0:T(8,128)(2,1)S(1)}, u32[]{:S(2)}, u32[]{:S(2)}) collective-permute-start(bf16[4,32,768]{2,1,0:T(8,128)(2,1)S(1)} %pad_maximum_fusion.1), channel_id=1, source_target_pairs={{0,2},{2,0},{4,6},{6,4},{8,10},{10,8},{12,14},{14,12},{1,3},{3,1},... | collective-permute-start | bytes 589832 | tf_op jit(solution)/shard_map/ppermute | solution.py:204
  14.6 4.0 %collective-permute-done.4 = bf16[4,32,768]{2,1,0:T(8,128)(2,1)S(1)} collective-permute-done((bf16[4,32,768]{2,1,0:T(8,128)(2,1)S(1)}, bf16[4,32,768]{2,1,0:T(8,128)(2,1)S(1)}, u32[]{:S(2)}, u32[]{:S(2)}) %collective-permute-start.4) | collective-permute-done | bytes 196640 | tf_op jit(solution)/shard_map/ppermute | solution.py:204
  18.6 0.0 copy-start
  18.6 0.1 collective-permute-start.5
  18.7 0.5 %collective-permute-start.1 = (f32[256,256]{1,0:T(8,128)}, f32[256,256]{1,0:T(8,128)S(1)}, u32[]{:S(2)}, u32[]{:S(2)}) collective-permute-start(f32[256,256]{1,0:T(8,128)} %eigen.1), channel_id=1, source_target_pairs={{0,1},{1,0},{2,3},{3,2},{4,5},{5,4},{6,7},{7,6},{8,9},{9,8},{10,11... | collective-permute-start | bytes 786440 | tf_op jit(solution)/shard_map/ppermute | solution.py:206
  20.5 2.9 %shard_map.91 = f32[8,8,512]{2,1,0:T(8,128)} custom-call(s32[1]{0:T(128)} %bitcast.1.place_ref, s32[1]{0:T(128)S(6)} %copy.11.tokens_ref, s32[1]{0:T(128)S(6)} %copy.12.ids_ref, bf16[64,3584]{1,0:T(8,128)(2,1)} %bitcast.4, bf16[64,1024]{1,0:T(8,128)(2,1)} %bitcast.5, bf16[3584,256]{1,0:T(8,128)(2,1)} %out_basis.1, bf16[1024,128]{1,0:T(8,128)(2,1)} %act_basis.1), custom_call_target="tpu_custom_call" | custom-call | flops 134217728 | bytes 2686976 | tf_op jit(solution)/shard_map/pallas_call | solution.py:91
  23.5 13.4 %all_to_all.5 = f32[8,8,512]{2,1,0:T(8,128)S(1)} all-to-all(f32[8,8,512]{2,1,0:T(8,128)} %shard_map.91), channel_id=1, replica_groups=mesh['groups'=2,'blk'=8,'fsdp'=2] {'blk'}, dimensions={0} | all-to-all | bytes 262144 | tf_op jit(solution)/shard_map/all_to_all | solution.py:210
  36.8 0.0 copy-start.3
  36.9 0.1 collective-permute-start
  36.9 1.2 %collective-permute-done.other = f32[8,512]{1,0:T(8,128)S(1)} collective-permute-done((f32[8,512]{1,0:T(8,128)S(1)}, f32[8,512]{1,0:T(8,128)S(1)}, u32[]{:S(2)}, u32[]{:S(2)}) %collective-permute-start) | collective-permute-done | bytes 16416 | tf_op jit(solution)/shard_map/ppermute | solution.py:211
  38.1 0.0 collective-permute-done.1.other_eigen
  38.1 0.0 copy-done.3
  38.1 0.6 %copy-done.4 = f32[8,512]{1,0:T(8,128)} copy-done((f32[8,512]{1,0:T(8,128)}, f32[8,512]{1,0:T(8,128)S(1)}, u32[]{:S(2)}) %copy-start.4) | copy-done | bytes 16408
  38.7 0.1 copy-done.2
  38.8 2.9 %shard_map.92.precond = bf16[2,512,256]{2,1,0:T(8,128)(2,1)} custom-call(s32[1]{0:T(128)} %bitcast.core_ref, f32[8,512]{1,0:T(8,128)} %copy-done.3, f32[8,512]{1,0:T(8,128)} %copy-done.4, f32[256,256]{1,0:T(8,128)} %eigen.1, f32[256,256]{1,0:T(8,128)} %copy-done.2), custom_call_target="tpu_custom_call" | custom-call | flops 8388608 | bytes 1048576 | tf_op jit(solution)/shard_map/pallas_call | solution.py:142
  41.7 0.0 collective-permute-done.5.other_block
  41.7 0.8 %copy-done.1 = bf16[8,32,768]{2,1,0:T(8,128)(2,1)} copy-done((bf16[8,32,768]{2,1,0:T(8,128)(2,1)}, bf16[8,32,768]{2,1,0:T(8,128)(2,1)S(1)}, u32[]{:S(2)}) %copy-start.1) | copy-done | bytes 393240
  42.5 2.4 %shard_map.93 = f32[2,16]{1,0:T(2,128)} custom-call(bf16[2,512,256]{2,1,0:T(8,128)(2,1)} %shard_map.92.precond, f32[8,512]{1,0:T(8,128)} %copy-done.3, f32[8,512]{1,0:T(8,128)} %copy-done.4, bf16[8,32,768]{2,1,0:T(8,128)(2,1)} %copy-done, bf16[8,32,768]{2,1,0:T(8,128)(2,1)} %copy-done.1), custom_call_target="tpu_custom_call" | custom-call | tf_op jit(solution)/shard_map/pallas_call | solution.py:176
  (8 shorter events, 0.1 us)
Async XLA Ops:
  1.5 6.6 %collective-permute-start.2 = (bf16[1,32,768]{2,1,0:T(8,128)(2,1)S(1)}, bf16[1,32,768]{2,1,0:T(8,128)(2,1)S(1)}, u32[]{:S(2)}, u32[]{:S(2)}) collective-permute-start(bf16[1,32,768]{2,1,0:T(8,128)(2,1)S(1)} %constant_dynamic-update-slice_fusion), channel_id=1, source_target_pairs={{0,8},{2,10},{4,12},{6,14},{8,0},{10,2},{12,4},{14,6},{1,9},{3,11}... | collective-permute-start | bytes 147464 | tf_op jit(solution)/shard_map/ppermute | solution.py:204
  8.1 4.7 %collective-permute-start.3 = (bf16[2,32,768]{2,1,0:T(8,128)(2,1)S(1)}, bf16[2,32,768]{2,1,0:T(8,128)(2,1)S(1)}, u32[]{:S(2)}, u32[]{:S(2)}) collective-permute-start(bf16[2,32,768]{2,1,0:T(8,128)(2,1)S(1)} %pad_maximum_fusion.2), channel_id=1, source_target_pairs={{0,4},{2,6},{4,0},{6,2},{8,12},{10,14},{12,8},{14,10},{1,5},{3,7},... | collective-permute-start | bytes 294920 | tf_op jit(solution)/shard_map/ppermute | solution.py:204
  12.8 5.7 %collective-permute-start.4 = (bf16[4,32,768]{2,1,0:T(8,128)(2,1)S(1)}, bf16[4,32,768]{2,1,0:T(8,128)(2,1)S(1)}, u32[]{:S(2)}, u32[]{:S(2)}) collective-permute-start(bf16[4,32,768]{2,1,0:T(8,128)(2,1)S(1)} %pad_maximum_fusion.1), channel_id=1, source_target_pairs={{0,2},{2,0},{4,6},{6,4},{8,10},{10,8},{12,14},{14,12},{1,3},{3,1},... | collective-permute-start | bytes 589832 | tf_op jit(solution)/shard_map/ppermute | solution.py:204
  18.6 23.1 %copy-start = (bf16[8,32,768]{2,1,0:T(8,128)(2,1)}, bf16[8,32,768]{2,1,0:T(8,128)(2,1)S(1)}, u32[]{:S(2)}) copy-start(bf16[8,32,768]{2,1,0:T(8,128)(2,1)S(1)} %pad_maximum_fusion.block) | copy-start | bytes 1179652
  18.6 23.1 %collective-permute-start.5 = (bf16[8,32,768]{2,1,0:T(8,128)(2,1)S(1)}, bf16[8,32,768]{2,1,0:T(8,128)(2,1)S(1)}, u32[]{:S(2)}, u32[]{:S(2)}) collective-permute-start(bf16[8,32,768]{2,1,0:T(8,128)(2,1)S(1)} %pad_maximum_fusion.block), channel_id=1, source_target_pairs={{0,1},{1,0},{2,3},{3,2},{4,5},{5,4},{6,7},{7,6},{8,9},{9,8},{10,11... | collective-permute-start | bytes 1179656 | tf_op jit(solution)/shard_map/ppermute | solution.py:205
  18.7 19.4 %collective-permute-start.1 = (f32[256,256]{1,0:T(8,128)}, f32[256,256]{1,0:T(8,128)S(1)}, u32[]{:S(2)}, u32[]{:S(2)}) collective-permute-start(f32[256,256]{1,0:T(8,128)} %eigen.1), channel_id=1, source_target_pairs={{0,1},{1,0},{2,3},{3,2},{4,5},{5,4},{6,7},{7,6},{8,9},{9,8},{10,11... | collective-permute-start | bytes 786440 | tf_op jit(solution)/shard_map/ppermute | solution.py:206
  36.8 1.3 %copy-start.3 = (f32[8,512]{1,0:T(8,128)}, f32[8,512]{1,0:T(8,128)S(1)}, u32[]{:S(2)}) copy-start(f32[8,512]{1,0:T(8,128)S(1)} %reduce_sum.9.own) | copy-start | bytes 49156
  36.9 1.2 %collective-permute-start = (f32[8,512]{1,0:T(8,128)S(1)}, f32[8,512]{1,0:T(8,128)S(1)}, u32[]{:S(2)}, u32[]{:S(2)}) collective-permute-start(f32[8,512]{1,0:T(8,128)S(1)} %reduce_sum.9.own), channel_id=1, source_target_pairs={{0,1},{1,0},{2,3},{3,2},{4,5},{5,4},{6,7},{7,6},{8,9},{9,8},{10,11... | collective-permute-start | bytes 49160 | tf_op jit(solution)/shard_map/ppermute | solution.py:211
  38.1 0.6 %copy-start.4 = (f32[8,512]{1,0:T(8,128)}, f32[8,512]{1,0:T(8,128)S(1)}, u32[]{:S(2)}) copy-start(f32[8,512]{1,0:T(8,128)S(1)} %collective-permute-done.other) | copy-start | bytes 49156
  38.1 0.7 %copy-start.2 = (f32[256,256]{1,0:T(8,128)}, f32[256,256]{1,0:T(8,128)S(1)}, u32[]{:S(2)}) copy-start(f32[256,256]{1,0:T(8,128)S(1)} %collective-permute-done.1.other_eigen) | copy-start | bytes 786436
  41.7 0.8 %copy-start.1 = (bf16[8,32,768]{2,1,0:T(8,128)(2,1)}, bf16[8,32,768]{2,1,0:T(8,128)(2,1)S(1)}, u32[]{:S(2)}) copy-start(bf16[8,32,768]{2,1,0:T(8,128)(2,1)S(1)} %collective-permute-done.5.other_block) | copy-start | bytes 1179652

commit v5 on v0

--- a/solution.py
+++ b/solution.py
@@ -1,12 +1,299 @@
+import functools
+
 import jax
 import jax.numpy as jnp
 from jax import lax
+from jax.experimental import pallas as pl
+from jax.experimental.pallas import tpu as pltpu
 from jax.sharding import PartitionSpec as P
 
 RQ = 4
+LANES = 128
+MOST_DIRECT = 16
 
 
 damping = 0.1
+
+
+def chunk_count(rows):
+    for chunks in (4, 2):
+        if rows % (chunks * LANES) == 0:
+            return chunks
+    return 1
+
+
+def pinned(x):
+    return pltpu.with_memory_space_constraint(x, pltpu.HBM)
+
+
+def spec(space):
+    return pl.BlockSpec(memory_space=space)
+
+
+def pack_kernel(train_out, train_act, packed, sems):
+    ks = train_out.shape[2]
+    copies = (
+        pltpu.make_async_copy(train_out, packed.at[:, :, :ks], sems.at[0]),
+        pltpu.make_async_copy(train_act, packed.at[:, :, ks:], sems.at[1]),
+    )
+    for copy in copies:
+        copy.start()
+    for copy in copies:
+        copy.wait()
+
+
+def pack(train_out, train_act):
+    examples, rows, ks = train_out.shape
+    shape = (examples, rows, ks + train_act.shape[2])
+    return pl.pallas_call(
+        pack_kernel,
+        out_shape=jax.ShapeDtypeStruct(shape, train_out.dtype),
+        in_specs=[spec(pltpu.HBM)] * 2,
+        out_specs=spec(pltpu.VMEM),
+        scratch_shapes=[pltpu.SemaphoreType.DMA((2,))],
+    )(pinned(train_out), pinned(train_act))
+
+
+def join_kernel(after, first, second, joined):
+    del after
+    count = first.shape[0]
+    joined[:count] = first[...]
+    joined[count:] = second[...]
+
+
+def joined_shape(first, second):
+    return jax.ShapeDtypeStruct(
+        (first.shape[0] + second.shape[0],) + first.shape[1:], first.dtype
+    )
+
+
+def join(after, first, second):
+    return pl.pallas_call(
+        join_kernel,
+        out_shape=joined_shape(first, second),
+        in_specs=[spec(pl.ANY)] + [spec(pltpu.VMEM)] * 2,
+        out_specs=spec(pltpu.VMEM),
+    )(after, first, second)
+
+
+def fold_kernel(held, summand, first, second, kept, moved, joined):
+    for part in range(kept.shape[0]):
+        kept[part] = held[2 * part] + summand[2 * part]
+        moved[part] = held[2 * part + 1] + summand[2 * part + 1]
+    join_kernel(None, first, second, joined)
+
+
+def fold(held, summand, first, second):
+    half = jax.ShapeDtypeStruct((held.shape[0] // 2,) + held.shape[1:], held.dtype)
+    return pl.pallas_call(
+        fold_kernel,
+        out_shape=[half, half, joined_shape(first, second)],
+        in_specs=[spec(pltpu.VMEM)] * 4,
+        out_specs=[spec(pltpu.VMEM)] * 3,
+    )(held, summand, first, second)
+
+
+def project_kernel(
+    chunks, query_out, query_act, out_basis, act_basis, total, q_out, q_act, b_out, b_act, sems
+):
+    rows = query_out.shape[1] // chunks
+    copies = []
+    for c in range(chunks):
+        cut = pl.ds(c * rows, rows)
+        copies.append(
+            (
+                pltpu.make_async_copy(query_out.at[:, cut], q_out.at[:, cut], sems.at[2 * c]),
+                pltpu.make_async_copy(out_basis.at[cut, :], b_out.at[cut, :], sems.at[2 * c + 1]),
+            )
+        )
+    copies.append(
+        (
+            pltpu.make_async_copy(query_act, q_act, sems.at[2 * chunks]),
+            pltpu.make_async_copy(act_basis, b_act, sems.at[2 * chunks + 1]),
+        )
+    )
+    for pair in copies:
+        for copy in pair:
+            copy.start()
+    half_ks = b_out.shape[1]
+    out_part = None
+    for c in range(chunks):
+        for copy in copies[c]:
+            copy.wait()
+        cut = pl.ds(c * rows, rows)
+        term = jnp.dot(q_out[:, cut], b_out[cut, :], preferred_element_type=jnp.float32)
+        out_part = term if out_part is None else out_part + term
+    total[:, :half_ks] = out_part
+    for copy in copies[chunks]:
+        copy.wait()
+    total[:, half_ks:] = jnp.dot(q_act[...], b_act[...], preferred_element_type=jnp.float32)
+
+
+def project(query_out, query_act, out_basis, act_basis):
+    columns = query_out.shape[0]
+    width = out_basis.shape[1] + act_basis.shape[1]
+    chunks = chunk_count(query_out.shape[1])
+    operands = (query_out, query_act, out_basis, act_basis)
+    return pl.pallas_call(
+        functools.partial(project_kernel, chunks),
+        out_shape=jax.ShapeDtypeStruct((columns, width), jnp.float32),
+        in_specs=[spec(pltpu.HBM)] * len(operands),
+        out_specs=spec(pltpu.VMEM),
+        scratch_shapes=[pltpu.VMEM(x.shape, x.dtype) for x in operands]
+        + [pltpu.SemaphoreType.DMA((2 * chunks + 2,))],
+        compiler_params=pltpu.CompilerParams(vmem_limit_bytes=16 * 2**20),
+        cost_estimate=pl.CostEstimate(
+            flops=2 * columns * (out_basis.size + act_basis.size),
+            bytes_accessed=2 * sum(x.size for x in operands),
+            transcendentals=0,
+        ),
+    )(*[pinned(x) for x in operands])
+
+
+def doubling_slot(distance, parts):
+    bits = parts.bit_length() - 1
+    return sum(1 << (bits - 1 - i) for i in range(bits) if distance >> i & 1)
+
+
+def spread_kernel(
+    place_ref, tokens_ref, ids_ref, after, total, first, second, kept, moved, joined
+):
+    del after
+    parts = 2 * kept.shape[0]
+    local_rows = kept.shape[1]
+    width = total.shape[1]
+    row = lax.broadcasted_iota(jnp.int32, (local_rows, LANES), 0)
+    lane = lax.broadcasted_iota(jnp.int32, (local_rows, LANES), 1)
+    facts = jnp.where(lane < LANES // 2, ids_ref[0], tokens_ref[0]).astype(jnp.float32)
+    for part in range(parts):
+        start = pl.multiple_of((place_ref[0] ^ part) * local_rows, local_rows)
+        piece = (moved if part % 2 else kept).at[part // 2]
+        piece[:, :width] = total[pl.ds(start, local_rows), :]
+        piece[:, width:] = jnp.where(row == doubling_slot(part, parts), facts, 0.0)
+    join_kernel(None, first, second, joined)
+
+
+def spread(place, tokens, ids, after, total, first, second, parts):
+    half = jax.ShapeDtypeStruct(
+        (parts // 2, total.shape[0] // parts, total.shape[1] + LANES), jnp.float32
+    )
+    return pl.pallas_call(
+        spread_kernel,
+        out_shape=[half, half, joined_shape(first, second)],
+        in_specs=[spec(pltpu.SMEM)] * 3 + [spec(pl.ANY)] + [spec(pltpu.VMEM)] * 3,
+        out_specs=[spec(pltpu.VMEM)] * 3,
+    )(place, tokens, ids, after, total, first, second)
+
+
+def split_three(x):
+    high = x.astype(jnp.bfloat16)
+    rest = x - high.astype(jnp.float32)
+    middle = rest.astype(jnp.bfloat16)
+    low = (rest - middle.astype(jnp.float32)).astype(jnp.bfloat16)
+    return high, middle, low
+
+
+def score_kernel(core_ref, own, other, eigen, other_eigen, block, other_block, out):
+    first = core_ref[0] == 0
+    half, ka = eigen.shape
+    examples, factor_rows, width = block.shape
+    ks = width - ka
+    coords = (
+        jnp.where(first, own[...], other[...]),
+        jnp.where(first, other[...], own[...]),
+    )
+    eigens = (
+        jnp.where(first, eigen[...], other_eigen[...]),
+        jnp.where(first, other_eigen[...], eigen[...]),
+    )
+    scales = [1.0 / (e + damping) for e in eigens]
+    act = jnp.concatenate([v[:, half : half + ka // 2] for v in coords], axis=1)
+    act_terms = split_three(act)
+    out_terms = [split_three(v[:, :half]) for v in coords]
+    order = ((0, 0), (0, 1), (1, 0), (1, 1), (0, 2), (2, 0))
+    weights, hot, flat = [], [], []
+    lane = lax.broadcasted_iota(jnp.int32, (examples, LANES), 1).astype(jnp.float32)
+    row = lax.broadcasted_iota(jnp.int32, (examples, factor_rows, ka), 1).astype(jnp.float32)
+    for facts, rows in ((own, block), (other, other_block)):
+        facts = facts[:, facts.shape[1] - LANES :]
+        hot.append(lane == facts[:, :1])
+        keep = row < facts[:, LANES // 2 : LANES // 2 + 1][:, :, None]
+        weights.append(jnp.where(keep, rows[:, :, ks:].astype(jnp.float32), 0.0))
+        flat.append(rows[:, :, :ks].reshape(examples * factor_rows, ks))
+    for q in range(out.shape[0]):
+        cut = slice(q * RQ, (q + 1) * RQ)
+        right = jnp.concatenate([act_terms[b][cut] for _, b in order], axis=0)
+        precond = []
+        for part in range(2):
+            left = jnp.concatenate([out_terms[part][a][cut] for a, _ in order], axis=0)
+            numer = lax.dot_general(
+                left, right, (((0,), (0,)), ((), ())), preferred_element_type=jnp.float32
+            )
+            precond.append((numer * scales[part]).astype(jnp.bfloat16))
+        precond = jnp.concatenate(precond, axis=0)
+        scores = 0.0
+        for side in range(2):
+            projected = jnp.dot(flat[side], precond, preferred_element_type=jnp.float32)
+            terms = projected.reshape(examples, factor_rows, ka) * weights[side]
+            per_example = jnp.sum(jnp.sum(terms, axis=1), axis=1, keepdims=True)
+            scores += jnp.sum(jnp.where(hot[side], per_example, 0.0), axis=0, keepdims=True)
+        out[q : q + 1, :] = scores[:, : out.shape[1]]
+
+
+def score(core, own, other, eigen, other_eigen, block, other_block):
+    return pl.pallas_call(
+        score_kernel,
+        out_shape=jax.ShapeDtypeStruct(
+            (own.shape[0] // RQ, block.shape[0] + other_block.shape[0]), jnp.float32
+        ),
+        in_specs=[spec(pltpu.SMEM)] + [spec(pltpu.VMEM)] * 6,
+        out_specs=spec(pltpu.VMEM),
+        compiler_params=pltpu.CompilerParams(vmem_limit_bytes=16 * 2**20),
+    )(core, own, other, eigen, other_eigen, block, other_block)
+
+
+def direct(
+    query_out,
+    query_act,
+    out_basis,
+    act_basis,
+    eigenvalues,
+    train_out,
+    train_act,
+    train_tokens,
+    train_ids,
+):
+    parts = lax.axis_size("blk")
+    steps = parts.bit_length() - 1
+    swap = [(0, 1), (1, 0)]
+
+    def across(x, i):
+        return lax.ppermute(x, "blk", [(s, s ^ (1 << i)) for s in range(parts)])
+
+    place = lax.axis_index("blk").reshape(1)
+    core = lax.axis_index("fsdp").reshape(1)
+    other_eigen = lax.ppermute(eigenvalues, "fsdp", swap)
+    block = pack(train_out, train_act)
+    arrived = across(block, steps - 1)
+    total = project(query_out.T, query_act.T, out_basis, act_basis)
+    kept, moved, block = spread(
+        place, train_tokens, train_ids, other_eigen, total, block, arrived, parts
+    )
+    for i in range(steps):
+        summand = across(moved, i)
+        if i < steps - 1:
+            arrived = across(block, steps - 2 - i)
+        if i < steps - 2:
+            kept, moved, block = fold(kept, summand, block, arrived)
+        elif i < steps - 1:
+            sums = kept + summand
+            kept, moved = sums[:1], sums[1:]
+    own = kept + summand
+    block = join(own, block, arrived)
+    own = own.reshape(own.shape[1:])
+    other = lax.ppermute(own, "fsdp", swap)
+    other_block = lax.ppermute(block, "fsdp", swap)
+    return score(core, own, other, eigenvalues, other_eigen, block, other_block)
 
 
 def score_block(precond, out_rows, act_rows, token_counts):
@@ -19,7 +306,7 @@
     return jnp.einsum("nrqj,nrj->qn", projected, weights, precision=lax.Precision.HIGHEST)
 
 
-def on_device(
+def gathered(
     query_out,
     query_act,
     out_basis,
@@ -56,15 +343,17 @@
     act_rows = lax.all_gather(train_act, "blk", axis=0, tiled=True)
     token_counts = lax.all_gather(train_tokens, "blk", axis=0, tiled=True)
     column_ids = lax.all_gather(train_ids, "blk", axis=0, tiled=True)
-    gathered = empty.at[:, column_ids].add(
+    scores = empty.at[:, column_ids].add(
         score_block(full_precond, out_rows, act_rows, token_counts)
     )
-    return lax.psum(gathered, "fsdp")
+    return lax.psum(scores, "fsdp")
 
 
 def solution(mesh):
+    parts = mesh.shape["blk"]
+    few = parts <= MOST_DIRECT and parts & (parts - 1) == 0 and mesh.shape["fsdp"] == 2
     return jax.shard_map(
-        on_device,
+        direct if few else gathered,
         mesh=mesh,
         in_specs=(
             P("blk", None),

time: 112 us -> 42.4 us (0.38)
  blocking collectives: 80.8 us -> 0 us
  between operations: 15.5 us -> 1.37 us
  waiting for transfers between devices: 0.02 us -> 11.7 us
  starting transfers between devices: 0.04 us -> 11.7 us
  Pallas kernels: 0 us -> 10.4 us
  matrix products: 7.52 us -> 0 us
    all_gather x4 -> x0, blocking collectives: 65.3 us -> none  [the longest x1 30.8 us: on_device(): out_rows = lax.all_gather(train_out, 'blk', axis=0, tiled=True)]
    unnamed x1 -> x0, blocking collectives: 13.1 us -> none
    ppermute x0 -> x9, waiting for transfers between devices: none -> 11.7 us  [the longest x6 10.3 us: across(): return lax.ppermute(x, 'blk', [(s, s ^ 1 << i) for s in range(parts)])]
    ppermute x0 -> x9, starting transfers between devices: none -> 11.7 us  [the longest x6 10.7 us: across(): return lax.ppermute(x, 'blk', [(s, s ^ 1 << i) for s in range(parts)])]
    pallas_call x0 -> x6, Pallas kernels: none -> 10.4 us  [the longest x1 2.33 us: project(): pl.pallas_call(functools.partial(project_kernel, chunks), out_shape=jax.S...]
    dot_general x5 -> x0, matrix products: 7.52 us -> none  [the longest x1 4.96 us: score_block(): jnp.einsum('nrqj,nrj->qn', projected, weights, precision=lax.Precision.HI...]
    psum x1 -> x0, blocking collectives: 2.5 us -> none  [on_device(): return lax.psum(gathered, 'fsdp')]
    unnamed x19 -> x20, local copies, waits for them, and re-layouts: 3.77 us -> 5.34 us
  transfers between devices with their start and end apart: 1 -> 9, of which waited for: 0 -> 5; matrix products, arithmetic and copies ran while one was open for 2% -> 1% of each run, Pallas kernels for 0% -> 9%
where the time goes in v5:
time: 42.4 us; the launch traced here: 41.9 us
  starting transfers between devices  11.7 us (28%)
  waiting for transfers between devices  11.7 us (28%)
  Pallas kernels  10.4 us (25%)
  local copies, waits for them, and re-layouts  5.34 us (13%)
  between operations  1.37 us (3%)
  other arithmetic  1.36 us (3%)
    ppermute x6, starting transfers between devices, across(): return lax.ppermute(x, 'blk', [(s, s ^ 1 << i) for s in range(parts)])  10.7 us
    ppermute x6, waiting for transfers between devices, across(): return lax.ppermute(x, 'blk', [(s, s ^ 1 << i) for s in range(parts)])  10.3 us
    unnamed x20, local copies, waits for them, and re-layouts  5.34 us
    pallas_call x1, Pallas kernels, project(): pl.pallas_call(functools.partial(project_kernel, chunks), out_shape=jax.S...  2.33 us
    pallas_call x1, Pallas kernels, join(): pl.pallas_call(join_kernel, out_shape=joined_shape(first, second), in_spe...  1.8 us
    pallas_call x1, Pallas kernels, fold(): pl.pallas_call(fold_kernel, out_shape=[half, half, joined_shape(first, se...  1.71 us
    pallas_call x1, Pallas kernels, spread(): pl.pallas_call(spread_kernel, out_shape=[half, half, joined_shape(first,...  1.63 us
    pallas_call x1, Pallas kernels, score(): pl.pallas_call(score_kernel, out_shape=jax.ShapeDtypeStruct((own.shape[0]...  1.54 us
  transfers between devices with their start and end apart: 9, of which 5 were waited for; matrix products, arithmetic and copies ran while one was open for 1% of the time, Pallas kernels for 9%

profile of v5, /device:TPU:0, one launch (start us, length us, event | category | flops | bytes accessed | tf_op | source)
XLA Modules:
  0.0 41.9 jit_solution(17610275009973612518)
XLA Ops:
  0.5 1.4 %shard_map.92.first = bf16[1,32,768]{2,1,0:T(8,128)(2,1)} custom-call(bf16[1,32,512]{2,1,0:T(8,128)(2,1)} %train_out.1, bf16[1,32,256]{2,1,0:T(8,128)(2,1)} %train_act.1), custom_call_target="tpu_custom_call" | custom-call | tf_op jit(solution)/shard_map/pallas_call | solution.py:48
  1.9 3.7 %collective-permute-start.1 = (bf16[1,32,768]{2,1,0:T(8,128)(2,1)}, bf16[1,32,768]{2,1,0:T(8,128)(2,1)S(1)}, u32[]{:S(2)}, u32[]{:S(2)}) collective-permute-start(bf16[1,32,768]{2,1,0:T(8,128)(2,1)} %shard_map.92.first), channel_id=1, source_target_pairs={{0,8},{2,10},{4,12},{6,14},{8,0},{10,2},{12,4},{14,6},{1,9},{3,11}... | collective-permute-start | bytes 147464 | tf_op jit(solution)/shard_map/ppermute | solution.py:271
  6.8 2.3 %shard_map.91.total = f32[64,384]{1,0:T(8,128)S(1)} custom-call(bf16[64,3584]{1,0:T(8,128)(2,1)} %bitcast.7, bf16[64,1024]{1,0:T(8,128)(2,1)} %bitcast.8, bf16[3584,256]{1,0:T(8,128)(2,1)} %out_basis.1, bf16[1024,128]{1,0:T(8,128)(2,1)} %act_basis.1), custom_call_target="tpu_custom_call" | custom-call | flops 134217728 | bytes 2686976 | tf_op jit(solution)/shard_map/pallas_call | solution.py:137
  9.2 0.6 %copy-done.3 = f32[64,384]{1,0:T(8,128)} copy-done((f32[64,384]{1,0:T(8,128)}, f32[64,384]{1,0:T(8,128)S(1)}, u32[]{:S(2)}) %copy-start.3) | copy-done | bytes 98328
  10.5 1.6 %shard_map.93 = (f32[4,8,512]{2,1,0:T(8,128)}, f32[4,8,512]{2,1,0:T(8,128)}, bf16[2,32,768]{2,1,0:T(8,128)(2,1)}) custom-call(s32[1]{0:T(128)} %bitcast.1.place_ref, s32[1]{0:T(128)S(6)} %copy.10.tokens_ref, s32[1]{0:T(128)S(6)} %copy.11.ids_ref, f32[256,256]{1,0:T(8,128)} %copy-done.1, f32[64,384]{1,0:T(8,128)} %copy-done.3, ...), custom_call_target="tpu_custom_call" | custom-call | tf_op jit(solution)/shard_map/pallas_call | solution.py:180
  12.1 1.6 %collective-permute-start.3 = (bf16[2,32,768]{2,1,0:T(8,128)(2,1)}, bf16[2,32,768]{2,1,0:T(8,128)(2,1)S(1)}, u32[]{:S(2)}, u32[]{:S(2)}) collective-permute-start(bf16[2,32,768]{2,1,0:T(8,128)(2,1)} %get-tuple-element.13.first), channel_id=1, source_target_pairs={{0,4},{2,6},{4,0},{6,2},{8,12},{10,14},{12,8},{14,10},{1,5},{3,7},... | collective-permute-start | bytes 294920 | tf_op jit(solution)/shard_map/ppermute | solution.py:271
  13.7 1.5 %collective-permute-start.2 = (f32[4,8,512]{2,1,0:T(8,128)}, f32[4,8,512]{2,1,0:T(8,128)S(1)}, u32[]{:S(2)}, u32[]{:S(2)}) collective-permute-start(f32[4,8,512]{2,1,0:T(8,128)} %get-tuple-element.12), channel_id=1, source_target_pairs={{0,2},{2,0},{4,6},{6,4},{8,10},{10,8},{12,14},{14,12},{1,3},{3,1},... | collective-permute-start | bytes 196616 | tf_op jit(solution)/shard_map/ppermute | solution.py:271
  15.2 3.0 %collective-permute-done.2.summand = f32[4,8,512]{2,1,0:T(8,128)S(1)} collective-permute-done((f32[4,8,512]{2,1,0:T(8,128)}, f32[4,8,512]{2,1,0:T(8,128)S(1)}, u32[]{:S(2)}, u32[]{:S(2)}) %collective-permute-start.2) | collective-permute-done | bytes 65568 | tf_op jit(solution)/shard_map/ppermute | solution.py:271
  18.2 0.6 %copy-done.8 = f32[4,8,512]{2,1,0:T(8,128)} copy-done((f32[4,8,512]{2,1,0:T(8,128)}, f32[4,8,512]{2,1,0:T(8,128)S(1)}, u32[]{:S(2)}) %copy-start.8) | copy-done | bytes 65560
  18.9 1.7 %shard_map.94 = (f32[2,8,512]{2,1,0:T(8,128)}, f32[2,8,512]{2,1,0:T(8,128)}, bf16[4,32,768]{2,1,0:T(8,128)(2,1)}) custom-call(f32[4,8,512]{2,1,0:T(8,128)} %get-tuple-element.11.held, f32[4,8,512]{2,1,0:T(8,128)} %copy-done.8, bf16[2,32,768]{2,1,0:T(8,128)(2,1)} %get-tuple-element.13.first, bf16[2,32,768]{2,1,0:T(8,128)(2,1)} %copy-done.7), custom_call_target="tpu_custom_call" | custom-call | tf_op jit(solution)/shard_map/pallas_call | solution.py:88
  20.6 0.6 %collective-permute-start.4 = (f32[2,8,512]{2,1,0:T(8,128)}, f32[2,8,512]{2,1,0:T(8,128)S(1)}, u32[]{:S(2)}, u32[]{:S(2)}) collective-permute-start(f32[2,8,512]{2,1,0:T(8,128)} %get-tuple-element.15), channel_id=1, source_target_pairs={{0,4},{2,6},{4,0},{6,2},{8,12},{10,14},{12,8},{14,10},{1,5},{3,7},... | collective-permute-start | bytes 98312 | tf_op jit(solution)/shard_map/ppermute | solution.py:271
  21.2 3.5 %collective-permute-done.4 = f32[2,8,512]{2,1,0:T(8,128)S(1)} collective-permute-done((f32[2,8,512]{2,1,0:T(8,128)}, f32[2,8,512]{2,1,0:T(8,128)S(1)}, u32[]{:S(2)}, u32[]{:S(2)}) %collective-permute-start.4) | collective-permute-done | bytes 32800 | tf_op jit(solution)/shard_map/ppermute | solution.py:271
  24.7 0.8 %add.6 = f32[2,8,512]{2,1,0:T(8,128)S(1)} add(f32[2,8,512]{2,1,0:T(8,128)} %get-tuple-element.14, f32[2,8,512]{2,1,0:T(8,128)S(1)} %collective-permute-done.4) | non-fusion elementwise | flops 8192 | bytes 98304 | tf_op jit(solution)/shard_map/add | solution.py:289
  25.5 1.9 %collective-permute-start.5 = (f32[1,8,512]{2,1,0:T(8,128)S(1)}, f32[1,8,512]{2,1,0:T(8,128)S(1)}, u32[]{:S(2)}, u32[]{:S(2)}) collective-permute-start(f32[1,8,512]{2,1,0:T(8,128)S(1)} %slice.9), channel_id=1, source_target_pairs={{0,8},{2,10},{4,12},{6,14},{8,0},{10,2},{12,4},{14,6},{1,9},{3,11}... | collective-permute-start | bytes 49160 | tf_op jit(solution)/shard_map/ppermute | solution.py:271
  27.4 1.5 %collective-permute-start.7 = (bf16[4,32,768]{2,1,0:T(8,128)(2,1)}, bf16[4,32,768]{2,1,0:T(8,128)(2,1)S(1)}, u32[]{:S(2)}, u32[]{:S(2)}) collective-permute-start(bf16[4,32,768]{2,1,0:T(8,128)(2,1)} %get-tuple-element.16.first), channel_id=1, source_target_pairs={{0,2},{2,0},{4,6},{6,4},{8,10},{10,8},{12,14},{14,12},{1,3},{3,1},... | collective-permute-start | bytes 589832 | tf_op jit(solution)/shard_map/ppermute | solution.py:271
  28.9 1.4 %collective-permute-done.5 = f32[1,8,512]{2,1,0:T(8,128)S(1)} collective-permute-done((f32[1,8,512]{2,1,0:T(8,128)S(1)}, f32[1,8,512]{2,1,0:T(8,128)S(1)}, u32[]{:S(2)}, u32[]{:S(2)}) %collective-permute-start.5) | collective-permute-done | bytes 16416 | tf_op jit(solution)/shard_map/ppermute | solution.py:271
  30.9 2.4 %collective-permute-done.7.second = bf16[4,32,768]{2,1,0:T(8,128)(2,1)S(1)} collective-permute-done((bf16[4,32,768]{2,1,0:T(8,128)(2,1)}, bf16[4,32,768]{2,1,0:T(8,128)(2,1)S(1)}, u32[]{:S(2)}, u32[]{:S(2)}) %collective-permute-start.7) | collective-permute-done | bytes 196640 | tf_op jit(solution)/shard_map/ppermute | solution.py:271
  33.3 0.7 %copy-done.6 = bf16[4,32,768]{2,1,0:T(8,128)(2,1)} copy-done((bf16[4,32,768]{2,1,0:T(8,128)(2,1)}, bf16[4,32,768]{2,1,0:T(8,128)(2,1)S(1)}, u32[]{:S(2)}) %copy-start.6) | copy-done | bytes 196632
  34.0 1.8 %shard_map.95.block = bf16[8,32,768]{2,1,0:T(8,128)(2,1)} custom-call(f32[1,8,512]{2,1,0:T(8,128)} %slice_add_fusion.after, bf16[4,32,768]{2,1,0:T(8,128)(2,1)} %get-tuple-element.16.first, bf16[4,32,768]{2,1,0:T(8,128)(2,1)} %copy-done.6), custom_call_target="tpu_custom_call" | custom-call | tf_op jit(solution)/shard_map/pallas_call | solution.py:71
  36.3 1.4 %collective-permute-done.6.other = f32[8,512]{1,0:T(8,128)S(1)} collective-permute-done((f32[8,512]{1,0:T(8,128)}, f32[8,512]{1,0:T(8,128)S(1)}, u32[]{:S(2)}, u32[]{:S(2)}) %collective-permute-start.6) | collective-permute-done | bytes 16416 | tf_op jit(solution)/shard_map/ppermute | solution.py:294
  37.7 1.0 %copy-done = bf16[8,32,768]{2,1,0:T(8,128)(2,1)S(1)} copy-done((bf16[8,32,768]{2,1,0:T(8,128)(2,1)S(1)}, bf16[8,32,768]{2,1,0:T(8,128)(2,1)}, u32[]{:S(2)}) %copy-start) | copy-done | bytes 393240
  38.7 0.9 %copy-done.2 = f32[256,256]{1,0:T(8,128)S(1)} copy-done((f32[256,256]{1,0:T(8,128)S(1)}, f32[256,256]{1,0:T(8,128)}, u32[]{:S(2)}) %copy-start.2) | copy-done | bytes 262168
  39.7 0.7 %copy-done.5 = f32[1,8,512]{2,1,0:T(8,128)S(1)} copy-done((f32[1,8,512]{2,1,0:T(8,128)S(1)}, f32[1,8,512]{2,1,0:T(8,128)}, u32[]{:S(2)}) %copy-start.5) | copy-done | bytes 16408
  40.4 1.5 %shard_map.96 = f32[2,16]{1,0:T(2,128)} custom-call(s32[1]{0:T(128)} %bitcast.core_ref, f32[8,512]{1,0:T(8,128)S(1)} %bitcast.6, f32[8,512]{1,0:T(8,128)S(1)} %collective-permute-done.6.other, f32[256,256]{1,0:T(8,128)S(1)} %copy-done.4, f32[256,256]{1,0:T(8,128)S(1)} %copy-done.2, bf16[8,32,768]{2,1,0:T(8,128)(2,1)S(1)} %copy-done, ...), custom_call_target="tpu_custom_call" | custom-call | tf_op jit(solution)/shard_map/pallas_call | solution.py:244
  (23 shorter events, 2.3 us)
Async XLA Ops:
  0.0 9.8 %collective-permute-start = (f32[256,256]{1,0:T(8,128)}, f32[256,256]{1,0:T(8,128)S(1)}, u32[]{:S(2)}, u32[]{:S(2)}) collective-permute-start(f32[256,256]{1,0:T(8,128)} %eigen.1), channel_id=1, source_target_pairs={{0,1},{1,0},{2,3},{3,2},{4,5},{5,4},{6,7},{7,6},{8,9},{9,8},{10,11... | collective-permute-start | bytes 786440 | tf_op jit(solution)/shard_map/ppermute | solution.py:275
  1.9 7.9 %collective-permute-start.1 = (bf16[1,32,768]{2,1,0:T(8,128)(2,1)}, bf16[1,32,768]{2,1,0:T(8,128)(2,1)S(1)}, u32[]{:S(2)}, u32[]{:S(2)}) collective-permute-start(bf16[1,32,768]{2,1,0:T(8,128)(2,1)} %shard_map.92.first), channel_id=1, source_target_pairs={{0,8},{2,10},{4,12},{6,14},{8,0},{10,2},{12,4},{14,6},{1,9},{3,11}... | collective-permute-start | bytes 147464 | tf_op jit(solution)/shard_map/ppermute | solution.py:271
  6.8 30.9 %copy-start.4 = (f32[256,256]{1,0:T(8,128)S(1)}, f32[256,256]{1,0:T(8,128)}, u32[]{:S(2)}) copy-start(f32[256,256]{1,0:T(8,128)} %eigen.1) | copy-start | bytes 786436
  9.2 0.6 %copy-start.3 = (f32[64,384]{1,0:T(8,128)}, f32[64,384]{1,0:T(8,128)S(1)}, u32[]{:S(2)}) copy-start(f32[64,384]{1,0:T(8,128)S(1)} %shard_map.91.total) | copy-start | bytes 294916
  9.8 0.6 %copy-start.9 = (bf16[1,32,768]{2,1,0:T(8,128)(2,1)}, bf16[1,32,768]{2,1,0:T(8,128)(2,1)S(1)}, u32[]{:S(2)}) copy-start(bf16[1,32,768]{2,1,0:T(8,128)(2,1)S(1)} %collective-permute-done.1.second) | copy-start | bytes 147460
  9.8 0.7 %copy-start.1 = (f32[256,256]{1,0:T(8,128)}, f32[256,256]{1,0:T(8,128)S(1)}, u32[]{:S(2)}) copy-start(f32[256,256]{1,0:T(8,128)S(1)} %collective-permute-done.after.other_eigen) | copy-start | bytes 786436
  12.1 6.1 %collective-permute-start.3 = (bf16[2,32,768]{2,1,0:T(8,128)(2,1)}, bf16[2,32,768]{2,1,0:T(8,128)(2,1)S(1)}, u32[]{:S(2)}, u32[]{:S(2)}) collective-permute-start(bf16[2,32,768]{2,1,0:T(8,128)(2,1)} %get-tuple-element.13.first), channel_id=1, source_target_pairs={{0,4},{2,6},{4,0},{6,2},{8,12},{10,14},{12,8},{14,10},{1,5},{3,7},... | collective-permute-start | bytes 294920 | tf_op jit(solution)/shard_map/ppermute | solution.py:271
  13.7 4.5 %collective-permute-start.2 = (f32[4,8,512]{2,1,0:T(8,128)}, f32[4,8,512]{2,1,0:T(8,128)S(1)}, u32[]{:S(2)}, u32[]{:S(2)}) collective-permute-start(f32[4,8,512]{2,1,0:T(8,128)} %get-tuple-element.12), channel_id=1, source_target_pairs={{0,2},{2,0},{4,6},{6,4},{8,10},{10,8},{12,14},{14,12},{1,3},{3,1},... | collective-permute-start | bytes 196616 | tf_op jit(solution)/shard_map/ppermute | solution.py:271
  18.2 0.6 %copy-start.8 = (f32[4,8,512]{2,1,0:T(8,128)}, f32[4,8,512]{2,1,0:T(8,128)S(1)}, u32[]{:S(2)}) copy-start(f32[4,8,512]{2,1,0:T(8,128)S(1)} %collective-permute-done.2.summand) | copy-start | bytes 196612
  18.2 0.7 %copy-start.7 = (bf16[2,32,768]{2,1,0:T(8,128)(2,1)}, bf16[2,32,768]{2,1,0:T(8,128)(2,1)S(1)}, u32[]{:S(2)}) copy-start(bf16[2,32,768]{2,1,0:T(8,128)(2,1)S(1)} %collective-permute-done.3.second) | copy-start | bytes 294916
  20.6 4.1 %collective-permute-start.4 = (f32[2,8,512]{2,1,0:T(8,128)}, f32[2,8,512]{2,1,0:T(8,128)S(1)}, u32[]{:S(2)}, u32[]{:S(2)}) collective-permute-start(f32[2,8,512]{2,1,0:T(8,128)} %get-tuple-element.15), channel_id=1, source_target_pairs={{0,4},{2,6},{4,0},{6,2},{8,12},{10,14},{12,8},{14,10},{1,5},{3,7},... | collective-permute-start | bytes 98312 | tf_op jit(solution)/shard_map/ppermute | solution.py:271
  25.5 4.8 %collective-permute-start.5 = (f32[1,8,512]{2,1,0:T(8,128)S(1)}, f32[1,8,512]{2,1,0:T(8,128)S(1)}, u32[]{:S(2)}, u32[]{:S(2)}) collective-permute-start(f32[1,8,512]{2,1,0:T(8,128)S(1)} %slice.9), channel_id=1, source_target_pairs={{0,8},{2,10},{4,12},{6,14},{8,0},{10,2},{12,4},{14,6},{1,9},{3,11}... | collective-permute-start | bytes 49160 | tf_op jit(solution)/shard_map/ppermute | solution.py:271
  27.4 5.9 %collective-permute-start.7 = (bf16[4,32,768]{2,1,0:T(8,128)(2,1)}, bf16[4,32,768]{2,1,0:T(8,128)(2,1)S(1)}, u32[]{:S(2)}, u32[]{:S(2)}) collective-permute-start(bf16[4,32,768]{2,1,0:T(8,128)(2,1)} %get-tuple-element.16.first), channel_id=1, source_target_pairs={{0,2},{2,0},{4,6},{6,4},{8,10},{10,8},{12,14},{14,12},{1,3},{3,1},... | collective-permute-start | bytes 589832 | tf_op jit(solution)/shard_map/ppermute | solution.py:271
  33.3 0.7 %copy-start.6 = (bf16[4,32,768]{2,1,0:T(8,128)(2,1)}, bf16[4,32,768]{2,1,0:T(8,128)(2,1)S(1)}, u32[]{:S(2)}) copy-start(bf16[4,32,768]{2,1,0:T(8,128)(2,1)S(1)} %collective-permute-done.7.second) | copy-start | bytes 589828
  35.8 2.0 %collective-permute-start.8 = (bf16[8,32,768]{2,1,0:T(8,128)(2,1)}, bf16[8,32,768]{2,1,0:T(8,128)(2,1)S(1)}, u32[]{:S(2)}, u32[]{:S(2)}) collective-permute-start(bf16[8,32,768]{2,1,0:T(8,128)(2,1)} %shard_map.95.block), channel_id=1, source_target_pairs={{0,1},{1,0},{2,3},{3,2},{4,5},{5,4},{6,7},{7,6},{8,9},{9,8},{10,11... | collective-permute-start | bytes 1179656 | tf_op jit(solution)/shard_map/ppermute | solution.py:295
  35.8 2.0 %collective-permute-start.6 = (f32[8,512]{1,0:T(8,128)}, f32[8,512]{1,0:T(8,128)S(1)}, u32[]{:S(2)}, u32[]{:S(2)}) collective-permute-start(f32[8,512]{1,0:T(8,128)} %bitcast.5), channel_id=1, source_target_pairs={{0,1},{1,0},{2,3},{3,2},{4,5},{5,4},{6,7},{7,6},{8,9},{9,8},{10,11... | collective-permute-start | bytes 49160 | tf_op jit(solution)/shard_map/ppermute | solution.py:294
  37.7 1.0 %copy-start = (bf16[8,32,768]{2,1,0:T(8,128)(2,1)S(1)}, bf16[8,32,768]{2,1,0:T(8,128)(2,1)}, u32[]{:S(2)}) copy-start(bf16[8,32,768]{2,1,0:T(8,128)(2,1)} %shard_map.95.block) | copy-start | bytes 1179652
  38.7 0.9 %copy-start.2 = (f32[256,256]{1,0:T(8,128)S(1)}, f32[256,256]{1,0:T(8,128)}, u32[]{:S(2)}) copy-start(f32[256,256]{1,0:T(8,128)} %copy-done.1) | copy-start | bytes 786436
  39.7 0.7 %copy-start.5 = (f32[1,8,512]{2,1,0:T(8,128)S(1)}, f32[1,8,512]{2,1,0:T(8,128)}, u32[]{:S(2)}) copy-start(f32[1,8,512]{2,1,0:T(8,128)} %slice_add_fusion.after) | copy-start | bytes 49156

commit v6 on v5

--- a/solution.py
+++ b/solution.py
@@ -26,6 +26,10 @@
     return pltpu.with_memory_space_constraint(x, pltpu.HBM)
 
 
+def grant(mebibytes):
+    return pltpu.CompilerParams(vmem_limit_bytes=mebibytes * 2**20)
+
+
 def spec(space):
     return pl.BlockSpec(memory_space=space)
 
@@ -51,6 +55,7 @@
         in_specs=[spec(pltpu.HBM)] * 2,
         out_specs=spec(pltpu.VMEM),
         scratch_shapes=[pltpu.SemaphoreType.DMA((2,))],
+        compiler_params=grant(2),
     )(pinned(train_out), pinned(train_act))
 
 
@@ -73,24 +78,8 @@
         out_shape=joined_shape(first, second),
         in_specs=[spec(pl.ANY)] + [spec(pltpu.VMEM)] * 2,
         out_specs=spec(pltpu.VMEM),
+        compiler_params=grant(4),
     )(after, first, second)
-
-
-def fold_kernel(held, summand, first, second, kept, moved, joined):
-    for part in range(kept.shape[0]):
-        kept[part] = held[2 * part] + summand[2 * part]
-        moved[part] = held[2 * part + 1] + summand[2 * part + 1]
-    join_kernel(None, first, second, joined)
-
-
-def fold(held, summand, first, second):
-    half = jax.ShapeDtypeStruct((held.shape[0] // 2,) + held.shape[1:], held.dtype)
-    return pl.pallas_call(
-        fold_kernel,
-        out_shape=[half, half, joined_shape(first, second)],
-        in_specs=[spec(pltpu.VMEM)] * 4,
-        out_specs=[spec(pltpu.VMEM)] * 3,
-    )(held, summand, first, second)
 
 
 def project_kernel(
@@ -141,7 +130,7 @@
         out_specs=spec(pltpu.VMEM),
         scratch_shapes=[pltpu.VMEM(x.shape, x.dtype) for x in operands]
         + [pltpu.SemaphoreType.DMA((2 * chunks + 2,))],
-        compiler_params=pltpu.CompilerParams(vmem_limit_bytes=16 * 2**20),
+        compiler_params=grant(8),
         cost_estimate=pl.CostEstimate(
             flops=2 * columns * (out_basis.size + act_basis.size),
             bytes_accessed=2 * sum(x.size for x in operands),
@@ -182,6 +171,7 @@
         out_shape=[half, half, joined_shape(first, second)],
         in_specs=[spec(pltpu.SMEM)] * 3 + [spec(pl.ANY)] + [spec(pltpu.VMEM)] * 3,
         out_specs=[spec(pltpu.VMEM)] * 3,
+        compiler_params=grant(4),
     )(place, tokens, ids, after, total, first, second)
 
 
@@ -248,7 +238,7 @@
         ),
         in_specs=[spec(pltpu.SMEM)] + [spec(pltpu.VMEM)] * 6,
         out_specs=spec(pltpu.VMEM),
-        compiler_params=pltpu.CompilerParams(vmem_limit_bytes=16 * 2**20),
+        compiler_params=grant(12),
     )(core, own, other, eigen, other_eigen, block, other_block)
 
 
@@ -279,18 +269,13 @@
     kept, moved, block = spread(
         place, train_tokens, train_ids, other_eigen, total, block, arrived, parts
     )
-    for i in range(steps):
-        summand = across(moved, i)
-        if i < steps - 1:
-            arrived = across(block, steps - 2 - i)
-        if i < steps - 2:
-            kept, moved, block = fold(kept, summand, block, arrived)
-        elif i < steps - 1:
-            sums = kept + summand
-            kept, moved = sums[:1], sums[1:]
-    own = kept + summand
-    block = join(own, block, arrived)
-    own = own.reshape(own.shape[1:])
+    for i in range(steps - 1):
+        sums = kept + across(moved, i)
+        sums = sums.reshape((sums.shape[0] // 2, 2) + sums.shape[1:])
+        arrived = across(block, steps - 2 - i)
+        kept, moved = sums[:, 0], sums[:, 1]
+        block = join(kept, block, arrived)
+    own = (kept + across(moved, steps - 1)).reshape(kept.shape[1:])
     other = lax.ppermute(own, "fsdp", swap)
     other_block = lax.ppermute(block, "fsdp", swap)
     return score(core, own, other, eigenvalues, other_eigen, block, other_block)

time: 42.4 us -> 28.6 us (0.67)
  Pallas kernels: 10.4 us -> 4.72 us
  local copies, waits for them, and re-layouts: 5.34 us -> 0.02 us
  waiting for transfers between devices: 11.7 us -> 9.78 us
  other arithmetic: 1.36 us -> 0.02 us
  starting transfers between devices: 11.7 us -> 12.4 us
    unnamed x20 -> x2, local copies, waits for them, and re-layouts: 5.34 us -> 0.01 us
    pallas_call x1 -> x2, Pallas kernels: 1.8 us -> 0.04 us  [join(): pl.pallas_call(join_kernel, out_shape=joined_shape(first, second), in_spe...]
    pallas_call x1 -> x0, Pallas kernels: 1.71 us -> none  [fold(): pl.pallas_call(fold_kernel, out_shape=[half, half, joined_shape(first, se...]
    ppermute x6, waiting for transfers between devices: 10.3 us -> 8.6 us  [across(): return lax.ppermute(x, 'blk', [(s, s ^ 1 << i) for s in range(parts)])]
    pallas_call x1, Pallas kernels: 1.63 us -> 0.02 us  [spread(): pl.pallas_call(spread_kernel, out_shape=[half, half, joined_shape(first,...]
    add x2 -> x1, other arithmetic: 1.36 us -> 0.01 us  [direct(): sums = kept + across(moved, i)]
    ppermute x6, starting transfers between devices: 10.7 us -> 11.9 us  [across(): return lax.ppermute(x, 'blk', [(s, s ^ 1 << i) for s in range(parts)])]
    pallas_call x1, Pallas kernels: 1.39 us -> 0.78 us  [pack(): pl.pallas_call(pack_kernel, out_shape=jax.ShapeDtypeStruct(shape, train_o...]
  transfers between devices with their start and end apart: 9 -> 9, of which waited for: 5 -> 6; matrix products, arithmetic and copies ran while one was open for 1% -> 0% of each run, Pallas kernels for 9% -> 11%
where the time goes in v6:
time: 28.6 us; the launch traced here: 28.3 us
  starting transfers between devices  12.4 us (43%)
  waiting for transfers between devices  9.78 us (34%)
  Pallas kernels  4.72 us (17%)
  between operations  1.39 us (5%)
    ppermute x6, starting transfers between devices, across(): return lax.ppermute(x, 'blk', [(s, s ^ 1 << i) for s in range(parts)])  11.9 us
    ppermute x6, waiting for transfers between devices, across(): return lax.ppermute(x, 'blk', [(s, s ^ 1 << i) for s in range(parts)])  8.6 us
    pallas_call x1, Pallas kernels, project(): pl.pallas_call(functools.partial(project_kernel, chunks), out_shape=jax.S...  2.33 us
    pallas_call x1, Pallas kernels, score(): pl.pallas_call(score_kernel, out_shape=jax.ShapeDtypeStruct((own.shape[0]...  1.55 us
    ppermute x1, waiting for transfers between devices, direct(): other = lax.ppermute(own, 'fsdp', swap)  1.17 us
    pallas_call x1, Pallas kernels, pack(): pl.pallas_call(pack_kernel, out_shape=jax.ShapeDtypeStruct(shape, train_o...  0.78 us
  transfers between devices with their start and end apart: 9, of which 6 were waited for; matrix products, arithmetic and copies ran while one was open for 0% of the time, Pallas kernels for 11%

profile of v6, /device:TPU:0, one launch (start us, length us, event | category | flops | bytes accessed | tf_op | source)
XLA Modules:
  0.0 28.3 jit_solution(9111195124463597574)
XLA Ops:
  0.0 0.5 %collective-permute-start = (f32[256,256]{1,0:T(8,128)}, f32[256,256]{1,0:T(8,128)S(1)}, u32[]{:S(2)}, u32[]{:S(2)}) collective-permute-start(f32[256,256]{1,0:T(8,128)} %eigen.1), channel_id=1, source_target_pairs={{0,1},{1,0},{2,3},{3,2},{4,5},{5,4},{6,7},{7,6},{8,9},{9,8},{10,11... | collective-permute-start | bytes 786440 | tf_op jit(solution)/shard_map/ppermute | solution.py:265
  0.5 0.8 %shard_map.92.first = bf16[1,32,768]{2,1,0:T(8,128)(2,1)S(1)} custom-call(bf16[1,32,512]{2,1,0:T(8,128)(2,1)} %train_out.1, bf16[1,32,256]{2,1,0:T(8,128)(2,1)} %train_act.1), custom_call_target="tpu_custom_call" | custom-call | tf_op jit(solution)/shard_map/pallas_call | solution.py:52
  1.2 3.7 %collective-permute-start.1 = (bf16[1,32,768]{2,1,0:T(8,128)(2,1)S(1)}, bf16[1,32,768]{2,1,0:T(8,128)(2,1)S(1)}, u32[]{:S(2)}, u32[]{:S(2)}) collective-permute-start(bf16[1,32,768]{2,1,0:T(8,128)(2,1)S(1)} %shard_map.92.first), channel_id=1, source_target_pairs={{0,8},{2,10},{4,12},{6,14},{8,0},{10,2},{12,4},{14,6},{1,9},{3,11}... | collective-permute-start | bytes 147464 | tf_op jit(solution)/shard_map/ppermute | solution.py:261
  6.2 0.0 copy-start
  6.2 2.3 %shard_map.91.total = f32[64,384]{1,0:T(8,128)S(1)} custom-call(bf16[64,3584]{1,0:T(8,128)(2,1)} %bitcast.25, bf16[64,1024]{1,0:T(8,128)(2,1)} %bitcast.28, bf16[3584,256]{1,0:T(8,128)(2,1)} %out_basis.1, bf16[1024,128]{1,0:T(8,128)(2,1)} %act_basis.1), custom_call_target="tpu_custom_call" | custom-call | flops 134217728 | bytes 2686976 | tf_op jit(solution)/shard_map/pallas_call | solution.py:126
  8.5 0.0 collective-permute-done.1.second
  8.6 0.0 collective-permute-done.after.other_eigen
  8.6 1.6 %collective-permute-start.2 = (f32[4,8,512]{2,1,0:T(8,128)S(1)}, f32[4,8,512]{2,1,0:T(8,128)S(1)}, u32[]{:S(2)}, u32[]{:S(2)}) collective-permute-start(f32[4,8,512]{2,1,0:T(8,128)S(1)} %get-tuple-element.9), channel_id=1, source_target_pairs={{0,2},{2,0},{4,6},{6,4},{8,10},{10,8},{12,14},{14,12},{1,3},{3,1},... | collective-permute-start | bytes 196616 | tf_op jit(solution)/shard_map/ppermute | solution.py:261
  10.2 1.6 %collective-permute-start.6 = (bf16[2,32,768]{2,1,0:T(8,128)(2,1)S(1)}, bf16[2,32,768]{2,1,0:T(8,128)(2,1)S(1)}, u32[]{:S(2)}, u32[]{:S(2)}) collective-permute-start(bf16[2,32,768]{2,1,0:T(8,128)(2,1)S(1)} %get-tuple-element.10.first), channel_id=1, source_target_pairs={{0,4},{2,6},{4,0},{6,2},{8,12},{10,14},{12,8},{14,10},{1,5},{3,7},... | collective-permute-start | bytes 294920 | tf_op jit(solution)/shard_map/ppermute | solution.py:261
  11.7 1.2 %collective-permute-done.2 = f32[4,8,512]{2,1,0:T(8,128)S(1)} collective-permute-done((f32[4,8,512]{2,1,0:T(8,128)S(1)}, f32[4,8,512]{2,1,0:T(8,128)S(1)}, u32[]{:S(2)}, u32[]{:S(2)}) %collective-permute-start.2) | collective-permute-done | bytes 65568 | tf_op jit(solution)/shard_map/ppermute | solution.py:261
  13.0 1.6 %collective-permute-start.3 = (f32[2,8,512]{2,1,0:T(8,128)S(1)}, f32[2,8,512]{2,1,0:T(8,128)S(1)}, u32[]{:S(2)}, u32[]{:S(2)}) collective-permute-start(f32[2,8,512]{2,1,0:T(8,128)S(1)} %get-tuple-element.12), channel_id=1, source_target_pairs={{0,4},{2,6},{4,0},{6,2},{8,12},{10,14},{12,8},{14,10},{1,5},{3,7},... | collective-permute-start | bytes 98312 | tf_op jit(solution)/shard_map/ppermute | solution.py:261
  14.6 0.3 %collective-permute-done.6.second = bf16[2,32,768]{2,1,0:T(8,128)(2,1)S(1)} collective-permute-done((bf16[2,32,768]{2,1,0:T(8,128)(2,1)S(1)}, bf16[2,32,768]{2,1,0:T(8,128)(2,1)S(1)}, u32[]{:S(2)}, u32[]{:S(2)}) %collective-permute-start.6) | collective-permute-done | bytes 98336 | tf_op jit(solution)/shard_map/ppermute | solution.py:261
  14.9 1.2 %collective-permute-start.7 = (bf16[4,32,768]{2,1,0:T(8,128)(2,1)S(1)}, bf16[4,32,768]{2,1,0:T(8,128)(2,1)S(1)}, u32[]{:S(2)}, u32[]{:S(2)}) collective-permute-start(bf16[4,32,768]{2,1,0:T(8,128)(2,1)S(1)} %shard_map.94.first), channel_id=1, source_target_pairs={{0,2},{2,0},{4,6},{6,4},{8,10},{10,8},{12,14},{14,12},{1,3},{3,1},... | collective-permute-start | bytes 589832 | tf_op jit(solution)/shard_map/ppermute | solution.py:261
  16.2 0.8 %collective-permute-done.3 = f32[2,8,512]{2,1,0:T(8,128)S(1)} collective-permute-done((f32[2,8,512]{2,1,0:T(8,128)S(1)}, f32[2,8,512]{2,1,0:T(8,128)S(1)}, u32[]{:S(2)}, u32[]{:S(2)}) %collective-permute-start.3) | collective-permute-done | bytes 32800 | tf_op jit(solution)/shard_map/ppermute | solution.py:261
  16.9 3.8 %collective-permute-done.7.second = bf16[4,32,768]{2,1,0:T(8,128)(2,1)S(1)} collective-permute-done((bf16[4,32,768]{2,1,0:T(8,128)(2,1)S(1)}, bf16[4,32,768]{2,1,0:T(8,128)(2,1)S(1)}, u32[]{:S(2)}, u32[]{:S(2)}) %collective-permute-start.7) | collective-permute-done | bytes 196640 | tf_op jit(solution)/shard_map/ppermute | solution.py:261
  20.8 0.1 collective-permute-start.8
  20.9 2.2 %collective-permute-start.4 = (f32[1,8,512]{2,1,0:T(8,128)S(1)}, f32[1,8,512]{2,1,0:T(8,128)S(1)}, u32[]{:S(2)}, u32[]{:S(2)}) collective-permute-start(f32[1,8,512]{2,1,0:T(8,128)S(1)} %get-tuple-element.14), channel_id=1, source_target_pairs={{0,8},{2,10},{4,12},{6,14},{8,0},{10,2},{12,4},{14,6},{1,9},{3,11}... | collective-permute-start | bytes 49160 | tf_op jit(solution)/shard_map/ppermute | solution.py:261
  23.1 2.5 %collective-permute-done.4 = f32[1,8,512]{2,1,0:T(8,128)S(1)} collective-permute-done((f32[1,8,512]{2,1,0:T(8,128)S(1)}, f32[1,8,512]{2,1,0:T(8,128)S(1)}, u32[]{:S(2)}, u32[]{:S(2)}) %collective-permute-start.4) | collective-permute-done | bytes 16416 | tf_op jit(solution)/shard_map/ppermute | solution.py:261
  25.6 0.0 collective-permute-start.5
  25.6 1.2 %collective-permute-done.5.other = f32[8,512]{1,0:T(8,128)S(1)} collective-permute-done((f32[8,512]{1,0:T(8,128)S(1)}, f32[8,512]{1,0:T(8,128)S(1)}, u32[]{:S(2)}, u32[]{:S(2)}) %collective-permute-start.5) | collective-permute-done | bytes 16416 | tf_op jit(solution)/shard_map/ppermute | solution.py:279
  26.8 0.0 collective-permute-done.8.other_block
  26.8 0.0 copy-done
  26.8 1.5 %shard_map.96 = f32[2,16]{1,0:T(2,128)} custom-call(s32[1]{0:T(128)} %bitcast.core_ref, f32[8,512]{1,0:T(8,128)S(1)} %add_bitcast_fusion.1.own, f32[8,512]{1,0:T(8,128)S(1)} %collective-permute-done.5.other, f32[256,256]{1,0:T(8,128)S(1)} %copy-done, f32[256,256]{1,0:T(8,128)S(1)} %collective-permute-done.after.other_eigen, ...), custom_call_target="tpu_custom_call" | custom-call | tf_op jit(solution)/shard_map/pallas_call | solution.py:234
  (8 shorter events, 0.1 us)
Async XLA Ops:
  0.0 8.6 %collective-permute-start = (f32[256,256]{1,0:T(8,128)}, f32[256,256]{1,0:T(8,128)S(1)}, u32[]{:S(2)}, u32[]{:S(2)}) collective-permute-start(f32[256,256]{1,0:T(8,128)} %eigen.1), channel_id=1, source_target_pairs={{0,1},{1,0},{2,3},{3,2},{4,5},{5,4},{6,7},{7,6},{8,9},{9,8},{10,11... | collective-permute-start | bytes 786440 | tf_op jit(solution)/shard_map/ppermute | solution.py:265
  1.2 7.3 %collective-permute-start.1 = (bf16[1,32,768]{2,1,0:T(8,128)(2,1)S(1)}, bf16[1,32,768]{2,1,0:T(8,128)(2,1)S(1)}, u32[]{:S(2)}, u32[]{:S(2)}) collective-permute-start(bf16[1,32,768]{2,1,0:T(8,128)(2,1)S(1)} %shard_map.92.first), channel_id=1, source_target_pairs={{0,8},{2,10},{4,12},{6,14},{8,0},{10,2},{12,4},{14,6},{1,9},{3,11}... | collective-permute-start | bytes 147464 | tf_op jit(solution)/shard_map/ppermute | solution.py:261
  6.2 20.6 %copy-start = (f32[256,256]{1,0:T(8,128)S(1)}, f32[256,256]{1,0:T(8,128)}, u32[]{:S(2)}) copy-start(f32[256,256]{1,0:T(8,128)} %eigen.1) | copy-start | bytes 786436
  8.6 4.3 %collective-permute-start.2 = (f32[4,8,512]{2,1,0:T(8,128)S(1)}, f32[4,8,512]{2,1,0:T(8,128)S(1)}, u32[]{:S(2)}, u32[]{:S(2)}) collective-permute-start(f32[4,8,512]{2,1,0:T(8,128)S(1)} %get-tuple-element.9), channel_id=1, source_target_pairs={{0,2},{2,0},{4,6},{6,4},{8,10},{10,8},{12,14},{14,12},{1,3},{3,1},... | collective-permute-start | bytes 196616 | tf_op jit(solution)/shard_map/ppermute | solution.py:261
  10.2 4.8 %collective-permute-start.6 = (bf16[2,32,768]{2,1,0:T(8,128)(2,1)S(1)}, bf16[2,32,768]{2,1,0:T(8,128)(2,1)S(1)}, u32[]{:S(2)}, u32[]{:S(2)}) collective-permute-start(bf16[2,32,768]{2,1,0:T(8,128)(2,1)S(1)} %get-tuple-element.10.first), channel_id=1, source_target_pairs={{0,4},{2,6},{4,0},{6,2},{8,12},{10,14},{12,8},{14,10},{1,5},{3,7},... | collective-permute-start | bytes 294920 | tf_op jit(solution)/shard_map/ppermute | solution.py:261
  13.0 4.0 %collective-permute-start.3 = (f32[2,8,512]{2,1,0:T(8,128)S(1)}, f32[2,8,512]{2,1,0:T(8,128)S(1)}, u32[]{:S(2)}, u32[]{:S(2)}) collective-permute-start(f32[2,8,512]{2,1,0:T(8,128)S(1)} %get-tuple-element.12), channel_id=1, source_target_pairs={{0,4},{2,6},{4,0},{6,2},{8,12},{10,14},{12,8},{14,10},{1,5},{3,7},... | collective-permute-start | bytes 98312 | tf_op jit(solution)/shard_map/ppermute | solution.py:261
  14.9 5.9 %collective-permute-start.7 = (bf16[4,32,768]{2,1,0:T(8,128)(2,1)S(1)}, bf16[4,32,768]{2,1,0:T(8,128)(2,1)S(1)}, u32[]{:S(2)}, u32[]{:S(2)}) collective-permute-start(bf16[4,32,768]{2,1,0:T(8,128)(2,1)S(1)} %shard_map.94.first), channel_id=1, source_target_pairs={{0,2},{2,0},{4,6},{6,4},{8,10},{10,8},{12,14},{14,12},{1,3},{3,1},... | collective-permute-start | bytes 589832 | tf_op jit(solution)/shard_map/ppermute | solution.py:261
  20.8 6.0 %collective-permute-start.8 = (bf16[8,32,768]{2,1,0:T(8,128)(2,1)S(1)}, bf16[8,32,768]{2,1,0:T(8,128)(2,1)S(1)}, u32[]{:S(2)}, u32[]{:S(2)}) collective-permute-start(bf16[8,32,768]{2,1,0:T(8,128)(2,1)S(1)} %shard_map.95.block), channel_id=1, source_target_pairs={{0,1},{1,0},{2,3},{3,2},{4,5},{5,4},{6,7},{7,6},{8,9},{9,8},{10,11... | collective-permute-start | bytes 1179656 | tf_op jit(solution)/shard_map/ppermute | solution.py:280
  20.9 4.7 %collective-permute-start.4 = (f32[1,8,512]{2,1,0:T(8,128)S(1)}, f32[1,8,512]{2,1,0:T(8,128)S(1)}, u32[]{:S(2)}, u32[]{:S(2)}) collective-permute-start(f32[1,8,512]{2,1,0:T(8,128)S(1)} %get-tuple-element.14), channel_id=1, source_target_pairs={{0,8},{2,10},{4,12},{6,14},{8,0},{10,2},{12,4},{14,6},{1,9},{3,11}... | collective-permute-start | bytes 49160 | tf_op jit(solution)/shard_map/ppermute | solution.py:261
  25.6 1.2 %collective-permute-start.5 = (f32[8,512]{1,0:T(8,128)S(1)}, f32[8,512]{1,0:T(8,128)S(1)}, u32[]{:S(2)}, u32[]{:S(2)}) collective-permute-start(f32[8,512]{1,0:T(8,128)S(1)} %add_bitcast_fusion.1.own), channel_id=1, source_target_pairs={{0,1},{1,0},{2,3},{3,2},{4,5},{5,4},{6,7},{7,6},{8,9},{9,8},{10,11... | collective-permute-start | bytes 49160 | tf_op jit(solution)/shard_map/ppermute | solution.py:279

commit v7 on v6

--- a/solution.py
+++ b/solution.py
@@ -9,7 +9,7 @@
 
 RQ = 4
 LANES = 128
-MOST_DIRECT = 16
+DIRECT_PARTS = 8
 
 
 damping = 0.1
@@ -59,27 +59,66 @@
     )(pinned(train_out), pinned(train_act))
 
 
-def join_kernel(after, first, second, joined):
+def joined_shape(blocks):
+    first = blocks[0]
+    count = sum(x.shape[0] for x in blocks)
+    return jax.ShapeDtypeStruct((count,) + first.shape[1:], first.dtype)
+
+
+def join_into(joined, blocks):
+    start = 0
+    for block in blocks:
+        joined[start : start + block.shape[0]] = block[...]
+        start += block.shape[0]
+
+
+def finish_kernel(held, summand, *rest):
+    blocks, (own, joined) = rest[:-2], rest[-2:]
+    own[...] = held[...] + summand[...]
+    join_into(joined, blocks)
+
+
+def finish(held, summand, blocks):
+    return pl.pallas_call(
+        finish_kernel,
+        out_shape=[jax.ShapeDtypeStruct(held.shape, held.dtype), joined_shape(blocks)],
+        in_specs=[spec(pltpu.VMEM)] * (2 + len(blocks)),
+        out_specs=[spec(pltpu.VMEM)] * 2,
+        compiler_params=grant(4),
+    )(held, summand, *blocks)
+
+
+def fold_kernel(after, held, summand, kept, moved):
     del after
-    count = first.shape[0]
-    joined[:count] = first[...]
-    joined[count:] = second[...]
-
-
-def joined_shape(first, second):
-    return jax.ShapeDtypeStruct(
-        (first.shape[0] + second.shape[0],) + first.shape[1:], first.dtype
-    )
-
-
-def join(after, first, second):
-    return pl.pallas_call(
-        join_kernel,
-        out_shape=joined_shape(first, second),
+    for part in range(kept.shape[0]):
+        kept[part] = held[2 * part] + summand[2 * part]
+        moved[part] = held[2 * part + 1] + summand[2 * part + 1]
+
+
+def fold(after, held, summand):
+    half = jax.ShapeDtypeStruct((held.shape[0] // 2,) + held.shape[1:], held.dtype)
+    return pl.pallas_call(
+        fold_kernel,
+        out_shape=[half, half],
         in_specs=[spec(pl.ANY)] + [spec(pltpu.VMEM)] * 2,
+        out_specs=[spec(pltpu.VMEM)] * 2,
+        compiler_params=grant(4),
+    )(after, held, summand)
+
+
+def relay_kernel(after, source, target):
+    del after
+    target[...] = source[...]
+
+
+def relay(after, source):
+    return pl.pallas_call(
+        relay_kernel,
+        out_shape=jax.ShapeDtypeStruct(source.shape, source.dtype),
+        in_specs=[spec(pl.ANY), spec(pltpu.VMEM)],
         out_specs=spec(pltpu.VMEM),
-        compiler_params=grant(4),
-    )(after, first, second)
+        compiler_params=grant(2),
+    )(after, source)
 
 
 def project_kernel(
@@ -159,7 +198,7 @@
         piece = (moved if part % 2 else kept).at[part // 2]
         piece[:, :width] = total[pl.ds(start, local_rows), :]
         piece[:, width:] = jnp.where(row == doubling_slot(part, parts), facts, 0.0)
-    join_kernel(None, first, second, joined)
+    join_into(joined, (first, second))
 
 
 def spread(place, tokens, ids, after, total, first, second, parts):
@@ -168,7 +207,7 @@
     )
     return pl.pallas_call(
         spread_kernel,
-        out_shape=[half, half, joined_shape(first, second)],
+        out_shape=[half, half, joined_shape((first, second))],
         in_specs=[spec(pltpu.SMEM)] * 3 + [spec(pl.ANY)] + [spec(pltpu.VMEM)] * 3,
         out_specs=[spec(pltpu.VMEM)] * 3,
         compiler_params=grant(4),
@@ -269,13 +308,12 @@
     kept, moved, block = spread(
         place, train_tokens, train_ids, other_eigen, total, block, arrived, parts
     )
-    for i in range(steps - 1):
-        sums = kept + across(moved, i)
-        sums = sums.reshape((sums.shape[0] // 2, 2) + sums.shape[1:])
-        arrived = across(block, steps - 2 - i)
-        kept, moved = sums[:, 0], sums[:, 1]
-        block = join(kept, block, arrived)
-    own = (kept + across(moved, steps - 1)).reshape(kept.shape[1:])
+    second = across(block, 1)
+    third = across(block, 0)
+    kept, moved = fold(block, kept, across(moved, 0))
+    fourth = across(relay(kept, second), 0)
+    kept, moved = fold(second, kept, across(moved, 1))
+    own, block = finish(kept[0], across(moved[0], 2), (block, second, third, fourth))
     other = lax.ppermute(own, "fsdp", swap)
     other_block = lax.ppermute(block, "fsdp", swap)
     return score(core, own, other, eigenvalues, other_eigen, block, other_block)
@@ -336,7 +374,7 @@
 
 def solution(mesh):
     parts = mesh.shape["blk"]
-    few = parts <= MOST_DIRECT and parts & (parts - 1) == 0 and mesh.shape["fsdp"] == 2
+    few = parts == DIRECT_PARTS and mesh.shape["fsdp"] == 2
     return jax.shard_map(
         direct if few else gathered,
         mesh=mesh,

time: 28.6 us -> 29.1 us (1.017)
  starting transfers between devices: 12.4 us -> 12.7 us
    ppermute x1, starting transfers between devices: 0.01 us -> 0.5 us  [direct(): other = lax.ppermute(own, 'fsdp', swap)]
    ppermute x6 -> x7, starting transfers between devices: 11.9 us -> 11.7 us  [across(): return lax.ppermute(x, 'blk', [(s, s ^ 1 << i) for s in range(parts)])]
    ppermute x6 -> x7, waiting for transfers between devices: 8.6 us -> 8.73 us  [across(): return lax.ppermute(x, 'blk', [(s, s ^ 1 << i) for s in range(parts)])]
  transfers between devices with their start and end apart: 9 -> 10, of which waited for: 6 -> 4; matrix products, arithmetic and copies ran while one was open for 0% -> 0% of each run, Pallas kernels for 11% -> 11%
where the time goes in v7:
time: 29.1 us; the launch traced here: 28.8 us
  starting transfers between devices  12.7 us (44%)
  waiting for transfers between devices  9.97 us (34%)
  Pallas kernels  4.73 us (16%)
  between operations  1.39 us (5%)
    ppermute x7, starting transfers between devices, across(): return lax.ppermute(x, 'blk', [(s, s ^ 1 << i) for s in range(parts)])  11.7 us
    ppermute x7, waiting for transfers between devices, across(): return lax.ppermute(x, 'blk', [(s, s ^ 1 << i) for s in range(parts)])  8.73 us
    pallas_call x1, Pallas kernels, project(): pl.pallas_call(functools.partial(project_kernel, chunks), out_shape=jax.S...  2.33 us
    pallas_call x1, Pallas kernels, score(): pl.pallas_call(score_kernel, out_shape=jax.ShapeDtypeStruct((own.shape[0]...  1.55 us
    ppermute x1, waiting for transfers between devices, direct(): other = lax.ppermute(own, 'fsdp', swap)  1.24 us
    pallas_call x1, Pallas kernels, pack(): pl.pallas_call(pack_kernel, out_shape=jax.ShapeDtypeStruct(shape, train_o...  0.78 us
  transfers between devices with their start and end apart: 10, of which 4 were waited for; matrix products, arithmetic and copies ran while one was open for 0% of the time, Pallas kernels for 11%

profile of v7, /device:TPU:0, one launch (start us, length us, event | category | flops | bytes accessed | tf_op | source)
XLA Modules:
  0.0 28.8 jit_solution(2196578489848325558)
XLA Ops:
  0.0 0.5 %collective-permute-start = (f32[256,256]{1,0:T(8,128)}, f32[256,256]{1,0:T(8,128)S(1)}, u32[]{:S(2)}, u32[]{:S(2)}) collective-permute-start(f32[256,256]{1,0:T(8,128)} %eigen.1), channel_id=1, source_target_pairs={{0,1},{1,0},{2,3},{3,2},{4,5},{5,4},{6,7},{7,6},{8,9},{9,8},{10,11... | collective-permute-start | bytes 786440 | tf_op jit(solution)/shard_map/ppermute | solution.py:304
  0.5 0.8 %shard_map.92.first = bf16[1,32,768]{2,1,0:T(8,128)(2,1)S(1)} custom-call(bf16[1,32,512]{2,1,0:T(8,128)(2,1)} %train_out.1, bf16[1,32,256]{2,1,0:T(8,128)(2,1)} %train_act.1), custom_call_target="tpu_custom_call" | custom-call | tf_op jit(solution)/shard_map/pallas_call | solution.py:52
  1.2 3.7 %collective-permute-start.1 = (bf16[1,32,768]{2,1,0:T(8,128)(2,1)S(1)}, bf16[1,32,768]{2,1,0:T(8,128)(2,1)S(1)}, u32[]{:S(2)}, u32[]{:S(2)}) collective-permute-start(bf16[1,32,768]{2,1,0:T(8,128)(2,1)S(1)} %shard_map.92.first), channel_id=1, source_target_pairs={{0,8},{2,10},{4,12},{6,14},{8,0},{10,2},{12,4},{14,6},{1,9},{3,11}... | collective-permute-start | bytes 147464 | tf_op jit(solution)/shard_map/ppermute | solution.py:300
  6.2 0.0 copy-start
  6.2 2.3 %shard_map.91.total = f32[64,384]{1,0:T(8,128)S(1)} custom-call(bf16[64,3584]{1,0:T(8,128)(2,1)} %bitcast.8, bf16[64,1024]{1,0:T(8,128)(2,1)} %bitcast.9, bf16[3584,256]{1,0:T(8,128)(2,1)} %out_basis.1, bf16[1024,128]{1,0:T(8,128)(2,1)} %act_basis.1), custom_call_target="tpu_custom_call" | custom-call | flops 134217728 | bytes 2686976 | tf_op jit(solution)/shard_map/pallas_call | solution.py:165
  8.5 0.0 collective-permute-done.1.second
  8.6 0.0 collective-permute-done.after.other_eigen
  8.6 1.6 %collective-permute-start.2 = (bf16[2,32,768]{2,1,0:T(8,128)(2,1)S(1)}, bf16[2,32,768]{2,1,0:T(8,128)(2,1)S(1)}, u32[]{:S(2)}, u32[]{:S(2)}) collective-permute-start(bf16[2,32,768]{2,1,0:T(8,128)(2,1)S(1)} %get-tuple-element.14.after.rest_0_), channel_id=1, source_target_pairs={{0,4},{2,6},{4,0},{6,2},{8,12},{10,14},{12,8},{14,10},{1,5},{3,7},... | collective-permute-start | bytes 294920 | tf_op jit(solution)/shard_map/ppermute | solution.py:300
  10.2 1.5 %collective-permute-start.3 = (f32[4,8,512]{2,1,0:T(8,128)S(1)}, f32[4,8,512]{2,1,0:T(8,128)S(1)}, u32[]{:S(2)}, u32[]{:S(2)}) collective-permute-start(f32[4,8,512]{2,1,0:T(8,128)S(1)} %get-tuple-element.16), channel_id=1, source_target_pairs={{0,2},{2,0},{4,6},{6,4},{8,10},{10,8},{12,14},{14,12},{1,3},{3,1},... | collective-permute-start | bytes 196616 | tf_op jit(solution)/shard_map/ppermute | solution.py:300
  11.7 0.5 %collective-permute-start.6 = (bf16[2,32,768]{2,1,0:T(8,128)(2,1)S(1)}, bf16[2,32,768]{2,1,0:T(8,128)(2,1)S(1)}, u32[]{:S(2)}, u32[]{:S(2)}) collective-permute-start(bf16[2,32,768]{2,1,0:T(8,128)(2,1)S(1)} %get-tuple-element.14.after.rest_0_), channel_id=1, source_target_pairs={{0,2},{2,0},{4,6},{6,4},{8,10},{10,8},{12,14},{14,12},{1,3},{3,1},... | collective-permute-start | bytes 294920 | tf_op jit(solution)/shard_map/ppermute | solution.py:300
  12.3 2.7 %collective-permute-done.3.summand = f32[4,8,512]{2,1,0:T(8,128)S(1)} collective-permute-done((f32[4,8,512]{2,1,0:T(8,128)S(1)}, f32[4,8,512]{2,1,0:T(8,128)S(1)}, u32[]{:S(2)}, u32[]{:S(2)}) %collective-permute-start.3) | collective-permute-done | bytes 65568 | tf_op jit(solution)/shard_map/ppermute | solution.py:300
  15.0 0.0 collective-permute-done.2.after.source.rest_1_
  15.0 1.7 %collective-permute-start.7 = (bf16[2,32,768]{2,1,0:T(8,128)(2,1)S(1)}, bf16[2,32,768]{2,1,0:T(8,128)(2,1)S(1)}, u32[]{:S(2)}, u32[]{:S(2)}) collective-permute-start(bf16[2,32,768]{2,1,0:T(8,128)(2,1)S(1)} %shard_map.96), channel_id=1, source_target_pairs={{0,2},{2,0},{4,6},{6,4},{8,10},{10,8},{12,14},{14,12},{1,3},{3,1},... | collective-permute-start | bytes 294920 | tf_op jit(solution)/shard_map/ppermute | solution.py:300
  16.8 0.4 %collective-permute-start.4 = (f32[2,8,512]{2,1,0:T(8,128)S(1)}, f32[2,8,512]{2,1,0:T(8,128)S(1)}, u32[]{:S(2)}, u32[]{:S(2)}) collective-permute-start(f32[2,8,512]{2,1,0:T(8,128)S(1)} %get-tuple-element.18), channel_id=1, source_target_pairs={{0,4},{2,6},{4,0},{6,2},{8,12},{10,14},{12,8},{14,10},{1,5},{3,7},... | collective-permute-start | bytes 98312 | tf_op jit(solution)/shard_map/ppermute | solution.py:300
  17.2 3.5 %collective-permute-done.4.summand = f32[2,8,512]{2,1,0:T(8,128)S(1)} collective-permute-done((f32[2,8,512]{2,1,0:T(8,128)S(1)}, f32[2,8,512]{2,1,0:T(8,128)S(1)}, u32[]{:S(2)}, u32[]{:S(2)}) %collective-permute-start.4) | collective-permute-done | bytes 32800 | tf_op jit(solution)/shard_map/ppermute | solution.py:300
  20.7 2.2 %collective-permute-start.5 = (f32[8,512]{1,0:T(8,128)S(1)}, f32[8,512]{1,0:T(8,128)S(1)}, u32[]{:S(2)}, u32[]{:S(2)}) collective-permute-start(f32[8,512]{1,0:T(8,128)S(1)} %bitcast.7), channel_id=1, source_target_pairs={{0,8},{2,10},{4,12},{6,14},{8,0},{10,2},{12,4},{14,6},{1,9},{3,11}... | collective-permute-start | bytes 49160 | tf_op jit(solution)/shard_map/ppermute | solution.py:300
  22.9 0.0 collective-permute-done.6.rest_2_
  22.9 2.5 %collective-permute-done.5.summand = f32[8,512]{1,0:T(8,128)S(1)} collective-permute-done((f32[8,512]{1,0:T(8,128)S(1)}, f32[8,512]{1,0:T(8,128)S(1)}, u32[]{:S(2)}, u32[]{:S(2)}) %collective-permute-start.5) | collective-permute-done | bytes 16416 | tf_op jit(solution)/shard_map/ppermute | solution.py:300
  25.4 0.0 collective-permute-done.7.rest_3_
  25.5 0.1 collective-permute-start.9
  25.5 0.5 %collective-permute-start.8 = (f32[8,512]{1,0:T(8,128)S(1)}, f32[8,512]{1,0:T(8,128)S(1)}, u32[]{:S(2)}, u32[]{:S(2)}) collective-permute-start(f32[8,512]{1,0:T(8,128)S(1)} %get-tuple-element.21.own), channel_id=1, source_target_pairs={{0,1},{1,0},{2,3},{3,2},{4,5},{5,4},{6,7},{7,6},{8,9},{9,8},{10,11... | collective-permute-start | bytes 49160 | tf_op jit(solution)/shard_map/ppermute | solution.py:317
  26.0 1.2 %collective-permute-done.8.other = f32[8,512]{1,0:T(8,128)S(1)} collective-permute-done((f32[8,512]{1,0:T(8,128)S(1)}, f32[8,512]{1,0:T(8,128)S(1)}, u32[]{:S(2)}, u32[]{:S(2)}) %collective-permute-start.8) | collective-permute-done | bytes 16416 | tf_op jit(solution)/shard_map/ppermute | solution.py:317
  27.3 0.0 collective-permute-done.9.other_block
  27.3 1.5 %shard_map.98 = f32[2,16]{1,0:T(2,128)} custom-call(s32[1]{0:T(128)} %bitcast.core_ref, f32[8,512]{1,0:T(8,128)S(1)} %get-tuple-element.21.own, f32[8,512]{1,0:T(8,128)S(1)} %collective-permute-done.8.other, f32[256,256]{1,0:T(8,128)S(1)} %copy-done, f32[256,256]{1,0:T(8,128)S(1)} %collective-permute-done.after.other_eigen, ...), custom_call_target="tpu_custom_call" | custom-call | tf_op jit(solution)/shard_map/pallas_call | solution.py:273
  (6 shorter events, 0.1 us)
Async XLA Ops:
  0.0 8.6 %collective-permute-start = (f32[256,256]{1,0:T(8,128)}, f32[256,256]{1,0:T(8,128)S(1)}, u32[]{:S(2)}, u32[]{:S(2)}) collective-permute-start(f32[256,256]{1,0:T(8,128)} %eigen.1), channel_id=1, source_target_pairs={{0,1},{1,0},{2,3},{3,2},{4,5},{5,4},{6,7},{7,6},{8,9},{9,8},{10,11... | collective-permute-start | bytes 786440 | tf_op jit(solution)/shard_map/ppermute | solution.py:304
  1.2 7.3 %collective-permute-start.1 = (bf16[1,32,768]{2,1,0:T(8,128)(2,1)S(1)}, bf16[1,32,768]{2,1,0:T(8,128)(2,1)S(1)}, u32[]{:S(2)}, u32[]{:S(2)}) collective-permute-start(bf16[1,32,768]{2,1,0:T(8,128)(2,1)S(1)} %shard_map.92.first), channel_id=1, source_target_pairs={{0,8},{2,10},{4,12},{6,14},{8,0},{10,2},{12,4},{14,6},{1,9},{3,11}... | collective-permute-start | bytes 147464 | tf_op jit(solution)/shard_map/ppermute | solution.py:300
  6.2 21.1 %copy-start = (f32[256,256]{1,0:T(8,128)S(1)}, f32[256,256]{1,0:T(8,128)}, u32[]{:S(2)}) copy-start(f32[256,256]{1,0:T(8,128)} %eigen.1) | copy-start | bytes 786436
  8.6 6.4 %collective-permute-start.2 = (bf16[2,32,768]{2,1,0:T(8,128)(2,1)S(1)}, bf16[2,32,768]{2,1,0:T(8,128)(2,1)S(1)}, u32[]{:S(2)}, u32[]{:S(2)}) collective-permute-start(bf16[2,32,768]{2,1,0:T(8,128)(2,1)S(1)} %get-tuple-element.14.after.rest_0_), channel_id=1, source_target_pairs={{0,4},{2,6},{4,0},{6,2},{8,12},{10,14},{12,8},{14,10},{1,5},{3,7},... | collective-permute-start | bytes 294920 | tf_op jit(solution)/shard_map/ppermute | solution.py:300
  10.2 4.8 %collective-permute-start.3 = (f32[4,8,512]{2,1,0:T(8,128)S(1)}, f32[4,8,512]{2,1,0:T(8,128)S(1)}, u32[]{:S(2)}, u32[]{:S(2)}) collective-permute-start(f32[4,8,512]{2,1,0:T(8,128)S(1)} %get-tuple-element.16), channel_id=1, source_target_pairs={{0,2},{2,0},{4,6},{6,4},{8,10},{10,8},{12,14},{14,12},{1,3},{3,1},... | collective-permute-start | bytes 196616 | tf_op jit(solution)/shard_map/ppermute | solution.py:300
  11.7 11.2 %collective-permute-start.6 = (bf16[2,32,768]{2,1,0:T(8,128)(2,1)S(1)}, bf16[2,32,768]{2,1,0:T(8,128)(2,1)S(1)}, u32[]{:S(2)}, u32[]{:S(2)}) collective-permute-start(bf16[2,32,768]{2,1,0:T(8,128)(2,1)S(1)} %get-tuple-element.14.after.rest_0_), channel_id=1, source_target_pairs={{0,2},{2,0},{4,6},{6,4},{8,10},{10,8},{12,14},{14,12},{1,3},{3,1},... | collective-permute-start | bytes 294920 | tf_op jit(solution)/shard_map/ppermute | solution.py:300
  15.0 10.4 %collective-permute-start.7 = (bf16[2,32,768]{2,1,0:T(8,128)(2,1)S(1)}, bf16[2,32,768]{2,1,0:T(8,128)(2,1)S(1)}, u32[]{:S(2)}, u32[]{:S(2)}) collective-permute-start(bf16[2,32,768]{2,1,0:T(8,128)(2,1)S(1)} %shard_map.96), channel_id=1, source_target_pairs={{0,2},{2,0},{4,6},{6,4},{8,10},{10,8},{12,14},{14,12},{1,3},{3,1},... | collective-permute-start | bytes 294920 | tf_op jit(solution)/shard_map/ppermute | solution.py:300
  16.8 3.9 %collective-permute-start.4 = (f32[2,8,512]{2,1,0:T(8,128)S(1)}, f32[2,8,512]{2,1,0:T(8,128)S(1)}, u32[]{:S(2)}, u32[]{:S(2)}) collective-permute-start(f32[2,8,512]{2,1,0:T(8,128)S(1)} %get-tuple-element.18), channel_id=1, source_target_pairs={{0,4},{2,6},{4,0},{6,2},{8,12},{10,14},{12,8},{14,10},{1,5},{3,7},... | collective-permute-start | bytes 98312 | tf_op jit(solution)/shard_map/ppermute | solution.py:300
  20.7 4.7 %collective-permute-start.5 = (f32[8,512]{1,0:T(8,128)S(1)}, f32[8,512]{1,0:T(8,128)S(1)}, u32[]{:S(2)}, u32[]{:S(2)}) collective-permute-start(f32[8,512]{1,0:T(8,128)S(1)} %bitcast.7), channel_id=1, source_target_pairs={{0,8},{2,10},{4,12},{6,14},{8,0},{10,2},{12,4},{14,6},{1,9},{3,11}... | collective-permute-start | bytes 49160 | tf_op jit(solution)/shard_map/ppermute | solution.py:300
  25.5 1.8 %collective-permute-start.9 = (bf16[8,32,768]{2,1,0:T(8,128)(2,1)S(1)}, bf16[8,32,768]{2,1,0:T(8,128)(2,1)S(1)}, u32[]{:S(2)}, u32[]{:S(2)}) collective-permute-start(bf16[8,32,768]{2,1,0:T(8,128)(2,1)S(1)} %get-tuple-element.22.block), channel_id=1, source_target_pairs={{0,1},{1,0},{2,3},{3,2},{4,5},{5,4},{6,7},{7,6},{8,9},{9,8},{10,11... | collective-permute-start | bytes 1179656 | tf_op jit(solution)/shard_map/ppermute | solution.py:318
  25.5 1.7 %collective-permute-start.8 = (f32[8,512]{1,0:T(8,128)S(1)}, f32[8,512]{1,0:T(8,128)S(1)}, u32[]{:S(2)}, u32[]{:S(2)}) collective-permute-start(f32[8,512]{1,0:T(8,128)S(1)} %get-tuple-element.21.own), channel_id=1, source_target_pairs={{0,1},{1,0},{2,3},{3,2},{4,5},{5,4},{6,7},{7,6},{8,9},{9,8},{10,11... | collective-permute-start | bytes 49160 | tf_op jit(solution)/shard_map/ppermute | solution.py:317

commit v8 on v6

--- a/solution.py
+++ b/solution.py
@@ -9,7 +9,7 @@
 
 RQ = 4
 LANES = 128
-MOST_DIRECT = 16
+DIRECT_PARTS = 8
 
 
 damping = 0.1
@@ -183,10 +183,13 @@
     return high, middle, low
 
 
-def score_kernel(core_ref, own, other, eigen, other_eigen, block, other_block, out):
+def score_kernel(core_ref, own, other, eigen, other_eigen, *rest):
+    out = rest[-1]
+    pairs = (rest[: len(rest) // 2], rest[len(rest) // 2 : -1])
     first = core_ref[0] == 0
     half, ka = eigen.shape
-    examples, factor_rows, width = block.shape
+    examples = sum(x.shape[0] for x in pairs[0])
+    _, factor_rows, width = pairs[0][0].shape
     ks = width - ka
     coords = (
         jnp.where(first, own[...], other[...]),
@@ -204,7 +207,8 @@
     weights, hot, flat = [], [], []
     lane = lax.broadcasted_iota(jnp.int32, (examples, LANES), 1).astype(jnp.float32)
     row = lax.broadcasted_iota(jnp.int32, (examples, factor_rows, ka), 1).astype(jnp.float32)
-    for facts, rows in ((own, block), (other, other_block)):
+    for facts, blocks in zip((own, other), pairs):
+        rows = jnp.concatenate([x[...] for x in blocks], axis=0)
         facts = facts[:, facts.shape[1] - LANES :]
         hot.append(lane == facts[:, :1])
         keep = row < facts[:, LANES // 2 : LANES // 2 + 1][:, :, None]
@@ -230,16 +234,15 @@
         out[q : q + 1, :] = scores[:, : out.shape[1]]
 
 
-def score(core, own, other, eigen, other_eigen, block, other_block):
+def score(core, own, other, eigen, other_eigen, blocks, other_blocks):
+    examples = sum(x.shape[0] for x in blocks + other_blocks)
     return pl.pallas_call(
         score_kernel,
-        out_shape=jax.ShapeDtypeStruct(
-            (own.shape[0] // RQ, block.shape[0] + other_block.shape[0]), jnp.float32
-        ),
-        in_specs=[spec(pltpu.SMEM)] + [spec(pltpu.VMEM)] * 6,
+        out_shape=jax.ShapeDtypeStruct((own.shape[0] // RQ, examples), jnp.float32),
+        in_specs=[spec(pltpu.SMEM)] + [spec(pltpu.VMEM)] * (4 + len(blocks + other_blocks)),
         out_specs=spec(pltpu.VMEM),
         compiler_params=grant(12),
-    )(core, own, other, eigen, other_eigen, block, other_block)
+    )(core, own, other, eigen, other_eigen, *blocks, *other_blocks)
 
 
 def direct(
@@ -269,16 +272,19 @@
     kept, moved, block = spread(
         place, train_tokens, train_ids, other_eigen, total, block, arrived, parts
     )
-    for i in range(steps - 1):
-        sums = kept + across(moved, i)
-        sums = sums.reshape((sums.shape[0] // 2, 2) + sums.shape[1:])
-        arrived = across(block, steps - 2 - i)
-        kept, moved = sums[:, 0], sums[:, 1]
-        block = join(kept, block, arrived)
-    own = (kept + across(moved, steps - 1)).reshape(kept.shape[1:])
+    sums = (kept + across(moved, 0)).reshape((2, 2) + kept.shape[1:])
+    arrived = across(block, 1)
+    kept, moved = sums[:, 0], sums[:, 1]
+    near = join(kept, block, arrived)
+    far = across(near, 0)
+    other_near = lax.ppermute(near, "fsdp", swap)
+    other_far = lax.ppermute(far, "fsdp", swap)
+    sums = kept + across(moved, 1)
+    own = sums[0] + across(sums[1], 2)
     other = lax.ppermute(own, "fsdp", swap)
-    other_block = lax.ppermute(block, "fsdp", swap)
-    return score(core, own, other, eigenvalues, other_eigen, block, other_block)
+    return score(
+        core, own, other, eigenvalues, other_eigen, (near, far), (other_near, other_far)
+    )
 
 
 def score_block(precond, out_rows, act_rows, token_counts):
@@ -336,7 +342,7 @@
 
 def solution(mesh):
     parts = mesh.shape["blk"]
-    few = parts <= MOST_DIRECT and parts & (parts - 1) == 0 and mesh.shape["fsdp"] == 2
+    few = parts == DIRECT_PARTS and mesh.shape["fsdp"] == 2
     return jax.shard_map(
         direct if few else gathered,
         mesh=mesh,

time: 28.6 us -> 24.6 us (0.86)
  waiting for transfers between devices: 9.78 us -> 6.21 us
  starting transfers between devices: 12.4 us -> 12.1 us
    ppermute x6, waiting for transfers between devices: 8.6 us -> 5.03 us  [across(): return lax.ppermute(x, 'blk', [(s, s ^ 1 << i) for s in range(parts)])]
  transfers between devices with their start and end apart: 9 -> 10, of which waited for: 6 -> 6; matrix products, arithmetic and copies ran while one was open for 0% -> 0% of each run, Pallas kernels for 11% -> 13%
where the time goes in v8:
time: 24.6 us; the launch traced here: 24.4 us
  starting transfers between devices  12.1 us (49%)
  waiting for transfers between devices  6.21 us (25%)
  Pallas kernels  4.69 us (19%)
  between operations  1.38 us (6%)
    ppermute x6, starting transfers between devices, across(): return lax.ppermute(x, 'blk', [(s, s ^ 1 << i) for s in range(parts)])  11.6 us
    ppermute x6, waiting for transfers between devices, across(): return lax.ppermute(x, 'blk', [(s, s ^ 1 << i) for s in range(parts)])  5.03 us
    pallas_call x1, Pallas kernels, project(): pl.pallas_call(functools.partial(project_kernel, chunks), out_shape=jax.S...  2.33 us
    pallas_call x1, Pallas kernels, score(): pl.pallas_call(score_kernel, out_shape=jax.ShapeDtypeStruct((own.shape[0]...  1.54 us
    ppermute x1, waiting for transfers between devices, direct(): other = lax.ppermute(own, 'fsdp', swap)  1.17 us
    pallas_call x1, Pallas kernels, pack(): pl.pallas_call(pack_kernel, out_shape=jax.ShapeDtypeStruct(shape, train_o...  0.78 us
  transfers between devices with their start and end apart: 10, of which 6 were waited for; matrix products, arithmetic and copies ran while one was open for 0% of the time, Pallas kernels for 13%

profile of v8, /device:TPU:0, one launch (start us, length us, event | category | flops | bytes accessed | tf_op | source)
XLA Modules:
  0.0 24.4 jit_solution(14859808432086979491)
XLA Ops:
  0.0 0.5 %collective-permute-start = (f32[256,256]{1,0:T(8,128)}, f32[256,256]{1,0:T(8,128)S(1)}, u32[]{:S(2)}, u32[]{:S(2)}) collective-permute-start(f32[256,256]{1,0:T(8,128)} %eigen.1), channel_id=1, source_target_pairs={{0,1},{1,0},{2,3},{3,2},{4,5},{5,4},{6,7},{7,6},{8,9},{9,8},{10,11... | collective-permute-start | bytes 786440 | tf_op jit(solution)/shard_map/ppermute | solution.py:268
  0.5 0.8 %shard_map.92.first = bf16[1,32,768]{2,1,0:T(8,128)(2,1)S(1)} custom-call(bf16[1,32,512]{2,1,0:T(8,128)(2,1)} %train_out.1, bf16[1,32,256]{2,1,0:T(8,128)(2,1)} %train_act.1), custom_call_target="tpu_custom_call" | custom-call | tf_op jit(solution)/shard_map/pallas_call | solution.py:52
  1.2 3.7 %collective-permute-start.1 = (bf16[1,32,768]{2,1,0:T(8,128)(2,1)S(1)}, bf16[1,32,768]{2,1,0:T(8,128)(2,1)S(1)}, u32[]{:S(2)}, u32[]{:S(2)}) collective-permute-start(bf16[1,32,768]{2,1,0:T(8,128)(2,1)S(1)} %shard_map.92.first), channel_id=1, source_target_pairs={{0,8},{2,10},{4,12},{6,14},{8,0},{10,2},{12,4},{14,6},{1,9},{3,11}... | collective-permute-start | bytes 147464 | tf_op jit(solution)/shard_map/ppermute | solution.py:264
  6.2 0.0 copy-start
  6.2 2.3 %shard_map.91.total = f32[64,384]{1,0:T(8,128)S(1)} custom-call(bf16[64,3584]{1,0:T(8,128)(2,1)} %bitcast.21, bf16[64,1024]{1,0:T(8,128)(2,1)} %bitcast.24, bf16[3584,256]{1,0:T(8,128)(2,1)} %out_basis.1, bf16[1024,128]{1,0:T(8,128)(2,1)} %act_basis.1), custom_call_target="tpu_custom_call" | custom-call | flops 134217728 | bytes 2686976 | tf_op jit(solution)/shard_map/pallas_call | solution.py:126
  8.5 0.0 collective-permute-done.1.second
  8.6 0.0 collective-permute-done.after.other_eigen
  8.6 1.6 %collective-permute-start.2 = (f32[4,8,512]{2,1,0:T(8,128)S(1)}, f32[4,8,512]{2,1,0:T(8,128)S(1)}, u32[]{:S(2)}, u32[]{:S(2)}) collective-permute-start(f32[4,8,512]{2,1,0:T(8,128)S(1)} %get-tuple-element.9), channel_id=1, source_target_pairs={{0,2},{2,0},{4,6},{6,4},{8,10},{10,8},{12,14},{14,12},{1,3},{3,1},... | collective-permute-start | bytes 196616 | tf_op jit(solution)/shard_map/ppermute | solution.py:264
  10.2 1.6 %collective-permute-start.6 = (bf16[2,32,768]{2,1,0:T(8,128)(2,1)S(1)}, bf16[2,32,768]{2,1,0:T(8,128)(2,1)S(1)}, u32[]{:S(2)}, u32[]{:S(2)}) collective-permute-start(bf16[2,32,768]{2,1,0:T(8,128)(2,1)S(1)} %get-tuple-element.10.first), channel_id=1, source_target_pairs={{0,4},{2,6},{4,0},{6,2},{8,12},{10,14},{12,8},{14,10},{1,5},{3,7},... | collective-permute-start | bytes 294920 | tf_op jit(solution)/shard_map/ppermute | solution.py:264
  11.7 1.2 %collective-permute-done.2 = f32[4,8,512]{2,1,0:T(8,128)S(1)} collective-permute-done((f32[4,8,512]{2,1,0:T(8,128)S(1)}, f32[4,8,512]{2,1,0:T(8,128)S(1)}, u32[]{:S(2)}, u32[]{:S(2)}) %collective-permute-start.2) | collective-permute-done | bytes 65568 | tf_op jit(solution)/shard_map/ppermute | solution.py:264
  13.0 1.6 %collective-permute-start.3 = (f32[2,8,512]{2,1,0:T(8,128)S(1)}, f32[2,8,512]{2,1,0:T(8,128)S(1)}, u32[]{:S(2)}, u32[]{:S(2)}) collective-permute-start(f32[2,8,512]{2,1,0:T(8,128)S(1)} %get-tuple-element.12), channel_id=1, source_target_pairs={{0,4},{2,6},{4,0},{6,2},{8,12},{10,14},{12,8},{14,10},{1,5},{3,7},... | collective-permute-start | bytes 98312 | tf_op jit(solution)/shard_map/ppermute | solution.py:264
  14.6 0.3 %collective-permute-done.6.second = bf16[2,32,768]{2,1,0:T(8,128)(2,1)S(1)} collective-permute-done((bf16[2,32,768]{2,1,0:T(8,128)(2,1)S(1)}, bf16[2,32,768]{2,1,0:T(8,128)(2,1)S(1)}, u32[]{:S(2)}, u32[]{:S(2)}) %collective-permute-start.6) | collective-permute-done | bytes 98336 | tf_op jit(solution)/shard_map/ppermute | solution.py:264
  14.9 1.2 %collective-permute-start.7 = (bf16[4,32,768]{2,1,0:T(8,128)(2,1)S(1)}, bf16[4,32,768]{2,1,0:T(8,128)(2,1)S(1)}, u32[]{:S(2)}, u32[]{:S(2)}) collective-permute-start(bf16[4,32,768]{2,1,0:T(8,128)(2,1)S(1)} %shard_map.94.rest_0_), channel_id=1, source_target_pairs={{0,2},{2,0},{4,6},{6,4},{8,10},{10,8},{12,14},{14,12},{1,3},{3,1},... | collective-permute-start | bytes 589832 | tf_op jit(solution)/shard_map/ppermute | solution.py:264
  16.2 0.8 %collective-permute-done.3 = f32[2,8,512]{2,1,0:T(8,128)S(1)} collective-permute-done((f32[2,8,512]{2,1,0:T(8,128)S(1)}, f32[2,8,512]{2,1,0:T(8,128)S(1)}, u32[]{:S(2)}, u32[]{:S(2)}) %collective-permute-start.3) | collective-permute-done | bytes 32800 | tf_op jit(solution)/shard_map/ppermute | solution.py:264
  16.9 1.9 %collective-permute-start.4 = (f32[8,512]{1,0:T(8,128)S(1)}, f32[8,512]{1,0:T(8,128)S(1)}, u32[]{:S(2)}, u32[]{:S(2)}) collective-permute-start(f32[8,512]{1,0:T(8,128)S(1)} %slice_bitcast_fusion.2), channel_id=1, source_target_pairs={{0,8},{2,10},{4,12},{6,14},{8,0},{10,2},{12,4},{14,6},{1,9},{3,11}... | collective-permute-start | bytes 49160 | tf_op jit(solution)/shard_map/ppermute | solution.py:264
  18.9 0.0 collective-permute-start.8
  18.9 1.9 %collective-permute-done.7.rest_1_ = bf16[4,32,768]{2,1,0:T(8,128)(2,1)S(1)} collective-permute-done((bf16[4,32,768]{2,1,0:T(8,128)(2,1)S(1)}, bf16[4,32,768]{2,1,0:T(8,128)(2,1)S(1)}, u32[]{:S(2)}, u32[]{:S(2)}) %collective-permute-start.7) | collective-permute-done | bytes 196640 | tf_op jit(solution)/shard_map/ppermute | solution.py:264
  20.8 0.0 collective-permute-start.9
  20.8 0.9 %collective-permute-done.4 = f32[8,512]{1,0:T(8,128)S(1)} collective-permute-done((f32[8,512]{1,0:T(8,128)S(1)}, f32[8,512]{1,0:T(8,128)S(1)}, u32[]{:S(2)}, u32[]{:S(2)}) %collective-permute-start.4) | collective-permute-done | bytes 16416 | tf_op jit(solution)/shard_map/ppermute | solution.py:264
  21.7 0.0 collective-permute-start.5
  21.7 1.2 %collective-permute-done.5.other = f32[8,512]{1,0:T(8,128)S(1)} collective-permute-done((f32[8,512]{1,0:T(8,128)S(1)}, f32[8,512]{1,0:T(8,128)S(1)}, u32[]{:S(2)}, u32[]{:S(2)}) %collective-permute-start.5) | collective-permute-done | bytes 16416 | tf_op jit(solution)/shard_map/ppermute | solution.py:284
  22.8 0.0 collective-permute-done.8.rest_2_
  22.8 0.0 collective-permute-done.9.rest_3_
  22.9 1.5 %shard_map.95 = f32[2,16]{1,0:T(2,128)} custom-call(s32[1]{0:T(128)} %bitcast.core_ref, f32[8,512]{1,0:T(8,128)S(1)} %fusion.own, f32[8,512]{1,0:T(8,128)S(1)} %collective-permute-done.5.other, f32[256,256]{1,0:T(8,128)S(1)} %copy-done, f32[256,256]{1,0:T(8,128)S(1)} %collective-permute-done.after.other_eigen, bf16[4,32,768]{2,1,0:T(8,128)(2,1)S(1)} %shard_map.94.rest_0_, ...), custom_call_target="tpu_custom_call" | custom-call | tf_op jit(solution)/shard_map/pallas_call | solution.py:239
  (8 shorter events, 0.1 us)
Async XLA Ops:
  0.0 8.6 %collective-permute-start = (f32[256,256]{1,0:T(8,128)}, f32[256,256]{1,0:T(8,128)S(1)}, u32[]{:S(2)}, u32[]{:S(2)}) collective-permute-start(f32[256,256]{1,0:T(8,128)} %eigen.1), channel_id=1, source_target_pairs={{0,1},{1,0},{2,3},{3,2},{4,5},{5,4},{6,7},{7,6},{8,9},{9,8},{10,11... | collective-permute-start | bytes 786440 | tf_op jit(solution)/shard_map/ppermute | solution.py:268
  1.2 7.3 %collective-permute-start.1 = (bf16[1,32,768]{2,1,0:T(8,128)(2,1)S(1)}, bf16[1,32,768]{2,1,0:T(8,128)(2,1)S(1)}, u32[]{:S(2)}, u32[]{:S(2)}) collective-permute-start(bf16[1,32,768]{2,1,0:T(8,128)(2,1)S(1)} %shard_map.92.first), channel_id=1, source_target_pairs={{0,8},{2,10},{4,12},{6,14},{8,0},{10,2},{12,4},{14,6},{1,9},{3,11}... | collective-permute-start | bytes 147464 | tf_op jit(solution)/shard_map/ppermute | solution.py:264
  6.2 16.7 %copy-start = (f32[256,256]{1,0:T(8,128)S(1)}, f32[256,256]{1,0:T(8,128)}, u32[]{:S(2)}) copy-start(f32[256,256]{1,0:T(8,128)} %eigen.1) | copy-start | bytes 786436
  8.6 4.3 %collective-permute-start.2 = (f32[4,8,512]{2,1,0:T(8,128)S(1)}, f32[4,8,512]{2,1,0:T(8,128)S(1)}, u32[]{:S(2)}, u32[]{:S(2)}) collective-permute-start(f32[4,8,512]{2,1,0:T(8,128)S(1)} %get-tuple-element.9), channel_id=1, source_target_pairs={{0,2},{2,0},{4,6},{6,4},{8,10},{10,8},{12,14},{14,12},{1,3},{3,1},... | collective-permute-start | bytes 196616 | tf_op jit(solution)/shard_map/ppermute | solution.py:264
  10.2 4.8 %collective-permute-start.6 = (bf16[2,32,768]{2,1,0:T(8,128)(2,1)S(1)}, bf16[2,32,768]{2,1,0:T(8,128)(2,1)S(1)}, u32[]{:S(2)}, u32[]{:S(2)}) collective-permute-start(bf16[2,32,768]{2,1,0:T(8,128)(2,1)S(1)} %get-tuple-element.10.first), channel_id=1, source_target_pairs={{0,4},{2,6},{4,0},{6,2},{8,12},{10,14},{12,8},{14,10},{1,5},{3,7},... | collective-permute-start | bytes 294920 | tf_op jit(solution)/shard_map/ppermute | solution.py:264
  13.0 4.0 %collective-permute-start.3 = (f32[2,8,512]{2,1,0:T(8,128)S(1)}, f32[2,8,512]{2,1,0:T(8,128)S(1)}, u32[]{:S(2)}, u32[]{:S(2)}) collective-permute-start(f32[2,8,512]{2,1,0:T(8,128)S(1)} %get-tuple-element.12), channel_id=1, source_target_pairs={{0,4},{2,6},{4,0},{6,2},{8,12},{10,14},{12,8},{14,10},{1,5},{3,7},... | collective-permute-start | bytes 98312 | tf_op jit(solution)/shard_map/ppermute | solution.py:264
  14.9 5.9 %collective-permute-start.7 = (bf16[4,32,768]{2,1,0:T(8,128)(2,1)S(1)}, bf16[4,32,768]{2,1,0:T(8,128)(2,1)S(1)}, u32[]{:S(2)}, u32[]{:S(2)}) collective-permute-start(bf16[4,32,768]{2,1,0:T(8,128)(2,1)S(1)} %shard_map.94.rest_0_), channel_id=1, source_target_pairs={{0,2},{2,0},{4,6},{6,4},{8,10},{10,8},{12,14},{14,12},{1,3},{3,1},... | collective-permute-start | bytes 589832 | tf_op jit(solution)/shard_map/ppermute | solution.py:264
  16.9 4.7 %collective-permute-start.4 = (f32[8,512]{1,0:T(8,128)S(1)}, f32[8,512]{1,0:T(8,128)S(1)}, u32[]{:S(2)}, u32[]{:S(2)}) collective-permute-start(f32[8,512]{1,0:T(8,128)S(1)} %slice_bitcast_fusion.2), channel_id=1, source_target_pairs={{0,8},{2,10},{4,12},{6,14},{8,0},{10,2},{12,4},{14,6},{1,9},{3,11}... | collective-permute-start | bytes 49160 | tf_op jit(solution)/shard_map/ppermute | solution.py:264
  18.9 4.0 %collective-permute-start.8 = (bf16[4,32,768]{2,1,0:T(8,128)(2,1)S(1)}, bf16[4,32,768]{2,1,0:T(8,128)(2,1)S(1)}, u32[]{:S(2)}, u32[]{:S(2)}) collective-permute-start(bf16[4,32,768]{2,1,0:T(8,128)(2,1)S(1)} %shard_map.94.rest_0_), channel_id=1, source_target_pairs={{0,1},{1,0},{2,3},{3,2},{4,5},{5,4},{6,7},{7,6},{8,9},{9,8},{10,11... | collective-permute-start | bytes 589832 | tf_op jit(solution)/shard_map/ppermute | solution.py:280
  20.8 2.1 %collective-permute-start.9 = (bf16[4,32,768]{2,1,0:T(8,128)(2,1)S(1)}, bf16[4,32,768]{2,1,0:T(8,128)(2,1)S(1)}, u32[]{:S(2)}, u32[]{:S(2)}) collective-permute-start(bf16[4,32,768]{2,1,0:T(8,128)(2,1)S(1)} %collective-permute-done.7.rest_1_), channel_id=1, source_target_pairs={{0,1},{1,0},{2,3},{3,2},{4,5},{5,4},{6,7},{7,6},{8,9},{9,8},{10,11... | collective-permute-start | bytes 589832 | tf_op jit(solution)/shard_map/ppermute | solution.py:281
  21.7 1.2 %collective-permute-start.5 = (f32[8,512]{1,0:T(8,128)S(1)}, f32[8,512]{1,0:T(8,128)S(1)}, u32[]{:S(2)}, u32[]{:S(2)}) collective-permute-start(f32[8,512]{1,0:T(8,128)S(1)} %fusion.own), channel_id=1, source_target_pairs={{0,1},{1,0},{2,3},{3,2},{4,5},{5,4},{6,7},{7,6},{8,9},{9,8},{10,11... | collective-permute-start | bytes 49160 | tf_op jit(solution)/shard_map/ppermute | solution.py:284

commit v9 on v8

--- a/solution.py
+++ b/solution.py
@@ -145,9 +145,8 @@
 
 
 def spread_kernel(
-    place_ref, tokens_ref, ids_ref, after, total, first, second, kept, moved, joined
+    place_ref, tokens_ref, ids_ref, total, first, second, kept, moved, joined
 ):
-    del after
     parts = 2 * kept.shape[0]
     local_rows = kept.shape[1]
     width = total.shape[1]
@@ -162,17 +161,17 @@
     join_kernel(None, first, second, joined)
 
 
-def spread(place, tokens, ids, after, total, first, second, parts):
+def spread(place, tokens, ids, total, first, second, parts):
     half = jax.ShapeDtypeStruct(
         (parts // 2, total.shape[0] // parts, total.shape[1] + LANES), jnp.float32
     )
     return pl.pallas_call(
         spread_kernel,
         out_shape=[half, half, joined_shape(first, second)],
-        in_specs=[spec(pltpu.SMEM)] * 3 + [spec(pl.ANY)] + [spec(pltpu.VMEM)] * 3,
+        in_specs=[spec(pltpu.SMEM)] * 3 + [spec(pltpu.VMEM)] * 3,
         out_specs=[spec(pltpu.VMEM)] * 3,
         compiler_params=grant(4),
-    )(place, tokens, ids, after, total, first, second)
+    )(place, tokens, ids, total, first, second)
 
 
 def split_three(x):
@@ -270,7 +269,7 @@
     arrived = across(block, steps - 1)
     total = project(query_out.T, query_act.T, out_basis, act_basis)
     kept, moved, block = spread(
-        place, train_tokens, train_ids, other_eigen, total, block, arrived, parts
+        place, train_tokens, train_ids, total, block, arrived, parts
     )
     sums = (kept + across(moved, 0)).reshape((2, 2) + kept.shape[1:])
     arrived = across(block, 1)

time: 24.6 us -> 25.3 us (1.028)
  waiting for transfers between devices: 6.21 us -> 6.93 us
    ppermute x6, waiting for transfers between devices: 5.03 us -> 6.04 us  [across(): return lax.ppermute(x, 'blk', [(s, s ^ 1 << i) for s in range(parts)])]
    ppermute x1, starting transfers between devices: 0.01 us -> 0.56 us  [direct(): other = lax.ppermute(own, 'fsdp', swap)]
    ppermute x1, starting transfers between devices: 0.45 us -> 0.01 us  [direct(): other_eigen = lax.ppermute(eigenvalues, 'fsdp', swap)]
    ppermute x1, waiting for transfers between devices: 1.17 us -> 0.89 us  [direct(): other = lax.ppermute(own, 'fsdp', swap)]
  transfers between devices with their start and end apart: 10 -> 10, of which waited for: 6 -> 5; matrix products, arithmetic and copies ran while one was open for 0% -> 0% of each run, Pallas kernels for 13% -> 9%
where the time goes in v9:
time: 25.3 us; the launch traced here: 25 us
  starting transfers between devices  12 us (47%)
  waiting for transfers between devices  6.93 us (27%)
  Pallas kernels  4.7 us (19%)
  between operations  1.37 us (5%)
    ppermute x6, starting transfers between devices, across(): return lax.ppermute(x, 'blk', [(s, s ^ 1 << i) for s in range(parts)])  11.4 us
    ppermute x6, waiting for transfers between devices, across(): return lax.ppermute(x, 'blk', [(s, s ^ 1 << i) for s in range(parts)])  6.04 us
    pallas_call x1, Pallas kernels, project(): pl.pallas_call(functools.partial(project_kernel, chunks), out_shape=jax.S...  2.3 us
    pallas_call x1, Pallas kernels, score(): pl.pallas_call(score_kernel, out_shape=jax.ShapeDtypeStruct((own.shape[0]...  1.55 us
    ppermute x1, waiting for transfers between devices, direct(): other = lax.ppermute(own, 'fsdp', swap)  0.89 us
    pallas_call x1, Pallas kernels, pack(): pl.pallas_call(pack_kernel, out_shape=jax.ShapeDtypeStruct(shape, train_o...  0.82 us
    ppermute x1, starting transfers between devices, direct(): other = lax.ppermute(own, 'fsdp', swap)  0.56 us
  transfers between devices with their start and end apart: 10, of which 5 were waited for; matrix products, arithmetic and copies ran while one was open for 0% of the time, Pallas kernels for 9%

profile of v9, /device:TPU:0, one launch (start us, length us, event | category | flops | bytes accessed | tf_op | source)
XLA Modules:
  0.0 25.0 jit_solution(12062494927725804219)
XLA Ops:
  0.0 0.8 %shard_map.92.first = bf16[1,32,768]{2,1,0:T(8,128)(2,1)S(1)} custom-call(bf16[1,32,512]{2,1,0:T(8,128)(2,1)} %train_out.1, bf16[1,32,256]{2,1,0:T(8,128)(2,1)} %train_act.1), custom_call_target="tpu_custom_call" | custom-call | tf_op jit(solution)/shard_map/pallas_call | solution.py:52
  0.8 4.1 %collective-permute-start = (bf16[1,32,768]{2,1,0:T(8,128)(2,1)S(1)}, bf16[1,32,768]{2,1,0:T(8,128)(2,1)S(1)}, u32[]{:S(2)}, u32[]{:S(2)}) collective-permute-start(bf16[1,32,768]{2,1,0:T(8,128)(2,1)S(1)} %shard_map.92.first), channel_id=1, source_target_pairs={{0,8},{2,10},{4,12},{6,14},{8,0},{10,2},{12,4},{14,6},{1,9},{3,11}... | collective-permute-start | bytes 147464 | tf_op jit(solution)/shard_map/ppermute | solution.py:263
  6.2 2.3 %shard_map.91.total = f32[64,384]{1,0:T(8,128)S(1)} custom-call(bf16[64,3584]{1,0:T(8,128)(2,1)} %bitcast.21, bf16[64,1024]{1,0:T(8,128)(2,1)} %bitcast.24, bf16[3584,256]{1,0:T(8,128)(2,1)} %out_basis.1, bf16[1024,128]{1,0:T(8,128)(2,1)} %act_basis.1), custom_call_target="tpu_custom_call" | custom-call | flops 134217728 | bytes 2686976 | tf_op jit(solution)/shard_map/pallas_call | solution.py:126
  8.5 0.0 collective-permute-done.second
  8.6 1.6 %collective-permute-start.1 = (f32[4,8,512]{2,1,0:T(8,128)S(1)}, f32[4,8,512]{2,1,0:T(8,128)S(1)}, u32[]{:S(2)}, u32[]{:S(2)}) collective-permute-start(f32[4,8,512]{2,1,0:T(8,128)S(1)} %get-tuple-element.9), channel_id=1, source_target_pairs={{0,2},{2,0},{4,6},{6,4},{8,10},{10,8},{12,14},{14,12},{1,3},{3,1},... | collective-permute-start | bytes 196616 | tf_op jit(solution)/shard_map/ppermute | solution.py:263
  10.1 1.6 %collective-permute-start.6 = (bf16[2,32,768]{2,1,0:T(8,128)(2,1)S(1)}, bf16[2,32,768]{2,1,0:T(8,128)(2,1)S(1)}, u32[]{:S(2)}, u32[]{:S(2)}) collective-permute-start(bf16[2,32,768]{2,1,0:T(8,128)(2,1)S(1)} %get-tuple-element.10.first), channel_id=1, source_target_pairs={{0,4},{2,6},{4,0},{6,2},{8,12},{10,14},{12,8},{14,10},{1,5},{3,7},... | collective-permute-start | bytes 294920 | tf_op jit(solution)/shard_map/ppermute | solution.py:263
  11.7 1.2 %collective-permute-done.1 = f32[4,8,512]{2,1,0:T(8,128)S(1)} collective-permute-done((f32[4,8,512]{2,1,0:T(8,128)S(1)}, f32[4,8,512]{2,1,0:T(8,128)S(1)}, u32[]{:S(2)}, u32[]{:S(2)}) %collective-permute-start.1) | collective-permute-done | bytes 65568 | tf_op jit(solution)/shard_map/ppermute | solution.py:263
  12.9 1.6 %collective-permute-start.2 = (f32[2,8,512]{2,1,0:T(8,128)S(1)}, f32[2,8,512]{2,1,0:T(8,128)S(1)}, u32[]{:S(2)}, u32[]{:S(2)}) collective-permute-start(f32[2,8,512]{2,1,0:T(8,128)S(1)} %get-tuple-element.12), channel_id=1, source_target_pairs={{0,4},{2,6},{4,0},{6,2},{8,12},{10,14},{12,8},{14,10},{1,5},{3,7},... | collective-permute-start | bytes 98312 | tf_op jit(solution)/shard_map/ppermute | solution.py:263
  14.6 0.0 copy-done
  14.6 0.0 collective-permute-start.5
  14.6 0.5 %collective-permute-done.6.second = bf16[2,32,768]{2,1,0:T(8,128)(2,1)S(1)} collective-permute-done((bf16[2,32,768]{2,1,0:T(8,128)(2,1)S(1)}, bf16[2,32,768]{2,1,0:T(8,128)(2,1)S(1)}, u32[]{:S(2)}, u32[]{:S(2)}) %collective-permute-start.6) | collective-permute-done | bytes 98336 | tf_op jit(solution)/shard_map/ppermute | solution.py:263
  15.1 1.1 %collective-permute-start.7 = (bf16[4,32,768]{2,1,0:T(8,128)(2,1)S(1)}, bf16[4,32,768]{2,1,0:T(8,128)(2,1)S(1)}, u32[]{:S(2)}, u32[]{:S(2)}) collective-permute-start(bf16[4,32,768]{2,1,0:T(8,128)(2,1)S(1)} %shard_map.94.rest_0_), channel_id=1, source_target_pairs={{0,2},{2,0},{4,6},{6,4},{8,10},{10,8},{12,14},{14,12},{1,3},{3,1},... | collective-permute-start | bytes 589832 | tf_op jit(solution)/shard_map/ppermute | solution.py:263
  16.2 0.7 %collective-permute-done.2 = f32[2,8,512]{2,1,0:T(8,128)S(1)} collective-permute-done((f32[2,8,512]{2,1,0:T(8,128)S(1)}, f32[2,8,512]{2,1,0:T(8,128)S(1)}, u32[]{:S(2)}, u32[]{:S(2)}) %collective-permute-start.2) | collective-permute-done | bytes 32800 | tf_op jit(solution)/shard_map/ppermute | solution.py:263
  16.9 1.5 %collective-permute-start.3 = (f32[8,512]{1,0:T(8,128)S(1)}, f32[8,512]{1,0:T(8,128)S(1)}, u32[]{:S(2)}, u32[]{:S(2)}) collective-permute-start(f32[8,512]{1,0:T(8,128)S(1)} %slice_bitcast_fusion.2), channel_id=1, source_target_pairs={{0,8},{2,10},{4,12},{6,14},{8,0},{10,2},{12,4},{14,6},{1,9},{3,11}... | collective-permute-start | bytes 49160 | tf_op jit(solution)/shard_map/ppermute | solution.py:263
  18.4 0.0 collective-permute-start.8
  18.4 3.6 %collective-permute-done.7.rest_1_ = bf16[4,32,768]{2,1,0:T(8,128)(2,1)S(1)} collective-permute-done((bf16[4,32,768]{2,1,0:T(8,128)(2,1)S(1)}, bf16[4,32,768]{2,1,0:T(8,128)(2,1)S(1)}, u32[]{:S(2)}, u32[]{:S(2)}) %collective-permute-start.7) | collective-permute-done | bytes 196640 | tf_op jit(solution)/shard_map/ppermute | solution.py:263
  22.0 0.0 collective-permute-start.9
  22.0 0.0 collective-permute-done.3
  22.0 0.6 %collective-permute-start.4 = (f32[8,512]{1,0:T(8,128)S(1)}, f32[8,512]{1,0:T(8,128)S(1)}, u32[]{:S(2)}, u32[]{:S(2)}) collective-permute-start(f32[8,512]{1,0:T(8,128)S(1)} %fusion.own), channel_id=1, source_target_pairs={{0,1},{1,0},{2,3},{3,2},{4,5},{5,4},{6,7},{7,6},{8,9},{9,8},{10,11... | collective-permute-start | bytes 49160 | tf_op jit(solution)/shard_map/ppermute | solution.py:283
  22.6 0.9 %collective-permute-done.4.other = f32[8,512]{1,0:T(8,128)S(1)} collective-permute-done((f32[8,512]{1,0:T(8,128)S(1)}, f32[8,512]{1,0:T(8,128)S(1)}, u32[]{:S(2)}, u32[]{:S(2)}) %collective-permute-start.4) | collective-permute-done | bytes 16416 | tf_op jit(solution)/shard_map/ppermute | solution.py:283
  23.5 0.0 collective-permute-done.5.other_eigen
  23.5 0.0 collective-permute-done.8.rest_2_
  23.5 0.0 collective-permute-done.9.rest_3_
  23.5 1.5 %shard_map.95 = f32[2,16]{1,0:T(2,128)} custom-call(s32[1]{0:T(128)} %bitcast.core_ref, f32[8,512]{1,0:T(8,128)S(1)} %fusion.own, f32[8,512]{1,0:T(8,128)S(1)} %collective-permute-done.4.other, f32[256,256]{1,0:T(8,128)S(1)} %copy-done, f32[256,256]{1,0:T(8,128)S(1)} %collective-permute-done.5.other_eigen, bf16[4,32,768]{2,1,0:T(8,128)(2,1)S(1)} %shard_map.94.rest_0_, ...), custom_call_target="tpu_custom_call" | custom-call | tf_op jit(solution)/shard_map/pallas_call | solution.py:238
  (8 shorter events, 0.1 us)
Async XLA Ops:
  0.0 14.6 %copy-start = (f32[256,256]{1,0:T(8,128)S(1)}, f32[256,256]{1,0:T(8,128)}, u32[]{:S(2)}) copy-start(f32[256,256]{1,0:T(8,128)} %eigen.1) | copy-start | bytes 786436
  0.8 7.7 %collective-permute-start = (bf16[1,32,768]{2,1,0:T(8,128)(2,1)S(1)}, bf16[1,32,768]{2,1,0:T(8,128)(2,1)S(1)}, u32[]{:S(2)}, u32[]{:S(2)}) collective-permute-start(bf16[1,32,768]{2,1,0:T(8,128)(2,1)S(1)} %shard_map.92.first), channel_id=1, source_target_pairs={{0,8},{2,10},{4,12},{6,14},{8,0},{10,2},{12,4},{14,6},{1,9},{3,11}... | collective-permute-start | bytes 147464 | tf_op jit(solution)/shard_map/ppermute | solution.py:263
  8.6 4.3 %collective-permute-start.1 = (f32[4,8,512]{2,1,0:T(8,128)S(1)}, f32[4,8,512]{2,1,0:T(8,128)S(1)}, u32[]{:S(2)}, u32[]{:S(2)}) collective-permute-start(f32[4,8,512]{2,1,0:T(8,128)S(1)} %get-tuple-element.9), channel_id=1, source_target_pairs={{0,2},{2,0},{4,6},{6,4},{8,10},{10,8},{12,14},{14,12},{1,3},{3,1},... | collective-permute-start | bytes 196616 | tf_op jit(solution)/shard_map/ppermute | solution.py:263
  10.1 5.0 %collective-permute-start.6 = (bf16[2,32,768]{2,1,0:T(8,128)(2,1)S(1)}, bf16[2,32,768]{2,1,0:T(8,128)(2,1)S(1)}, u32[]{:S(2)}, u32[]{:S(2)}) collective-permute-start(bf16[2,32,768]{2,1,0:T(8,128)(2,1)S(1)} %get-tuple-element.10.first), channel_id=1, source_target_pairs={{0,4},{2,6},{4,0},{6,2},{8,12},{10,14},{12,8},{14,10},{1,5},{3,7},... | collective-permute-start | bytes 294920 | tf_op jit(solution)/shard_map/ppermute | solution.py:263
  12.9 4.0 %collective-permute-start.2 = (f32[2,8,512]{2,1,0:T(8,128)S(1)}, f32[2,8,512]{2,1,0:T(8,128)S(1)}, u32[]{:S(2)}, u32[]{:S(2)}) collective-permute-start(f32[2,8,512]{2,1,0:T(8,128)S(1)} %get-tuple-element.12), channel_id=1, source_target_pairs={{0,4},{2,6},{4,0},{6,2},{8,12},{10,14},{12,8},{14,10},{1,5},{3,7},... | collective-permute-start | bytes 98312 | tf_op jit(solution)/shard_map/ppermute | solution.py:263
  14.6 8.9 %collective-permute-start.5 = (f32[256,256]{1,0:T(8,128)S(1)}, f32[256,256]{1,0:T(8,128)S(1)}, u32[]{:S(2)}, u32[]{:S(2)}) collective-permute-start(f32[256,256]{1,0:T(8,128)S(1)} %copy-done), channel_id=1, source_target_pairs={{0,1},{1,0},{2,3},{3,2},{4,5},{5,4},{6,7},{7,6},{8,9},{9,8},{10,11... | collective-permute-start | bytes 786440 | tf_op jit(solution)/shard_map/ppermute | solution.py:267
  15.1 6.9 %collective-permute-start.7 = (bf16[4,32,768]{2,1,0:T(8,128)(2,1)S(1)}, bf16[4,32,768]{2,1,0:T(8,128)(2,1)S(1)}, u32[]{:S(2)}, u32[]{:S(2)}) collective-permute-start(bf16[4,32,768]{2,1,0:T(8,128)(2,1)S(1)} %shard_map.94.rest_0_), channel_id=1, source_target_pairs={{0,2},{2,0},{4,6},{6,4},{8,10},{10,8},{12,14},{14,12},{1,3},{3,1},... | collective-permute-start | bytes 589832 | tf_op jit(solution)/shard_map/ppermute | solution.py:263
  16.9 5.1 %collective-permute-start.3 = (f32[8,512]{1,0:T(8,128)S(1)}, f32[8,512]{1,0:T(8,128)S(1)}, u32[]{:S(2)}, u32[]{:S(2)}) collective-permute-start(f32[8,512]{1,0:T(8,128)S(1)} %slice_bitcast_fusion.2), channel_id=1, source_target_pairs={{0,8},{2,10},{4,12},{6,14},{8,0},{10,2},{12,4},{14,6},{1,9},{3,11}... | collective-permute-start | bytes 49160 | tf_op jit(solution)/shard_map/ppermute | solution.py:263
  18.4 5.1 %collective-permute-start.8 = (bf16[4,32,768]{2,1,0:T(8,128)(2,1)S(1)}, bf16[4,32,768]{2,1,0:T(8,128)(2,1)S(1)}, u32[]{:S(2)}, u32[]{:S(2)}) collective-permute-start(bf16[4,32,768]{2,1,0:T(8,128)(2,1)S(1)} %shard_map.94.rest_0_), channel_id=1, source_target_pairs={{0,1},{1,0},{2,3},{3,2},{4,5},{5,4},{6,7},{7,6},{8,9},{9,8},{10,11... | collective-permute-start | bytes 589832 | tf_op jit(solution)/shard_map/ppermute | solution.py:279
  22.0 1.5 %collective-permute-start.9 = (bf16[4,32,768]{2,1,0:T(8,128)(2,1)S(1)}, bf16[4,32,768]{2,1,0:T(8,128)(2,1)S(1)}, u32[]{:S(2)}, u32[]{:S(2)}) collective-permute-start(bf16[4,32,768]{2,1,0:T(8,128)(2,1)S(1)} %collective-permute-done.7.rest_1_), channel_id=1, source_target_pairs={{0,1},{1,0},{2,3},{3,2},{4,5},{5,4},{6,7},{7,6},{8,9},{9,8},{10,11... | collective-permute-start | bytes 589832 | tf_op jit(solution)/shard_map/ppermute | solution.py:280
  22.0 1.5 %collective-permute-start.4 = (f32[8,512]{1,0:T(8,128)S(1)}, f32[8,512]{1,0:T(8,128)S(1)}, u32[]{:S(2)}, u32[]{:S(2)}) collective-permute-start(f32[8,512]{1,0:T(8,128)S(1)} %fusion.own), channel_id=1, source_target_pairs={{0,1},{1,0},{2,3},{3,2},{4,5},{5,4},{6,7},{7,6},{8,9},{9,8},{10,11... | collective-permute-start | bytes 49160 | tf_op jit(solution)/shard_map/ppermute | solution.py:283

commit v10 on v8

--- a/solution.py
+++ b/solution.py
@@ -10,16 +10,10 @@
 RQ = 4
 LANES = 128
 DIRECT_PARTS = 8
+WAIT_FLOPS = 10**9
 
 
 damping = 0.1
-
-
-def chunk_count(rows):
-    for chunks in (4, 2):
-        if rows % (chunks * LANES) == 0:
-            return chunks
-    return 1
 
 
 def pinned(x):
@@ -56,6 +50,7 @@
         out_specs=spec(pltpu.VMEM),
         scratch_shapes=[pltpu.SemaphoreType.DMA((2,))],
         compiler_params=grant(2),
+        cost_estimate=pl.CostEstimate(flops=WAIT_FLOPS, bytes_accessed=0, transcendentals=0),
     )(pinned(train_out), pinned(train_act))
 
 
@@ -82,61 +77,32 @@
     )(after, first, second)
 
 
-def project_kernel(
-    chunks, query_out, query_act, out_basis, act_basis, total, q_out, q_act, b_out, b_act, sems
-):
-    rows = query_out.shape[1] // chunks
-    copies = []
-    for c in range(chunks):
-        cut = pl.ds(c * rows, rows)
-        copies.append(
-            (
-                pltpu.make_async_copy(query_out.at[:, cut], q_out.at[:, cut], sems.at[2 * c]),
-                pltpu.make_async_copy(out_basis.at[cut, :], b_out.at[cut, :], sems.at[2 * c + 1]),
-            )
-        )
-    copies.append(
-        (
-            pltpu.make_async_copy(query_act, q_act, sems.at[2 * chunks]),
-            pltpu.make_async_copy(act_basis, b_act, sems.at[2 * chunks + 1]),
-        )
-    )
-    for pair in copies:
-        for copy in pair:
-            copy.start()
-    half_ks = b_out.shape[1]
-    out_part = None
-    for c in range(chunks):
-        for copy in copies[c]:
-            copy.wait()
-        cut = pl.ds(c * rows, rows)
-        term = jnp.dot(q_out[:, cut], b_out[cut, :], preferred_element_type=jnp.float32)
-        out_part = term if out_part is None else out_part + term
-    total[:, :half_ks] = out_part
-    for copy in copies[chunks]:
-        copy.wait()
-    total[:, half_ks:] = jnp.dot(q_act[...], b_act[...], preferred_element_type=jnp.float32)
+def project_kernel(query_out, query_act, out_basis, act_basis, total):
+    half_ks = out_basis.shape[1]
+    total[:, :half_ks] = jnp.dot(
+        query_out[...], out_basis[...], preferred_element_type=jnp.float32
+    )
+    total[:, half_ks:] = jnp.dot(
+        query_act[...], act_basis[...], preferred_element_type=jnp.float32
+    )
 
 
 def project(query_out, query_act, out_basis, act_basis):
     columns = query_out.shape[0]
     width = out_basis.shape[1] + act_basis.shape[1]
-    chunks = chunk_count(query_out.shape[1])
     operands = (query_out, query_act, out_basis, act_basis)
     return pl.pallas_call(
-        functools.partial(project_kernel, chunks),
+        project_kernel,
         out_shape=jax.ShapeDtypeStruct((columns, width), jnp.float32),
-        in_specs=[spec(pltpu.HBM)] * len(operands),
+        in_specs=[spec(pltpu.VMEM)] * len(operands),
         out_specs=spec(pltpu.VMEM),
-        scratch_shapes=[pltpu.VMEM(x.shape, x.dtype) for x in operands]
-        + [pltpu.SemaphoreType.DMA((2 * chunks + 2,))],
         compiler_params=grant(8),
         cost_estimate=pl.CostEstimate(
             flops=2 * columns * (out_basis.size + act_basis.size),
             bytes_accessed=2 * sum(x.size for x in operands),
             transcendentals=0,
         ),
-    )(*[pinned(x) for x in operands])
+    )(*operands)
 
 
 def doubling_slot(distance, parts):

time: 24.6 us -> 24.2 us (0.984)
  Pallas kernels: 4.69 us -> 3.08 us
  waiting for transfers between devices: 6.21 us -> 7.8 us
  starting transfers between devices: 12.1 us -> 11.6 us
    pallas_call x1, Pallas kernels: 2.33 us -> 0.48 us  [project(): pl.pallas_call(project_kernel, out_shape=jax.ShapeDtypeStruct((columns, w...]
    ppermute x6, waiting for transfers between devices: 5.03 us -> 6.62 us  [across(): return lax.ppermute(x, 'blk', [(s, s ^ 1 << i) for s in range(parts)])]
    ppermute x6, starting transfers between devices: 11.6 us -> 11 us  [across(): return lax.ppermute(x, 'blk', [(s, s ^ 1 << i) for s in range(parts)])]
    pallas_call x1, Pallas kernels: 0.78 us -> 1.04 us  [pack(): pl.pallas_call(pack_kernel, out_shape=jax.ShapeDtypeStruct(shape, train_o...]
  transfers between devices with their start and end apart: 10 -> 10, of which waited for: 6 -> 7; matrix products, arithmetic and copies ran while one was open for 0% -> 0% of each run, Pallas kernels for 13% -> 6%
where the time goes in v10:
time: 24.2 us; the launch traced here: 23.9 us
  starting transfers between devices  11.6 us (48%)
  waiting for transfers between devices  7.8 us (32%)
  Pallas kernels  3.08 us (13%)
  between operations  1.4 us (6%)
    ppermute x6, starting transfers between devices, across(): return lax.ppermute(x, 'blk', [(s, s ^ 1 << i) for s in range(parts)])  11 us
    ppermute x6, waiting for transfers between devices, across(): return lax.ppermute(x, 'blk', [(s, s ^ 1 << i) for s in range(parts)])  6.62 us
    pallas_call x1, Pallas kernels, score(): pl.pallas_call(score_kernel, out_shape=jax.ShapeDtypeStruct((own.shape[0]...  1.54 us
    ppermute x1, waiting for transfers between devices, direct(): other = lax.ppermute(own, 'fsdp', swap)  1.17 us
    pallas_call x1, Pallas kernels, pack(): pl.pallas_call(pack_kernel, out_shape=jax.ShapeDtypeStruct(shape, train_o...  1.04 us
    ppermute x1, starting transfers between devices, direct(): other_eigen = lax.ppermute(eigenvalues, 'fsdp', swap)  0.53 us
  transfers between devices with their start and end apart: 10, of which 7 were waited for; matrix products, arithmetic and copies ran while one was open for 0% of the time, Pallas kernels for 6%

profile of v10, /device:TPU:0, one launch (start us, length us, event | category | flops | bytes accessed | tf_op | source)
XLA Modules:
  0.0 23.9 jit_solution(13408117011498844309)
XLA Ops:
  0.0 0.5 %collective-permute-start = (f32[256,256]{1,0:T(8,128)}, f32[256,256]{1,0:T(8,128)S(1)}, u32[]{:S(2)}, u32[]{:S(2)}) collective-permute-start(f32[256,256]{1,0:T(8,128)} %eigen.1), channel_id=1, source_target_pairs={{0,1},{1,0},{2,3},{3,2},{4,5},{5,4},{6,7},{7,6},{8,9},{9,8},{10,11... | collective-permute-start | bytes 786440 | tf_op jit(solution)/shard_map/ppermute | solution.py:234
  0.5 1.0 %shard_map.92.first = bf16[1,32,768]{2,1,0:T(8,128)(2,1)S(1)} custom-call(bf16[1,32,512]{2,1,0:T(8,128)(2,1)} %train_out.1, bf16[1,32,256]{2,1,0:T(8,128)(2,1)} %train_act.1), custom_call_target="tpu_custom_call" | custom-call | flops 1000000000 | tf_op jit(solution)/shard_map/pallas_call | solution.py:46
  1.6 3.6 %collective-permute-start.1 = (bf16[1,32,768]{2,1,0:T(8,128)(2,1)S(1)}, bf16[1,32,768]{2,1,0:T(8,128)(2,1)S(1)}, u32[]{:S(2)}, u32[]{:S(2)}) collective-permute-start(bf16[1,32,768]{2,1,0:T(8,128)(2,1)S(1)} %shard_map.92.first), channel_id=1, source_target_pairs={{0,8},{2,10},{4,12},{6,14},{8,0},{10,2},{12,4},{14,6},{1,9},{3,11}... | collective-permute-start | bytes 147464 | tf_op jit(solution)/shard_map/ppermute | solution.py:230
  6.5 0.0 copy-start.2
  6.5 0.5 %shard_map.91.total = f32[64,384]{1,0:T(8,128)S(1)} custom-call(bf16[64,3584]{1,0:T(8,128)(2,1)S(1)} %bitcast.21, bf16[64,1024]{1,0:T(8,128)(2,1)S(1)} %bitcast.22, bf16[3584,256]{1,0:T(8,128)(2,1)S(1)} %copy-done, bf16[1024,128]{1,0:T(8,128)(2,1)S(1)} %copy-done.3), custom_call_target="tpu_custom_call" | custom-call | flops 134217728 | bytes 2686976 | tf_op jit(solution)/shard_map/pallas_call | solution.py:94
  7.0 0.4 %collective-permute-done.1.second = bf16[1,32,768]{2,1,0:T(8,128)(2,1)S(1)} collective-permute-done((bf16[1,32,768]{2,1,0:T(8,128)(2,1)S(1)}, bf16[1,32,768]{2,1,0:T(8,128)(2,1)S(1)}, u32[]{:S(2)}, u32[]{:S(2)}) %collective-permute-start.1) | collective-permute-done | bytes 49184 | tf_op jit(solution)/shard_map/ppermute | solution.py:230
  7.4 0.0 collective-permute-done.after.other_eigen
  7.5 2.7 %collective-permute-start.2 = (f32[4,8,512]{2,1,0:T(8,128)S(1)}, f32[4,8,512]{2,1,0:T(8,128)S(1)}, u32[]{:S(2)}, u32[]{:S(2)}) collective-permute-start(f32[4,8,512]{2,1,0:T(8,128)S(1)} %get-tuple-element.9), channel_id=1, source_target_pairs={{0,2},{2,0},{4,6},{6,4},{8,10},{10,8},{12,14},{14,12},{1,3},{3,1},... | collective-permute-start | bytes 196616 | tf_op jit(solution)/shard_map/ppermute | solution.py:230
  10.2 0.6 %collective-permute-start.6 = (bf16[2,32,768]{2,1,0:T(8,128)(2,1)S(1)}, bf16[2,32,768]{2,1,0:T(8,128)(2,1)S(1)}, u32[]{:S(2)}, u32[]{:S(2)}) collective-permute-start(bf16[2,32,768]{2,1,0:T(8,128)(2,1)S(1)} %get-tuple-element.10.first), channel_id=1, source_target_pairs={{0,4},{2,6},{4,0},{6,2},{8,12},{10,14},{12,8},{14,10},{1,5},{3,7},... | collective-permute-start | bytes 294920 | tf_op jit(solution)/shard_map/ppermute | solution.py:230
  10.8 1.7 %collective-permute-done.2 = f32[4,8,512]{2,1,0:T(8,128)S(1)} collective-permute-done((f32[4,8,512]{2,1,0:T(8,128)S(1)}, f32[4,8,512]{2,1,0:T(8,128)S(1)}, u32[]{:S(2)}, u32[]{:S(2)}) %collective-permute-start.2) | collective-permute-done | bytes 65568 | tf_op jit(solution)/shard_map/ppermute | solution.py:230
  12.5 1.2 %collective-permute-start.3 = (f32[2,8,512]{2,1,0:T(8,128)S(1)}, f32[2,8,512]{2,1,0:T(8,128)S(1)}, u32[]{:S(2)}, u32[]{:S(2)}) collective-permute-start(f32[2,8,512]{2,1,0:T(8,128)S(1)} %get-tuple-element.12), channel_id=1, source_target_pairs={{0,4},{2,6},{4,0},{6,2},{8,12},{10,14},{12,8},{14,10},{1,5},{3,7},... | collective-permute-start | bytes 98312 | tf_op jit(solution)/shard_map/ppermute | solution.py:230
  13.7 1.2 %collective-permute-done.6.second = bf16[2,32,768]{2,1,0:T(8,128)(2,1)S(1)} collective-permute-done((bf16[2,32,768]{2,1,0:T(8,128)(2,1)S(1)}, bf16[2,32,768]{2,1,0:T(8,128)(2,1)S(1)}, u32[]{:S(2)}, u32[]{:S(2)}) %collective-permute-start.6) | collective-permute-done | bytes 98336 | tf_op jit(solution)/shard_map/ppermute | solution.py:230
  14.8 0.4 %collective-permute-start.7 = (bf16[4,32,768]{2,1,0:T(8,128)(2,1)S(1)}, bf16[4,32,768]{2,1,0:T(8,128)(2,1)S(1)}, u32[]{:S(2)}, u32[]{:S(2)}) collective-permute-start(bf16[4,32,768]{2,1,0:T(8,128)(2,1)S(1)} %shard_map.94.rest_0_), channel_id=1, source_target_pairs={{0,2},{2,0},{4,6},{6,4},{8,10},{10,8},{12,14},{14,12},{1,3},{3,1},... | collective-permute-start | bytes 589832 | tf_op jit(solution)/shard_map/ppermute | solution.py:230
  15.2 1.2 %collective-permute-done.3 = f32[2,8,512]{2,1,0:T(8,128)S(1)} collective-permute-done((f32[2,8,512]{2,1,0:T(8,128)S(1)}, f32[2,8,512]{2,1,0:T(8,128)S(1)}, u32[]{:S(2)}, u32[]{:S(2)}) %collective-permute-start.3) | collective-permute-done | bytes 32800 | tf_op jit(solution)/shard_map/ppermute | solution.py:230
  16.5 2.5 %collective-permute-start.4 = (f32[8,512]{1,0:T(8,128)S(1)}, f32[8,512]{1,0:T(8,128)S(1)}, u32[]{:S(2)}, u32[]{:S(2)}) collective-permute-start(f32[8,512]{1,0:T(8,128)S(1)} %slice_bitcast_fusion.2), channel_id=1, source_target_pairs={{0,8},{2,10},{4,12},{6,14},{8,0},{10,2},{12,4},{14,6},{1,9},{3,11}... | collective-permute-start | bytes 49160 | tf_op jit(solution)/shard_map/ppermute | solution.py:230
  19.0 0.0 collective-permute-start.8
  19.0 1.6 %collective-permute-done.7.rest_1_ = bf16[4,32,768]{2,1,0:T(8,128)(2,1)S(1)} collective-permute-done((bf16[4,32,768]{2,1,0:T(8,128)(2,1)S(1)}, bf16[4,32,768]{2,1,0:T(8,128)(2,1)S(1)}, u32[]{:S(2)}, u32[]{:S(2)}) %collective-permute-start.7) | collective-permute-done | bytes 196640 | tf_op jit(solution)/shard_map/ppermute | solution.py:230
  20.6 0.0 collective-permute-start.9
  20.6 0.6 %collective-permute-done.4 = f32[8,512]{1,0:T(8,128)S(1)} collective-permute-done((f32[8,512]{1,0:T(8,128)S(1)}, f32[8,512]{1,0:T(8,128)S(1)}, u32[]{:S(2)}, u32[]{:S(2)}) %collective-permute-start.4) | collective-permute-done | bytes 16416 | tf_op jit(solution)/shard_map/ppermute | solution.py:230
  21.2 0.0 collective-permute-start.5
  21.2 1.2 %collective-permute-done.5.other = f32[8,512]{1,0:T(8,128)S(1)} collective-permute-done((f32[8,512]{1,0:T(8,128)S(1)}, f32[8,512]{1,0:T(8,128)S(1)}, u32[]{:S(2)}, u32[]{:S(2)}) %collective-permute-start.5) | collective-permute-done | bytes 16416 | tf_op jit(solution)/shard_map/ppermute | solution.py:250
  22.4 0.0 collective-permute-done.8.rest_2_
  22.4 0.0 collective-permute-done.9.rest_3_
  22.4 1.5 %shard_map.95 = f32[2,16]{1,0:T(2,128)} custom-call(s32[1]{0:T(128)} %bitcast.core_ref, f32[8,512]{1,0:T(8,128)S(1)} %fusion.own, f32[8,512]{1,0:T(8,128)S(1)} %collective-permute-done.5.other, f32[256,256]{1,0:T(8,128)S(1)} %copy-done.2, f32[256,256]{1,0:T(8,128)S(1)} %collective-permute-done.after.other_eigen, bf16[4,32,768]{2,1,0:T(8,128)(2,1)S(1)} %shard_map.94.rest_0_, ...), custom_call_target="tpu_custom_call" | custom-call | tf_op jit(solution)/shard_map/pallas_call | solution.py:205
  (16 shorter events, 0.1 us)
Async XLA Ops:
  0.0 6.5 %copy-start.3 = (bf16[1024,128]{1,0:T(8,128)(2,1)S(1)}, bf16[1024,128]{1,0:T(8,128)(2,1)}, u32[]{:S(2)}) copy-start(bf16[1024,128]{1,0:T(8,128)(2,1)} %act_basis.1) | copy-start | bytes 786436
  0.0 6.5 %copy-start = (bf16[3584,256]{1,0:T(8,128)(2,1)S(1)}, bf16[3584,256]{1,0:T(8,128)(2,1)}, u32[]{:S(2)}) copy-start(bf16[3584,256]{1,0:T(8,128)(2,1)} %out_basis.1) | copy-start | bytes 5505028
  0.0 6.5 %copy-start.4 = (bf16[1024,64]{0,1:T(8,128)(2,1)S(1)}, bf16[1024,64]{0,1:T(8,128)(2,1)}, u32[]{:S(2)}) copy-start(bf16[1024,64]{0,1:T(8,128)(2,1)} %param.10) | copy-start | bytes 393220
  0.0 6.5 %copy-start.1 = (bf16[3584,64]{0,1:T(8,128)(2,1)S(1)}, bf16[3584,64]{0,1:T(8,128)(2,1)}, u32[]{:S(2)}) copy-start(bf16[3584,64]{0,1:T(8,128)(2,1)} %param.9) | copy-start | bytes 1376260
  0.0 7.4 %collective-permute-start = (f32[256,256]{1,0:T(8,128)}, f32[256,256]{1,0:T(8,128)S(1)}, u32[]{:S(2)}, u32[]{:S(2)}) collective-permute-start(f32[256,256]{1,0:T(8,128)} %eigen.1), channel_id=1, source_target_pairs={{0,1},{1,0},{2,3},{3,2},{4,5},{5,4},{6,7},{7,6},{8,9},{9,8},{10,11... | collective-permute-start | bytes 786440 | tf_op jit(solution)/shard_map/ppermute | solution.py:234
  1.6 5.9 %collective-permute-start.1 = (bf16[1,32,768]{2,1,0:T(8,128)(2,1)S(1)}, bf16[1,32,768]{2,1,0:T(8,128)(2,1)S(1)}, u32[]{:S(2)}, u32[]{:S(2)}) collective-permute-start(bf16[1,32,768]{2,1,0:T(8,128)(2,1)S(1)} %shard_map.92.first), channel_id=1, source_target_pairs={{0,8},{2,10},{4,12},{6,14},{8,0},{10,2},{12,4},{14,6},{1,9},{3,11}... | collective-permute-start | bytes 147464 | tf_op jit(solution)/shard_map/ppermute | solution.py:230
  6.5 15.9 %copy-start.2 = (f32[256,256]{1,0:T(8,128)S(1)}, f32[256,256]{1,0:T(8,128)}, u32[]{:S(2)}) copy-start(f32[256,256]{1,0:T(8,128)} %eigen.1) | copy-start | bytes 786436
  7.5 5.0 %collective-permute-start.2 = (f32[4,8,512]{2,1,0:T(8,128)S(1)}, f32[4,8,512]{2,1,0:T(8,128)S(1)}, u32[]{:S(2)}, u32[]{:S(2)}) collective-permute-start(f32[4,8,512]{2,1,0:T(8,128)S(1)} %get-tuple-element.9), channel_id=1, source_target_pairs={{0,2},{2,0},{4,6},{6,4},{8,10},{10,8},{12,14},{14,12},{1,3},{3,1},... | collective-permute-start | bytes 196616 | tf_op jit(solution)/shard_map/ppermute | solution.py:230
  10.2 4.6 %collective-permute-start.6 = (bf16[2,32,768]{2,1,0:T(8,128)(2,1)S(1)}, bf16[2,32,768]{2,1,0:T(8,128)(2,1)S(1)}, u32[]{:S(2)}, u32[]{:S(2)}) collective-permute-start(bf16[2,32,768]{2,1,0:T(8,128)(2,1)S(1)} %get-tuple-element.10.first), channel_id=1, source_target_pairs={{0,4},{2,6},{4,0},{6,2},{8,12},{10,14},{12,8},{14,10},{1,5},{3,7},... | collective-permute-start | bytes 294920 | tf_op jit(solution)/shard_map/ppermute | solution.py:230
  12.5 4.0 %collective-permute-start.3 = (f32[2,8,512]{2,1,0:T(8,128)S(1)}, f32[2,8,512]{2,1,0:T(8,128)S(1)}, u32[]{:S(2)}, u32[]{:S(2)}) collective-permute-start(f32[2,8,512]{2,1,0:T(8,128)S(1)} %get-tuple-element.12), channel_id=1, source_target_pairs={{0,4},{2,6},{4,0},{6,2},{8,12},{10,14},{12,8},{14,10},{1,5},{3,7},... | collective-permute-start | bytes 98312 | tf_op jit(solution)/shard_map/ppermute | solution.py:230
  14.8 5.7 %collective-permute-start.7 = (bf16[4,32,768]{2,1,0:T(8,128)(2,1)S(1)}, bf16[4,32,768]{2,1,0:T(8,128)(2,1)S(1)}, u32[]{:S(2)}, u32[]{:S(2)}) collective-permute-start(bf16[4,32,768]{2,1,0:T(8,128)(2,1)S(1)} %shard_map.94.rest_0_), channel_id=1, source_target_pairs={{0,2},{2,0},{4,6},{6,4},{8,10},{10,8},{12,14},{14,12},{1,3},{3,1},... | collective-permute-start | bytes 589832 | tf_op jit(solution)/shard_map/ppermute | solution.py:230
  16.5 4.7 %collective-permute-start.4 = (f32[8,512]{1,0:T(8,128)S(1)}, f32[8,512]{1,0:T(8,128)S(1)}, u32[]{:S(2)}, u32[]{:S(2)}) collective-permute-start(f32[8,512]{1,0:T(8,128)S(1)} %slice_bitcast_fusion.2), channel_id=1, source_target_pairs={{0,8},{2,10},{4,12},{6,14},{8,0},{10,2},{12,4},{14,6},{1,9},{3,11}... | collective-permute-start | bytes 49160 | tf_op jit(solution)/shard_map/ppermute | solution.py:230
  19.0 3.4 %collective-permute-start.8 = (bf16[4,32,768]{2,1,0:T(8,128)(2,1)S(1)}, bf16[4,32,768]{2,1,0:T(8,128)(2,1)S(1)}, u32[]{:S(2)}, u32[]{:S(2)}) collective-permute-start(bf16[4,32,768]{2,1,0:T(8,128)(2,1)S(1)} %shard_map.94.rest_0_), channel_id=1, source_target_pairs={{0,1},{1,0},{2,3},{3,2},{4,5},{5,4},{6,7},{7,6},{8,9},{9,8},{10,11... | collective-permute-start | bytes 589832 | tf_op jit(solution)/shard_map/ppermute | solution.py:246
  20.6 1.8 %collective-permute-start.9 = (bf16[4,32,768]{2,1,0:T(8,128)(2,1)S(1)}, bf16[4,32,768]{2,1,0:T(8,128)(2,1)S(1)}, u32[]{:S(2)}, u32[]{:S(2)}) collective-permute-start(bf16[4,32,768]{2,1,0:T(8,128)(2,1)S(1)} %collective-permute-done.7.rest_1_), channel_id=1, source_target_pairs={{0,1},{1,0},{2,3},{3,2},{4,5},{5,4},{6,7},{7,6},{8,9},{9,8},{10,11... | collective-permute-start | bytes 589832 | tf_op jit(solution)/shard_map/ppermute | solution.py:247
  21.2 1.2 %collective-permute-start.5 = (f32[8,512]{1,0:T(8,128)S(1)}, f32[8,512]{1,0:T(8,128)S(1)}, u32[]{:S(2)}, u32[]{:S(2)}) collective-permute-start(f32[8,512]{1,0:T(8,128)S(1)} %fusion.own), channel_id=1, source_target_pairs={{0,1},{1,0},{2,3},{3,2},{4,5},{5,4},{6,7},{7,6},{8,9},{9,8},{10,11... | collective-permute-start | bytes 49160 | tf_op jit(solution)/shard_map/ppermute | solution.py:250

commit v11 on v10

--- a/solution.py
+++ b/solution.py
@@ -77,7 +77,8 @@
     )(after, first, second)
 
 
-def project_kernel(query_out, query_act, out_basis, act_basis, total):
+def project_kernel(after, query_out, query_act, out_basis, act_basis, total):
+    del after
     half_ks = out_basis.shape[1]
     total[:, :half_ks] = jnp.dot(
         query_out[...], out_basis[...], preferred_element_type=jnp.float32
@@ -87,14 +88,14 @@
     )
 
 
-def project(query_out, query_act, out_basis, act_basis):
+def project(after, query_out, query_act, out_basis, act_basis):
     columns = query_out.shape[0]
     width = out_basis.shape[1] + act_basis.shape[1]
     operands = (query_out, query_act, out_basis, act_basis)
     return pl.pallas_call(
         project_kernel,
         out_shape=jax.ShapeDtypeStruct((columns, width), jnp.float32),
-        in_specs=[spec(pltpu.VMEM)] * len(operands),
+        in_specs=[spec(pl.ANY)] + [spec(pltpu.VMEM)] * len(operands),
         out_specs=spec(pltpu.VMEM),
         compiler_params=grant(8),
         cost_estimate=pl.CostEstimate(
@@ -102,7 +103,7 @@
             bytes_accessed=2 * sum(x.size for x in operands),
             transcendentals=0,
         ),
-    )(*operands)
+    )(after, *operands)
 
 
 def doubling_slot(distance, parts):
@@ -110,35 +111,33 @@
     return sum(1 << (bits - 1 - i) for i in range(bits) if distance >> i & 1)
 
 
-def spread_kernel(
-    place_ref, tokens_ref, ids_ref, after, total, first, second, kept, moved, joined
-):
+def spread_kernel(place_ref, tokens_ref, ids_ref, after, total, kept, moved):
     del after
-    parts = 2 * kept.shape[0]
-    local_rows = kept.shape[1]
+    lines, rows, _ = kept.shape
+    lines = 2 * lines
     width = total.shape[1]
-    row = lax.broadcasted_iota(jnp.int32, (local_rows, LANES), 0)
-    lane = lax.broadcasted_iota(jnp.int32, (local_rows, LANES), 1)
+    line = place_ref[0] // 2
+    row = lax.broadcasted_iota(jnp.int32, (rows, LANES), 0)
+    lane = lax.broadcasted_iota(jnp.int32, (rows, LANES), 1)
     facts = jnp.where(lane < LANES // 2, ids_ref[0], tokens_ref[0]).astype(jnp.float32)
-    for part in range(parts):
-        start = pl.multiple_of((place_ref[0] ^ part) * local_rows, local_rows)
-        piece = (moved if part % 2 else kept).at[part // 2]
-        piece[:, :width] = total[pl.ds(start, local_rows), :]
-        piece[:, width:] = jnp.where(row == doubling_slot(part, parts), facts, 0.0)
-    join_kernel(None, first, second, joined)
-
-
-def spread(place, tokens, ids, after, total, first, second, parts):
+    for k in range(lines):
+        start = pl.multiple_of((line ^ k) * rows, rows)
+        piece = (moved if k % 2 else kept).at[k // 2]
+        piece[:, :width] = total[pl.ds(start, rows), :]
+        piece[:, width:] = jnp.where(row == doubling_slot(k, lines), facts, 0.0)
+
+
+def spread(place, tokens, ids, after, total, lines):
     half = jax.ShapeDtypeStruct(
-        (parts // 2, total.shape[0] // parts, total.shape[1] + LANES), jnp.float32
+        (lines // 2, total.shape[0] // lines, total.shape[1] + LANES), jnp.float32
     )
     return pl.pallas_call(
         spread_kernel,
-        out_shape=[half, half, joined_shape(first, second)],
-        in_specs=[spec(pltpu.SMEM)] * 3 + [spec(pl.ANY)] + [spec(pltpu.VMEM)] * 3,
-        out_specs=[spec(pltpu.VMEM)] * 3,
+        out_shape=[half, half],
+        in_specs=[spec(pltpu.SMEM)] * 3 + [spec(pl.ANY), spec(pltpu.VMEM)],
+        out_specs=[spec(pltpu.VMEM)] * 2,
         compiler_params=grant(4),
-    )(place, tokens, ids, after, total, first, second)
+    )(place, tokens, ids, after, total)
 
 
 def split_three(x):
@@ -149,13 +148,12 @@
     return high, middle, low
 
 
-def score_kernel(core_ref, own, other, eigen, other_eigen, *rest):
-    out = rest[-1]
-    pairs = (rest[: len(rest) // 2], rest[len(rest) // 2 : -1])
+def score_kernel(
+    core_ref, place_ref, own, other, eigen, other_eigen, block, other_block, mine, theirs
+):
     first = core_ref[0] == 0
     half, ka = eigen.shape
-    examples = sum(x.shape[0] for x in pairs[0])
-    _, factor_rows, width = pairs[0][0].shape
+    examples, factor_rows, width = block.shape
     ks = width - ka
     coords = (
         jnp.where(first, own[...], other[...]),
@@ -170,17 +168,17 @@
     act_terms = split_three(act)
     out_terms = [split_three(v[:, :half]) for v in coords]
     order = ((0, 0), (0, 1), (1, 0), (1, 1), (0, 2), (2, 0))
-    weights, hot, flat = [], [], []
+    facts = jnp.concatenate([v[:examples, v.shape[1] - LANES :] for v in (own, other)], axis=0)
+    rows = jnp.concatenate([block[...], other_block[...]], axis=0)
+    examples = rows.shape[0]
     lane = lax.broadcasted_iota(jnp.int32, (examples, LANES), 1).astype(jnp.float32)
     row = lax.broadcasted_iota(jnp.int32, (examples, factor_rows, ka), 1).astype(jnp.float32)
-    for facts, blocks in zip((own, other), pairs):
-        rows = jnp.concatenate([x[...] for x in blocks], axis=0)
-        facts = facts[:, facts.shape[1] - LANES :]
-        hot.append(lane == facts[:, :1])
-        keep = row < facts[:, LANES // 2 : LANES // 2 + 1][:, :, None]
-        weights.append(jnp.where(keep, rows[:, :, ks:].astype(jnp.float32), 0.0))
-        flat.append(rows[:, :, :ks].reshape(examples * factor_rows, ks))
-    for q in range(out.shape[0]):
+    hot = lane == facts[:, :1]
+    keep = row < facts[:, LANES // 2 : LANES // 2 + 1][:, :, None]
+    weights = jnp.where(keep, rows[:, :, ks:].astype(jnp.float32), 0.0)
+    flat = rows[:, :, :ks].reshape(examples * factor_rows, ks)
+    results = []
+    for q in range(act.shape[0] // RQ):
         cut = slice(q * RQ, (q + 1) * RQ)
         right = jnp.concatenate([act_terms[b][cut] for _, b in order], axis=0)
         precond = []
@@ -191,24 +189,27 @@
             )
             precond.append((numer * scales[part]).astype(jnp.bfloat16))
         precond = jnp.concatenate(precond, axis=0)
-        scores = 0.0
-        for side in range(2):
-            projected = jnp.dot(flat[side], precond, preferred_element_type=jnp.float32)
-            terms = projected.reshape(examples, factor_rows, ka) * weights[side]
-            per_example = jnp.sum(jnp.sum(terms, axis=1), axis=1, keepdims=True)
-            scores += jnp.sum(jnp.where(hot[side], per_example, 0.0), axis=0, keepdims=True)
-        out[q : q + 1, :] = scores[:, : out.shape[1]]
-
-
-def score(core, own, other, eigen, other_eigen, blocks, other_blocks):
-    examples = sum(x.shape[0] for x in blocks + other_blocks)
+        projected = jnp.dot(flat, precond, preferred_element_type=jnp.float32)
+        terms = projected.reshape(examples, factor_rows, ka) * weights
+        per_example = jnp.sum(jnp.sum(terms, axis=1), axis=1, keepdims=True)
+        results.append(jnp.sum(jnp.where(hot, per_example, 0.0), axis=0, keepdims=True))
+    queries, total = mine.shape
+    low = place_ref[0] % 2 == 0
+    for q in range(queries):
+        here, there = results[q][:, :total], results[queries + q][:, :total]
+        mine[q : q + 1, :] = jnp.where(low, here, there)
+        theirs[q : q + 1, :] = jnp.where(low, there, here)
+
+
+def score(core, place, own, other, eigen, other_eigen, block, other_block, total):
+    half = jax.ShapeDtypeStruct((own.shape[0] // (2 * RQ), total), jnp.float32)
     return pl.pallas_call(
         score_kernel,
-        out_shape=jax.ShapeDtypeStruct((own.shape[0] // RQ, examples), jnp.float32),
-        in_specs=[spec(pltpu.SMEM)] + [spec(pltpu.VMEM)] * (4 + len(blocks + other_blocks)),
-        out_specs=spec(pltpu.VMEM),
+        out_shape=[half, half],
+        in_specs=[spec(pltpu.SMEM)] * 2 + [spec(pltpu.VMEM)] * 6,
+        out_specs=[spec(pltpu.VMEM)] * 2,
         compiler_params=grant(12),
-    )(core, own, other, eigen, other_eigen, *blocks, *other_blocks)
+    )(core, place, own, other, eigen, other_eigen, block, other_block)
 
 
 def direct(
@@ -223,34 +224,39 @@
     train_ids,
 ):
     parts = lax.axis_size("blk")
-    steps = parts.bit_length() - 1
+    lines = parts // 2
     swap = [(0, 1), (1, 0)]
 
-    def across(x, i):
-        return lax.ppermute(x, "blk", [(s, s ^ (1 << i)) for s in range(parts)])
+    def across(x, distance):
+        return lax.ppermute(x, "blk", [(s, s ^ distance) for s in range(parts)])
 
     place = lax.axis_index("blk").reshape(1)
     core = lax.axis_index("fsdp").reshape(1)
     other_eigen = lax.ppermute(eigenvalues, "fsdp", swap)
     block = pack(train_out, train_act)
-    arrived = across(block, steps - 1)
-    total = project(query_out.T, query_act.T, out_basis, act_basis)
-    kept, moved, block = spread(
-        place, train_tokens, train_ids, other_eigen, total, block, arrived, parts
-    )
-    sums = (kept + across(moved, 0)).reshape((2, 2) + kept.shape[1:])
-    arrived = across(block, 1)
-    kept, moved = sums[:, 0], sums[:, 1]
-    near = join(kept, block, arrived)
-    far = across(near, 0)
-    other_near = lax.ppermute(near, "fsdp", swap)
-    other_far = lax.ppermute(far, "fsdp", swap)
-    sums = kept + across(moved, 1)
-    own = sums[0] + across(sums[1], 2)
+    total = project(block, query_out.T, query_act.T, out_basis, act_basis)
+    kept, moved = spread(place, train_tokens, train_ids, other_eigen, total, lines)
+    block = join(kept, block, across(block, 4))
+    sums = kept + across(moved, 2)
+    block = join(sums, block, across(block, 2))
+    other_block = lax.ppermute(block, "fsdp", swap)
+    sums = sums[0] + across(sums[1], 4)
+    shared = sums.shape[1] - LANES
+    coords = sums[:, :shared] + across(sums[:, :shared], 1)
+    own = jnp.concatenate([coords, sums[:, shared:]], axis=1)
     other = lax.ppermute(own, "fsdp", swap)
-    return score(
-        core, own, other, eigenvalues, other_eigen, (near, far), (other_near, other_far)
-    )
+    mine, theirs = score(
+        core,
+        place,
+        own,
+        other,
+        eigenvalues,
+        other_eigen,
+        block,
+        other_block,
+        parts * 2 * train_out.shape[0],
+    )
+    return mine + across(theirs, 1)
 
 
 def score_block(precond, out_rows, act_rows, token_counts):

time: 24.2 us -> 25.5 us (1.054)
  starting transfers between devices: 11.6 us -> 14.2 us
  waiting for transfers between devices: 7.8 us -> 5.69 us
  local copies, waits for them, and re-layouts: 0.03 us -> 0.75 us
  other arithmetic: 0.02 us -> 0.59 us
  Pallas kernels: 3.08 us -> 2.59 us
    ppermute x8 -> x7, starting transfers between devices: 11 us -> 13.7 us  [the longest x6 13.6 us: across(): return lax.ppermute(x, 'blk', [(s, s ^ distance) for s in range(parts)])]
    ppermute x8 -> x7, waiting for transfers between devices: 6.62 us -> 4.5 us  [the longest x6 4.5 us: across(): return lax.ppermute(x, 'blk', [(s, s ^ distance) for s in range(parts)])]
    unnamed x10, local copies, waits for them, and re-layouts: 0.02 us -> 0.74 us
    add x3 -> x4, other arithmetic: 0.02 us -> 0.59 us  [the longest x1 0.56 us: direct(): return mine + across(theirs, 1)]
    pallas_call x2, Pallas kernels: 1.56 us -> 1.17 us  [the longest x1 1.15 us: score(): pl.pallas_call(score_kernel, out_shape=[half, half], in_specs=[spec(pltpu...]
  transfers between devices with their start and end apart: 10 -> 9, of which waited for: 7 -> 5; matrix products, arithmetic and copies ran while one was open for 0% -> 0% of each run, Pallas kernels for 6% -> 6%
where the time goes in v11:
time: 25.5 us; the launch traced here: 25.3 us
  starting transfers between devices  14.2 us (56%)
  waiting for transfers between devices  5.69 us (22%)
  Pallas kernels  2.59 us (10%)
  between operations  1.42 us (6%)
  local copies, waits for them, and re-layouts  0.75 us (3%)
  other arithmetic  0.59 us (2%)
    ppermute x6, starting transfers between devices, across(): return lax.ppermute(x, 'blk', [(s, s ^ distance) for s in range(parts)])  13.6 us
    ppermute x6, waiting for transfers between devices, across(): return lax.ppermute(x, 'blk', [(s, s ^ distance) for s in range(parts)])  4.5 us
    ppermute x1, waiting for transfers between devices, direct(): other = lax.ppermute(own, 'fsdp', swap)  1.19 us
    pallas_call x1, Pallas kernels, score(): pl.pallas_call(score_kernel, out_shape=[half, half], in_specs=[spec(pltpu...  1.15 us
    pallas_call x1, Pallas kernels, pack(): pl.pallas_call(pack_kernel, out_shape=jax.ShapeDtypeStruct(shape, train_o...  0.93 us
    unnamed x10, local copies, waits for them, and re-layouts  0.74 us
    add x1, other arithmetic, direct(): return mine + across(theirs, 1)  0.56 us
  transfers between devices with their start and end apart: 9, of which 5 were waited for; matrix products, arithmetic and copies ran while one was open for 0% of the time, Pallas kernels for 6%

profile of v11, /device:TPU:0, one launch (start us, length us, event | category | flops | bytes accessed | tf_op | source)
XLA Modules:
  0.0 25.3 jit_solution(8635159404183419431)
XLA Ops:
  0.0 0.5 %collective-permute-start = (f32[256,256]{1,0:T(8,128)}, f32[256,256]{1,0:T(8,128)S(1)}, u32[]{:S(2)}, u32[]{:S(2)}) collective-permute-start(f32[256,256]{1,0:T(8,128)} %eigen.1), channel_id=1, source_target_pairs={{0,1},{1,0},{2,3},{3,2},{4,5},{5,4},{6,7},{7,6},{8,9},{9,8},{10,11... | collective-permute-start | bytes 786440 | tf_op jit(solution)/shard_map/ppermute | solution.py:235
  1.8 0.9 %shard_map.91.after.first = bf16[1,32,768]{2,1,0:T(8,128)(2,1)S(1)} custom-call(bf16[1,32,512]{2,1,0:T(8,128)(2,1)} %train_out.1, bf16[1,32,256]{2,1,0:T(8,128)(2,1)} %train_act.1), custom_call_target="tpu_custom_call" | custom-call | flops 1000000000 | tf_op jit(solution)/shard_map/pallas_call | solution.py:46
  2.7 0.6 %copy-done = bf16[3584,256]{1,0:T(8,128)(2,1)S(1)} copy-done((bf16[3584,256]{1,0:T(8,128)(2,1)S(1)}, bf16[3584,256]{1,0:T(8,128)(2,1)}, u32[]{:S(2)}) %copy-start) | copy-done | bytes 1835032
  3.3 0.1 copy-done.1
  3.4 0.1 copy-done.3
  3.4 0.0 copy-done.4
  3.5 0.5 %shard_map.92.total = f32[64,384]{1,0:T(8,128)S(1)} custom-call(bf16[1,32,768]{2,1,0:T(8,128)(2,1)S(1)} %shard_map.91.after.first, bf16[64,3584]{1,0:T(8,128)(2,1)S(1)} %bitcast.10, bf16[64,1024]{1,0:T(8,128)(2,1)S(1)} %bitcast.11, bf16[3584,256]{1,0:T(8,128)(2,1)S(1)} %copy-done, bf16[1024,128]{1,0:T(8,128)(2,1)S(1)} %copy-done.3), custom_call_target="tpu_custom_call" | custom-call | flops 134217728 | bytes 2686976 | tf_op jit(solution)/shard_map/pallas_call | solution.py:95
  4.0 2.6 %collective-permute-start.1 = (f32[2,16,512]{2,1,0:T(8,128)S(1)}, f32[2,16,512]{2,1,0:T(8,128)S(1)}, u32[]{:S(2)}, u32[]{:S(2)}) collective-permute-start(f32[2,16,512]{2,1,0:T(8,128)S(1)} %get-tuple-element.10), channel_id=1, source_target_pairs={{0,4},{2,6},{4,0},{6,2},{8,12},{10,14},{12,8},{14,10},{1,5},{3,7},... | collective-permute-start | bytes 196616 | tf_op jit(solution)/shard_map/ppermute | solution.py:231
  6.6 2.6 %collective-permute-start.5 = (bf16[1,32,768]{2,1,0:T(8,128)(2,1)S(1)}, bf16[1,32,768]{2,1,0:T(8,128)(2,1)S(1)}, u32[]{:S(2)}, u32[]{:S(2)}) collective-permute-start(bf16[1,32,768]{2,1,0:T(8,128)(2,1)S(1)} %shard_map.91.after.first), channel_id=1, source_target_pairs={{0,8},{2,10},{4,12},{6,14},{8,0},{10,2},{12,4},{14,6},{1,9},{3,11}... | collective-permute-start | bytes 147464 | tf_op jit(solution)/shard_map/ppermute | solution.py:231
  9.2 0.2 collective-permute-done.1
  9.4 3.2 %collective-permute-start.2 = (f32[16,512]{1,0:T(8,128)S(1)}, f32[16,512]{1,0:T(8,128)S(1)}, u32[]{:S(2)}, u32[]{:S(2)}) collective-permute-start(f32[16,512]{1,0:T(8,128)S(1)} %slice_bitcast_fusion), channel_id=1, source_target_pairs={{0,8},{2,10},{4,12},{6,14},{8,0},{10,2},{12,4},{14,6},{1,9},{3,11}... | collective-permute-start | bytes 98312 | tf_op jit(solution)/shard_map/ppermute | solution.py:231
  12.6 0.0 collective-permute-done.5.second
  12.6 2.2 %collective-permute-start.6 = (bf16[2,32,768]{2,1,0:T(8,128)(2,1)S(1)}, bf16[2,32,768]{2,1,0:T(8,128)(2,1)S(1)}, u32[]{:S(2)}, u32[]{:S(2)}) collective-permute-start(bf16[2,32,768]{2,1,0:T(8,128)(2,1)S(1)} %shard_map.94.first), channel_id=1, source_target_pairs={{0,4},{2,6},{4,0},{6,2},{8,12},{10,14},{12,8},{14,10},{1,5},{3,7},... | collective-permute-start | bytes 294920 | tf_op jit(solution)/shard_map/ppermute | solution.py:231
  14.8 0.0 collective-permute-done.2
  14.8 1.6 %collective-permute-start.3 = (f32[16,384]{1,0:T(8,128)S(1)}, f32[16,384]{1,0:T(8,128)S(1)}, u32[]{:S(2)}, u32[]{:S(2)}) collective-permute-start(f32[16,384]{1,0:T(8,128)S(1)} %slice.19), channel_id=1, source_target_pairs={{0,2},{2,0},{4,6},{6,4},{8,10},{10,8},{12,14},{14,12},{1,3},{3,1},... | collective-permute-start | bytes 73736 | tf_op jit(solution)/shard_map/ppermute | solution.py:231
  16.4 1.0 %collective-permute-done.6.second = bf16[2,32,768]{2,1,0:T(8,128)(2,1)S(1)} collective-permute-done((bf16[2,32,768]{2,1,0:T(8,128)(2,1)S(1)}, bf16[2,32,768]{2,1,0:T(8,128)(2,1)S(1)}, u32[]{:S(2)}, u32[]{:S(2)}) %collective-permute-start.6) | collective-permute-done | bytes 98336 | tf_op jit(solution)/shard_map/ppermute | solution.py:231
  17.4 0.1 collective-permute-start.7
  17.5 1.2 %collective-permute-done.3 = f32[16,384]{1,0:T(8,128)S(1)} collective-permute-done((f32[16,384]{1,0:T(8,128)S(1)}, f32[16,384]{1,0:T(8,128)S(1)}, u32[]{:S(2)}, u32[]{:S(2)}) %collective-permute-start.3) | collective-permute-done | bytes 24608 | tf_op jit(solution)/shard_map/ppermute | solution.py:231
  18.7 0.1 collective-permute-start.4
  18.8 1.2 %collective-permute-done.4.other = f32[16,512]{1,0:T(8,128)S(1)} collective-permute-done((f32[16,512]{1,0:T(8,128)S(1)}, f32[16,512]{1,0:T(8,128)S(1)}, u32[]{:S(2)}, u32[]{:S(2)}) %collective-permute-start.4) | collective-permute-done | bytes 32800 | tf_op jit(solution)/shard_map/ppermute | solution.py:247
  20.0 1.1 %shard_map.96 = (f32[2,16]{1,0:T(2,128)S(1)}, f32[2,16]{1,0:T(2,128)S(1)}) custom-call(s32[1]{0:T(128)} %bitcast.core_ref, s32[1]{0:T(128)} %bitcast.1.place_ref, f32[16,512]{1,0:T(8,128)S(1)} %pad_maximum_fusion.own, f32[16,512]{1,0:T(8,128)S(1)} %collective-permute-done.4.other, f32[256,256]{1,0:T(8,128)S(1)} %copy-done.2, ...), custom_call_target="tpu_custom_call" | custom-call | tf_op jit(solution)/shard_map/pallas_call | solution.py:206
  21.1 1.5 %collective-permute-start.8 = (f32[2,16]{1,0:T(2,128)S(1)}, f32[2,16]{1,0:T(2,128)S(1)}, u32[]{:S(2)}, u32[]{:S(2)}) collective-permute-start(f32[2,16]{1,0:T(2,128)S(1)} %get-tuple-element.12), channel_id=1, source_target_pairs={{0,2},{2,0},{4,6},{6,4},{8,10},{10,8},{12,14},{14,12},{1,3},{3,1},... | collective-permute-start | bytes 392 | tf_op jit(solution)/shard_map/ppermute | solution.py:231
  22.6 2.1 %collective-permute-done.8 = f32[2,16]{1,0:T(2,128)S(1)} collective-permute-done((f32[2,16]{1,0:T(2,128)S(1)}, f32[2,16]{1,0:T(2,128)S(1)}, u32[]{:S(2)}, u32[]{:S(2)}) %collective-permute-start.8) | collective-permute-done | bytes 160 | tf_op jit(solution)/shard_map/ppermute | solution.py:231
  24.7 0.6 %add.15 = f32[2,16]{1,0:T(2,128)} add(f32[2,16]{1,0:T(2,128)S(1)} %get-tuple-element.11, f32[2,16]{1,0:T(2,128)S(1)} %collective-permute-done.8) | non-fusion elementwise | flops 32 | bytes 384 | tf_op jit(solution)/shard_map/add | solution.py:259
  (18 shorter events, 0.1 us)
Async XLA Ops:
  0.0 3.9 %collective-permute-start = (f32[256,256]{1,0:T(8,128)}, f32[256,256]{1,0:T(8,128)S(1)}, u32[]{:S(2)}, u32[]{:S(2)}) collective-permute-start(f32[256,256]{1,0:T(8,128)} %eigen.1), channel_id=1, source_target_pairs={{0,1},{1,0},{2,3},{3,2},{4,5},{5,4},{6,7},{7,6},{8,9},{9,8},{10,11... | collective-permute-start | bytes 786440 | tf_op jit(solution)/shard_map/ppermute | solution.py:235
  1.8 1.5 %copy-start = (bf16[3584,256]{1,0:T(8,128)(2,1)S(1)}, bf16[3584,256]{1,0:T(8,128)(2,1)}, u32[]{:S(2)}) copy-start(bf16[3584,256]{1,0:T(8,128)(2,1)} %out_basis.1) | copy-start | bytes 5505028
  1.8 1.6 %copy-start.1 = (bf16[3584,64]{0,1:T(8,128)(2,1)S(1)}, bf16[3584,64]{0,1:T(8,128)(2,1)}, u32[]{:S(2)}) copy-start(bf16[3584,64]{0,1:T(8,128)(2,1)} %param.9) | copy-start | bytes 1376260
  1.8 1.7 %copy-start.3 = (bf16[1024,128]{1,0:T(8,128)(2,1)S(1)}, bf16[1024,128]{1,0:T(8,128)(2,1)}, u32[]{:S(2)}) copy-start(bf16[1024,128]{1,0:T(8,128)(2,1)} %act_basis.1) | copy-start | bytes 786436
  1.8 1.7 %copy-start.4 = (bf16[1024,64]{0,1:T(8,128)(2,1)S(1)}, bf16[1024,64]{0,1:T(8,128)(2,1)}, u32[]{:S(2)}) copy-start(bf16[1024,64]{0,1:T(8,128)(2,1)} %param.10) | copy-start | bytes 393220
  3.5 16.5 %copy-start.2 = (f32[256,256]{1,0:T(8,128)S(1)}, f32[256,256]{1,0:T(8,128)}, u32[]{:S(2)}) copy-start(f32[256,256]{1,0:T(8,128)} %eigen.1) | copy-start | bytes 786436
  4.0 5.4 %collective-permute-start.1 = (f32[2,16,512]{2,1,0:T(8,128)S(1)}, f32[2,16,512]{2,1,0:T(8,128)S(1)}, u32[]{:S(2)}, u32[]{:S(2)}) collective-permute-start(f32[2,16,512]{2,1,0:T(8,128)S(1)} %get-tuple-element.10), channel_id=1, source_target_pairs={{0,4},{2,6},{4,0},{6,2},{8,12},{10,14},{12,8},{14,10},{1,5},{3,7},... | collective-permute-start | bytes 196616 | tf_op jit(solution)/shard_map/ppermute | solution.py:231
  6.6 6.0 %collective-permute-start.5 = (bf16[1,32,768]{2,1,0:T(8,128)(2,1)S(1)}, bf16[1,32,768]{2,1,0:T(8,128)(2,1)S(1)}, u32[]{:S(2)}, u32[]{:S(2)}) collective-permute-start(bf16[1,32,768]{2,1,0:T(8,128)(2,1)S(1)} %shard_map.91.after.first), channel_id=1, source_target_pairs={{0,8},{2,10},{4,12},{6,14},{8,0},{10,2},{12,4},{14,6},{1,9},{3,11}... | collective-permute-start | bytes 147464 | tf_op jit(solution)/shard_map/ppermute | solution.py:231
  9.4 5.4 %collective-permute-start.2 = (f32[16,512]{1,0:T(8,128)S(1)}, f32[16,512]{1,0:T(8,128)S(1)}, u32[]{:S(2)}, u32[]{:S(2)}) collective-permute-start(f32[16,512]{1,0:T(8,128)S(1)} %slice_bitcast_fusion), channel_id=1, source_target_pairs={{0,8},{2,10},{4,12},{6,14},{8,0},{10,2},{12,4},{14,6},{1,9},{3,11}... | collective-permute-start | bytes 98312 | tf_op jit(solution)/shard_map/ppermute | solution.py:231
  12.6 4.8 %collective-permute-start.6 = (bf16[2,32,768]{2,1,0:T(8,128)(2,1)S(1)}, bf16[2,32,768]{2,1,0:T(8,128)(2,1)S(1)}, u32[]{:S(2)}, u32[]{:S(2)}) collective-permute-start(bf16[2,32,768]{2,1,0:T(8,128)(2,1)S(1)} %shard_map.94.first), channel_id=1, source_target_pairs={{0,4},{2,6},{4,0},{6,2},{8,12},{10,14},{12,8},{14,10},{1,5},{3,7},... | collective-permute-start | bytes 294920 | tf_op jit(solution)/shard_map/ppermute | solution.py:231
  14.8 3.9 %collective-permute-start.3 = (f32[16,384]{1,0:T(8,128)S(1)}, f32[16,384]{1,0:T(8,128)S(1)}, u32[]{:S(2)}, u32[]{:S(2)}) collective-permute-start(f32[16,384]{1,0:T(8,128)S(1)} %slice.19), channel_id=1, source_target_pairs={{0,2},{2,0},{4,6},{6,4},{8,10},{10,8},{12,14},{14,12},{1,3},{3,1},... | collective-permute-start | bytes 73736 | tf_op jit(solution)/shard_map/ppermute | solution.py:231
  17.4 2.6 %collective-permute-start.7 = (bf16[4,32,768]{2,1,0:T(8,128)(2,1)S(1)}, bf16[4,32,768]{2,1,0:T(8,128)(2,1)S(1)}, u32[]{:S(2)}, u32[]{:S(2)}) collective-permute-start(bf16[4,32,768]{2,1,0:T(8,128)(2,1)S(1)} %shard_map.95.block), channel_id=1, source_target_pairs={{0,1},{1,0},{2,3},{3,2},{4,5},{5,4},{6,7},{7,6},{8,9},{9,8},{10,11... | collective-permute-start | bytes 589832 | tf_op jit(solution)/shard_map/ppermute | solution.py:242
  18.7 1.3 %collective-permute-start.4 = (f32[16,512]{1,0:T(8,128)S(1)}, f32[16,512]{1,0:T(8,128)S(1)}, u32[]{:S(2)}, u32[]{:S(2)}) collective-permute-start(f32[16,512]{1,0:T(8,128)S(1)} %pad_maximum_fusion.own), channel_id=1, source_target_pairs={{0,1},{1,0},{2,3},{3,2},{4,5},{5,4},{6,7},{7,6},{8,9},{9,8},{10,11... | collective-permute-start | bytes 98312 | tf_op jit(solution)/shard_map/ppermute | solution.py:247
  21.1 3.6 %collective-permute-start.8 = (f32[2,16]{1,0:T(2,128)S(1)}, f32[2,16]{1,0:T(2,128)S(1)}, u32[]{:S(2)}, u32[]{:S(2)}) collective-permute-start(f32[2,16]{1,0:T(2,128)S(1)} %get-tuple-element.12), channel_id=1, source_target_pairs={{0,2},{2,0},{4,6},{6,4},{8,10},{10,8},{12,14},{14,12},{1,3},{3,1},... | collective-permute-start | bytes 392 | tf_op jit(solution)/shard_map/ppermute | solution.py:231

commit v12 on v11

--- a/solution.py
+++ b/solution.py
@@ -149,11 +149,11 @@
 
 
 def score_kernel(
-    core_ref, place_ref, own, other, eigen, other_eigen, block, other_block, mine, theirs
+    core_ref, place_ref, own, other, eigen, other_eigen, blocks, handed, mine, theirs
 ):
     first = core_ref[0] == 0
     half, ka = eigen.shape
-    examples, factor_rows, width = block.shape
+    examples, factor_rows, width = blocks.shape
     ks = width - ka
     coords = (
         jnp.where(first, own[...], other[...]),
@@ -168,9 +168,11 @@
     act_terms = split_three(act)
     out_terms = [split_three(v[:, :half]) for v in coords]
     order = ((0, 0), (0, 1), (1, 0), (1, 1), (0, 2), (2, 0))
-    facts = jnp.concatenate([v[:examples, v.shape[1] - LANES :] for v in (own, other)], axis=0)
-    rows = jnp.concatenate([block[...], other_block[...]], axis=0)
-    examples = rows.shape[0]
+    facts = [v[: examples // 2, v.shape[1] - LANES :] for v in coords]
+    facts = jnp.concatenate(facts, axis=0)
+    rows = jnp.where(first, handed[...], blocks[...])
+    rows = rows.reshape(examples // 2, 2, factor_rows, width)
+    rows = jnp.concatenate([rows[:, 0], rows[:, 1]], axis=0)
     lane = lax.broadcasted_iota(jnp.int32, (examples, LANES), 1).astype(jnp.float32)
     row = lax.broadcasted_iota(jnp.int32, (examples, factor_rows, ka), 1).astype(jnp.float32)
     hot = lane == facts[:, :1]
@@ -201,7 +203,7 @@
         theirs[q : q + 1, :] = jnp.where(low, there, here)
 
 
-def score(core, place, own, other, eigen, other_eigen, block, other_block, total):
+def score(core, place, own, other, eigen, other_eigen, blocks, handed, total):
     half = jax.ShapeDtypeStruct((own.shape[0] // (2 * RQ), total), jnp.float32)
     return pl.pallas_call(
         score_kernel,
@@ -209,7 +211,7 @@
         in_specs=[spec(pltpu.SMEM)] * 2 + [spec(pltpu.VMEM)] * 6,
         out_specs=[spec(pltpu.VMEM)] * 2,
         compiler_params=grant(12),
-    )(core, place, own, other, eigen, other_eigen, block, other_block)
+    )(core, place, own, other, eigen, other_eigen, blocks, handed)
 
 
 def direct(
@@ -230,16 +232,21 @@
     def across(x, distance):
         return lax.ppermute(x, "blk", [(s, s ^ distance) for s in range(parts)])
 
+    def second_core(x, distance):
+        pairs = [(2 * s + 1, 2 * (s ^ distance) + 1) for s in range(parts)]
+        return lax.ppermute(x, ("blk", "fsdp"), pairs)
+
     place = lax.axis_index("blk").reshape(1)
     core = lax.axis_index("fsdp").reshape(1)
     other_eigen = lax.ppermute(eigenvalues, "fsdp", swap)
     block = pack(train_out, train_act)
-    total = project(block, query_out.T, query_act.T, out_basis, act_basis)
+    pair = join(block, lax.ppermute(block, "fsdp", [(0, 1)]), block)
+    total = project(pair, query_out.T, query_act.T, out_basis, act_basis)
     kept, moved = spread(place, train_tokens, train_ids, other_eigen, total, lines)
-    block = join(kept, block, across(block, 4))
+    pairs = join(kept, pair, second_core(pair, 4))
     sums = kept + across(moved, 2)
-    block = join(sums, block, across(block, 2))
-    other_block = lax.ppermute(block, "fsdp", swap)
+    blocks = join(sums, pairs, second_core(pairs, 2))
+    handed = lax.ppermute(blocks, "fsdp", [(1, 0)])
     sums = sums[0] + across(sums[1], 4)
     shared = sums.shape[1] - LANES
     coords = sums[:, :shared] + across(sums[:, :shared], 1)
@@ -252,8 +259,8 @@
         other,
         eigenvalues,
         other_eigen,
-        block,
-        other_block,
+        blocks,
+        handed,
         parts * 2 * train_out.shape[0],
     )
     return mine + across(theirs, 1)

time: 25.5 us -> 29.6 us (1.16)
  starting transfers between devices: 14.2 us -> 18.1 us
  waiting for transfers between devices: 5.69 us -> 6.51 us
  local copies, waits for them, and re-layouts: 0.75 us -> 0.03 us
    ppermute x1 -> x4, starting transfers between devices: 0.07 us -> 4.46 us  [the longest x1 1.84 us: direct(): pair = join(block, lax.ppermute(block, 'fsdp', [(0, 1)]), block)]
    ppermute x6 -> x4, starting transfers between devices: 13.6 us -> 10 us  [across(): return lax.ppermute(x, 'blk', [(s, s ^ distance) for s in range(parts)])]
    ppermute x1, starting transfers between devices: 0.07 us -> 3.04 us  [direct(): other = lax.ppermute(own, 'fsdp', swap)]
    ppermute x6 -> x4, waiting for transfers between devices: 4.5 us -> 5.39 us  [across(): return lax.ppermute(x, 'blk', [(s, s ^ distance) for s in range(parts)])]
    unnamed x10, local copies, waits for them, and re-layouts: 0.74 us -> 0.02 us
  transfers between devices with their start and end apart: 9 -> 10, of which waited for: 5 -> 5; matrix products, arithmetic and copies ran while one was open for 0% -> 0% of each run, Pallas kernels for 6% -> 5%
where the time goes in v12:
time: 29.6 us; the launch traced here: 29.4 us
  starting transfers between devices  18.1 us (61%)
  waiting for transfers between devices  6.51 us (22%)
  Pallas kernels  2.73 us (9%)
  between operations  1.46 us (5%)
  other arithmetic  0.59 us (2%)
    ppermute x4, starting transfers between devices, across(): return lax.ppermute(x, 'blk', [(s, s ^ distance) for s in range(parts)])  10 us
    ppermute x4, waiting for transfers between devices, across(): return lax.ppermute(x, 'blk', [(s, s ^ distance) for s in range(parts)])  5.39 us
    ppermute x1, starting transfers between devices, direct(): other = lax.ppermute(own, 'fsdp', swap)  3.04 us
    ppermute x1, starting transfers between devices, direct(): pair = join(block, lax.ppermute(block, 'fsdp', [(0, 1)]), block)  1.84 us
    ppermute x2, starting transfers between devices, second_core(): return lax.ppermute(x, ('blk', 'fsdp'), pairs)  1.33 us
    ppermute x1, starting transfers between devices, direct(): handed = lax.ppermute(blocks, 'fsdp', [(1, 0)])  1.29 us
    pallas_call x1, Pallas kernels, score(): pl.pallas_call(score_kernel, out_shape=[half, half], in_specs=[spec(pltpu...  1.15 us
    ppermute x1, waiting for transfers between devices, direct(): other = lax.ppermute(own, 'fsdp', swap)  1.1 us
  transfers between devices with their start and end apart: 10, of which 5 were waited for; matrix products, arithmetic and copies ran while one was open for 0% of the time, Pallas kernels for 5%

profile of v12, /device:TPU:0, one launch (start us, length us, event | category | flops | bytes accessed | tf_op | source)
XLA Modules:
  0.0 29.4 jit_solution(1257325635749371203)
XLA Ops:
  0.0 0.5 %collective-permute-start = (f32[256,256]{1,0:T(8,128)}, f32[256,256]{1,0:T(8,128)S(1)}, u32[]{:S(2)}, u32[]{:S(2)}) collective-permute-start(f32[256,256]{1,0:T(8,128)} %eigen.1), channel_id=1, source_target_pairs={{0,1},{1,0},{2,3},{3,2},{4,5},{5,4},{6,7},{7,6},{8,9},{9,8},{10,11... | collective-permute-start | bytes 786440 | tf_op jit(solution)/shard_map/ppermute | solution.py:241
  0.5 1.0 %shard_map.91.after.second = bf16[1,32,768]{2,1,0:T(8,128)(2,1)S(1)} custom-call(bf16[1,32,512]{2,1,0:T(8,128)(2,1)} %train_out.1, bf16[1,32,256]{2,1,0:T(8,128)(2,1)} %train_act.1), custom_call_target="tpu_custom_call" | custom-call | flops 1000000000 | tf_op jit(solution)/shard_map/pallas_call | solution.py:46
  1.6 1.8 %collective-permute-start.1 = (bf16[1,32,768]{2,1,0:T(8,128)(2,1)S(1)}, bf16[1,32,768]{2,1,0:T(8,128)(2,1)S(1)}, u32[]{:S(2)}, u32[]{:S(2)}) collective-permute-start(bf16[1,32,768]{2,1,0:T(8,128)(2,1)S(1)} %shard_map.91.after.second), channel_id=1, source_target_pairs={{0,1},{2,3},{4,5},{6,7},{8,9},{10,11},{12,13},{14,15},{16,17},{18,... | collective-permute-start | bytes 147464 | tf_op jit(solution)/shard_map/ppermute | solution.py:243
  4.7 0.0 collective-permute-done.1.first
  4.8 0.5 %shard_map.93.total = f32[64,384]{1,0:T(8,128)S(1)} custom-call(bf16[2,32,768]{2,1,0:T(8,128)(2,1)S(1)} %shard_map.92.after.first, bf16[64,3584]{1,0:T(8,128)(2,1)S(1)} %bitcast.10, bf16[64,1024]{1,0:T(8,128)(2,1)S(1)} %bitcast.11, bf16[3584,256]{1,0:T(8,128)(2,1)S(1)} %copy-done, bf16[1024,128]{1,0:T(8,128)(2,1)S(1)} %copy-done.3), custom_call_target="tpu_custom_call" | custom-call | flops 134217728 | bytes 2686976 | tf_op jit(solution)/shard_map/pallas_call | solution.py:95
  5.3 0.0 copy-start.2
  5.3 0.0 collective-permute-done.after.other_eigen
  5.3 3.0 %collective-permute-start.2 = (f32[2,16,512]{2,1,0:T(8,128)S(1)}, f32[2,16,512]{2,1,0:T(8,128)S(1)}, u32[]{:S(2)}, u32[]{:S(2)}) collective-permute-start(f32[2,16,512]{2,1,0:T(8,128)S(1)} %get-tuple-element.10), channel_id=1, source_target_pairs={{0,4},{2,6},{4,0},{6,2},{8,12},{10,14},{12,8},{14,10},{1,5},{3,7},... | collective-permute-start | bytes 196616 | tf_op jit(solution)/shard_map/ppermute | solution.py:233
  8.3 0.7 %collective-permute-start.6 = (bf16[2,32,768]{2,1,0:T(8,128)(2,1)S(1)}, bf16[2,32,768]{2,1,0:T(8,128)(2,1)S(1)}, u32[]{:S(2)}, u32[]{:S(2)}) collective-permute-start(bf16[2,32,768]{2,1,0:T(8,128)(2,1)S(1)} %shard_map.92.after.first), channel_id=1, source_target_pairs={{1,9},{3,11},{5,13},{7,15},{9,1},{11,3},{13,5},{15,7},{17,25},{19,... | collective-permute-start | bytes 294920 | tf_op jit(solution)/shard_map/ppermute | solution.py:237
  9.0 1.6 %collective-permute-done.2 = f32[2,16,512]{2,1,0:T(8,128)S(1)} collective-permute-done((f32[2,16,512]{2,1,0:T(8,128)S(1)}, f32[2,16,512]{2,1,0:T(8,128)S(1)}, u32[]{:S(2)}, u32[]{:S(2)}) %collective-permute-start.2) | collective-permute-done | bytes 65568 | tf_op jit(solution)/shard_map/ppermute | solution.py:233
  10.6 3.1 %collective-permute-start.3 = (f32[16,512]{1,0:T(8,128)S(1)}, f32[16,512]{1,0:T(8,128)S(1)}, u32[]{:S(2)}, u32[]{:S(2)}) collective-permute-start(f32[16,512]{1,0:T(8,128)S(1)} %slice_bitcast_fusion), channel_id=1, source_target_pairs={{0,8},{2,10},{4,12},{6,14},{8,0},{10,2},{12,4},{14,6},{1,9},{3,11}... | collective-permute-start | bytes 98312 | tf_op jit(solution)/shard_map/ppermute | solution.py:233
  13.7 0.7 %collective-permute-start.7 = (bf16[4,32,768]{2,1,0:T(8,128)(2,1)S(1)}, bf16[4,32,768]{2,1,0:T(8,128)(2,1)S(1)}, u32[]{:S(2)}, u32[]{:S(2)}) collective-permute-start(bf16[4,32,768]{2,1,0:T(8,128)(2,1)S(1)} %shard_map.95.first), channel_id=1, source_target_pairs={{1,5},{3,7},{5,1},{7,3},{9,13},{11,15},{13,9},{15,11},{17,21},{19,... | collective-permute-start | bytes 589832 | tf_op jit(solution)/shard_map/ppermute | solution.py:237
  14.4 1.2 %collective-permute-done.3 = f32[16,512]{1,0:T(8,128)S(1)} collective-permute-done((f32[16,512]{1,0:T(8,128)S(1)}, f32[16,512]{1,0:T(8,128)S(1)}, u32[]{:S(2)}, u32[]{:S(2)}) %collective-permute-start.3) | collective-permute-done | bytes 32800 | tf_op jit(solution)/shard_map/ppermute | solution.py:233
  15.6 2.4 %collective-permute-start.4 = (f32[16,384]{1,0:T(8,128)S(1)}, f32[16,384]{1,0:T(8,128)S(1)}, u32[]{:S(2)}, u32[]{:S(2)}) collective-permute-start(f32[16,384]{1,0:T(8,128)S(1)} %slice.19), channel_id=1, source_target_pairs={{0,2},{2,0},{4,6},{6,4},{8,10},{10,8},{12,14},{14,12},{1,3},{3,1},... | collective-permute-start | bytes 73736 | tf_op jit(solution)/shard_map/ppermute | solution.py:233
  18.0 0.0 collective-permute-done.7.second
  18.1 1.3 %collective-permute-start.8 = (bf16[8,32,768]{2,1,0:T(8,128)(2,1)S(1)}, bf16[8,32,768]{2,1,0:T(8,128)(2,1)S(1)}, u32[]{:S(2)}, u32[]{:S(2)}) collective-permute-start(bf16[8,32,768]{2,1,0:T(8,128)(2,1)S(1)} %shard_map.96.blocks), channel_id=1, source_target_pairs={{1,0},{3,2},{5,4},{7,6},{9,8},{11,10},{13,12},{15,14},{17,16},{19,... | collective-permute-start | bytes 1179656 | tf_op jit(solution)/shard_map/ppermute | solution.py:249
  19.4 0.6 %collective-permute-done.4 = f32[16,384]{1,0:T(8,128)S(1)} collective-permute-done((f32[16,384]{1,0:T(8,128)S(1)}, f32[16,384]{1,0:T(8,128)S(1)}, u32[]{:S(2)}, u32[]{:S(2)}) %collective-permute-start.4) | collective-permute-done | bytes 24608 | tf_op jit(solution)/shard_map/ppermute | solution.py:233
  19.9 3.0 %collective-permute-start.5 = (f32[16,512]{1,0:T(8,128)S(1)}, f32[16,512]{1,0:T(8,128)S(1)}, u32[]{:S(2)}, u32[]{:S(2)}) collective-permute-start(f32[16,512]{1,0:T(8,128)S(1)} %pad_maximum_fusion.own), channel_id=1, source_target_pairs={{0,1},{1,0},{2,3},{3,2},{4,5},{5,4},{6,7},{7,6},{8,9},{9,8},{10,11... | collective-permute-start | bytes 98312 | tf_op jit(solution)/shard_map/ppermute | solution.py:254
  23.0 1.1 %collective-permute-done.5.other = f32[16,512]{1,0:T(8,128)S(1)} collective-permute-done((f32[16,512]{1,0:T(8,128)S(1)}, f32[16,512]{1,0:T(8,128)S(1)}, u32[]{:S(2)}, u32[]{:S(2)}) %collective-permute-start.5) | collective-permute-done | bytes 32800 | tf_op jit(solution)/shard_map/ppermute | solution.py:254
  24.1 0.0 collective-permute-done.8.handed
  24.1 1.1 %shard_map.97 = (f32[2,16]{1,0:T(2,128)S(1)}, f32[2,16]{1,0:T(2,128)S(1)}) custom-call(s32[1]{0:T(128)} %bitcast.core_ref, s32[1]{0:T(128)} %bitcast.1.place_ref, f32[16,512]{1,0:T(8,128)S(1)} %pad_maximum_fusion.own, f32[16,512]{1,0:T(8,128)S(1)} %collective-permute-done.5.other, f32[256,256]{1,0:T(8,128)S(1)} %copy-done.2, ...), custom_call_target="tpu_custom_call" | custom-call | tf_op jit(solution)/shard_map/pallas_call | solution.py:208
  25.2 1.5 %collective-permute-start.9 = (f32[2,16]{1,0:T(2,128)S(1)}, f32[2,16]{1,0:T(2,128)S(1)}, u32[]{:S(2)}, u32[]{:S(2)}) collective-permute-start(f32[2,16]{1,0:T(2,128)S(1)} %get-tuple-element.12), channel_id=1, source_target_pairs={{0,2},{2,0},{4,6},{6,4},{8,10},{10,8},{12,14},{14,12},{1,3},{3,1},... | collective-permute-start | bytes 392 | tf_op jit(solution)/shard_map/ppermute | solution.py:233
  26.8 2.0 %collective-permute-done.9 = f32[2,16]{1,0:T(2,128)S(1)} collective-permute-done((f32[2,16]{1,0:T(2,128)S(1)}, f32[2,16]{1,0:T(2,128)S(1)}, u32[]{:S(2)}, u32[]{:S(2)}) %collective-permute-start.9) | collective-permute-done | bytes 160 | tf_op jit(solution)/shard_map/ppermute | solution.py:233
  28.8 0.6 %add.15 = f32[2,16]{1,0:T(2,128)} add(f32[2,16]{1,0:T(2,128)S(1)} %get-tuple-element.11, f32[2,16]{1,0:T(2,128)S(1)} %collective-permute-done.9) | non-fusion elementwise | flops 32 | bytes 384 | tf_op jit(solution)/shard_map/add | solution.py:266
  (21 shorter events, 0.1 us)
Async XLA Ops:
  0.0 4.8 %copy-start.3 = (bf16[1024,128]{1,0:T(8,128)(2,1)S(1)}, bf16[1024,128]{1,0:T(8,128)(2,1)}, u32[]{:S(2)}) copy-start(bf16[1024,128]{1,0:T(8,128)(2,1)} %act_basis.1) | copy-start | bytes 786436
  0.0 4.8 %copy-start = (bf16[3584,256]{1,0:T(8,128)(2,1)S(1)}, bf16[3584,256]{1,0:T(8,128)(2,1)}, u32[]{:S(2)}) copy-start(bf16[3584,256]{1,0:T(8,128)(2,1)} %out_basis.1) | copy-start | bytes 5505028
  0.0 4.8 %copy-start.4 = (bf16[1024,64]{0,1:T(8,128)(2,1)S(1)}, bf16[1024,64]{0,1:T(8,128)(2,1)}, u32[]{:S(2)}) copy-start(bf16[1024,64]{0,1:T(8,128)(2,1)} %param.10) | copy-start | bytes 393220
  0.0 4.8 %copy-start.1 = (bf16[3584,64]{0,1:T(8,128)(2,1)S(1)}, bf16[3584,64]{0,1:T(8,128)(2,1)}, u32[]{:S(2)}) copy-start(bf16[3584,64]{0,1:T(8,128)(2,1)} %param.9) | copy-start | bytes 1376260
  0.0 5.3 %collective-permute-start = (f32[256,256]{1,0:T(8,128)}, f32[256,256]{1,0:T(8,128)S(1)}, u32[]{:S(2)}, u32[]{:S(2)}) collective-permute-start(f32[256,256]{1,0:T(8,128)} %eigen.1), channel_id=1, source_target_pairs={{0,1},{1,0},{2,3},{3,2},{4,5},{5,4},{6,7},{7,6},{8,9},{9,8},{10,11... | collective-permute-start | bytes 786440 | tf_op jit(solution)/shard_map/ppermute | solution.py:241
  1.6 3.1 %collective-permute-start.1 = (bf16[1,32,768]{2,1,0:T(8,128)(2,1)S(1)}, bf16[1,32,768]{2,1,0:T(8,128)(2,1)S(1)}, u32[]{:S(2)}, u32[]{:S(2)}) collective-permute-start(bf16[1,32,768]{2,1,0:T(8,128)(2,1)S(1)} %shard_map.91.after.second), channel_id=1, source_target_pairs={{0,1},{2,3},{4,5},{6,7},{8,9},{10,11},{12,13},{14,15},{16,17},{18,... | collective-permute-start | bytes 147464 | tf_op jit(solution)/shard_map/ppermute | solution.py:243
  5.3 18.8 %copy-start.2 = (f32[256,256]{1,0:T(8,128)S(1)}, f32[256,256]{1,0:T(8,128)}, u32[]{:S(2)}) copy-start(f32[256,256]{1,0:T(8,128)} %eigen.1) | copy-start | bytes 786436
  5.3 5.2 %collective-permute-start.2 = (f32[2,16,512]{2,1,0:T(8,128)S(1)}, f32[2,16,512]{2,1,0:T(8,128)S(1)}, u32[]{:S(2)}, u32[]{:S(2)}) collective-permute-start(f32[2,16,512]{2,1,0:T(8,128)S(1)} %get-tuple-element.10), channel_id=1, source_target_pairs={{0,4},{2,6},{4,0},{6,2},{8,12},{10,14},{12,8},{14,10},{1,5},{3,7},... | collective-permute-start | bytes 196616 | tf_op jit(solution)/shard_map/ppermute | solution.py:233
  8.3 5.4 %collective-permute-start.6 = (bf16[2,32,768]{2,1,0:T(8,128)(2,1)S(1)}, bf16[2,32,768]{2,1,0:T(8,128)(2,1)S(1)}, u32[]{:S(2)}, u32[]{:S(2)}) collective-permute-start(bf16[2,32,768]{2,1,0:T(8,128)(2,1)S(1)} %shard_map.92.after.first), channel_id=1, source_target_pairs={{1,9},{3,11},{5,13},{7,15},{9,1},{11,3},{13,5},{15,7},{17,25},{19,... | collective-permute-start | bytes 294920 | tf_op jit(solution)/shard_map/ppermute | solution.py:237
  10.6 5.0 %collective-permute-start.3 = (f32[16,512]{1,0:T(8,128)S(1)}, f32[16,512]{1,0:T(8,128)S(1)}, u32[]{:S(2)}, u32[]{:S(2)}) collective-permute-start(f32[16,512]{1,0:T(8,128)S(1)} %slice_bitcast_fusion), channel_id=1, source_target_pairs={{0,8},{2,10},{4,12},{6,14},{8,0},{10,2},{12,4},{14,6},{1,9},{3,11}... | collective-permute-start | bytes 98312 | tf_op jit(solution)/shard_map/ppermute | solution.py:233
  13.7 4.3 %collective-permute-start.7 = (bf16[4,32,768]{2,1,0:T(8,128)(2,1)S(1)}, bf16[4,32,768]{2,1,0:T(8,128)(2,1)S(1)}, u32[]{:S(2)}, u32[]{:S(2)}) collective-permute-start(bf16[4,32,768]{2,1,0:T(8,128)(2,1)S(1)} %shard_map.95.first), channel_id=1, source_target_pairs={{1,5},{3,7},{5,1},{7,3},{9,13},{11,15},{13,9},{15,11},{17,21},{19,... | collective-permute-start | bytes 589832 | tf_op jit(solution)/shard_map/ppermute | solution.py:237
  15.6 4.3 %collective-permute-start.4 = (f32[16,384]{1,0:T(8,128)S(1)}, f32[16,384]{1,0:T(8,128)S(1)}, u32[]{:S(2)}, u32[]{:S(2)}) collective-permute-start(f32[16,384]{1,0:T(8,128)S(1)} %slice.19), channel_id=1, source_target_pairs={{0,2},{2,0},{4,6},{6,4},{8,10},{10,8},{12,14},{14,12},{1,3},{3,1},... | collective-permute-start | bytes 73736 | tf_op jit(solution)/shard_map/ppermute | solution.py:233
  18.1 6.0 %collective-permute-start.8 = (bf16[8,32,768]{2,1,0:T(8,128)(2,1)S(1)}, bf16[8,32,768]{2,1,0:T(8,128)(2,1)S(1)}, u32[]{:S(2)}, u32[]{:S(2)}) collective-permute-start(bf16[8,32,768]{2,1,0:T(8,128)(2,1)S(1)} %shard_map.96.blocks), channel_id=1, source_target_pairs={{1,0},{3,2},{5,4},{7,6},{9,8},{11,10},{13,12},{15,14},{17,16},{19,... | collective-permute-start | bytes 1179656 | tf_op jit(solution)/shard_map/ppermute | solution.py:249
  19.9 4.1 %collective-permute-start.5 = (f32[16,512]{1,0:T(8,128)S(1)}, f32[16,512]{1,0:T(8,128)S(1)}, u32[]{:S(2)}, u32[]{:S(2)}) collective-permute-start(f32[16,512]{1,0:T(8,128)S(1)} %pad_maximum_fusion.own), channel_id=1, source_target_pairs={{0,1},{1,0},{2,3},{3,2},{4,5},{5,4},{6,7},{7,6},{8,9},{9,8},{10,11... | collective-permute-start | bytes 98312 | tf_op jit(solution)/shard_map/ppermute | solution.py:254
  25.2 3.6 %collective-permute-start.9 = (f32[2,16]{1,0:T(2,128)S(1)}, f32[2,16]{1,0:T(2,128)S(1)}, u32[]{:S(2)}, u32[]{:S(2)}) collective-permute-start(f32[2,16]{1,0:T(2,128)S(1)} %get-tuple-element.12), channel_id=1, source_target_pairs={{0,2},{2,0},{4,6},{6,4},{8,10},{10,8},{12,14},{14,12},{1,3},{3,1},... | collective-permute-start | bytes 392 | tf_op jit(solution)/shard_map/ppermute | solution.py:233

commit v13 on v11

--- a/solution.py
+++ b/solution.py
@@ -75,6 +75,21 @@
         out_specs=spec(pltpu.VMEM),
         compiler_params=grant(4),
     )(after, first, second)
+
+
+def relay_kernel(after, source, target):
+    del after
+    target[...] = source[...]
+
+
+def relay(after, source):
+    return pl.pallas_call(
+        relay_kernel,
+        out_shape=jax.ShapeDtypeStruct(source.shape, source.dtype),
+        in_specs=[spec(pl.ANY), spec(pltpu.VMEM)],
+        out_specs=spec(pltpu.VMEM),
+        compiler_params=grant(2),
+    )(after, source)
 
 
 def project_kernel(after, query_out, query_act, out_basis, act_basis, total):
@@ -155,20 +170,21 @@
     half, ka = eigen.shape
     examples, factor_rows, width = block.shape
     ks = width - ka
-    coords = (
-        jnp.where(first, own[...], other[...]),
-        jnp.where(first, other[...], own[...]),
-    )
+    shared = half + ka // 2
+    far = shared + LANES
+    near = own[:, :shared] + other[:, far:]
+    away = other[:, :shared] + own[:, far:]
+    coords = (jnp.where(first, near, away), jnp.where(first, away, near))
     eigens = (
         jnp.where(first, eigen[...], other_eigen[...]),
         jnp.where(first, other_eigen[...], eigen[...]),
     )
     scales = [1.0 / (e + damping) for e in eigens]
-    act = jnp.concatenate([v[:, half : half + ka // 2] for v in coords], axis=1)
+    act = jnp.concatenate([v[:, half:] for v in coords], axis=1)
     act_terms = split_three(act)
     out_terms = [split_three(v[:, :half]) for v in coords]
     order = ((0, 0), (0, 1), (1, 0), (1, 1), (0, 2), (2, 0))
-    facts = jnp.concatenate([v[:examples, v.shape[1] - LANES :] for v in (own, other)], axis=0)
+    facts = jnp.concatenate([v[:examples, shared:far] for v in (own, other)], axis=0)
     rows = jnp.concatenate([block[...], other_block[...]], axis=0)
     examples = rows.shape[0]
     lane = lax.broadcasted_iota(jnp.int32, (examples, LANES), 1).astype(jnp.float32)
@@ -230,25 +246,29 @@
     def across(x, distance):
         return lax.ppermute(x, "blk", [(s, s ^ distance) for s in range(parts)])
 
+    def crossed(x):
+        pairs = [(2 * s + f, 2 * (s ^ 1) + 1 - f) for s in range(parts) for f in range(2)]
+        return lax.ppermute(x, ("blk", "fsdp"), pairs)
+
     place = lax.axis_index("blk").reshape(1)
     core = lax.axis_index("fsdp").reshape(1)
-    other_eigen = lax.ppermute(eigenvalues, "fsdp", swap)
     block = pack(train_out, train_act)
+    other_eigen = lax.ppermute(relay(block, eigenvalues), "fsdp", swap)
     total = project(block, query_out.T, query_act.T, out_basis, act_basis)
     kept, moved = spread(place, train_tokens, train_ids, other_eigen, total, lines)
-    block = join(kept, block, across(block, 4))
+    arrived = across(block, 4)
     sums = kept + across(moved, 2)
-    block = join(sums, block, across(block, 2))
+    block = join(sums, block, arrived)
+    arrived = across(block, 2)
+    sums = sums[0] + across(sums[1], 4)
+    sums = jnp.concatenate([sums, crossed(sums[:, : sums.shape[1] - LANES])], axis=1)
+    block = join(sums, block, arrived)
     other_block = lax.ppermute(block, "fsdp", swap)
-    sums = sums[0] + across(sums[1], 4)
-    shared = sums.shape[1] - LANES
-    coords = sums[:, :shared] + across(sums[:, :shared], 1)
-    own = jnp.concatenate([coords, sums[:, shared:]], axis=1)
-    other = lax.ppermute(own, "fsdp", swap)
+    other = lax.ppermute(sums, "fsdp", swap)
     mine, theirs = score(
         core,
         place,
-        own,
+        sums,
         other,
         eigenvalues,
         other_eigen,
@@ -256,7 +276,7 @@
         other_block,
         parts * 2 * train_out.shape[0],
     )
-    return mine + across(theirs, 1)
+    return mine + crossed(theirs)
 
 
 def score_block(precond, out_rows, act_rows, token_counts):

time: 25.5 us -> 27.9 us (1.094)
  waiting for transfers between devices: 5.69 us -> 13.2 us
  starting transfers between devices: 14.2 us -> 9.77 us
  local copies, waits for them, and re-layouts: 0.75 us -> 0.03 us
    ppermute x6 -> x4, starting transfers between devices: 13.6 us -> 7.28 us  [across(): return lax.ppermute(x, 'blk', [(s, s ^ distance) for s in range(parts)])]
    ppermute x6 -> x4, waiting for transfers between devices: 4.5 us -> 10.5 us  [across(): return lax.ppermute(x, 'blk', [(s, s ^ distance) for s in range(parts)])]
    ppermute x2 -> x4, starting transfers between devices: 0.52 us -> 2.42 us  [the longest x2 1.39 us: crossed(): return lax.ppermute(x, ('blk', 'fsdp'), pairs)]
    ppermute x2 -> x4, waiting for transfers between devices: 1.19 us -> 2.69 us  [the longest x2 1.68 us: crossed(): return lax.ppermute(x, ('blk', 'fsdp'), pairs)]
    unnamed x10, local copies, waits for them, and re-layouts: 0.74 us -> 0.02 us
    add x2 -> x1, other arithmetic: 0.57 us -> 0.56 us  [direct(): return mine + crossed(theirs)]
  transfers between devices with their start and end apart: 9 -> 9, of which waited for: 5 -> 6; matrix products, arithmetic and copies ran while one was open for 0% -> 0% of each run, Pallas kernels for 6% -> 2%
where the time goes in v13:
time: 27.9 us; the launch traced here: 27.6 us
  waiting for transfers between devices  13.2 us (47%)
  starting transfers between devices  9.77 us (35%)
  Pallas kernels  2.62 us (9%)
  between operations  1.43 us (5%)
  other arithmetic  0.59 us (2%)
    ppermute x4, waiting for transfers between devices, across(): return lax.ppermute(x, 'blk', [(s, s ^ distance) for s in range(parts)])  10.5 us
    ppermute x4, starting transfers between devices, across(): return lax.ppermute(x, 'blk', [(s, s ^ distance) for s in range(parts)])  7.28 us
    ppermute x2, waiting for transfers between devices, crossed(): return lax.ppermute(x, ('blk', 'fsdp'), pairs)  1.68 us
    ppermute x2, starting transfers between devices, crossed(): return lax.ppermute(x, ('blk', 'fsdp'), pairs)  1.39 us
    pallas_call x1, Pallas kernels, score(): pl.pallas_call(score_kernel, out_shape=[half, half], in_specs=[spec(pltpu...  1.15 us
    ppermute x1, waiting for transfers between devices, direct(): other = lax.ppermute(sums, 'fsdp', swap)  1.01 us
    pallas_call x1, Pallas kernels, pack(): pl.pallas_call(pack_kernel, out_shape=jax.ShapeDtypeStruct(shape, train_o...  0.93 us
    add x1, other arithmetic, direct(): return mine + crossed(theirs)  0.56 us
  transfers between devices with their start and end apart: 9, of which 6 were waited for; matrix products, arithmetic and copies ran while one was open for 0% of the time, Pallas kernels for 2%

profile of v13, /device:TPU:0, one launch (start us, length us, event | category | flops | bytes accessed | tf_op | source)
XLA Modules:
  0.0 27.6 jit_solution(13151661341660454741)
XLA Ops:
  0.0 0.9 %shard_map.91.after.first = bf16[1,32,768]{2,1,0:T(8,128)(2,1)S(1)} custom-call(bf16[1,32,512]{2,1,0:T(8,128)(2,1)} %train_out.1, bf16[1,32,256]{2,1,0:T(8,128)(2,1)} %train_act.1), custom_call_target="tpu_custom_call" | custom-call | flops 1000000000 | tf_op jit(solution)/shard_map/pallas_call | solution.py:46
  1.0 0.0 copy-done.1
  1.0 0.5 %collective-permute-start = (f32[256,256]{1,0:T(8,128)S(1)}, f32[256,256]{1,0:T(8,128)S(1)}, u32[]{:S(2)}, u32[]{:S(2)}) collective-permute-start(f32[256,256]{1,0:T(8,128)S(1)} %shard_map.92), channel_id=1, source_target_pairs={{0,1},{1,0},{2,3},{3,2},{4,5},{5,4},{6,7},{7,6},{8,9},{9,8},{10,11... | collective-permute-start | bytes 786440 | tf_op jit(solution)/shard_map/ppermute | solution.py:256
  2.8 0.0 copy-done.3
  2.9 0.5 %shard_map.93.total = f32[64,384]{1,0:T(8,128)S(1)} custom-call(bf16[1,32,768]{2,1,0:T(8,128)(2,1)S(1)} %shard_map.91.after.first, bf16[64,3584]{1,0:T(8,128)(2,1)S(1)} %bitcast.10, bf16[64,1024]{1,0:T(8,128)(2,1)S(1)} %bitcast.11, bf16[3584,256]{1,0:T(8,128)(2,1)S(1)} %copy-done, bf16[1024,128]{1,0:T(8,128)(2,1)S(1)} %copy-done.3), custom_call_target="tpu_custom_call" | custom-call | flops 134217728 | bytes 2686976 | tf_op jit(solution)/shard_map/pallas_call | solution.py:110
  3.3 0.0 collective-permute-done.after.other_eigen
  3.4 2.7 %collective-permute-start.1 = (f32[2,16,512]{2,1,0:T(8,128)S(1)}, f32[2,16,512]{2,1,0:T(8,128)S(1)}, u32[]{:S(2)}, u32[]{:S(2)}) collective-permute-start(f32[2,16,512]{2,1,0:T(8,128)S(1)} %get-tuple-element.10), channel_id=1, source_target_pairs={{0,4},{2,6},{4,0},{6,2},{8,12},{10,14},{12,8},{14,10},{1,5},{3,7},... | collective-permute-start | bytes 196616 | tf_op jit(solution)/shard_map/ppermute | solution.py:247
  6.0 2.8 %collective-permute-done.1 = f32[2,16,512]{2,1,0:T(8,128)S(1)} collective-permute-done((f32[2,16,512]{2,1,0:T(8,128)S(1)}, f32[2,16,512]{2,1,0:T(8,128)S(1)}, u32[]{:S(2)}, u32[]{:S(2)}) %collective-permute-start.1) | collective-permute-done | bytes 65568 | tf_op jit(solution)/shard_map/ppermute | solution.py:247
  8.8 2.8 %collective-permute-start.2 = (f32[16,512]{1,0:T(8,128)S(1)}, f32[16,512]{1,0:T(8,128)S(1)}, u32[]{:S(2)}, u32[]{:S(2)}) collective-permute-start(f32[16,512]{1,0:T(8,128)S(1)} %slice_bitcast_fusion), channel_id=1, source_target_pairs={{0,8},{2,10},{4,12},{6,14},{8,0},{10,2},{12,4},{14,6},{1,9},{3,11}... | collective-permute-start | bytes 98312 | tf_op jit(solution)/shard_map/ppermute | solution.py:247
  11.6 0.2 collective-permute-start.5
  11.8 2.2 %collective-permute-done.2 = f32[16,512]{1,0:T(8,128)S(1)} collective-permute-done((f32[16,512]{1,0:T(8,128)S(1)}, f32[16,512]{1,0:T(8,128)S(1)}, u32[]{:S(2)}, u32[]{:S(2)}) %collective-permute-start.2) | collective-permute-done | bytes 32800 | tf_op jit(solution)/shard_map/ppermute | solution.py:247
  14.0 0.1 collective-permute-start.3
  14.1 2.6 %collective-permute-done.5.second = bf16[1,32,768]{2,1,0:T(8,128)(2,1)S(1)} collective-permute-done((bf16[1,32,768]{2,1,0:T(8,128)(2,1)S(1)}, bf16[1,32,768]{2,1,0:T(8,128)(2,1)S(1)}, u32[]{:S(2)}, u32[]{:S(2)}) %collective-permute-start.5) | collective-permute-done | bytes 49184 | tf_op jit(solution)/shard_map/ppermute | solution.py:247
  16.6 1.6 %collective-permute-start.6 = (bf16[2,32,768]{2,1,0:T(8,128)(2,1)S(1)}, bf16[2,32,768]{2,1,0:T(8,128)(2,1)S(1)}, u32[]{:S(2)}, u32[]{:S(2)}) collective-permute-start(bf16[2,32,768]{2,1,0:T(8,128)(2,1)S(1)} %shard_map.95.first), channel_id=1, source_target_pairs={{0,4},{2,6},{4,0},{6,2},{8,12},{10,14},{12,8},{14,10},{1,5},{3,7},... | collective-permute-start | bytes 294920 | tf_op jit(solution)/shard_map/ppermute | solution.py:247
  18.3 0.0 collective-permute-done.3
  18.3 3.0 %collective-permute-done.6.second = bf16[2,32,768]{2,1,0:T(8,128)(2,1)S(1)} collective-permute-done((bf16[2,32,768]{2,1,0:T(8,128)(2,1)S(1)}, bf16[2,32,768]{2,1,0:T(8,128)(2,1)S(1)}, u32[]{:S(2)}, u32[]{:S(2)}) %collective-permute-start.6) | collective-permute-done | bytes 98336 | tf_op jit(solution)/shard_map/ppermute | solution.py:247
  21.3 0.1 collective-permute-start.7
  21.4 0.5 %collective-permute-start.4 = (f32[16,896]{1,0:T(8,128)S(1)}, f32[16,896]{1,0:T(8,128)S(1)}, u32[]{:S(2)}, u32[]{:S(2)}) collective-permute-start(f32[16,896]{1,0:T(8,128)S(1)} %pad_maximum_fusion.after.own), channel_id=1, source_target_pairs={{0,1},{1,0},{2,3},{3,2},{4,5},{5,4},{6,7},{7,6},{8,9},{9,8},{10,11... | collective-permute-start | bytes 172040 | tf_op jit(solution)/shard_map/ppermute | solution.py:267
  21.9 1.0 %collective-permute-done.4.other = f32[16,896]{1,0:T(8,128)S(1)} collective-permute-done((f32[16,896]{1,0:T(8,128)S(1)}, f32[16,896]{1,0:T(8,128)S(1)}, u32[]{:S(2)}, u32[]{:S(2)}) %collective-permute-start.4) | collective-permute-done | bytes 57376 | tf_op jit(solution)/shard_map/ppermute | solution.py:267
  22.9 0.0 collective-permute-done.7.other_block
  22.9 1.2 %shard_map.97 = (f32[2,16]{1,0:T(2,128)S(1)}, f32[2,16]{1,0:T(2,128)S(1)}) custom-call(s32[1]{0:T(128)} %bitcast.core_ref, s32[1]{0:T(128)} %bitcast.1.place_ref, f32[16,896]{1,0:T(8,128)S(1)} %pad_maximum_fusion.after.own, f32[16,896]{1,0:T(8,128)S(1)} %collective-permute-done.4.other, f32[256,256]{1,0:T(8,128)S(1)} %copy-done.1, ...), custom_call_target="tpu_custom_call" | custom-call | tf_op jit(solution)/shard_map/pallas_call | solution.py:222
  24.1 1.3 %collective-permute-start.8 = (f32[2,16]{1,0:T(2,128)S(1)}, f32[2,16]{1,0:T(2,128)S(1)}, u32[]{:S(2)}, u32[]{:S(2)}) collective-permute-start(f32[2,16]{1,0:T(2,128)S(1)} %get-tuple-element.12), channel_id=1, source_target_pairs={{0,3},{1,2},{2,1},{3,0},{4,7},{5,6},{6,5},{7,4},{8,11},{9,10},{10,... | collective-permute-start | bytes 392 | tf_op jit(solution)/shard_map/ppermute | solution.py:251
  25.4 1.7 %collective-permute-done.8 = f32[2,16]{1,0:T(2,128)S(1)} collective-permute-done((f32[2,16]{1,0:T(2,128)S(1)}, f32[2,16]{1,0:T(2,128)S(1)}, u32[]{:S(2)}, u32[]{:S(2)}) %collective-permute-start.8) | collective-permute-done | bytes 160 | tf_op jit(solution)/shard_map/ppermute | solution.py:251
  27.1 0.6 %add.11 = f32[2,16]{1,0:T(2,128)} add(f32[2,16]{1,0:T(2,128)S(1)} %get-tuple-element.11, f32[2,16]{1,0:T(2,128)S(1)} %collective-permute-done.8) | non-fusion elementwise | flops 32 | bytes 384 | tf_op jit(solution)/shard_map/add | solution.py:279
  (17 shorter events, 0.1 us)
Async XLA Ops:
  0.0 1.0 %copy-start.1 = (f32[256,256]{1,0:T(8,128)S(1)}, f32[256,256]{1,0:T(8,128)}, u32[]{:S(2)}) copy-start(f32[256,256]{1,0:T(8,128)} %eigen.1) | copy-start | bytes 786436
  0.0 2.8 %copy-start.3 = (bf16[1024,128]{1,0:T(8,128)(2,1)S(1)}, bf16[1024,128]{1,0:T(8,128)(2,1)}, u32[]{:S(2)}) copy-start(bf16[1024,128]{1,0:T(8,128)(2,1)} %act_basis.1) | copy-start | bytes 786436
  0.0 2.8 %copy-start = (bf16[3584,256]{1,0:T(8,128)(2,1)S(1)}, bf16[3584,256]{1,0:T(8,128)(2,1)}, u32[]{:S(2)}) copy-start(bf16[3584,256]{1,0:T(8,128)(2,1)} %out_basis.1) | copy-start | bytes 5505028
  0.0 2.8 %copy-start.4 = (bf16[1024,64]{0,1:T(8,128)(2,1)S(1)}, bf16[1024,64]{0,1:T(8,128)(2,1)}, u32[]{:S(2)}) copy-start(bf16[1024,64]{0,1:T(8,128)(2,1)} %param.10) | copy-start | bytes 393220
  0.0 2.8 %copy-start.2 = (bf16[3584,64]{0,1:T(8,128)(2,1)S(1)}, bf16[3584,64]{0,1:T(8,128)(2,1)}, u32[]{:S(2)}) copy-start(bf16[3584,64]{0,1:T(8,128)(2,1)} %param.9) | copy-start | bytes 1376260
  1.0 2.4 %collective-permute-start = (f32[256,256]{1,0:T(8,128)S(1)}, f32[256,256]{1,0:T(8,128)S(1)}, u32[]{:S(2)}, u32[]{:S(2)}) collective-permute-start(f32[256,256]{1,0:T(8,128)S(1)} %shard_map.92), channel_id=1, source_target_pairs={{0,1},{1,0},{2,3},{3,2},{4,5},{5,4},{6,7},{7,6},{8,9},{9,8},{10,11... | collective-permute-start | bytes 786440 | tf_op jit(solution)/shard_map/ppermute | solution.py:256
  3.4 5.4 %collective-permute-start.1 = (f32[2,16,512]{2,1,0:T(8,128)S(1)}, f32[2,16,512]{2,1,0:T(8,128)S(1)}, u32[]{:S(2)}, u32[]{:S(2)}) collective-permute-start(f32[2,16,512]{2,1,0:T(8,128)S(1)} %get-tuple-element.10), channel_id=1, source_target_pairs={{0,4},{2,6},{4,0},{6,2},{8,12},{10,14},{12,8},{14,10},{1,5},{3,7},... | collective-permute-start | bytes 196616 | tf_op jit(solution)/shard_map/ppermute | solution.py:247
  8.8 5.2 %collective-permute-start.2 = (f32[16,512]{1,0:T(8,128)S(1)}, f32[16,512]{1,0:T(8,128)S(1)}, u32[]{:S(2)}, u32[]{:S(2)}) collective-permute-start(f32[16,512]{1,0:T(8,128)S(1)} %slice_bitcast_fusion), channel_id=1, source_target_pairs={{0,8},{2,10},{4,12},{6,14},{8,0},{10,2},{12,4},{14,6},{1,9},{3,11}... | collective-permute-start | bytes 98312 | tf_op jit(solution)/shard_map/ppermute | solution.py:247
  11.6 5.0 %collective-permute-start.5 = (bf16[1,32,768]{2,1,0:T(8,128)(2,1)S(1)}, bf16[1,32,768]{2,1,0:T(8,128)(2,1)S(1)}, u32[]{:S(2)}, u32[]{:S(2)}) collective-permute-start(bf16[1,32,768]{2,1,0:T(8,128)(2,1)S(1)} %shard_map.91.after.first), channel_id=1, source_target_pairs={{0,8},{2,10},{4,12},{6,14},{8,0},{10,2},{12,4},{14,6},{1,9},{3,11}... | collective-permute-start | bytes 147464 | tf_op jit(solution)/shard_map/ppermute | solution.py:247
  14.0 4.3 %collective-permute-start.3 = (f32[16,384]{1,0:T(8,128)S(1)}, f32[16,384]{1,0:T(8,128)S(1)}, u32[]{:S(2)}, u32[]{:S(2)}) collective-permute-start(f32[16,384]{1,0:T(8,128)S(1)} %slice.14), channel_id=1, source_target_pairs={{0,3},{1,2},{2,1},{3,0},{4,7},{5,6},{6,5},{7,4},{8,11},{9,10},{10,... | collective-permute-start | bytes 73736 | tf_op jit(solution)/shard_map/ppermute | solution.py:251
  16.6 4.7 %collective-permute-start.6 = (bf16[2,32,768]{2,1,0:T(8,128)(2,1)S(1)}, bf16[2,32,768]{2,1,0:T(8,128)(2,1)S(1)}, u32[]{:S(2)}, u32[]{:S(2)}) collective-permute-start(bf16[2,32,768]{2,1,0:T(8,128)(2,1)S(1)} %shard_map.95.first), channel_id=1, source_target_pairs={{0,4},{2,6},{4,0},{6,2},{8,12},{10,14},{12,8},{14,10},{1,5},{3,7},... | collective-permute-start | bytes 294920 | tf_op jit(solution)/shard_map/ppermute | solution.py:247
  21.3 1.6 %collective-permute-start.7 = (bf16[4,32,768]{2,1,0:T(8,128)(2,1)S(1)}, bf16[4,32,768]{2,1,0:T(8,128)(2,1)S(1)}, u32[]{:S(2)}, u32[]{:S(2)}) collective-permute-start(bf16[4,32,768]{2,1,0:T(8,128)(2,1)S(1)} %shard_map.96.block), channel_id=1, source_target_pairs={{0,1},{1,0},{2,3},{3,2},{4,5},{5,4},{6,7},{7,6},{8,9},{9,8},{10,11... | collective-permute-start | bytes 589832 | tf_op jit(solution)/shard_map/ppermute | solution.py:266
  21.4 1.5 %collective-permute-start.4 = (f32[16,896]{1,0:T(8,128)S(1)}, f32[16,896]{1,0:T(8,128)S(1)}, u32[]{:S(2)}, u32[]{:S(2)}) collective-permute-start(f32[16,896]{1,0:T(8,128)S(1)} %pad_maximum_fusion.after.own), channel_id=1, source_target_pairs={{0,1},{1,0},{2,3},{3,2},{4,5},{5,4},{6,7},{7,6},{8,9},{9,8},{10,11... | collective-permute-start | bytes 172040 | tf_op jit(solution)/shard_map/ppermute | solution.py:267
  24.1 3.0 %collective-permute-start.8 = (f32[2,16]{1,0:T(2,128)S(1)}, f32[2,16]{1,0:T(2,128)S(1)}, u32[]{:S(2)}, u32[]{:S(2)}) collective-permute-start(f32[2,16]{1,0:T(2,128)S(1)} %get-tuple-element.12), channel_id=1, source_target_pairs={{0,3},{1,2},{2,1},{3,0},{4,7},{5,6},{6,5},{7,4},{8,11},{9,10},{10,... | collective-permute-start | bytes 392 | tf_op jit(solution)/shard_map/ppermute | solution.py:251

commit v14 on v10

--- a/solution.py
+++ b/solution.py
@@ -150,36 +150,37 @@
 
 
 def score_kernel(core_ref, own, other, eigen, other_eigen, *rest):
-    out = rest[-1]
-    pairs = (rest[: len(rest) // 2], rest[len(rest) // 2 : -1])
+    blocks, out = rest[:-1], rest[-1]
     first = core_ref[0] == 0
     half, ka = eigen.shape
-    examples = sum(x.shape[0] for x in pairs[0])
-    _, factor_rows, width = pairs[0][0].shape
+    factor_rows, width = blocks[0].shape[1:]
     ks = width - ka
-    coords = (
-        jnp.where(first, own[...], other[...]),
-        jnp.where(first, other[...], own[...]),
-    )
+    shared = own.shape[1] - LANES
+    mine, theirs = own[...], other[...]
+    coords = (jnp.where(first, mine, theirs), jnp.where(first, theirs, mine))
     eigens = (
         jnp.where(first, eigen[...], other_eigen[...]),
         jnp.where(first, other_eigen[...], eigen[...]),
     )
     scales = [1.0 / (e + damping) for e in eigens]
-    act = jnp.concatenate([v[:, half : half + ka // 2] for v in coords], axis=1)
+    act = jnp.concatenate([v[:, half:shared] for v in coords], axis=1)
     act_terms = split_three(act)
     out_terms = [split_three(v[:, :half]) for v in coords]
     order = ((0, 0), (0, 1), (1, 0), (1, 1), (0, 2), (2, 0))
-    weights, hot, flat = [], [], []
+    slot = lax.broadcasted_iota(jnp.int32, (mine.shape[0], LANES), 0)
+    even = (slot // 4 + slot // 2 + slot) % 2 == 0
+    facts = (mine[:, shared:], theirs[:, shared:])
+    facts = jnp.concatenate(
+        [jnp.where(even, facts[0], facts[1]), jnp.where(even, facts[1], facts[0])], axis=0
+    )
+    rows = jnp.concatenate([x[...] for x in blocks], axis=0)
+    examples = rows.shape[0]
     lane = lax.broadcasted_iota(jnp.int32, (examples, LANES), 1).astype(jnp.float32)
     row = lax.broadcasted_iota(jnp.int32, (examples, factor_rows, ka), 1).astype(jnp.float32)
-    for facts, blocks in zip((own, other), pairs):
-        rows = jnp.concatenate([x[...] for x in blocks], axis=0)
-        facts = facts[:, facts.shape[1] - LANES :]
-        hot.append(lane == facts[:, :1])
-        keep = row < facts[:, LANES // 2 : LANES // 2 + 1][:, :, None]
-        weights.append(jnp.where(keep, rows[:, :, ks:].astype(jnp.float32), 0.0))
-        flat.append(rows[:, :, :ks].reshape(examples * factor_rows, ks))
+    hot = lane == facts[:, :1]
+    keep = row < facts[:, LANES // 2 : LANES // 2 + 1][:, :, None]
+    weights = jnp.where(keep, rows[:, :, ks:].astype(jnp.float32), 0.0)
+    flat = rows[:, :, :ks].reshape(examples * factor_rows, ks)
     for q in range(out.shape[0]):
         cut = slice(q * RQ, (q + 1) * RQ)
         right = jnp.concatenate([act_terms[b][cut] for _, b in order], axis=0)
@@ -191,24 +192,22 @@
             )
             precond.append((numer * scales[part]).astype(jnp.bfloat16))
         precond = jnp.concatenate(precond, axis=0)
-        scores = 0.0
-        for side in range(2):
-            projected = jnp.dot(flat[side], precond, preferred_element_type=jnp.float32)
-            terms = projected.reshape(examples, factor_rows, ka) * weights[side]
-            per_example = jnp.sum(jnp.sum(terms, axis=1), axis=1, keepdims=True)
-            scores += jnp.sum(jnp.where(hot[side], per_example, 0.0), axis=0, keepdims=True)
+        projected = jnp.dot(flat, precond, preferred_element_type=jnp.float32)
+        terms = projected.reshape(examples, factor_rows, ka) * weights
+        per_example = jnp.sum(jnp.sum(terms, axis=1), axis=1, keepdims=True)
+        scores = jnp.sum(jnp.where(hot, per_example, 0.0), axis=0, keepdims=True)
         out[q : q + 1, :] = scores[:, : out.shape[1]]
 
 
-def score(core, own, other, eigen, other_eigen, blocks, other_blocks):
-    examples = sum(x.shape[0] for x in blocks + other_blocks)
+def score(core, own, other, eigen, other_eigen, blocks):
+    examples = sum(x.shape[0] for x in blocks)
     return pl.pallas_call(
         score_kernel,
         out_shape=jax.ShapeDtypeStruct((own.shape[0] // RQ, examples), jnp.float32),
-        in_specs=[spec(pltpu.SMEM)] + [spec(pltpu.VMEM)] * (4 + len(blocks + other_blocks)),
+        in_specs=[spec(pltpu.SMEM)] + [spec(pltpu.VMEM)] * (4 + len(blocks)),
         out_specs=spec(pltpu.VMEM),
         compiler_params=grant(12),
-    )(core, own, other, eigen, other_eigen, *blocks, *other_blocks)
+    )(core, own, other, eigen, other_eigen, *blocks)
 
 
 def direct(
@@ -229,27 +228,33 @@
     def across(x, i):
         return lax.ppermute(x, "blk", [(s, s ^ (1 << i)) for s in range(parts)])
 
+    def crossed(x, i):
+        pairs = [
+            (2 * s + f, 2 * (s ^ (1 << i)) + 1 - f) for s in range(parts) for f in range(2)
+        ]
+        return lax.ppermute(x, ("blk", "fsdp"), pairs)
+
     place = lax.axis_index("blk").reshape(1)
     core = lax.axis_index("fsdp").reshape(1)
     other_eigen = lax.ppermute(eigenvalues, "fsdp", swap)
     block = pack(train_out, train_act)
-    arrived = across(block, steps - 1)
+    arrived = crossed(block, 2)
     total = project(query_out.T, query_act.T, out_basis, act_basis)
     kept, moved, block = spread(
         place, train_tokens, train_ids, other_eigen, total, block, arrived, parts
     )
     sums = (kept + across(moved, 0)).reshape((2, 2) + kept.shape[1:])
-    arrived = across(block, 1)
+    arrived = crossed(block, 1)
     kept, moved = sums[:, 0], sums[:, 1]
     near = join(kept, block, arrived)
-    far = across(near, 0)
+    far = crossed(near, 0)
     other_near = lax.ppermute(near, "fsdp", swap)
     other_far = lax.ppermute(far, "fsdp", swap)
     sums = kept + across(moved, 1)
     own = sums[0] + across(sums[1], 2)
     other = lax.ppermute(own, "fsdp", swap)
     return score(
-        core, own, other, eigenvalues, other_eigen, (near, far), (other_near, other_far)
+        core, own, other, eigenvalues, other_eigen, (near, far, other_near, other_far)
     )
 
 

time: 24.2 us -> 24.1 us (level)
  starting transfers between devices: 11.6 us -> 13.4 us
  waiting for transfers between devices: 7.8 us -> 6.04 us
    ppermute x0 -> x3, starting transfers between devices: none -> 5.3 us  [crossed(): return lax.ppermute(x, ('blk', 'fsdp'), pairs)]
    ppermute x6 -> x3, starting transfers between devices: 11 us -> 7 us  [across(): return lax.ppermute(x, 'blk', [(s, s ^ 1 << i) for s in range(parts)])]
    ppermute x6 -> x3, waiting for transfers between devices: 6.62 us -> 3.03 us  [across(): return lax.ppermute(x, 'blk', [(s, s ^ 1 << i) for s in range(parts)])]
    ppermute x0 -> x3, waiting for transfers between devices: none -> 2.12 us  [crossed(): return lax.ppermute(x, ('blk', 'fsdp'), pairs)]
    ppermute x1, starting transfers between devices: 0.01 us -> 0.46 us  [direct(): other = lax.ppermute(own, 'fsdp', swap)]
    ppermute x1, waiting for transfers between devices: 1.17 us -> 0.89 us  [direct(): other = lax.ppermute(own, 'fsdp', swap)]
  transfers between devices with their start and end apart: 10 -> 10, of which waited for: 7 -> 5; matrix products, arithmetic and copies ran while one was open for 0% -> 0% of each run, Pallas kernels for 6% -> 6%
where the time goes in v14:
time: 24.1 us; the launch traced here: 23.8 us
  starting transfers between devices  13.4 us (56%)
  waiting for transfers between devices  6.04 us (25%)
  Pallas kernels  2.88 us (12%)
  between operations  1.39 us (6%)
    ppermute x3, starting transfers between devices, across(): return lax.ppermute(x, 'blk', [(s, s ^ 1 << i) for s in range(parts)])  7 us
    ppermute x3, starting transfers between devices, crossed(): return lax.ppermute(x, ('blk', 'fsdp'), pairs)  5.3 us
    ppermute x3, waiting for transfers between devices, across(): return lax.ppermute(x, 'blk', [(s, s ^ 1 << i) for s in range(parts)])  3.03 us
    ppermute x3, waiting for transfers between devices, crossed(): return lax.ppermute(x, ('blk', 'fsdp'), pairs)  2.12 us
    pallas_call x1, Pallas kernels, score(): pl.pallas_call(score_kernel, out_shape=jax.ShapeDtypeStruct((own.shape[0]...  1.34 us
    pallas_call x1, Pallas kernels, pack(): pl.pallas_call(pack_kernel, out_shape=jax.ShapeDtypeStruct(shape, train_o...  1.04 us
    ppermute x1, waiting for transfers between devices, direct(): other = lax.ppermute(own, 'fsdp', swap)  0.89 us
    ppermute x1, starting transfers between devices, direct(): other_eigen = lax.ppermute(eigenvalues, 'fsdp', swap)  0.53 us
  transfers between devices with their start and end apart: 10, of which 5 were waited for; matrix products, arithmetic and copies ran while one was open for 0% of the time, Pallas kernels for 6%

profile of v14, /device:TPU:0, one launch (start us, length us, event | category | flops | bytes accessed | tf_op | source)
XLA Modules:
  0.0 23.8 jit_solution(4302907264026848844)
XLA Ops:
  0.0 0.5 %collective-permute-start = (f32[256,256]{1,0:T(8,128)}, f32[256,256]{1,0:T(8,128)S(1)}, u32[]{:S(2)}, u32[]{:S(2)}) collective-permute-start(f32[256,256]{1,0:T(8,128)} %eigen.1), channel_id=1, source_target_pairs={{0,1},{1,0},{2,3},{3,2},{4,5},{5,4},{6,7},{7,6},{8,9},{9,8},{10,11... | collective-permute-start | bytes 786440 | tf_op jit(solution)/shard_map/ppermute | solution.py:239
  0.5 1.0 %shard_map.92.first = bf16[1,32,768]{2,1,0:T(8,128)(2,1)S(1)} custom-call(bf16[1,32,512]{2,1,0:T(8,128)(2,1)} %train_out.1, bf16[1,32,256]{2,1,0:T(8,128)(2,1)} %train_act.1), custom_call_target="tpu_custom_call" | custom-call | flops 1000000000 | tf_op jit(solution)/shard_map/pallas_call | solution.py:46
  1.6 3.6 %collective-permute-start.1 = (bf16[1,32,768]{2,1,0:T(8,128)(2,1)S(1)}, bf16[1,32,768]{2,1,0:T(8,128)(2,1)S(1)}, u32[]{:S(2)}, u32[]{:S(2)}) collective-permute-start(bf16[1,32,768]{2,1,0:T(8,128)(2,1)S(1)} %shard_map.92.first), channel_id=1, source_target_pairs={{0,9},{1,8},{2,11},{3,10},{4,13},{5,12},{6,15},{7,14},{8,1},{9,0},... | collective-permute-start | bytes 147464 | tf_op jit(solution)/shard_map/ppermute | solution.py:235
  6.5 0.0 copy-start.2
  6.5 0.5 %shard_map.91.total = f32[64,384]{1,0:T(8,128)S(1)} custom-call(bf16[64,3584]{1,0:T(8,128)(2,1)S(1)} %bitcast.21, bf16[64,1024]{1,0:T(8,128)(2,1)S(1)} %bitcast.22, bf16[3584,256]{1,0:T(8,128)(2,1)S(1)} %copy-done, bf16[1024,128]{1,0:T(8,128)(2,1)S(1)} %copy-done.3), custom_call_target="tpu_custom_call" | custom-call | flops 134217728 | bytes 2686976 | tf_op jit(solution)/shard_map/pallas_call | solution.py:94
  7.0 0.2 collective-permute-done.1.second
  7.1 0.0 collective-permute-done.after.other_eigen
  7.2 1.4 %collective-permute-start.2 = (f32[4,8,512]{2,1,0:T(8,128)S(1)}, f32[4,8,512]{2,1,0:T(8,128)S(1)}, u32[]{:S(2)}, u32[]{:S(2)}) collective-permute-start(f32[4,8,512]{2,1,0:T(8,128)S(1)} %get-tuple-element.9), channel_id=1, source_target_pairs={{0,2},{2,0},{4,6},{6,4},{8,10},{10,8},{12,14},{14,12},{1,3},{3,1},... | collective-permute-start | bytes 196616 | tf_op jit(solution)/shard_map/ppermute | solution.py:229
  8.6 1.6 %collective-permute-start.6 = (bf16[2,32,768]{2,1,0:T(8,128)(2,1)S(1)}, bf16[2,32,768]{2,1,0:T(8,128)(2,1)S(1)}, u32[]{:S(2)}, u32[]{:S(2)}) collective-permute-start(bf16[2,32,768]{2,1,0:T(8,128)(2,1)S(1)} %get-tuple-element.10.first), channel_id=1, source_target_pairs={{0,5},{1,4},{2,7},{3,6},{4,1},{5,0},{6,3},{7,2},{8,13},{9,12},{10,... | collective-permute-start | bytes 294920 | tf_op jit(solution)/shard_map/ppermute | solution.py:235
  10.2 1.3 %collective-permute-done.2 = f32[4,8,512]{2,1,0:T(8,128)S(1)} collective-permute-done((f32[4,8,512]{2,1,0:T(8,128)S(1)}, f32[4,8,512]{2,1,0:T(8,128)S(1)}, u32[]{:S(2)}, u32[]{:S(2)}) %collective-permute-start.2) | collective-permute-done | bytes 65568 | tf_op jit(solution)/shard_map/ppermute | solution.py:229
  11.5 2.2 %collective-permute-start.3 = (f32[2,8,512]{2,1,0:T(8,128)S(1)}, f32[2,8,512]{2,1,0:T(8,128)S(1)}, u32[]{:S(2)}, u32[]{:S(2)}) collective-permute-start(f32[2,8,512]{2,1,0:T(8,128)S(1)} %get-tuple-element.12), channel_id=1, source_target_pairs={{0,4},{2,6},{4,0},{6,2},{8,12},{10,14},{12,8},{14,10},{1,5},{3,7},... | collective-permute-start | bytes 98312 | tf_op jit(solution)/shard_map/ppermute | solution.py:229
  13.7 0.0 collective-permute-done.6.second
  13.7 0.1 collective-permute-start.7
  13.9 1.8 %collective-permute-done.3 = f32[2,8,512]{2,1,0:T(8,128)S(1)} collective-permute-done((f32[2,8,512]{2,1,0:T(8,128)S(1)}, f32[2,8,512]{2,1,0:T(8,128)S(1)}, u32[]{:S(2)}, u32[]{:S(2)}) %collective-permute-start.3) | collective-permute-done | bytes 32800 | tf_op jit(solution)/shard_map/ppermute | solution.py:229
  15.6 3.4 %collective-permute-start.4 = (f32[8,512]{1,0:T(8,128)S(1)}, f32[8,512]{1,0:T(8,128)S(1)}, u32[]{:S(2)}, u32[]{:S(2)}) collective-permute-start(f32[8,512]{1,0:T(8,128)S(1)} %slice_bitcast_fusion.2), channel_id=1, source_target_pairs={{0,8},{2,10},{4,12},{6,14},{8,0},{10,2},{12,4},{14,6},{1,9},{3,11}... | collective-permute-start | bytes 49160 | tf_op jit(solution)/shard_map/ppermute | solution.py:229
  19.0 0.0 collective-permute-start.8
  19.0 1.9 %collective-permute-done.7.rest_1_ = bf16[4,32,768]{2,1,0:T(8,128)(2,1)S(1)} collective-permute-done((bf16[4,32,768]{2,1,0:T(8,128)(2,1)S(1)}, bf16[4,32,768]{2,1,0:T(8,128)(2,1)S(1)}, u32[]{:S(2)}, u32[]{:S(2)}) %collective-permute-start.7) | collective-permute-done | bytes 196640 | tf_op jit(solution)/shard_map/ppermute | solution.py:235
  21.0 0.1 collective-permute-start.9
  21.1 0.0 collective-permute-done.4
  21.1 0.5 %collective-permute-start.5 = (f32[8,512]{1,0:T(8,128)S(1)}, f32[8,512]{1,0:T(8,128)S(1)}, u32[]{:S(2)}, u32[]{:S(2)}) collective-permute-start(f32[8,512]{1,0:T(8,128)S(1)} %fusion.own), channel_id=1, source_target_pairs={{0,1},{1,0},{2,3},{3,2},{4,5},{5,4},{6,7},{7,6},{8,9},{9,8},{10,11... | collective-permute-start | bytes 49160 | tf_op jit(solution)/shard_map/ppermute | solution.py:255
  21.5 0.9 %collective-permute-done.5.other = f32[8,512]{1,0:T(8,128)S(1)} collective-permute-done((f32[8,512]{1,0:T(8,128)S(1)}, f32[8,512]{1,0:T(8,128)S(1)}, u32[]{:S(2)}, u32[]{:S(2)}) %collective-permute-start.5) | collective-permute-done | bytes 16416 | tf_op jit(solution)/shard_map/ppermute | solution.py:255
  22.4 0.0 collective-permute-done.8.rest_2_
  22.4 0.0 collective-permute-done.9.rest_3_
  22.4 1.3 %shard_map.95 = f32[2,16]{1,0:T(2,128)} custom-call(s32[1]{0:T(128)} %bitcast.core_ref, f32[8,512]{1,0:T(8,128)S(1)} %fusion.own, f32[8,512]{1,0:T(8,128)S(1)} %collective-permute-done.5.other, f32[256,256]{1,0:T(8,128)S(1)} %copy-done.2, f32[256,256]{1,0:T(8,128)S(1)} %collective-permute-done.after.other_eigen, bf16[4,32,768]{2,1,0:T(8,128)(2,1)S(1)} %shard_map.94.rest_0_, ...), custom_call_target="tpu_custom_call" | custom-call | tf_op jit(solution)/shard_map/pallas_call | solution.py:204
  (16 shorter events, 0.1 us)
Async XLA Ops:
  0.0 6.4 %copy-start.3 = (bf16[1024,128]{1,0:T(8,128)(2,1)S(1)}, bf16[1024,128]{1,0:T(8,128)(2,1)}, u32[]{:S(2)}) copy-start(bf16[1024,128]{1,0:T(8,128)(2,1)} %act_basis.1) | copy-start | bytes 786436
  0.0 6.4 %copy-start = (bf16[3584,256]{1,0:T(8,128)(2,1)S(1)}, bf16[3584,256]{1,0:T(8,128)(2,1)}, u32[]{:S(2)}) copy-start(bf16[3584,256]{1,0:T(8,128)(2,1)} %out_basis.1) | copy-start | bytes 5505028
  0.0 6.4 %copy-start.4 = (bf16[1024,64]{0,1:T(8,128)(2,1)S(1)}, bf16[1024,64]{0,1:T(8,128)(2,1)}, u32[]{:S(2)}) copy-start(bf16[1024,64]{0,1:T(8,128)(2,1)} %param.10) | copy-start | bytes 393220
  0.0 6.5 %copy-start.1 = (bf16[3584,64]{0,1:T(8,128)(2,1)S(1)}, bf16[3584,64]{0,1:T(8,128)(2,1)}, u32[]{:S(2)}) copy-start(bf16[3584,64]{0,1:T(8,128)(2,1)} %param.9) | copy-start | bytes 1376260
  0.0 7.1 %collective-permute-start = (f32[256,256]{1,0:T(8,128)}, f32[256,256]{1,0:T(8,128)S(1)}, u32[]{:S(2)}, u32[]{:S(2)}) collective-permute-start(f32[256,256]{1,0:T(8,128)} %eigen.1), channel_id=1, source_target_pairs={{0,1},{1,0},{2,3},{3,2},{4,5},{5,4},{6,7},{7,6},{8,9},{9,8},{10,11... | collective-permute-start | bytes 786440 | tf_op jit(solution)/shard_map/ppermute | solution.py:239
  1.6 5.6 %collective-permute-start.1 = (bf16[1,32,768]{2,1,0:T(8,128)(2,1)S(1)}, bf16[1,32,768]{2,1,0:T(8,128)(2,1)S(1)}, u32[]{:S(2)}, u32[]{:S(2)}) collective-permute-start(bf16[1,32,768]{2,1,0:T(8,128)(2,1)S(1)} %shard_map.92.first), channel_id=1, source_target_pairs={{0,9},{1,8},{2,11},{3,10},{4,13},{5,12},{6,15},{7,14},{8,1},{9,0},... | collective-permute-start | bytes 147464 | tf_op jit(solution)/shard_map/ppermute | solution.py:235
  6.5 16.0 %copy-start.2 = (f32[256,256]{1,0:T(8,128)S(1)}, f32[256,256]{1,0:T(8,128)}, u32[]{:S(2)}) copy-start(f32[256,256]{1,0:T(8,128)} %eigen.1) | copy-start | bytes 786436
  7.2 4.3 %collective-permute-start.2 = (f32[4,8,512]{2,1,0:T(8,128)S(1)}, f32[4,8,512]{2,1,0:T(8,128)S(1)}, u32[]{:S(2)}, u32[]{:S(2)}) collective-permute-start(f32[4,8,512]{2,1,0:T(8,128)S(1)} %get-tuple-element.9), channel_id=1, source_target_pairs={{0,2},{2,0},{4,6},{6,4},{8,10},{10,8},{12,14},{14,12},{1,3},{3,1},... | collective-permute-start | bytes 196616 | tf_op jit(solution)/shard_map/ppermute | solution.py:229
  8.6 5.1 %collective-permute-start.6 = (bf16[2,32,768]{2,1,0:T(8,128)(2,1)S(1)}, bf16[2,32,768]{2,1,0:T(8,128)(2,1)S(1)}, u32[]{:S(2)}, u32[]{:S(2)}) collective-permute-start(bf16[2,32,768]{2,1,0:T(8,128)(2,1)S(1)} %get-tuple-element.10.first), channel_id=1, source_target_pairs={{0,5},{1,4},{2,7},{3,6},{4,1},{5,0},{6,3},{7,2},{8,13},{9,12},{10,... | collective-permute-start | bytes 294920 | tf_op jit(solution)/shard_map/ppermute | solution.py:235
  11.5 4.1 %collective-permute-start.3 = (f32[2,8,512]{2,1,0:T(8,128)S(1)}, f32[2,8,512]{2,1,0:T(8,128)S(1)}, u32[]{:S(2)}, u32[]{:S(2)}) collective-permute-start(f32[2,8,512]{2,1,0:T(8,128)S(1)} %get-tuple-element.12), channel_id=1, source_target_pairs={{0,4},{2,6},{4,0},{6,2},{8,12},{10,14},{12,8},{14,10},{1,5},{3,7},... | collective-permute-start | bytes 98312 | tf_op jit(solution)/shard_map/ppermute | solution.py:229
  13.7 7.2 %collective-permute-start.7 = (bf16[4,32,768]{2,1,0:T(8,128)(2,1)S(1)}, bf16[4,32,768]{2,1,0:T(8,128)(2,1)S(1)}, u32[]{:S(2)}, u32[]{:S(2)}) collective-permute-start(bf16[4,32,768]{2,1,0:T(8,128)(2,1)S(1)} %shard_map.94.rest_0_), channel_id=1, source_target_pairs={{0,3},{1,2},{2,1},{3,0},{4,7},{5,6},{6,5},{7,4},{8,11},{9,10},{10,... | collective-permute-start | bytes 589832 | tf_op jit(solution)/shard_map/ppermute | solution.py:235
  15.6 5.5 %collective-permute-start.4 = (f32[8,512]{1,0:T(8,128)S(1)}, f32[8,512]{1,0:T(8,128)S(1)}, u32[]{:S(2)}, u32[]{:S(2)}) collective-permute-start(f32[8,512]{1,0:T(8,128)S(1)} %slice_bitcast_fusion.2), channel_id=1, source_target_pairs={{0,8},{2,10},{4,12},{6,14},{8,0},{10,2},{12,4},{14,6},{1,9},{3,11}... | collective-permute-start | bytes 49160 | tf_op jit(solution)/shard_map/ppermute | solution.py:229
  19.0 3.4 %collective-permute-start.8 = (bf16[4,32,768]{2,1,0:T(8,128)(2,1)S(1)}, bf16[4,32,768]{2,1,0:T(8,128)(2,1)S(1)}, u32[]{:S(2)}, u32[]{:S(2)}) collective-permute-start(bf16[4,32,768]{2,1,0:T(8,128)(2,1)S(1)} %shard_map.94.rest_0_), channel_id=1, source_target_pairs={{0,1},{1,0},{2,3},{3,2},{4,5},{5,4},{6,7},{7,6},{8,9},{9,8},{10,11... | collective-permute-start | bytes 589832 | tf_op jit(solution)/shard_map/ppermute | solution.py:251
  21.0 1.5 %collective-permute-start.9 = (bf16[4,32,768]{2,1,0:T(8,128)(2,1)S(1)}, bf16[4,32,768]{2,1,0:T(8,128)(2,1)S(1)}, u32[]{:S(2)}, u32[]{:S(2)}) collective-permute-start(bf16[4,32,768]{2,1,0:T(8,128)(2,1)S(1)} %collective-permute-done.7.rest_1_), channel_id=1, source_target_pairs={{0,1},{1,0},{2,3},{3,2},{4,5},{5,4},{6,7},{7,6},{8,9},{9,8},{10,11... | collective-permute-start | bytes 589832 | tf_op jit(solution)/shard_map/ppermute | solution.py:252
  21.1 1.3 %collective-permute-start.5 = (f32[8,512]{1,0:T(8,128)S(1)}, f32[8,512]{1,0:T(8,128)S(1)}, u32[]{:S(2)}, u32[]{:S(2)}) collective-permute-start(f32[8,512]{1,0:T(8,128)S(1)} %fusion.own), channel_id=1, source_target_pairs={{0,1},{1,0},{2,3},{3,2},{4,5},{5,4},{6,7},{7,6},{8,9},{9,8},{10,11... | collective-permute-start | bytes 49160 | tf_op jit(solution)/shard_map/ppermute | solution.py:255

commit v15 on v14

--- a/solution.py
+++ b/solution.py
@@ -50,7 +50,6 @@
         out_specs=spec(pltpu.VMEM),
         scratch_shapes=[pltpu.SemaphoreType.DMA((2,))],
         compiler_params=grant(2),
-        cost_estimate=pl.CostEstimate(flops=WAIT_FLOPS, bytes_accessed=0, transcendentals=0),
     )(pinned(train_out), pinned(train_act))
 
 
@@ -75,6 +74,39 @@
         out_specs=spec(pltpu.VMEM),
         compiler_params=grant(4),
     )(after, first, second)
+
+
+def relay_kernel(source, target):
+    target[...] = source[...]
+
+
+def relay(source):
+    return pl.pallas_call(
+        relay_kernel,
+        out_shape=jax.ShapeDtypeStruct(source.shape, source.dtype),
+        in_specs=[spec(pltpu.VMEM)],
+        out_specs=spec(pltpu.VMEM),
+        compiler_params=grant(2),
+        cost_estimate=pl.CostEstimate(flops=WAIT_FLOPS, bytes_accessed=0, transcendentals=0),
+    )(source)
+
+
+def gather_sum_kernel(after, *refs):
+    del after
+    total = refs[0][...]
+    for term in refs[1:-1]:
+        total = total + term[...]
+    refs[-1][...] = total
+
+
+def gather_sum(after, terms):
+    return pl.pallas_call(
+        gather_sum_kernel,
+        out_shape=jax.ShapeDtypeStruct(terms[0].shape, terms[0].dtype),
+        in_specs=[spec(pl.ANY)] + [spec(pltpu.VMEM)] * len(terms),
+        out_specs=spec(pltpu.VMEM),
+        compiler_params=grant(4),
+    )(after, *terms)
 
 
 def project_kernel(query_out, query_act, out_basis, act_basis, total):
@@ -110,33 +142,36 @@
     return sum(1 << (bits - 1 - i) for i in range(bits) if distance >> i & 1)
 
 
-def spread_kernel(
-    place_ref, tokens_ref, ids_ref, after, total, first, second, kept, moved, joined
-):
+def spread_kernel(place_ref, tokens_ref, ids_ref, after, total, first, second, *rest):
     del after
-    parts = 2 * kept.shape[0]
-    local_rows = kept.shape[1]
+    pieces, joined = rest[:-1], rest[-1]
+    groups = len(pieces)
+    each, local_rows, _ = pieces[0].shape
+    parts = groups * each
     width = total.shape[1]
     row = lax.broadcasted_iota(jnp.int32, (local_rows, LANES), 0)
     lane = lax.broadcasted_iota(jnp.int32, (local_rows, LANES), 1)
     facts = jnp.where(lane < LANES // 2, ids_ref[0], tokens_ref[0]).astype(jnp.float32)
     for part in range(parts):
         start = pl.multiple_of((place_ref[0] ^ part) * local_rows, local_rows)
-        piece = (moved if part % 2 else kept).at[part // 2]
+        piece = pieces[part % groups].at[part // groups]
         piece[:, :width] = total[pl.ds(start, local_rows), :]
         piece[:, width:] = jnp.where(row == doubling_slot(part, parts), facts, 0.0)
     join_kernel(None, first, second, joined)
 
 
-def spread(place, tokens, ids, after, total, first, second, parts):
-    half = jax.ShapeDtypeStruct(
-        (parts // 2, total.shape[0] // parts, total.shape[1] + LANES), jnp.float32
+def spread(place, tokens, ids, after, total, first, second, parts, groups):
+    piece = jax.ShapeDtypeStruct(
+        (parts // groups, total.shape[0] // parts, total.shape[1] + LANES), jnp.float32
+    )
+    joined = jax.ShapeDtypeStruct(
+        (first.shape[0] + second.shape[0],) + first.shape[1:], first.dtype
     )
     return pl.pallas_call(
         spread_kernel,
-        out_shape=[half, half, joined_shape(first, second)],
+        out_shape=[piece] * groups + [joined],
         in_specs=[spec(pltpu.SMEM)] * 3 + [spec(pl.ANY)] + [spec(pltpu.VMEM)] * 3,
-        out_specs=[spec(pltpu.VMEM)] * 3,
+        out_specs=[spec(pltpu.VMEM)] * (groups + 1),
         compiler_params=grant(4),
     )(place, tokens, ids, after, total, first, second)
 
@@ -225,8 +260,8 @@
     steps = parts.bit_length() - 1
     swap = [(0, 1), (1, 0)]
 
-    def across(x, i):
-        return lax.ppermute(x, "blk", [(s, s ^ (1 << i)) for s in range(parts)])
+    def apart(x, distance):
+        return lax.ppermute(x, "blk", [(s, s ^ distance) for s in range(parts)])
 
     def crossed(x, i):
         pairs = [
@@ -237,21 +272,18 @@
     place = lax.axis_index("blk").reshape(1)
     core = lax.axis_index("fsdp").reshape(1)
     other_eigen = lax.ppermute(eigenvalues, "fsdp", swap)
-    block = pack(train_out, train_act)
+    block = relay(pack(train_out, train_act))
     arrived = crossed(block, 2)
     total = project(query_out.T, query_act.T, out_basis, act_basis)
-    kept, moved, block = spread(
-        place, train_tokens, train_ids, other_eigen, total, block, arrived, parts
-    )
-    sums = (kept + across(moved, 0)).reshape((2, 2) + kept.shape[1:])
-    arrived = crossed(block, 1)
-    kept, moved = sums[:, 0], sums[:, 1]
-    near = join(kept, block, arrived)
+    *pieces, block = spread(
+        place, train_tokens, train_ids, other_eigen, total, block, arrived, parts, parts // 2
+    )
+    near = join(pieces[0], block, crossed(block, 1))
+    sums = gather_sum(near, [pieces[0]] + [apart(pieces[d], d) for d in range(1, len(pieces))])
     far = crossed(near, 0)
     other_near = lax.ppermute(near, "fsdp", swap)
     other_far = lax.ppermute(far, "fsdp", swap)
-    sums = kept + across(moved, 1)
-    own = sums[0] + across(sums[1], 2)
+    own = sums[0] + apart(sums[1], 4)
     other = lax.ppermute(own, "fsdp", swap)
     return score(
         core, own, other, eigenvalues, other_eigen, (near, far, other_near, other_far)

time: 24.1 us -> 24 us (level)
    ppermute x3, starting transfers between devices: 5.3 us -> 7.05 us  [crossed(): return lax.ppermute(x, ('blk', 'fsdp'), pairs)]
    ppermute x3, waiting for transfers between devices: 2.12 us -> 0.85 us  [crossed(): return lax.ppermute(x, ('blk', 'fsdp'), pairs)]
    ppermute x3 -> x4, starting transfers between devices: 7 us -> 5.8 us  [apart(): return lax.ppermute(x, 'blk', [(s, s ^ distance) for s in range(parts)])]
    ppermute x3 -> x4, waiting for transfers between devices: 3.03 us -> 4.04 us  [apart(): return lax.ppermute(x, 'blk', [(s, s ^ distance) for s in range(parts)])]
    ppermute x1, starting transfers between devices: 0.46 us -> 0.01 us  [direct(): other = lax.ppermute(own, 'fsdp', swap)]
    ppermute x1, waiting for transfers between devices: 0.89 us -> 1.17 us  [direct(): other = lax.ppermute(own, 'fsdp', swap)]
    pallas_call x1, Pallas kernels: 1.04 us -> 0.78 us  [pack(): pl.pallas_call(pack_kernel, out_shape=jax.ShapeDtypeStruct(shape, train_o...]
  transfers between devices with their start and end apart: 10 -> 11, of which waited for: 5 -> 6; matrix products, arithmetic and copies ran while one was open for 0% -> 0% of each run, Pallas kernels for 6% -> 5%
where the time goes in v15:
time: 24 us; the launch traced here: 23.7 us
  starting transfers between devices  13.6 us (57%)
  waiting for transfers between devices  6.07 us (25%)
  Pallas kernels  2.64 us (11%)
  between operations  1.44 us (6%)
    ppermute x3, starting transfers between devices, crossed(): return lax.ppermute(x, ('blk', 'fsdp'), pairs)  7.05 us
    ppermute x4, starting transfers between devices, apart(): return lax.ppermute(x, 'blk', [(s, s ^ distance) for s in range(parts)])  5.8 us
    ppermute x4, waiting for transfers between devices, apart(): return lax.ppermute(x, 'blk', [(s, s ^ distance) for s in range(parts)])  4.04 us
    pallas_call x1, Pallas kernels, score(): pl.pallas_call(score_kernel, out_shape=jax.ShapeDtypeStruct((own.shape[0]...  1.34 us
    ppermute x1, waiting for transfers between devices, direct(): other = lax.ppermute(own, 'fsdp', swap)  1.17 us
    ppermute x3, waiting for transfers between devices, crossed(): return lax.ppermute(x, ('blk', 'fsdp'), pairs)  0.85 us
    pallas_call x1, Pallas kernels, pack(): pl.pallas_call(pack_kernel, out_shape=jax.ShapeDtypeStruct(shape, train_o...  0.78 us
  transfers between devices with their start and end apart: 11, of which 6 were waited for; matrix products, arithmetic and copies ran while one was open for 0% of the time, Pallas kernels for 5%

profile of v15, /device:TPU:0, one launch (start us, length us, event | category | flops | bytes accessed | tf_op | source)
XLA Modules:
  0.0 23.7 jit_solution(16919611397076512808)
XLA Ops:
  0.0 0.5 %collective-permute-start = (f32[256,256]{1,0:T(8,128)}, f32[256,256]{1,0:T(8,128)S(1)}, u32[]{:S(2)}, u32[]{:S(2)}) collective-permute-start(f32[256,256]{1,0:T(8,128)} %eigen.1), channel_id=1, source_target_pairs={{0,1},{1,0},{2,3},{3,2},{4,5},{5,4},{6,7},{7,6},{8,9},{9,8},{10,11... | collective-permute-start | bytes 786440 | tf_op jit(solution)/shard_map/ppermute | solution.py:274
  0.5 0.8 %shard_map.92.source = bf16[1,32,768]{2,1,0:T(8,128)(2,1)S(1)} custom-call(bf16[1,32,512]{2,1,0:T(8,128)(2,1)} %train_out.1, bf16[1,32,256]{2,1,0:T(8,128)(2,1)} %train_act.1), custom_call_target="tpu_custom_call" | custom-call | tf_op jit(solution)/shard_map/pallas_call | solution.py:46
  1.2 0.0 copy-start
  1.2 0.0 copy-start.1
  1.3 0.0 copy-start.3
  1.3 0.0 copy-start.4
  1.3 3.8 %collective-permute-start.1 = (bf16[1,32,768]{2,1,0:T(8,128)(2,1)S(1)}, bf16[1,32,768]{2,1,0:T(8,128)(2,1)S(1)}, u32[]{:S(2)}, u32[]{:S(2)}) collective-permute-start(bf16[1,32,768]{2,1,0:T(8,128)(2,1)S(1)} %shard_map.93.first), channel_id=1, source_target_pairs={{0,9},{1,8},{2,11},{3,10},{4,13},{5,12},{6,15},{7,14},{8,1},{9,0},... | collective-permute-start | bytes 147464 | tf_op jit(solution)/shard_map/ppermute | solution.py:270
  6.4 0.0 copy-start.2
  6.4 0.5 %shard_map.91.total = f32[64,384]{1,0:T(8,128)S(1)} custom-call(bf16[64,3584]{1,0:T(8,128)(2,1)S(1)} %bitcast.10, bf16[64,1024]{1,0:T(8,128)(2,1)S(1)} %bitcast.11, bf16[3584,256]{1,0:T(8,128)(2,1)S(1)} %copy-done, bf16[1024,128]{1,0:T(8,128)(2,1)S(1)} %copy-done.3), custom_call_target="tpu_custom_call" | custom-call | flops 134217728 | bytes 2686976 | tf_op jit(solution)/shard_map/pallas_call | solution.py:126
  6.9 0.3 %collective-permute-done.1.second = bf16[1,32,768]{2,1,0:T(8,128)(2,1)S(1)} collective-permute-done((bf16[1,32,768]{2,1,0:T(8,128)(2,1)S(1)}, bf16[1,32,768]{2,1,0:T(8,128)(2,1)S(1)}, u32[]{:S(2)}, u32[]{:S(2)}) %collective-permute-start.1) | collective-permute-done | bytes 49184 | tf_op jit(solution)/shard_map/ppermute | solution.py:270
  7.2 1.4 %collective-permute-start.2 = (bf16[2,32,768]{2,1,0:T(8,128)(2,1)S(1)}, bf16[2,32,768]{2,1,0:T(8,128)(2,1)S(1)}, u32[]{:S(2)}, u32[]{:S(2)}) collective-permute-start(bf16[2,32,768]{2,1,0:T(8,128)(2,1)S(1)} %get-tuple-element.11.first), channel_id=1, source_target_pairs={{0,5},{1,4},{2,7},{3,6},{4,1},{5,0},{6,3},{7,2},{8,13},{9,12},{10,... | collective-permute-start | bytes 294920 | tf_op jit(solution)/shard_map/ppermute | solution.py:270
  8.6 1.5 %collective-permute-start.3 = (f32[2,8,512]{2,1,0:T(8,128)S(1)}, f32[2,8,512]{2,1,0:T(8,128)S(1)}, u32[]{:S(2)}, u32[]{:S(2)}) collective-permute-start(f32[2,8,512]{2,1,0:T(8,128)S(1)} %get-tuple-element.12), channel_id=1, source_target_pairs={{0,2},{2,0},{4,6},{6,4},{8,10},{10,8},{12,14},{14,12},{1,3},{3,1},... | collective-permute-start | bytes 98312 | tf_op jit(solution)/shard_map/ppermute | solution.py:264
  10.1 1.5 %collective-permute-start.4 = (f32[2,8,512]{2,1,0:T(8,128)S(1)}, f32[2,8,512]{2,1,0:T(8,128)S(1)}, u32[]{:S(2)}, u32[]{:S(2)}) collective-permute-start(f32[2,8,512]{2,1,0:T(8,128)S(1)} %get-tuple-element.13), channel_id=1, source_target_pairs={{0,4},{2,6},{4,0},{6,2},{8,12},{10,14},{12,8},{14,10},{1,5},{3,7},... | collective-permute-start | bytes 98312 | tf_op jit(solution)/shard_map/ppermute | solution.py:264
  11.6 0.5 %collective-permute-start.5 = (f32[2,8,512]{2,1,0:T(8,128)S(1)}, f32[2,8,512]{2,1,0:T(8,128)S(1)}, u32[]{:S(2)}, u32[]{:S(2)}) collective-permute-start(f32[2,8,512]{2,1,0:T(8,128)S(1)} %get-tuple-element.14), channel_id=1, source_target_pairs={{0,6},{2,4},{4,2},{6,0},{8,14},{10,12},{12,10},{14,8},{1,7},{3,5},... | collective-permute-start | bytes 98312 | tf_op jit(solution)/shard_map/ppermute | solution.py:264
  12.1 1.9 %collective-permute-start.8 = (bf16[4,32,768]{2,1,0:T(8,128)(2,1)S(1)}, bf16[4,32,768]{2,1,0:T(8,128)(2,1)S(1)}, u32[]{:S(2)}, u32[]{:S(2)}) collective-permute-start(bf16[4,32,768]{2,1,0:T(8,128)(2,1)S(1)} %shard_map.95.after.rest_0_), channel_id=1, source_target_pairs={{0,3},{1,2},{2,1},{3,0},{4,7},{5,6},{6,5},{7,4},{8,11},{9,10},{10,... | collective-permute-start | bytes 589832 | tf_op jit(solution)/shard_map/ppermute | solution.py:270
  14.0 0.1 collective-permute-done.4.refs_2_
  14.1 2.3 %collective-permute-done.5.refs_3_ = f32[2,8,512]{2,1,0:T(8,128)S(1)} collective-permute-done((f32[2,8,512]{2,1,0:T(8,128)S(1)}, f32[2,8,512]{2,1,0:T(8,128)S(1)}, u32[]{:S(2)}, u32[]{:S(2)}) %collective-permute-start.5) | collective-permute-done | bytes 32800 | tf_op jit(solution)/shard_map/ppermute | solution.py:264
  16.5 2.3 %collective-permute-start.6 = (f32[8,512]{1,0:T(8,128)S(1)}, f32[8,512]{1,0:T(8,128)S(1)}, u32[]{:S(2)}, u32[]{:S(2)}) collective-permute-start(f32[8,512]{1,0:T(8,128)S(1)} %slice_bitcast_fusion), channel_id=1, source_target_pairs={{0,8},{2,10},{4,12},{6,14},{8,0},{10,2},{12,4},{14,6},{1,9},{3,11}... | collective-permute-start | bytes 49160 | tf_op jit(solution)/shard_map/ppermute | solution.py:264
  18.8 0.6 %collective-permute-done.8.rest_1_ = bf16[4,32,768]{2,1,0:T(8,128)(2,1)S(1)} collective-permute-done((bf16[4,32,768]{2,1,0:T(8,128)(2,1)S(1)}, bf16[4,32,768]{2,1,0:T(8,128)(2,1)S(1)}, u32[]{:S(2)}, u32[]{:S(2)}) %collective-permute-start.8) | collective-permute-done | bytes 196640 | tf_op jit(solution)/shard_map/ppermute | solution.py:270
  19.4 0.2 %collective-permute-start.10 = (bf16[4,32,768]{2,1,0:T(8,128)(2,1)S(1)}, bf16[4,32,768]{2,1,0:T(8,128)(2,1)S(1)}, u32[]{:S(2)}, u32[]{:S(2)}) collective-permute-start(bf16[4,32,768]{2,1,0:T(8,128)(2,1)S(1)} %collective-permute-done.8.rest_1_), channel_id=1, source_target_pairs={{0,1},{1,0},{2,3},{3,2},{4,5},{5,4},{6,7},{7,6},{8,9},{9,8},{10,11... | collective-permute-start | bytes 589832 | tf_op jit(solution)/shard_map/ppermute | solution.py:285
  19.6 1.6 %collective-permute-done.6 = f32[8,512]{1,0:T(8,128)S(1)} collective-permute-done((f32[8,512]{1,0:T(8,128)S(1)}, f32[8,512]{1,0:T(8,128)S(1)}, u32[]{:S(2)}, u32[]{:S(2)}) %collective-permute-start.6) | collective-permute-done | bytes 16416 | tf_op jit(solution)/shard_map/ppermute | solution.py:264
  21.2 0.0 collective-permute-start.7
  21.2 1.2 %collective-permute-done.7.other = f32[8,512]{1,0:T(8,128)S(1)} collective-permute-done((f32[8,512]{1,0:T(8,128)S(1)}, f32[8,512]{1,0:T(8,128)S(1)}, u32[]{:S(2)}, u32[]{:S(2)}) %collective-permute-start.7) | collective-permute-done | bytes 16416 | tf_op jit(solution)/shard_map/ppermute | solution.py:287
  22.4 1.3 %shard_map.97 = f32[2,16]{1,0:T(2,128)} custom-call(s32[1]{0:T(128)} %bitcast.core_ref, f32[8,512]{1,0:T(8,128)S(1)} %fusion.own, f32[8,512]{1,0:T(8,128)S(1)} %collective-permute-done.7.other, f32[256,256]{1,0:T(8,128)S(1)} %copy-done.2, f32[256,256]{1,0:T(8,128)S(1)} %collective-permute-done.after.other_eigen, ...), custom_call_target="tpu_custom_call" | custom-call | tf_op jit(solution)/shard_map/pallas_call | solution.py:239
  (17 shorter events, 0.1 us)
Async XLA Ops:
  0.0 7.2 %collective-permute-start = (f32[256,256]{1,0:T(8,128)}, f32[256,256]{1,0:T(8,128)S(1)}, u32[]{:S(2)}, u32[]{:S(2)}) collective-permute-start(f32[256,256]{1,0:T(8,128)} %eigen.1), channel_id=1, source_target_pairs={{0,1},{1,0},{2,3},{3,2},{4,5},{5,4},{6,7},{7,6},{8,9},{9,8},{10,11... | collective-permute-start | bytes 786440 | tf_op jit(solution)/shard_map/ppermute | solution.py:274
  1.2 5.1 %copy-start = (bf16[3584,256]{1,0:T(8,128)(2,1)S(1)}, bf16[3584,256]{1,0:T(8,128)(2,1)}, u32[]{:S(2)}) copy-start(bf16[3584,256]{1,0:T(8,128)(2,1)} %out_basis.1) | copy-start | bytes 5505028
  1.2 5.1 %copy-start.1 = (bf16[3584,64]{0,1:T(8,128)(2,1)S(1)}, bf16[3584,64]{0,1:T(8,128)(2,1)}, u32[]{:S(2)}) copy-start(bf16[3584,64]{0,1:T(8,128)(2,1)} %param.9) | copy-start | bytes 1376260
  1.3 5.1 %copy-start.3 = (bf16[1024,128]{1,0:T(8,128)(2,1)S(1)}, bf16[1024,128]{1,0:T(8,128)(2,1)}, u32[]{:S(2)}) copy-start(bf16[1024,128]{1,0:T(8,128)(2,1)} %act_basis.1) | copy-start | bytes 786436
  1.3 5.1 %copy-start.4 = (bf16[1024,64]{0,1:T(8,128)(2,1)S(1)}, bf16[1024,64]{0,1:T(8,128)(2,1)}, u32[]{:S(2)}) copy-start(bf16[1024,64]{0,1:T(8,128)(2,1)} %param.10) | copy-start | bytes 393220
  1.3 5.9 %collective-permute-start.1 = (bf16[1,32,768]{2,1,0:T(8,128)(2,1)S(1)}, bf16[1,32,768]{2,1,0:T(8,128)(2,1)S(1)}, u32[]{:S(2)}, u32[]{:S(2)}) collective-permute-start(bf16[1,32,768]{2,1,0:T(8,128)(2,1)S(1)} %shard_map.93.first), channel_id=1, source_target_pairs={{0,9},{1,8},{2,11},{3,10},{4,13},{5,12},{6,15},{7,14},{8,1},{9,0},... | collective-permute-start | bytes 147464 | tf_op jit(solution)/shard_map/ppermute | solution.py:270
  6.4 16.0 %copy-start.2 = (f32[256,256]{1,0:T(8,128)S(1)}, f32[256,256]{1,0:T(8,128)}, u32[]{:S(2)}) copy-start(f32[256,256]{1,0:T(8,128)} %eigen.1) | copy-start | bytes 786436
  7.2 4.8 %collective-permute-start.2 = (bf16[2,32,768]{2,1,0:T(8,128)(2,1)S(1)}, bf16[2,32,768]{2,1,0:T(8,128)(2,1)S(1)}, u32[]{:S(2)}, u32[]{:S(2)}) collective-permute-start(bf16[2,32,768]{2,1,0:T(8,128)(2,1)S(1)} %get-tuple-element.11.first), channel_id=1, source_target_pairs={{0,5},{1,4},{2,7},{3,6},{4,1},{5,0},{6,3},{7,2},{8,13},{9,12},{10,... | collective-permute-start | bytes 294920 | tf_op jit(solution)/shard_map/ppermute | solution.py:270
  8.6 5.4 %collective-permute-start.3 = (f32[2,8,512]{2,1,0:T(8,128)S(1)}, f32[2,8,512]{2,1,0:T(8,128)S(1)}, u32[]{:S(2)}, u32[]{:S(2)}) collective-permute-start(f32[2,8,512]{2,1,0:T(8,128)S(1)} %get-tuple-element.12), channel_id=1, source_target_pairs={{0,2},{2,0},{4,6},{6,4},{8,10},{10,8},{12,14},{14,12},{1,3},{3,1},... | collective-permute-start | bytes 98312 | tf_op jit(solution)/shard_map/ppermute | solution.py:264
  10.1 4.1 %collective-permute-start.4 = (f32[2,8,512]{2,1,0:T(8,128)S(1)}, f32[2,8,512]{2,1,0:T(8,128)S(1)}, u32[]{:S(2)}, u32[]{:S(2)}) collective-permute-start(f32[2,8,512]{2,1,0:T(8,128)S(1)} %get-tuple-element.13), channel_id=1, source_target_pairs={{0,4},{2,6},{4,0},{6,2},{8,12},{10,14},{12,8},{14,10},{1,5},{3,7},... | collective-permute-start | bytes 98312 | tf_op jit(solution)/shard_map/ppermute | solution.py:264
  11.6 4.9 %collective-permute-start.5 = (f32[2,8,512]{2,1,0:T(8,128)S(1)}, f32[2,8,512]{2,1,0:T(8,128)S(1)}, u32[]{:S(2)}, u32[]{:S(2)}) collective-permute-start(f32[2,8,512]{2,1,0:T(8,128)S(1)} %get-tuple-element.14), channel_id=1, source_target_pairs={{0,6},{2,4},{4,2},{6,0},{8,14},{10,12},{12,10},{14,8},{1,7},{3,5},... | collective-permute-start | bytes 98312 | tf_op jit(solution)/shard_map/ppermute | solution.py:264
  12.1 7.3 %collective-permute-start.8 = (bf16[4,32,768]{2,1,0:T(8,128)(2,1)S(1)}, bf16[4,32,768]{2,1,0:T(8,128)(2,1)S(1)}, u32[]{:S(2)}, u32[]{:S(2)}) collective-permute-start(bf16[4,32,768]{2,1,0:T(8,128)(2,1)S(1)} %shard_map.95.after.rest_0_), channel_id=1, source_target_pairs={{0,3},{1,2},{2,1},{3,0},{4,7},{5,6},{6,5},{7,4},{8,11},{9,10},{10,... | collective-permute-start | bytes 589832 | tf_op jit(solution)/shard_map/ppermute | solution.py:270
  16.5 4.7 %collective-permute-start.6 = (f32[8,512]{1,0:T(8,128)S(1)}, f32[8,512]{1,0:T(8,128)S(1)}, u32[]{:S(2)}, u32[]{:S(2)}) collective-permute-start(f32[8,512]{1,0:T(8,128)S(1)} %slice_bitcast_fusion), channel_id=1, source_target_pairs={{0,8},{2,10},{4,12},{6,14},{8,0},{10,2},{12,4},{14,6},{1,9},{3,11}... | collective-permute-start | bytes 49160 | tf_op jit(solution)/shard_map/ppermute | solution.py:264
  18.8 3.6 %collective-permute-start.9 = (bf16[4,32,768]{2,1,0:T(8,128)(2,1)S(1)}, bf16[4,32,768]{2,1,0:T(8,128)(2,1)S(1)}, u32[]{:S(2)}, u32[]{:S(2)}) collective-permute-start(bf16[4,32,768]{2,1,0:T(8,128)(2,1)S(1)} %shard_map.95.after.rest_0_), channel_id=1, source_target_pairs={{0,1},{1,0},{2,3},{3,2},{4,5},{5,4},{6,7},{7,6},{8,9},{9,8},{10,11... | collective-permute-start | bytes 589832 | tf_op jit(solution)/shard_map/ppermute | solution.py:284
  19.4 3.0 %collective-permute-start.10 = (bf16[4,32,768]{2,1,0:T(8,128)(2,1)S(1)}, bf16[4,32,768]{2,1,0:T(8,128)(2,1)S(1)}, u32[]{:S(2)}, u32[]{:S(2)}) collective-permute-start(bf16[4,32,768]{2,1,0:T(8,128)(2,1)S(1)} %collective-permute-done.8.rest_1_), channel_id=1, source_target_pairs={{0,1},{1,0},{2,3},{3,2},{4,5},{5,4},{6,7},{7,6},{8,9},{9,8},{10,11... | collective-permute-start | bytes 589832 | tf_op jit(solution)/shard_map/ppermute | solution.py:285
  21.2 1.2 %collective-permute-start.7 = (f32[8,512]{1,0:T(8,128)S(1)}, f32[8,512]{1,0:T(8,128)S(1)}, u32[]{:S(2)}, u32[]{:S(2)}) collective-permute-start(f32[8,512]{1,0:T(8,128)S(1)} %fusion.own), channel_id=1, source_target_pairs={{0,1},{1,0},{2,3},{3,2},{4,5},{5,4},{6,7},{7,6},{8,9},{9,8},{10,11... | collective-permute-start | bytes 49160 | tf_op jit(solution)/shard_map/ppermute | solution.py:287

commit v16 on v15

--- a/solution.py
+++ b/solution.py
@@ -279,7 +279,9 @@
         place, train_tokens, train_ids, other_eigen, total, block, arrived, parts, parts // 2
     )
     near = join(pieces[0], block, crossed(block, 1))
-    sums = gather_sum(near, [pieces[0]] + [apart(pieces[d], d) for d in range(1, len(pieces))])
+    far_first = reversed(range(1, len(pieces)))
+    terms = [pieces[0]] + [apart(pieces[d], d) for d in far_first]
+    sums = gather_sum(near, terms)
     far = crossed(near, 0)
     other_near = lax.ppermute(near, "fsdp", swap)
     other_far = lax.ppermute(far, "fsdp", swap)

time: 24 us -> 24 us (level)
  waiting for transfers between devices: 6.07 us -> 3.96 us
  starting transfers between devices: 13.6 us -> 15.7 us
    ppermute x4, waiting for transfers between devices: 4.04 us -> 2.16 us  [apart(): return lax.ppermute(x, 'blk', [(s, s ^ distance) for s in range(parts)])]
    ppermute x4, starting transfers between devices: 5.8 us -> 7.35 us  [apart(): return lax.ppermute(x, 'blk', [(s, s ^ distance) for s in range(parts)])]
    ppermute x3, starting transfers between devices: 7.05 us -> 7.69 us  [crossed(): return lax.ppermute(x, ('blk', 'fsdp'), pairs)]
  transfers between devices with their start and end apart: 11 -> 11, of which waited for: 6 -> 7; matrix products, arithmetic and copies ran while one was open for 0% -> 0% of each run, Pallas kernels for 5% -> 5%
where the time goes in v16:
time: 24 us; the launch traced here: 23.8 us
  starting transfers between devices  15.7 us (65%)
  waiting for transfers between devices  3.96 us (16%)
  Pallas kernels  2.64 us (11%)
  between operations  1.44 us (6%)
    ppermute x3, starting transfers between devices, crossed(): return lax.ppermute(x, ('blk', 'fsdp'), pairs)  7.69 us
    ppermute x4, starting transfers between devices, apart(): return lax.ppermute(x, 'blk', [(s, s ^ distance) for s in range(parts)])  7.35 us
    ppermute x4, waiting for transfers between devices, apart(): return lax.ppermute(x, 'blk', [(s, s ^ distance) for s in range(parts)])  2.16 us
    pallas_call x1, Pallas kernels, score(): pl.pallas_call(score_kernel, out_shape=jax.ShapeDtypeStruct((own.shape[0]...  1.34 us
    ppermute x1, waiting for transfers between devices, direct(): other = lax.ppermute(own, 'fsdp', swap)  1.17 us
    pallas_call x1, Pallas kernels, pack(): pl.pallas_call(pack_kernel, out_shape=jax.ShapeDtypeStruct(shape, train_o...  0.78 us
    ppermute x3, waiting for transfers between devices, crossed(): return lax.ppermute(x, ('blk', 'fsdp'), pairs)  0.62 us
  transfers between devices with their start and end apart: 11, of which 7 were waited for; matrix products, arithmetic and copies ran while one was open for 0% of the time, Pallas kernels for 5%

profile of v16, /device:TPU:0, one launch (start us, length us, event | category | flops | bytes accessed | tf_op | source)
XLA Modules:
  0.0 23.8 jit_solution(3346750537624326237)
XLA Ops:
  0.0 0.5 %collective-permute-start = (f32[256,256]{1,0:T(8,128)}, f32[256,256]{1,0:T(8,128)S(1)}, u32[]{:S(2)}, u32[]{:S(2)}) collective-permute-start(f32[256,256]{1,0:T(8,128)} %eigen.1), channel_id=1, source_target_pairs={{0,1},{1,0},{2,3},{3,2},{4,5},{5,4},{6,7},{7,6},{8,9},{9,8},{10,11... | collective-permute-start | bytes 786440 | tf_op jit(solution)/shard_map/ppermute | solution.py:274
  0.5 0.8 %shard_map.92.source = bf16[1,32,768]{2,1,0:T(8,128)(2,1)S(1)} custom-call(bf16[1,32,512]{2,1,0:T(8,128)(2,1)} %train_out.1, bf16[1,32,256]{2,1,0:T(8,128)(2,1)} %train_act.1), custom_call_target="tpu_custom_call" | custom-call | tf_op jit(solution)/shard_map/pallas_call | solution.py:46
  1.2 0.0 copy-start
  1.2 0.0 copy-start.1
  1.3 0.0 copy-start.3
  1.3 0.0 copy-start.4
  1.3 3.8 %collective-permute-start.1 = (bf16[1,32,768]{2,1,0:T(8,128)(2,1)S(1)}, bf16[1,32,768]{2,1,0:T(8,128)(2,1)S(1)}, u32[]{:S(2)}, u32[]{:S(2)}) collective-permute-start(bf16[1,32,768]{2,1,0:T(8,128)(2,1)S(1)} %shard_map.93.first), channel_id=1, source_target_pairs={{0,9},{1,8},{2,11},{3,10},{4,13},{5,12},{6,15},{7,14},{8,1},{9,0},... | collective-permute-start | bytes 147464 | tf_op jit(solution)/shard_map/ppermute | solution.py:270
  6.4 0.0 copy-start.2
  6.4 0.5 %shard_map.91.total = f32[64,384]{1,0:T(8,128)S(1)} custom-call(bf16[64,3584]{1,0:T(8,128)(2,1)S(1)} %bitcast.10, bf16[64,1024]{1,0:T(8,128)(2,1)S(1)} %bitcast.11, bf16[3584,256]{1,0:T(8,128)(2,1)S(1)} %copy-done, bf16[1024,128]{1,0:T(8,128)(2,1)S(1)} %copy-done.3), custom_call_target="tpu_custom_call" | custom-call | flops 134217728 | bytes 2686976 | tf_op jit(solution)/shard_map/pallas_call | solution.py:126
  6.9 0.3 %collective-permute-done.1.second = bf16[1,32,768]{2,1,0:T(8,128)(2,1)S(1)} collective-permute-done((bf16[1,32,768]{2,1,0:T(8,128)(2,1)S(1)}, bf16[1,32,768]{2,1,0:T(8,128)(2,1)S(1)}, u32[]{:S(2)}, u32[]{:S(2)}) %collective-permute-start.1) | collective-permute-done | bytes 49184 | tf_op jit(solution)/shard_map/ppermute | solution.py:270
  7.2 1.4 %collective-permute-start.2 = (bf16[2,32,768]{2,1,0:T(8,128)(2,1)S(1)}, bf16[2,32,768]{2,1,0:T(8,128)(2,1)S(1)}, u32[]{:S(2)}, u32[]{:S(2)}) collective-permute-start(bf16[2,32,768]{2,1,0:T(8,128)(2,1)S(1)} %get-tuple-element.11.first), channel_id=1, source_target_pairs={{0,5},{1,4},{2,7},{3,6},{4,1},{5,0},{6,3},{7,2},{8,13},{9,12},{10,... | collective-permute-start | bytes 294920 | tf_op jit(solution)/shard_map/ppermute | solution.py:270
  8.6 2.4 %collective-permute-start.3 = (f32[2,8,512]{2,1,0:T(8,128)S(1)}, f32[2,8,512]{2,1,0:T(8,128)S(1)}, u32[]{:S(2)}, u32[]{:S(2)}) collective-permute-start(f32[2,8,512]{2,1,0:T(8,128)S(1)} %get-tuple-element.12), channel_id=1, source_target_pairs={{0,6},{2,4},{4,2},{6,0},{8,14},{10,12},{12,10},{14,8},{1,7},{3,5},... | collective-permute-start | bytes 98312 | tf_op jit(solution)/shard_map/ppermute | solution.py:264
  11.0 0.5 %collective-permute-start.4 = (f32[2,8,512]{2,1,0:T(8,128)S(1)}, f32[2,8,512]{2,1,0:T(8,128)S(1)}, u32[]{:S(2)}, u32[]{:S(2)}) collective-permute-start(f32[2,8,512]{2,1,0:T(8,128)S(1)} %get-tuple-element.13), channel_id=1, source_target_pairs={{0,4},{2,6},{4,0},{6,2},{8,12},{10,14},{12,8},{14,10},{1,5},{3,7},... | collective-permute-start | bytes 98312 | tf_op jit(solution)/shard_map/ppermute | solution.py:264
  11.5 0.5 %collective-permute-start.5 = (f32[2,8,512]{2,1,0:T(8,128)S(1)}, f32[2,8,512]{2,1,0:T(8,128)S(1)}, u32[]{:S(2)}, u32[]{:S(2)}) collective-permute-start(f32[2,8,512]{2,1,0:T(8,128)S(1)} %get-tuple-element.14), channel_id=1, source_target_pairs={{0,2},{2,0},{4,6},{6,4},{8,10},{10,8},{12,14},{14,12},{1,3},{3,1},... | collective-permute-start | bytes 98312 | tf_op jit(solution)/shard_map/ppermute | solution.py:264
  12.1 2.6 %collective-permute-start.8 = (bf16[4,32,768]{2,1,0:T(8,128)(2,1)S(1)}, bf16[4,32,768]{2,1,0:T(8,128)(2,1)S(1)}, u32[]{:S(2)}, u32[]{:S(2)}) collective-permute-start(bf16[4,32,768]{2,1,0:T(8,128)(2,1)S(1)} %shard_map.95.after.rest_0_), channel_id=1, source_target_pairs={{0,3},{1,2},{2,1},{3,0},{4,7},{5,6},{6,5},{7,4},{8,11},{9,10},{10,... | collective-permute-start | bytes 589832 | tf_op jit(solution)/shard_map/ppermute | solution.py:270
  14.6 0.1 collective-permute-done.3.refs_1_
  14.7 0.2 collective-permute-done.4.refs_2_
  14.9 0.5 %collective-permute-done.5.refs_3_ = f32[2,8,512]{2,1,0:T(8,128)S(1)} collective-permute-done((f32[2,8,512]{2,1,0:T(8,128)S(1)}, f32[2,8,512]{2,1,0:T(8,128)S(1)}, u32[]{:S(2)}, u32[]{:S(2)}) %collective-permute-start.5) | collective-permute-done | bytes 32800 | tf_op jit(solution)/shard_map/ppermute | solution.py:264
  15.5 3.9 %collective-permute-start.6 = (f32[8,512]{1,0:T(8,128)S(1)}, f32[8,512]{1,0:T(8,128)S(1)}, u32[]{:S(2)}, u32[]{:S(2)}) collective-permute-start(f32[8,512]{1,0:T(8,128)S(1)} %slice_bitcast_fusion), channel_id=1, source_target_pairs={{0,8},{2,10},{4,12},{6,14},{8,0},{10,2},{12,4},{14,6},{1,9},{3,11}... | collective-permute-start | bytes 49160 | tf_op jit(solution)/shard_map/ppermute | solution.py:264
  19.3 0.3 %collective-permute-done.8.rest_1_ = bf16[4,32,768]{2,1,0:T(8,128)(2,1)S(1)} collective-permute-done((bf16[4,32,768]{2,1,0:T(8,128)(2,1)S(1)}, bf16[4,32,768]{2,1,0:T(8,128)(2,1)S(1)}, u32[]{:S(2)}, u32[]{:S(2)}) %collective-permute-start.8) | collective-permute-done | bytes 196640 | tf_op jit(solution)/shard_map/ppermute | solution.py:270
  19.7 0.2 collective-permute-start.10
  19.8 1.4 %collective-permute-done.6 = f32[8,512]{1,0:T(8,128)S(1)} collective-permute-done((f32[8,512]{1,0:T(8,128)S(1)}, f32[8,512]{1,0:T(8,128)S(1)}, u32[]{:S(2)}, u32[]{:S(2)}) %collective-permute-start.6) | collective-permute-done | bytes 16416 | tf_op jit(solution)/shard_map/ppermute | solution.py:264
  21.2 1.2 %collective-permute-done.7.other = f32[8,512]{1,0:T(8,128)S(1)} collective-permute-done((f32[8,512]{1,0:T(8,128)S(1)}, f32[8,512]{1,0:T(8,128)S(1)}, u32[]{:S(2)}, u32[]{:S(2)}) %collective-permute-start.7) | collective-permute-done | bytes 16416 | tf_op jit(solution)/shard_map/ppermute | solution.py:289
  22.4 1.3 %shard_map.97 = f32[2,16]{1,0:T(2,128)} custom-call(s32[1]{0:T(128)} %bitcast.core_ref, f32[8,512]{1,0:T(8,128)S(1)} %fusion.own, f32[8,512]{1,0:T(8,128)S(1)} %collective-permute-done.7.other, f32[256,256]{1,0:T(8,128)S(1)} %copy-done.2, f32[256,256]{1,0:T(8,128)S(1)} %collective-permute-done.after.other_eigen, ...), custom_call_target="tpu_custom_call" | custom-call | tf_op jit(solution)/shard_map/pallas_call | solution.py:239
  (17 shorter events, 0.1 us)
Async XLA Ops:
  0.0 7.2 %collective-permute-start = (f32[256,256]{1,0:T(8,128)}, f32[256,256]{1,0:T(8,128)S(1)}, u32[]{:S(2)}, u32[]{:S(2)}) collective-permute-start(f32[256,256]{1,0:T(8,128)} %eigen.1), channel_id=1, source_target_pairs={{0,1},{1,0},{2,3},{3,2},{4,5},{5,4},{6,7},{7,6},{8,9},{9,8},{10,11... | collective-permute-start | bytes 786440 | tf_op jit(solution)/shard_map/ppermute | solution.py:274
  1.2 5.1 %copy-start = (bf16[3584,256]{1,0:T(8,128)(2,1)S(1)}, bf16[3584,256]{1,0:T(8,128)(2,1)}, u32[]{:S(2)}) copy-start(bf16[3584,256]{1,0:T(8,128)(2,1)} %out_basis.1) | copy-start | bytes 5505028
  1.2 5.1 %copy-start.1 = (bf16[3584,64]{0,1:T(8,128)(2,1)S(1)}, bf16[3584,64]{0,1:T(8,128)(2,1)}, u32[]{:S(2)}) copy-start(bf16[3584,64]{0,1:T(8,128)(2,1)} %param.9) | copy-start | bytes 1376260
  1.3 5.1 %copy-start.3 = (bf16[1024,128]{1,0:T(8,128)(2,1)S(1)}, bf16[1024,128]{1,0:T(8,128)(2,1)}, u32[]{:S(2)}) copy-start(bf16[1024,128]{1,0:T(8,128)(2,1)} %act_basis.1) | copy-start | bytes 786436
  1.3 5.1 %copy-start.4 = (bf16[1024,64]{0,1:T(8,128)(2,1)S(1)}, bf16[1024,64]{0,1:T(8,128)(2,1)}, u32[]{:S(2)}) copy-start(bf16[1024,64]{0,1:T(8,128)(2,1)} %param.10) | copy-start | bytes 393220
  1.3 5.9 %collective-permute-start.1 = (bf16[1,32,768]{2,1,0:T(8,128)(2,1)S(1)}, bf16[1,32,768]{2,1,0:T(8,128)(2,1)S(1)}, u32[]{:S(2)}, u32[]{:S(2)}) collective-permute-start(bf16[1,32,768]{2,1,0:T(8,128)(2,1)S(1)} %shard_map.93.first), channel_id=1, source_target_pairs={{0,9},{1,8},{2,11},{3,10},{4,13},{5,12},{6,15},{7,14},{8,1},{9,0},... | collective-permute-start | bytes 147464 | tf_op jit(solution)/shard_map/ppermute | solution.py:270
  6.4 16.0 %copy-start.2 = (f32[256,256]{1,0:T(8,128)S(1)}, f32[256,256]{1,0:T(8,128)}, u32[]{:S(2)}) copy-start(f32[256,256]{1,0:T(8,128)} %eigen.1) | copy-start | bytes 786436
  7.2 4.8 %collective-permute-start.2 = (bf16[2,32,768]{2,1,0:T(8,128)(2,1)S(1)}, bf16[2,32,768]{2,1,0:T(8,128)(2,1)S(1)}, u32[]{:S(2)}, u32[]{:S(2)}) collective-permute-start(bf16[2,32,768]{2,1,0:T(8,128)(2,1)S(1)} %get-tuple-element.11.first), channel_id=1, source_target_pairs={{0,5},{1,4},{2,7},{3,6},{4,1},{5,0},{6,3},{7,2},{8,13},{9,12},{10,... | collective-permute-start | bytes 294920 | tf_op jit(solution)/shard_map/ppermute | solution.py:270
  8.6 6.2 %collective-permute-start.3 = (f32[2,8,512]{2,1,0:T(8,128)S(1)}, f32[2,8,512]{2,1,0:T(8,128)S(1)}, u32[]{:S(2)}, u32[]{:S(2)}) collective-permute-start(f32[2,8,512]{2,1,0:T(8,128)S(1)} %get-tuple-element.12), channel_id=1, source_target_pairs={{0,6},{2,4},{4,2},{6,0},{8,14},{10,12},{12,10},{14,8},{1,7},{3,5},... | collective-permute-start | bytes 98312 | tf_op jit(solution)/shard_map/ppermute | solution.py:264
  11.0 3.9 %collective-permute-start.4 = (f32[2,8,512]{2,1,0:T(8,128)S(1)}, f32[2,8,512]{2,1,0:T(8,128)S(1)}, u32[]{:S(2)}, u32[]{:S(2)}) collective-permute-start(f32[2,8,512]{2,1,0:T(8,128)S(1)} %get-tuple-element.13), channel_id=1, source_target_pairs={{0,4},{2,6},{4,0},{6,2},{8,12},{10,14},{12,8},{14,10},{1,5},{3,7},... | collective-permute-start | bytes 98312 | tf_op jit(solution)/shard_map/ppermute | solution.py:264
  11.5 3.9 %collective-permute-start.5 = (f32[2,8,512]{2,1,0:T(8,128)S(1)}, f32[2,8,512]{2,1,0:T(8,128)S(1)}, u32[]{:S(2)}, u32[]{:S(2)}) collective-permute-start(f32[2,8,512]{2,1,0:T(8,128)S(1)} %get-tuple-element.14), channel_id=1, source_target_pairs={{0,2},{2,0},{4,6},{6,4},{8,10},{10,8},{12,14},{14,12},{1,3},{3,1},... | collective-permute-start | bytes 98312 | tf_op jit(solution)/shard_map/ppermute | solution.py:264
  12.1 7.6 %collective-permute-start.8 = (bf16[4,32,768]{2,1,0:T(8,128)(2,1)S(1)}, bf16[4,32,768]{2,1,0:T(8,128)(2,1)S(1)}, u32[]{:S(2)}, u32[]{:S(2)}) collective-permute-start(bf16[4,32,768]{2,1,0:T(8,128)(2,1)S(1)} %shard_map.95.after.rest_0_), channel_id=1, source_target_pairs={{0,3},{1,2},{2,1},{3,0},{4,7},{5,6},{6,5},{7,4},{8,11},{9,10},{10,... | collective-permute-start | bytes 589832 | tf_op jit(solution)/shard_map/ppermute | solution.py:270
  15.5 5.8 %collective-permute-start.6 = (f32[8,512]{1,0:T(8,128)S(1)}, f32[8,512]{1,0:T(8,128)S(1)}, u32[]{:S(2)}, u32[]{:S(2)}) collective-permute-start(f32[8,512]{1,0:T(8,128)S(1)} %slice_bitcast_fusion), channel_id=1, source_target_pairs={{0,8},{2,10},{4,12},{6,14},{8,0},{10,2},{12,4},{14,6},{1,9},{3,11}... | collective-permute-start | bytes 49160 | tf_op jit(solution)/shard_map/ppermute | solution.py:264
  19.3 3.1 %collective-permute-start.9 = (bf16[4,32,768]{2,1,0:T(8,128)(2,1)S(1)}, bf16[4,32,768]{2,1,0:T(8,128)(2,1)S(1)}, u32[]{:S(2)}, u32[]{:S(2)}) collective-permute-start(bf16[4,32,768]{2,1,0:T(8,128)(2,1)S(1)} %shard_map.95.after.rest_0_), channel_id=1, source_target_pairs={{0,1},{1,0},{2,3},{3,2},{4,5},{5,4},{6,7},{7,6},{8,9},{9,8},{10,11... | collective-permute-start | bytes 589832 | tf_op jit(solution)/shard_map/ppermute | solution.py:286
  19.7 2.8 %collective-permute-start.10 = (bf16[4,32,768]{2,1,0:T(8,128)(2,1)S(1)}, bf16[4,32,768]{2,1,0:T(8,128)(2,1)S(1)}, u32[]{:S(2)}, u32[]{:S(2)}) collective-permute-start(bf16[4,32,768]{2,1,0:T(8,128)(2,1)S(1)} %collective-permute-done.8.rest_1_), channel_id=1, source_target_pairs={{0,1},{1,0},{2,3},{3,2},{4,5},{5,4},{6,7},{7,6},{8,9},{9,8},{10,11... | collective-permute-start | bytes 589832 | tf_op jit(solution)/shard_map/ppermute | solution.py:287
  21.2 1.2 %collective-permute-start.7 = (f32[8,512]{1,0:T(8,128)S(1)}, f32[8,512]{1,0:T(8,128)S(1)}, u32[]{:S(2)}, u32[]{:S(2)}) collective-permute-start(f32[8,512]{1,0:T(8,128)S(1)} %fusion.own), channel_id=1, source_target_pairs={{0,1},{1,0},{2,3},{3,2},{4,5},{5,4},{6,7},{7,6},{8,9},{9,8},{10,11... | collective-permute-start | bytes 49160 | tf_op jit(solution)/shard_map/ppermute | solution.py:289

commit v17 on v15

--- a/solution.py
+++ b/solution.py
@@ -10,6 +10,8 @@
 RQ = 4
 LANES = 128
 DIRECT_PARTS = 8
+DIRECT_STEPS = (0, 5, 4, 1)
+LAST_STEP = 2
 WAIT_FLOPS = 10**9
 
 
@@ -145,33 +147,32 @@
 def spread_kernel(place_ref, tokens_ref, ids_ref, after, total, first, second, *rest):
     del after
     pieces, joined = rest[:-1], rest[-1]
-    groups = len(pieces)
     each, local_rows, _ = pieces[0].shape
-    parts = groups * each
+    parts = each * len(pieces)
     width = total.shape[1]
     row = lax.broadcasted_iota(jnp.int32, (local_rows, LANES), 0)
     lane = lax.broadcasted_iota(jnp.int32, (local_rows, LANES), 1)
     facts = jnp.where(lane < LANES // 2, ids_ref[0], tokens_ref[0]).astype(jnp.float32)
     for part in range(parts):
         start = pl.multiple_of((place_ref[0] ^ part) * local_rows, local_rows)
-        piece = pieces[part % groups].at[part // groups]
+        piece = pieces[DIRECT_STEPS.index(part & DIRECT_STEPS[1])].at[int(part & LAST_STEP > 0)]
         piece[:, :width] = total[pl.ds(start, local_rows), :]
         piece[:, width:] = jnp.where(row == doubling_slot(part, parts), facts, 0.0)
     join_kernel(None, first, second, joined)
 
 
-def spread(place, tokens, ids, after, total, first, second, parts, groups):
+def spread(place, tokens, ids, after, total, first, second, parts):
     piece = jax.ShapeDtypeStruct(
-        (parts // groups, total.shape[0] // parts, total.shape[1] + LANES), jnp.float32
+        (parts // len(DIRECT_STEPS), total.shape[0] // parts, total.shape[1] + LANES), jnp.float32
     )
     joined = jax.ShapeDtypeStruct(
         (first.shape[0] + second.shape[0],) + first.shape[1:], first.dtype
     )
     return pl.pallas_call(
         spread_kernel,
-        out_shape=[piece] * groups + [joined],
+        out_shape=[piece] * len(DIRECT_STEPS) + [joined],
         in_specs=[spec(pltpu.SMEM)] * 3 + [spec(pl.ANY)] + [spec(pltpu.VMEM)] * 3,
-        out_specs=[spec(pltpu.VMEM)] * (groups + 1),
+        out_specs=[spec(pltpu.VMEM)] * (len(DIRECT_STEPS) + 1),
         compiler_params=grant(4),
     )(place, tokens, ids, after, total, first, second)
 
@@ -276,14 +277,15 @@
     arrived = crossed(block, 2)
     total = project(query_out.T, query_act.T, out_basis, act_basis)
     *pieces, block = spread(
-        place, train_tokens, train_ids, other_eigen, total, block, arrived, parts, parts // 2
+        place, train_tokens, train_ids, other_eigen, total, block, arrived, parts
     )
     near = join(pieces[0], block, crossed(block, 1))
-    sums = gather_sum(near, [pieces[0]] + [apart(pieces[d], d) for d in range(1, len(pieces))])
+    terms = [apart(piece, step) for piece, step in zip(pieces[1:], DIRECT_STEPS[1:])]
+    sums = gather_sum(near, [pieces[0]] + terms)
     far = crossed(near, 0)
     other_near = lax.ppermute(near, "fsdp", swap)
     other_far = lax.ppermute(far, "fsdp", swap)
-    own = sums[0] + apart(sums[1], 4)
+    own = sums[0] + apart(sums[1], LAST_STEP)
     other = lax.ppermute(own, "fsdp", swap)
     return score(
         core, own, other, eigenvalues, other_eigen, (near, far, other_near, other_far)

time: 24 us -> 24.6 us (1.025)
  waiting for transfers between devices: 6.07 us -> 8.23 us
  starting transfers between devices: 13.6 us -> 12 us
    ppermute x3, waiting for transfers between devices: 0.85 us -> 2.85 us  [crossed(): return lax.ppermute(x, ('blk', 'fsdp'), pairs)]
    ppermute x3, starting transfers between devices: 7.05 us -> 6.12 us  [crossed(): return lax.ppermute(x, ('blk', 'fsdp'), pairs)]
    ppermute x4, starting transfers between devices: 5.8 us -> 5.29 us  [apart(): return lax.ppermute(x, 'blk', [(s, s ^ distance) for s in range(parts)])]
where the time goes in v17:
time: 24.6 us; the launch traced here: 24.3 us
  starting transfers between devices  12 us (49%)
  waiting for transfers between devices  8.23 us (33%)
  Pallas kernels  2.64 us (11%)
  between operations  1.44 us (6%)
    ppermute x3, starting transfers between devices, crossed(): return lax.ppermute(x, ('blk', 'fsdp'), pairs)  6.12 us
    ppermute x4, starting transfers between devices, apart(): return lax.ppermute(x, 'blk', [(s, s ^ distance) for s in range(parts)])  5.29 us
    ppermute x4, waiting for transfers between devices, apart(): return lax.ppermute(x, 'blk', [(s, s ^ distance) for s in range(parts)])  4.2 us
    ppermute x3, waiting for transfers between devices, crossed(): return lax.ppermute(x, ('blk', 'fsdp'), pairs)  2.85 us
    pallas_call x1, Pallas kernels, score(): pl.pallas_call(score_kernel, out_shape=jax.ShapeDtypeStruct((own.shape[0]...  1.34 us
    ppermute x1, waiting for transfers between devices, direct(): other = lax.ppermute(own, 'fsdp', swap)  1.17 us
    pallas_call x1, Pallas kernels, pack(): pl.pallas_call(pack_kernel, out_shape=jax.ShapeDtypeStruct(shape, train_o...  0.78 us
  transfers between devices with their start and end apart: 11, of which 6 were waited for; matrix products, arithmetic and copies ran while one was open for 0% of the time, Pallas kernels for 5%

profile of v17, /device:TPU:0, one launch (start us, length us, event | category | flops | bytes accessed | tf_op | source)
XLA Modules:
  0.0 24.3 jit_solution(7413978579672413351)
XLA Ops:
  0.0 0.5 %collective-permute-start = (f32[256,256]{1,0:T(8,128)}, f32[256,256]{1,0:T(8,128)S(1)}, u32[]{:S(2)}, u32[]{:S(2)}) collective-permute-start(f32[256,256]{1,0:T(8,128)} %eigen.1), channel_id=1, source_target_pairs={{0,1},{1,0},{2,3},{3,2},{4,5},{5,4},{6,7},{7,6},{8,9},{9,8},{10,11... | collective-permute-start | bytes 786440 | tf_op jit(solution)/shard_map/ppermute | solution.py:275
  0.5 0.8 %shard_map.92.source = bf16[1,32,768]{2,1,0:T(8,128)(2,1)S(1)} custom-call(bf16[1,32,512]{2,1,0:T(8,128)(2,1)} %train_out.1, bf16[1,32,256]{2,1,0:T(8,128)(2,1)} %train_act.1), custom_call_target="tpu_custom_call" | custom-call | tf_op jit(solution)/shard_map/pallas_call | solution.py:48
  1.2 0.0 copy-start
  1.2 0.0 copy-start.1
  1.3 0.0 copy-start.3
  1.3 0.0 copy-start.4
  1.3 3.8 %collective-permute-start.1 = (bf16[1,32,768]{2,1,0:T(8,128)(2,1)S(1)}, bf16[1,32,768]{2,1,0:T(8,128)(2,1)S(1)}, u32[]{:S(2)}, u32[]{:S(2)}) collective-permute-start(bf16[1,32,768]{2,1,0:T(8,128)(2,1)S(1)} %shard_map.93.first), channel_id=1, source_target_pairs={{0,9},{1,8},{2,11},{3,10},{4,13},{5,12},{6,15},{7,14},{8,1},{9,0},... | collective-permute-start | bytes 147464 | tf_op jit(solution)/shard_map/ppermute | solution.py:271
  6.4 0.0 copy-start.2
  6.4 0.5 %shard_map.91.total = f32[64,384]{1,0:T(8,128)S(1)} custom-call(bf16[64,3584]{1,0:T(8,128)(2,1)S(1)} %bitcast.10, bf16[64,1024]{1,0:T(8,128)(2,1)S(1)} %bitcast.11, bf16[3584,256]{1,0:T(8,128)(2,1)S(1)} %copy-done, bf16[1024,128]{1,0:T(8,128)(2,1)S(1)} %copy-done.3), custom_call_target="tpu_custom_call" | custom-call | flops 134217728 | bytes 2686976 | tf_op jit(solution)/shard_map/pallas_call | solution.py:128
  6.9 0.3 %collective-permute-done.1.second = bf16[1,32,768]{2,1,0:T(8,128)(2,1)S(1)} collective-permute-done((bf16[1,32,768]{2,1,0:T(8,128)(2,1)S(1)}, bf16[1,32,768]{2,1,0:T(8,128)(2,1)S(1)}, u32[]{:S(2)}, u32[]{:S(2)}) %collective-permute-start.1) | collective-permute-done | bytes 49184 | tf_op jit(solution)/shard_map/ppermute | solution.py:271
  7.2 0.0 collective-permute-done.after.other_eigen
  7.2 1.4 %collective-permute-start.2 = (bf16[2,32,768]{2,1,0:T(8,128)(2,1)S(1)}, bf16[2,32,768]{2,1,0:T(8,128)(2,1)S(1)}, u32[]{:S(2)}, u32[]{:S(2)}) collective-permute-start(bf16[2,32,768]{2,1,0:T(8,128)(2,1)S(1)} %get-tuple-element.11.first), channel_id=1, source_target_pairs={{0,5},{1,4},{2,7},{3,6},{4,1},{5,0},{6,3},{7,2},{8,13},{9,12},{10,... | collective-permute-start | bytes 294920 | tf_op jit(solution)/shard_map/ppermute | solution.py:271
  8.6 4.4 %collective-permute-start.3 = (f32[2,8,512]{2,1,0:T(8,128)S(1)}, f32[2,8,512]{2,1,0:T(8,128)S(1)}, u32[]{:S(2)}, u32[]{:S(2)}) collective-permute-start(f32[2,8,512]{2,1,0:T(8,128)S(1)} %get-tuple-element.12), channel_id=1, source_target_pairs={{0,10},{2,8},{4,14},{6,12},{8,2},{10,0},{12,6},{14,4},{1,11},{3,9}... | collective-permute-start | bytes 98312 | tf_op jit(solution)/shard_map/ppermute | solution.py:265
  13.0 0.0 collective-permute-start.4
  13.0 0.6 %collective-permute-start.5 = (f32[2,8,512]{2,1,0:T(8,128)S(1)}, f32[2,8,512]{2,1,0:T(8,128)S(1)}, u32[]{:S(2)}, u32[]{:S(2)}) collective-permute-start(f32[2,8,512]{2,1,0:T(8,128)S(1)} %get-tuple-element.14), channel_id=1, source_target_pairs={{0,2},{2,0},{4,6},{6,4},{8,10},{10,8},{12,14},{14,12},{1,3},{3,1},... | collective-permute-start | bytes 98312 | tf_op jit(solution)/shard_map/ppermute | solution.py:265
  13.6 1.0 %collective-permute-start.8 = (bf16[4,32,768]{2,1,0:T(8,128)(2,1)S(1)}, bf16[4,32,768]{2,1,0:T(8,128)(2,1)S(1)}, u32[]{:S(2)}, u32[]{:S(2)}) collective-permute-start(bf16[4,32,768]{2,1,0:T(8,128)(2,1)S(1)} %shard_map.95.after.rest_0_), channel_id=1, source_target_pairs={{0,3},{1,2},{2,1},{3,0},{4,7},{5,6},{6,5},{7,4},{8,11},{9,10},{10,... | collective-permute-start | bytes 589832 | tf_op jit(solution)/shard_map/ppermute | solution.py:271
  14.6 0.4 %collective-permute-done.3.refs_1_ = f32[2,8,512]{2,1,0:T(8,128)S(1)} collective-permute-done((f32[2,8,512]{2,1,0:T(8,128)S(1)}, f32[2,8,512]{2,1,0:T(8,128)S(1)}, u32[]{:S(2)}, u32[]{:S(2)}) %collective-permute-start.3) | collective-permute-done | bytes 32800 | tf_op jit(solution)/shard_map/ppermute | solution.py:265
  14.9 3.0 %collective-permute-done.4.refs_2_ = f32[2,8,512]{2,1,0:T(8,128)S(1)} collective-permute-done((f32[2,8,512]{2,1,0:T(8,128)S(1)}, f32[2,8,512]{2,1,0:T(8,128)S(1)}, u32[]{:S(2)}, u32[]{:S(2)}) %collective-permute-start.4) | collective-permute-done | bytes 32800 | tf_op jit(solution)/shard_map/ppermute | solution.py:265
  18.0 0.3 %collective-permute-start.6 = (f32[8,512]{1,0:T(8,128)S(1)}, f32[8,512]{1,0:T(8,128)S(1)}, u32[]{:S(2)}, u32[]{:S(2)}) collective-permute-start(f32[8,512]{1,0:T(8,128)S(1)} %slice_bitcast_fusion), channel_id=1, source_target_pairs={{0,4},{2,6},{4,0},{6,2},{8,12},{10,14},{12,8},{14,10},{1,5},{3,7},... | collective-permute-start | bytes 49160 | tf_op jit(solution)/shard_map/ppermute | solution.py:265
  18.3 2.6 %collective-permute-done.8.rest_1_ = bf16[4,32,768]{2,1,0:T(8,128)(2,1)S(1)} collective-permute-done((bf16[4,32,768]{2,1,0:T(8,128)(2,1)S(1)}, bf16[4,32,768]{2,1,0:T(8,128)(2,1)S(1)}, u32[]{:S(2)}, u32[]{:S(2)}) %collective-permute-start.8) | collective-permute-done | bytes 196640 | tf_op jit(solution)/shard_map/ppermute | solution.py:271
  20.8 0.1 collective-permute-start.10
  21.0 0.8 %collective-permute-done.6 = f32[8,512]{1,0:T(8,128)S(1)} collective-permute-done((f32[8,512]{1,0:T(8,128)S(1)}, f32[8,512]{1,0:T(8,128)S(1)}, u32[]{:S(2)}, u32[]{:S(2)}) %collective-permute-start.6) | collective-permute-done | bytes 16416 | tf_op jit(solution)/shard_map/ppermute | solution.py:265
  21.8 1.2 %collective-permute-done.7.other = f32[8,512]{1,0:T(8,128)S(1)} collective-permute-done((f32[8,512]{1,0:T(8,128)S(1)}, f32[8,512]{1,0:T(8,128)S(1)}, u32[]{:S(2)}, u32[]{:S(2)}) %collective-permute-start.7) | collective-permute-done | bytes 16416 | tf_op jit(solution)/shard_map/ppermute | solution.py:289
  23.0 1.3 %shard_map.97 = f32[2,16]{1,0:T(2,128)} custom-call(s32[1]{0:T(128)} %bitcast.core_ref, f32[8,512]{1,0:T(8,128)S(1)} %fusion.own, f32[8,512]{1,0:T(8,128)S(1)} %collective-permute-done.7.other, f32[256,256]{1,0:T(8,128)S(1)} %copy-done.2, f32[256,256]{1,0:T(8,128)S(1)} %collective-permute-done.after.other_eigen, ...), custom_call_target="tpu_custom_call" | custom-call | tf_op jit(solution)/shard_map/pallas_call | solution.py:240
  (17 shorter events, 0.1 us)
Async XLA Ops:
  0.0 7.2 %collective-permute-start = (f32[256,256]{1,0:T(8,128)}, f32[256,256]{1,0:T(8,128)S(1)}, u32[]{:S(2)}, u32[]{:S(2)}) collective-permute-start(f32[256,256]{1,0:T(8,128)} %eigen.1), channel_id=1, source_target_pairs={{0,1},{1,0},{2,3},{3,2},{4,5},{5,4},{6,7},{7,6},{8,9},{9,8},{10,11... | collective-permute-start | bytes 786440 | tf_op jit(solution)/shard_map/ppermute | solution.py:275
  1.2 5.1 %copy-start = (bf16[3584,256]{1,0:T(8,128)(2,1)S(1)}, bf16[3584,256]{1,0:T(8,128)(2,1)}, u32[]{:S(2)}) copy-start(bf16[3584,256]{1,0:T(8,128)(2,1)} %out_basis.1) | copy-start | bytes 5505028
  1.2 5.1 %copy-start.1 = (bf16[3584,64]{0,1:T(8,128)(2,1)S(1)}, bf16[3584,64]{0,1:T(8,128)(2,1)}, u32[]{:S(2)}) copy-start(bf16[3584,64]{0,1:T(8,128)(2,1)} %param.9) | copy-start | bytes 1376260
  1.3 5.1 %copy-start.3 = (bf16[1024,128]{1,0:T(8,128)(2,1)S(1)}, bf16[1024,128]{1,0:T(8,128)(2,1)}, u32[]{:S(2)}) copy-start(bf16[1024,128]{1,0:T(8,128)(2,1)} %act_basis.1) | copy-start | bytes 786436
  1.3 5.1 %copy-start.4 = (bf16[1024,64]{0,1:T(8,128)(2,1)S(1)}, bf16[1024,64]{0,1:T(8,128)(2,1)}, u32[]{:S(2)}) copy-start(bf16[1024,64]{0,1:T(8,128)(2,1)} %param.10) | copy-start | bytes 393220
  1.3 5.9 %collective-permute-start.1 = (bf16[1,32,768]{2,1,0:T(8,128)(2,1)S(1)}, bf16[1,32,768]{2,1,0:T(8,128)(2,1)S(1)}, u32[]{:S(2)}, u32[]{:S(2)}) collective-permute-start(bf16[1,32,768]{2,1,0:T(8,128)(2,1)S(1)} %shard_map.93.first), channel_id=1, source_target_pairs={{0,9},{1,8},{2,11},{3,10},{4,13},{5,12},{6,15},{7,14},{8,1},{9,0},... | collective-permute-start | bytes 147464 | tf_op jit(solution)/shard_map/ppermute | solution.py:271
  6.4 16.6 %copy-start.2 = (f32[256,256]{1,0:T(8,128)S(1)}, f32[256,256]{1,0:T(8,128)}, u32[]{:S(2)}) copy-start(f32[256,256]{1,0:T(8,128)} %eigen.1) | copy-start | bytes 786436
  7.2 6.3 %collective-permute-start.2 = (bf16[2,32,768]{2,1,0:T(8,128)(2,1)S(1)}, bf16[2,32,768]{2,1,0:T(8,128)(2,1)S(1)}, u32[]{:S(2)}, u32[]{:S(2)}) collective-permute-start(bf16[2,32,768]{2,1,0:T(8,128)(2,1)S(1)} %get-tuple-element.11.first), channel_id=1, source_target_pairs={{0,5},{1,4},{2,7},{3,6},{4,1},{5,0},{6,3},{7,2},{8,13},{9,12},{10,... | collective-permute-start | bytes 294920 | tf_op jit(solution)/shard_map/ppermute | solution.py:271
  8.6 6.4 %collective-permute-start.3 = (f32[2,8,512]{2,1,0:T(8,128)S(1)}, f32[2,8,512]{2,1,0:T(8,128)S(1)}, u32[]{:S(2)}, u32[]{:S(2)}) collective-permute-start(f32[2,8,512]{2,1,0:T(8,128)S(1)} %get-tuple-element.12), channel_id=1, source_target_pairs={{0,10},{2,8},{4,14},{6,12},{8,2},{10,0},{12,6},{14,4},{1,11},{3,9}... | collective-permute-start | bytes 98312 | tf_op jit(solution)/shard_map/ppermute | solution.py:265
  13.0 5.0 %collective-permute-start.4 = (f32[2,8,512]{2,1,0:T(8,128)S(1)}, f32[2,8,512]{2,1,0:T(8,128)S(1)}, u32[]{:S(2)}, u32[]{:S(2)}) collective-permute-start(f32[2,8,512]{2,1,0:T(8,128)S(1)} %get-tuple-element.13), channel_id=1, source_target_pairs={{0,8},{2,10},{4,12},{6,14},{8,0},{10,2},{12,4},{14,6},{1,9},{3,11}... | collective-permute-start | bytes 98312 | tf_op jit(solution)/shard_map/ppermute | solution.py:265
  13.0 5.0 %collective-permute-start.5 = (f32[2,8,512]{2,1,0:T(8,128)S(1)}, f32[2,8,512]{2,1,0:T(8,128)S(1)}, u32[]{:S(2)}, u32[]{:S(2)}) collective-permute-start(f32[2,8,512]{2,1,0:T(8,128)S(1)} %get-tuple-element.14), channel_id=1, source_target_pairs={{0,2},{2,0},{4,6},{6,4},{8,10},{10,8},{12,14},{14,12},{1,3},{3,1},... | collective-permute-start | bytes 98312 | tf_op jit(solution)/shard_map/ppermute | solution.py:265
  13.6 7.3 %collective-permute-start.8 = (bf16[4,32,768]{2,1,0:T(8,128)(2,1)S(1)}, bf16[4,32,768]{2,1,0:T(8,128)(2,1)S(1)}, u32[]{:S(2)}, u32[]{:S(2)}) collective-permute-start(bf16[4,32,768]{2,1,0:T(8,128)(2,1)S(1)} %shard_map.95.after.rest_0_), channel_id=1, source_target_pairs={{0,3},{1,2},{2,1},{3,0},{4,7},{5,6},{6,5},{7,4},{8,11},{9,10},{10,... | collective-permute-start | bytes 589832 | tf_op jit(solution)/shard_map/ppermute | solution.py:271
  18.0 3.8 %collective-permute-start.6 = (f32[8,512]{1,0:T(8,128)S(1)}, f32[8,512]{1,0:T(8,128)S(1)}, u32[]{:S(2)}, u32[]{:S(2)}) collective-permute-start(f32[8,512]{1,0:T(8,128)S(1)} %slice_bitcast_fusion), channel_id=1, source_target_pairs={{0,4},{2,6},{4,0},{6,2},{8,12},{10,14},{12,8},{14,10},{1,5},{3,7},... | collective-permute-start | bytes 49160 | tf_op jit(solution)/shard_map/ppermute | solution.py:265
  18.3 4.7 %collective-permute-start.9 = (bf16[4,32,768]{2,1,0:T(8,128)(2,1)S(1)}, bf16[4,32,768]{2,1,0:T(8,128)(2,1)S(1)}, u32[]{:S(2)}, u32[]{:S(2)}) collective-permute-start(bf16[4,32,768]{2,1,0:T(8,128)(2,1)S(1)} %shard_map.95.after.rest_0_), channel_id=1, source_target_pairs={{0,1},{1,0},{2,3},{3,2},{4,5},{5,4},{6,7},{7,6},{8,9},{9,8},{10,11... | collective-permute-start | bytes 589832 | tf_op jit(solution)/shard_map/ppermute | solution.py:286
  20.8 2.1 %collective-permute-start.10 = (bf16[4,32,768]{2,1,0:T(8,128)(2,1)S(1)}, bf16[4,32,768]{2,1,0:T(8,128)(2,1)S(1)}, u32[]{:S(2)}, u32[]{:S(2)}) collective-permute-start(bf16[4,32,768]{2,1,0:T(8,128)(2,1)S(1)} %collective-permute-done.8.rest_1_), channel_id=1, source_target_pairs={{0,1},{1,0},{2,3},{3,2},{4,5},{5,4},{6,7},{7,6},{8,9},{9,8},{10,11... | collective-permute-start | bytes 589832 | tf_op jit(solution)/shard_map/ppermute | solution.py:287
  21.8 1.2 %collective-permute-start.7 = (f32[8,512]{1,0:T(8,128)S(1)}, f32[8,512]{1,0:T(8,128)S(1)}, u32[]{:S(2)}, u32[]{:S(2)}) collective-permute-start(f32[8,512]{1,0:T(8,128)S(1)} %fusion.own), channel_id=1, source_target_pairs={{0,1},{1,0},{2,3},{3,2},{4,5},{5,4},{6,7},{7,6},{8,9},{9,8},{10,11... | collective-permute-start | bytes 49160 | tf_op jit(solution)/shard_map/ppermute | solution.py:289

commit v18 on v16

--- a/solution.py
+++ b/solution.py
@@ -138,8 +138,7 @@
 
 
 def doubling_slot(distance, parts):
-    bits = parts.bit_length() - 1
-    return sum(1 << (bits - 1 - i) for i in range(bits) if distance >> i & 1)
+    return distance // 2 + distance % 2 * (parts // 2)
 
 
 def spread_kernel(place_ref, tokens_ref, ids_ref, after, total, first, second, *rest):
@@ -273,12 +272,12 @@
     core = lax.axis_index("fsdp").reshape(1)
     other_eigen = lax.ppermute(eigenvalues, "fsdp", swap)
     block = relay(pack(train_out, train_act))
-    arrived = crossed(block, 2)
+    arrived = crossed(block, 1)
     total = project(query_out.T, query_act.T, out_basis, act_basis)
     *pieces, block = spread(
         place, train_tokens, train_ids, other_eigen, total, block, arrived, parts, parts // 2
     )
-    near = join(pieces[0], block, crossed(block, 1))
+    near = join(pieces[0], block, crossed(block, 2))
     far_first = reversed(range(1, len(pieces)))
     terms = [pieces[0]] + [apart(pieces[d], d) for d in far_first]
     sums = gather_sum(near, terms)

time: 24 us -> 24.2 us (level)
  waiting for transfers between devices: 3.96 us -> 8.14 us
  starting transfers between devices: 15.7 us -> 11.7 us
    ppermute x3, waiting for transfers between devices: 0.62 us -> 7.13 us  [crossed(): return lax.ppermute(x, ('blk', 'fsdp'), pairs)]
    ppermute x4, starting transfers between devices: 7.35 us -> 4.22 us  [apart(): return lax.ppermute(x, 'blk', [(s, s ^ distance) for s in range(parts)])]
    ppermute x4, waiting for transfers between devices: 2.16 us -> 0.11 us  [apart(): return lax.ppermute(x, 'blk', [(s, s ^ distance) for s in range(parts)])]
    ppermute x3, starting transfers between devices: 7.69 us -> 6.48 us  [crossed(): return lax.ppermute(x, ('blk', 'fsdp'), pairs)]
    ppermute x1, starting transfers between devices: 0.01 us -> 0.45 us  [direct(): other = lax.ppermute(own, 'fsdp', swap)]
    ppermute x1, waiting for transfers between devices: 1.17 us -> 0.89 us  [direct(): other = lax.ppermute(own, 'fsdp', swap)]
  transfers between devices with their start and end apart: 11 -> 11, of which waited for: 7 -> 5; matrix products, arithmetic and copies ran while one was open for 0% -> 0% of each run, Pallas kernels for 5% -> 5%
where the time goes in v18:
time: 24.2 us; the launch traced here: 24 us
  starting transfers between devices  11.7 us (48%)
  waiting for transfers between devices  8.14 us (34%)
  Pallas kernels  2.64 us (11%)
  between operations  1.43 us (6%)
    ppermute x3, waiting for transfers between devices, crossed(): return lax.ppermute(x, ('blk', 'fsdp'), pairs)  7.13 us
    ppermute x3, starting transfers between devices, crossed(): return lax.ppermute(x, ('blk', 'fsdp'), pairs)  6.48 us
    ppermute x4, starting transfers between devices, apart(): return lax.ppermute(x, 'blk', [(s, s ^ distance) for s in range(parts)])  4.22 us
    pallas_call x1, Pallas kernels, score(): pl.pallas_call(score_kernel, out_shape=jax.ShapeDtypeStruct((own.shape[0]...  1.34 us
    ppermute x1, waiting for transfers between devices, direct(): other = lax.ppermute(own, 'fsdp', swap)  0.89 us
    pallas_call x1, Pallas kernels, pack(): pl.pallas_call(pack_kernel, out_shape=jax.ShapeDtypeStruct(shape, train_o...  0.78 us
  transfers between devices with their start and end apart: 11, of which 5 were waited for; matrix products, arithmetic and copies ran while one was open for 0% of the time, Pallas kernels for 5%

profile of v18, /device:TPU:0, one launch (start us, length us, event | category | flops | bytes accessed | tf_op | source)
XLA Modules:
  0.0 24.0 jit_solution(11662633605407312728)
XLA Ops:
  0.0 0.5 %collective-permute-start = (f32[256,256]{1,0:T(8,128)}, f32[256,256]{1,0:T(8,128)S(1)}, u32[]{:S(2)}, u32[]{:S(2)}) collective-permute-start(f32[256,256]{1,0:T(8,128)} %eigen.1), channel_id=1, source_target_pairs={{0,1},{1,0},{2,3},{3,2},{4,5},{5,4},{6,7},{7,6},{8,9},{9,8},{10,11... | collective-permute-start | bytes 786440 | tf_op jit(solution)/shard_map/ppermute | solution.py:273
  0.5 0.8 %shard_map.92.source = bf16[1,32,768]{2,1,0:T(8,128)(2,1)S(1)} custom-call(bf16[1,32,512]{2,1,0:T(8,128)(2,1)} %train_out.1, bf16[1,32,256]{2,1,0:T(8,128)(2,1)} %train_act.1), custom_call_target="tpu_custom_call" | custom-call | tf_op jit(solution)/shard_map/pallas_call | solution.py:46
  1.2 0.0 copy-start
  1.2 0.0 copy-start.1
  1.3 0.0 copy-start.3
  1.3 0.0 copy-start.4
  1.3 2.8 %collective-permute-start.1 = (bf16[1,32,768]{2,1,0:T(8,128)(2,1)S(1)}, bf16[1,32,768]{2,1,0:T(8,128)(2,1)S(1)}, u32[]{:S(2)}, u32[]{:S(2)}) collective-permute-start(bf16[1,32,768]{2,1,0:T(8,128)(2,1)S(1)} %shard_map.93.first), channel_id=1, source_target_pairs={{0,5},{1,4},{2,7},{3,6},{4,1},{5,0},{6,3},{7,2},{8,13},{9,12},{10,... | collective-permute-start | bytes 147464 | tf_op jit(solution)/shard_map/ppermute | solution.py:269
  5.4 0.0 copy-start.2
  5.4 0.5 %shard_map.91.total = f32[64,384]{1,0:T(8,128)S(1)} custom-call(bf16[64,3584]{1,0:T(8,128)(2,1)S(1)} %bitcast.10, bf16[64,1024]{1,0:T(8,128)(2,1)S(1)} %bitcast.11, bf16[3584,256]{1,0:T(8,128)(2,1)S(1)} %copy-done, bf16[1024,128]{1,0:T(8,128)(2,1)S(1)} %copy-done.3), custom_call_target="tpu_custom_call" | custom-call | flops 134217728 | bytes 2686976 | tf_op jit(solution)/shard_map/pallas_call | solution.py:126
  5.9 0.3 %collective-permute-done.1.second = bf16[1,32,768]{2,1,0:T(8,128)(2,1)S(1)} collective-permute-done((bf16[1,32,768]{2,1,0:T(8,128)(2,1)S(1)}, bf16[1,32,768]{2,1,0:T(8,128)(2,1)S(1)}, u32[]{:S(2)}, u32[]{:S(2)}) %collective-permute-start.1) | collective-permute-done | bytes 49184 | tf_op jit(solution)/shard_map/ppermute | solution.py:269
  6.2 2.5 %collective-permute-start.2 = (bf16[2,32,768]{2,1,0:T(8,128)(2,1)S(1)}, bf16[2,32,768]{2,1,0:T(8,128)(2,1)S(1)}, u32[]{:S(2)}, u32[]{:S(2)}) collective-permute-start(bf16[2,32,768]{2,1,0:T(8,128)(2,1)S(1)} %get-tuple-element.11.first), channel_id=1, source_target_pairs={{0,9},{1,8},{2,11},{3,10},{4,13},{5,12},{6,15},{7,14},{8,1},{9,0},... | collective-permute-start | bytes 294920 | tf_op jit(solution)/shard_map/ppermute | solution.py:269
  8.7 2.5 %collective-permute-start.3 = (f32[2,8,512]{2,1,0:T(8,128)S(1)}, f32[2,8,512]{2,1,0:T(8,128)S(1)}, u32[]{:S(2)}, u32[]{:S(2)}) collective-permute-start(f32[2,8,512]{2,1,0:T(8,128)S(1)} %get-tuple-element.12), channel_id=1, source_target_pairs={{0,6},{2,4},{4,2},{6,0},{8,14},{10,12},{12,10},{14,8},{1,7},{3,5},... | collective-permute-start | bytes 98312 | tf_op jit(solution)/shard_map/ppermute | solution.py:263
  11.2 0.5 %collective-permute-start.4 = (f32[2,8,512]{2,1,0:T(8,128)S(1)}, f32[2,8,512]{2,1,0:T(8,128)S(1)}, u32[]{:S(2)}, u32[]{:S(2)}) collective-permute-start(f32[2,8,512]{2,1,0:T(8,128)S(1)} %get-tuple-element.13), channel_id=1, source_target_pairs={{0,4},{2,6},{4,0},{6,2},{8,12},{10,14},{12,8},{14,10},{1,5},{3,7},... | collective-permute-start | bytes 98312 | tf_op jit(solution)/shard_map/ppermute | solution.py:263
  11.6 0.5 %collective-permute-start.5 = (f32[2,8,512]{2,1,0:T(8,128)S(1)}, f32[2,8,512]{2,1,0:T(8,128)S(1)}, u32[]{:S(2)}, u32[]{:S(2)}) collective-permute-start(f32[2,8,512]{2,1,0:T(8,128)S(1)} %get-tuple-element.14), channel_id=1, source_target_pairs={{0,2},{2,0},{4,6},{6,4},{8,10},{10,8},{12,14},{14,12},{1,3},{3,1},... | collective-permute-start | bytes 98312 | tf_op jit(solution)/shard_map/ppermute | solution.py:263
  12.2 2.0 %collective-permute-done.2.second = bf16[2,32,768]{2,1,0:T(8,128)(2,1)S(1)} collective-permute-done((bf16[2,32,768]{2,1,0:T(8,128)(2,1)S(1)}, bf16[2,32,768]{2,1,0:T(8,128)(2,1)S(1)}, u32[]{:S(2)}, u32[]{:S(2)}) %collective-permute-start.2) | collective-permute-done | bytes 98336 | tf_op jit(solution)/shard_map/ppermute | solution.py:269
  14.2 1.2 %collective-permute-start.8 = (bf16[4,32,768]{2,1,0:T(8,128)(2,1)S(1)}, bf16[4,32,768]{2,1,0:T(8,128)(2,1)S(1)}, u32[]{:S(2)}, u32[]{:S(2)}) collective-permute-start(bf16[4,32,768]{2,1,0:T(8,128)(2,1)S(1)} %shard_map.95.after.rest_0_), channel_id=1, source_target_pairs={{0,3},{1,2},{2,1},{3,0},{4,7},{5,6},{6,5},{7,4},{8,11},{9,10},{10,... | collective-permute-start | bytes 589832 | tf_op jit(solution)/shard_map/ppermute | solution.py:269
  15.4 0.1 collective-permute-done.5.refs_3_
  15.6 0.7 %collective-permute-start.6 = (f32[8,512]{1,0:T(8,128)S(1)}, f32[8,512]{1,0:T(8,128)S(1)}, u32[]{:S(2)}, u32[]{:S(2)}) collective-permute-start(f32[8,512]{1,0:T(8,128)S(1)} %slice_bitcast_fusion), channel_id=1, source_target_pairs={{0,8},{2,10},{4,12},{6,14},{8,0},{10,2},{12,4},{14,6},{1,9},{3,11}... | collective-permute-start | bytes 49160 | tf_op jit(solution)/shard_map/ppermute | solution.py:263
  16.3 0.0 collective-permute-start.9
  16.3 4.8 %collective-permute-done.8.rest_1_ = bf16[4,32,768]{2,1,0:T(8,128)(2,1)S(1)} collective-permute-done((bf16[4,32,768]{2,1,0:T(8,128)(2,1)S(1)}, bf16[4,32,768]{2,1,0:T(8,128)(2,1)S(1)}, u32[]{:S(2)}, u32[]{:S(2)}) %collective-permute-start.8) | collective-permute-done | bytes 196640 | tf_op jit(solution)/shard_map/ppermute | solution.py:269
  21.1 0.1 collective-permute-start.10
  21.3 0.5 %collective-permute-start.7 = (f32[8,512]{1,0:T(8,128)S(1)}, f32[8,512]{1,0:T(8,128)S(1)}, u32[]{:S(2)}, u32[]{:S(2)}) collective-permute-start(f32[8,512]{1,0:T(8,128)S(1)} %fusion.own), channel_id=1, source_target_pairs={{0,1},{1,0},{2,3},{3,2},{4,5},{5,4},{6,7},{7,6},{8,9},{9,8},{10,11... | collective-permute-start | bytes 49160 | tf_op jit(solution)/shard_map/ppermute | solution.py:288
  21.7 0.9 %collective-permute-done.7.other = f32[8,512]{1,0:T(8,128)S(1)} collective-permute-done((f32[8,512]{1,0:T(8,128)S(1)}, f32[8,512]{1,0:T(8,128)S(1)}, u32[]{:S(2)}, u32[]{:S(2)}) %collective-permute-start.7) | collective-permute-done | bytes 16416 | tf_op jit(solution)/shard_map/ppermute | solution.py:288
  22.6 1.3 %shard_map.97 = f32[2,16]{1,0:T(2,128)} custom-call(s32[1]{0:T(128)} %bitcast.core_ref, f32[8,512]{1,0:T(8,128)S(1)} %fusion.own, f32[8,512]{1,0:T(8,128)S(1)} %collective-permute-done.7.other, f32[256,256]{1,0:T(8,128)S(1)} %copy-done.2, f32[256,256]{1,0:T(8,128)S(1)} %collective-permute-done.after.other_eigen, ...), custom_call_target="tpu_custom_call" | custom-call | tf_op jit(solution)/shard_map/pallas_call | solution.py:238
  (17 shorter events, 0.1 us)
Async XLA Ops:
  0.0 6.2 %collective-permute-start = (f32[256,256]{1,0:T(8,128)}, f32[256,256]{1,0:T(8,128)S(1)}, u32[]{:S(2)}, u32[]{:S(2)}) collective-permute-start(f32[256,256]{1,0:T(8,128)} %eigen.1), channel_id=1, source_target_pairs={{0,1},{1,0},{2,3},{3,2},{4,5},{5,4},{6,7},{7,6},{8,9},{9,8},{10,11... | collective-permute-start | bytes 786440 | tf_op jit(solution)/shard_map/ppermute | solution.py:273
  1.2 4.1 %copy-start = (bf16[3584,256]{1,0:T(8,128)(2,1)S(1)}, bf16[3584,256]{1,0:T(8,128)(2,1)}, u32[]{:S(2)}) copy-start(bf16[3584,256]{1,0:T(8,128)(2,1)} %out_basis.1) | copy-start | bytes 5505028
  1.2 4.1 %copy-start.1 = (bf16[3584,64]{0,1:T(8,128)(2,1)S(1)}, bf16[3584,64]{0,1:T(8,128)(2,1)}, u32[]{:S(2)}) copy-start(bf16[3584,64]{0,1:T(8,128)(2,1)} %param.9) | copy-start | bytes 1376260
  1.3 4.1 %copy-start.3 = (bf16[1024,128]{1,0:T(8,128)(2,1)S(1)}, bf16[1024,128]{1,0:T(8,128)(2,1)}, u32[]{:S(2)}) copy-start(bf16[1024,128]{1,0:T(8,128)(2,1)} %act_basis.1) | copy-start | bytes 786436
  1.3 4.1 %copy-start.4 = (bf16[1024,64]{0,1:T(8,128)(2,1)S(1)}, bf16[1024,64]{0,1:T(8,128)(2,1)}, u32[]{:S(2)}) copy-start(bf16[1024,64]{0,1:T(8,128)(2,1)} %param.10) | copy-start | bytes 393220
  1.3 4.9 %collective-permute-start.1 = (bf16[1,32,768]{2,1,0:T(8,128)(2,1)S(1)}, bf16[1,32,768]{2,1,0:T(8,128)(2,1)S(1)}, u32[]{:S(2)}, u32[]{:S(2)}) collective-permute-start(bf16[1,32,768]{2,1,0:T(8,128)(2,1)S(1)} %shard_map.93.first), channel_id=1, source_target_pairs={{0,5},{1,4},{2,7},{3,6},{4,1},{5,0},{6,3},{7,2},{8,13},{9,12},{10,... | collective-permute-start | bytes 147464 | tf_op jit(solution)/shard_map/ppermute | solution.py:269
  5.4 17.2 %copy-start.2 = (f32[256,256]{1,0:T(8,128)S(1)}, f32[256,256]{1,0:T(8,128)}, u32[]{:S(2)}) copy-start(f32[256,256]{1,0:T(8,128)} %eigen.1) | copy-start | bytes 786436
  6.2 8.0 %collective-permute-start.2 = (bf16[2,32,768]{2,1,0:T(8,128)(2,1)S(1)}, bf16[2,32,768]{2,1,0:T(8,128)(2,1)S(1)}, u32[]{:S(2)}, u32[]{:S(2)}) collective-permute-start(bf16[2,32,768]{2,1,0:T(8,128)(2,1)S(1)} %get-tuple-element.11.first), channel_id=1, source_target_pairs={{0,9},{1,8},{2,11},{3,10},{4,13},{5,12},{6,15},{7,14},{8,1},{9,0},... | collective-permute-start | bytes 294920 | tf_op jit(solution)/shard_map/ppermute | solution.py:269
  8.7 6.8 %collective-permute-start.3 = (f32[2,8,512]{2,1,0:T(8,128)S(1)}, f32[2,8,512]{2,1,0:T(8,128)S(1)}, u32[]{:S(2)}, u32[]{:S(2)}) collective-permute-start(f32[2,8,512]{2,1,0:T(8,128)S(1)} %get-tuple-element.12), channel_id=1, source_target_pairs={{0,6},{2,4},{4,2},{6,0},{8,14},{10,12},{12,10},{14,8},{1,7},{3,5},... | collective-permute-start | bytes 98312 | tf_op jit(solution)/shard_map/ppermute | solution.py:263
  11.2 4.3 %collective-permute-start.4 = (f32[2,8,512]{2,1,0:T(8,128)S(1)}, f32[2,8,512]{2,1,0:T(8,128)S(1)}, u32[]{:S(2)}, u32[]{:S(2)}) collective-permute-start(f32[2,8,512]{2,1,0:T(8,128)S(1)} %get-tuple-element.13), channel_id=1, source_target_pairs={{0,4},{2,6},{4,0},{6,2},{8,12},{10,14},{12,8},{14,10},{1,5},{3,7},... | collective-permute-start | bytes 98312 | tf_op jit(solution)/shard_map/ppermute | solution.py:263
  11.6 3.9 %collective-permute-start.5 = (f32[2,8,512]{2,1,0:T(8,128)S(1)}, f32[2,8,512]{2,1,0:T(8,128)S(1)}, u32[]{:S(2)}, u32[]{:S(2)}) collective-permute-start(f32[2,8,512]{2,1,0:T(8,128)S(1)} %get-tuple-element.14), channel_id=1, source_target_pairs={{0,2},{2,0},{4,6},{6,4},{8,10},{10,8},{12,14},{14,12},{1,3},{3,1},... | collective-permute-start | bytes 98312 | tf_op jit(solution)/shard_map/ppermute | solution.py:263
  14.2 7.0 %collective-permute-start.8 = (bf16[4,32,768]{2,1,0:T(8,128)(2,1)S(1)}, bf16[4,32,768]{2,1,0:T(8,128)(2,1)S(1)}, u32[]{:S(2)}, u32[]{:S(2)}) collective-permute-start(bf16[4,32,768]{2,1,0:T(8,128)(2,1)S(1)} %shard_map.95.after.rest_0_), channel_id=1, source_target_pairs={{0,3},{1,2},{2,1},{3,0},{4,7},{5,6},{6,5},{7,4},{8,11},{9,10},{10,... | collective-permute-start | bytes 589832 | tf_op jit(solution)/shard_map/ppermute | solution.py:269
  15.6 5.7 %collective-permute-start.6 = (f32[8,512]{1,0:T(8,128)S(1)}, f32[8,512]{1,0:T(8,128)S(1)}, u32[]{:S(2)}, u32[]{:S(2)}) collective-permute-start(f32[8,512]{1,0:T(8,128)S(1)} %slice_bitcast_fusion), channel_id=1, source_target_pairs={{0,8},{2,10},{4,12},{6,14},{8,0},{10,2},{12,4},{14,6},{1,9},{3,11}... | collective-permute-start | bytes 49160 | tf_op jit(solution)/shard_map/ppermute | solution.py:263
  16.3 6.3 %collective-permute-start.9 = (bf16[4,32,768]{2,1,0:T(8,128)(2,1)S(1)}, bf16[4,32,768]{2,1,0:T(8,128)(2,1)S(1)}, u32[]{:S(2)}, u32[]{:S(2)}) collective-permute-start(bf16[4,32,768]{2,1,0:T(8,128)(2,1)S(1)} %shard_map.95.after.rest_0_), channel_id=1, source_target_pairs={{0,1},{1,0},{2,3},{3,2},{4,5},{5,4},{6,7},{7,6},{8,9},{9,8},{10,11... | collective-permute-start | bytes 589832 | tf_op jit(solution)/shard_map/ppermute | solution.py:285
  21.1 1.5 %collective-permute-start.10 = (bf16[4,32,768]{2,1,0:T(8,128)(2,1)S(1)}, bf16[4,32,768]{2,1,0:T(8,128)(2,1)S(1)}, u32[]{:S(2)}, u32[]{:S(2)}) collective-permute-start(bf16[4,32,768]{2,1,0:T(8,128)(2,1)S(1)} %collective-permute-done.8.rest_1_), channel_id=1, source_target_pairs={{0,1},{1,0},{2,3},{3,2},{4,5},{5,4},{6,7},{7,6},{8,9},{9,8},{10,11... | collective-permute-start | bytes 589832 | tf_op jit(solution)/shard_map/ppermute | solution.py:286
  21.3 1.3 %collective-permute-start.7 = (f32[8,512]{1,0:T(8,128)S(1)}, f32[8,512]{1,0:T(8,128)S(1)}, u32[]{:S(2)}, u32[]{:S(2)}) collective-permute-start(f32[8,512]{1,0:T(8,128)S(1)} %fusion.own), channel_id=1, source_target_pairs={{0,1},{1,0},{2,3},{3,2},{4,5},{5,4},{6,7},{7,6},{8,9},{9,8},{10,11... | collective-permute-start | bytes 49160 | tf_op jit(solution)/shard_map/ppermute | solution.py:288

commit v19 on v16

--- a/solution.py
+++ b/solution.py
@@ -107,6 +107,21 @@
         out_specs=spec(pltpu.VMEM),
         compiler_params=grant(4),
     )(after, *terms)
+
+
+def hold_kernel(after, source, target):
+    del after
+    target[...] = source[...]
+
+
+def hold(after, source):
+    return pl.pallas_call(
+        hold_kernel,
+        out_shape=jax.ShapeDtypeStruct(source.shape, source.dtype),
+        in_specs=[spec(pl.ANY), spec(pltpu.VMEM)],
+        out_specs=spec(pltpu.VMEM),
+        compiler_params=grant(2),
+    )(after, source)
 
 
 def project_kernel(query_out, query_act, out_basis, act_basis, total):
@@ -142,8 +157,7 @@
     return sum(1 << (bits - 1 - i) for i in range(bits) if distance >> i & 1)
 
 
-def spread_kernel(place_ref, tokens_ref, ids_ref, after, total, first, second, *rest):
-    del after
+def spread_kernel(place_ref, tokens_ref, ids_ref, total, first, second, *rest):
     pieces, joined = rest[:-1], rest[-1]
     groups = len(pieces)
     each, local_rows, _ = pieces[0].shape
@@ -160,7 +174,7 @@
     join_kernel(None, first, second, joined)
 
 
-def spread(place, tokens, ids, after, total, first, second, parts, groups):
+def spread(place, tokens, ids, total, first, second, parts, groups):
     piece = jax.ShapeDtypeStruct(
         (parts // groups, total.shape[0] // parts, total.shape[1] + LANES), jnp.float32
     )
@@ -170,10 +184,10 @@
     return pl.pallas_call(
         spread_kernel,
         out_shape=[piece] * groups + [joined],
-        in_specs=[spec(pltpu.SMEM)] * 3 + [spec(pl.ANY)] + [spec(pltpu.VMEM)] * 3,
+        in_specs=[spec(pltpu.SMEM)] * 3 + [spec(pltpu.VMEM)] * 3,
         out_specs=[spec(pltpu.VMEM)] * (groups + 1),
         compiler_params=grant(4),
-    )(place, tokens, ids, after, total, first, second)
+    )(place, tokens, ids, total, first, second)
 
 
 def split_three(x):
@@ -271,18 +285,18 @@
 
     place = lax.axis_index("blk").reshape(1)
     core = lax.axis_index("fsdp").reshape(1)
-    other_eigen = lax.ppermute(eigenvalues, "fsdp", swap)
     block = relay(pack(train_out, train_act))
     arrived = crossed(block, 2)
     total = project(query_out.T, query_act.T, out_basis, act_basis)
     *pieces, block = spread(
-        place, train_tokens, train_ids, other_eigen, total, block, arrived, parts, parts // 2
+        place, train_tokens, train_ids, total, block, arrived, parts, parts // 2
     )
     near = join(pieces[0], block, crossed(block, 1))
     far_first = reversed(range(1, len(pieces)))
     terms = [pieces[0]] + [apart(pieces[d], d) for d in far_first]
     sums = gather_sum(near, terms)
     far = crossed(near, 0)
+    other_eigen = lax.ppermute(hold(near, eigenvalues), "fsdp", swap)
     other_near = lax.ppermute(near, "fsdp", swap)
     other_far = lax.ppermute(far, "fsdp", swap)
     own = sums[0] + apart(sums[1], 4)

time: 24 us -> 24 us (level)
  starting transfers between devices: 15.7 us -> 14.8 us
  waiting for transfers between devices: 3.96 us -> 4.76 us
    ppermute x4, waiting for transfers between devices: 2.16 us -> 3.1 us  [apart(): return lax.ppermute(x, 'blk', [(s, s ^ distance) for s in range(parts)])]
    ppermute x3, starting transfers between devices: 7.69 us -> 7.12 us  [crossed(): return lax.ppermute(x, ('blk', 'fsdp'), pairs)]
    ppermute x4, starting transfers between devices: 7.35 us -> 6.93 us  [apart(): return lax.ppermute(x, 'blk', [(s, s ^ distance) for s in range(parts)])]
  transfers between devices with their start and end apart: 11 -> 11, of which waited for: 7 -> 6; matrix products, arithmetic and copies ran while one was open for 0% -> 0% of each run, Pallas kernels for 5% -> 2%
where the time goes in v19:
time: 24 us; the launch traced here: 23.7 us
  starting transfers between devices  14.8 us (62%)
  waiting for transfers between devices  4.76 us (20%)
  Pallas kernels  2.66 us (11%)
  between operations  1.44 us (6%)
    ppermute x3, starting transfers between devices, crossed(): return lax.ppermute(x, ('blk', 'fsdp'), pairs)  7.12 us
    ppermute x4, starting transfers between devices, apart(): return lax.ppermute(x, 'blk', [(s, s ^ distance) for s in range(parts)])  6.93 us
    ppermute x4, waiting for transfers between devices, apart(): return lax.ppermute(x, 'blk', [(s, s ^ distance) for s in range(parts)])  3.1 us
    pallas_call x1, Pallas kernels, score(): pl.pallas_call(score_kernel, out_shape=jax.ShapeDtypeStruct((own.shape[0]...  1.34 us
    ppermute x1, waiting for transfers between devices, direct(): other = lax.ppermute(own, 'fsdp', swap)  1.17 us
    pallas_call x1, Pallas kernels, pack(): pl.pallas_call(pack_kernel, out_shape=jax.ShapeDtypeStruct(shape, train_o...  0.78 us
  transfers between devices with their start and end apart: 11, of which 6 were waited for; matrix products, arithmetic and copies ran while one was open for 0% of the time, Pallas kernels for 2%

profile of v19, /device:TPU:0, one launch (start us, length us, event | category | flops | bytes accessed | tf_op | source)
XLA Modules:
  0.0 23.7 jit_solution(17511238689808391869)
XLA Ops:
  0.0 0.8 %shard_map.92.source = bf16[1,32,768]{2,1,0:T(8,128)(2,1)S(1)} custom-call(bf16[1,32,512]{2,1,0:T(8,128)(2,1)} %train_out.1, bf16[1,32,256]{2,1,0:T(8,128)(2,1)} %train_act.1), custom_call_target="tpu_custom_call" | custom-call | tf_op jit(solution)/shard_map/pallas_call | solution.py:46
  0.8 0.0 copy-start
  0.8 0.0 copy-start.2
  0.8 0.0 copy-start.3
  0.8 0.0 copy-start.4
  0.8 0.0 copy-start.1
  0.9 3.5 %collective-permute-start = (bf16[1,32,768]{2,1,0:T(8,128)(2,1)S(1)}, bf16[1,32,768]{2,1,0:T(8,128)(2,1)S(1)}, u32[]{:S(2)}, u32[]{:S(2)}) collective-permute-start(bf16[1,32,768]{2,1,0:T(8,128)(2,1)S(1)} %shard_map.93.first), channel_id=1, source_target_pairs={{0,9},{1,8},{2,11},{3,10},{4,13},{5,12},{6,15},{7,14},{8,1},{9,0},... | collective-permute-start | bytes 147464 | tf_op jit(solution)/shard_map/ppermute | solution.py:284
  5.7 0.5 %shard_map.91.total = f32[64,384]{1,0:T(8,128)S(1)} custom-call(bf16[64,3584]{1,0:T(8,128)(2,1)S(1)} %bitcast.10, bf16[64,1024]{1,0:T(8,128)(2,1)S(1)} %bitcast.11, bf16[3584,256]{1,0:T(8,128)(2,1)S(1)} %copy-done, bf16[1024,128]{1,0:T(8,128)(2,1)S(1)} %copy-done.3), custom_call_target="tpu_custom_call" | custom-call | flops 134217728 | bytes 2686976 | tf_op jit(solution)/shard_map/pallas_call | solution.py:141
  6.2 0.3 %collective-permute-done.second = bf16[1,32,768]{2,1,0:T(8,128)(2,1)S(1)} collective-permute-done((bf16[1,32,768]{2,1,0:T(8,128)(2,1)S(1)}, bf16[1,32,768]{2,1,0:T(8,128)(2,1)S(1)}, u32[]{:S(2)}, u32[]{:S(2)}) %collective-permute-start) | collective-permute-done | bytes 49184 | tf_op jit(solution)/shard_map/ppermute | solution.py:284
  6.6 2.3 %collective-permute-start.1 = (bf16[2,32,768]{2,1,0:T(8,128)(2,1)S(1)}, bf16[2,32,768]{2,1,0:T(8,128)(2,1)S(1)}, u32[]{:S(2)}, u32[]{:S(2)}) collective-permute-start(bf16[2,32,768]{2,1,0:T(8,128)(2,1)S(1)} %get-tuple-element.11.first), channel_id=1, source_target_pairs={{0,5},{1,4},{2,7},{3,6},{4,1},{5,0},{6,3},{7,2},{8,13},{9,12},{10,... | collective-permute-start | bytes 294920 | tf_op jit(solution)/shard_map/ppermute | solution.py:284
  8.8 1.3 %collective-permute-start.2 = (f32[2,8,512]{2,1,0:T(8,128)S(1)}, f32[2,8,512]{2,1,0:T(8,128)S(1)}, u32[]{:S(2)}, u32[]{:S(2)}) collective-permute-start(f32[2,8,512]{2,1,0:T(8,128)S(1)} %get-tuple-element.12), channel_id=1, source_target_pairs={{0,6},{2,4},{4,2},{6,0},{8,14},{10,12},{12,10},{14,8},{1,7},{3,5},... | collective-permute-start | bytes 98312 | tf_op jit(solution)/shard_map/ppermute | solution.py:278
  10.1 1.7 %collective-permute-start.3 = (f32[2,8,512]{2,1,0:T(8,128)S(1)}, f32[2,8,512]{2,1,0:T(8,128)S(1)}, u32[]{:S(2)}, u32[]{:S(2)}) collective-permute-start(f32[2,8,512]{2,1,0:T(8,128)S(1)} %get-tuple-element.13), channel_id=1, source_target_pairs={{0,4},{2,6},{4,0},{6,2},{8,12},{10,14},{12,8},{14,10},{1,5},{3,7},... | collective-permute-start | bytes 98312 | tf_op jit(solution)/shard_map/ppermute | solution.py:278
  11.8 0.5 %collective-permute-start.4 = (f32[2,8,512]{2,1,0:T(8,128)S(1)}, f32[2,8,512]{2,1,0:T(8,128)S(1)}, u32[]{:S(2)}, u32[]{:S(2)}) collective-permute-start(f32[2,8,512]{2,1,0:T(8,128)S(1)} %get-tuple-element.14), channel_id=1, source_target_pairs={{0,2},{2,0},{4,6},{6,4},{8,10},{10,8},{12,14},{14,12},{1,3},{3,1},... | collective-permute-start | bytes 98312 | tf_op jit(solution)/shard_map/ppermute | solution.py:278
  12.4 0.0 collective-permute-done.1.second
  12.4 1.3 %collective-permute-start.8 = (bf16[4,32,768]{2,1,0:T(8,128)(2,1)S(1)}, bf16[4,32,768]{2,1,0:T(8,128)(2,1)S(1)}, u32[]{:S(2)}, u32[]{:S(2)}) collective-permute-start(bf16[4,32,768]{2,1,0:T(8,128)(2,1)S(1)} %shard_map.95.after.rest_0_), channel_id=1, source_target_pairs={{0,3},{1,2},{2,1},{3,0},{4,7},{5,6},{6,5},{7,4},{8,11},{9,10},{10,... | collective-permute-start | bytes 589832 | tf_op jit(solution)/shard_map/ppermute | solution.py:284
  13.7 0.4 %collective-permute-start.7 = (f32[256,256]{1,0:T(8,128)S(1)}, f32[256,256]{1,0:T(8,128)S(1)}, u32[]{:S(2)}, u32[]{:S(2)}) collective-permute-start(f32[256,256]{1,0:T(8,128)S(1)} %shard_map.97), channel_id=1, source_target_pairs={{0,1},{1,0},{2,3},{3,2},{4,5},{5,4},{6,7},{7,6},{8,9},{9,8},{10,11... | collective-permute-start | bytes 786440 | tf_op jit(solution)/shard_map/ppermute | solution.py:299
  14.1 0.1 collective-permute-done.2.refs_1_
  14.2 1.8 %collective-permute-done.4.refs_3_ = f32[2,8,512]{2,1,0:T(8,128)S(1)} collective-permute-done((f32[2,8,512]{2,1,0:T(8,128)S(1)}, f32[2,8,512]{2,1,0:T(8,128)S(1)}, u32[]{:S(2)}, u32[]{:S(2)}) %collective-permute-start.4) | collective-permute-done | bytes 32800 | tf_op jit(solution)/shard_map/ppermute | solution.py:278
  16.1 3.4 %collective-permute-start.5 = (f32[8,512]{1,0:T(8,128)S(1)}, f32[8,512]{1,0:T(8,128)S(1)}, u32[]{:S(2)}, u32[]{:S(2)}) collective-permute-start(f32[8,512]{1,0:T(8,128)S(1)} %slice_bitcast_fusion), channel_id=1, source_target_pairs={{0,8},{2,10},{4,12},{6,14},{8,0},{10,2},{12,4},{14,6},{1,9},{3,11}... | collective-permute-start | bytes 49160 | tf_op jit(solution)/shard_map/ppermute | solution.py:278
  19.5 0.2 collective-permute-done.8.rest_1_
  19.6 0.3 %collective-permute-start.10 = (bf16[4,32,768]{2,1,0:T(8,128)(2,1)S(1)}, bf16[4,32,768]{2,1,0:T(8,128)(2,1)S(1)}, u32[]{:S(2)}, u32[]{:S(2)}) collective-permute-start(bf16[4,32,768]{2,1,0:T(8,128)(2,1)S(1)} %collective-permute-done.8.rest_1_), channel_id=1, source_target_pairs={{0,1},{1,0},{2,3},{3,2},{4,5},{5,4},{6,7},{7,6},{8,9},{9,8},{10,11... | collective-permute-start | bytes 589832 | tf_op jit(solution)/shard_map/ppermute | solution.py:301
  20.0 1.2 %collective-permute-done.5 = f32[8,512]{1,0:T(8,128)S(1)} collective-permute-done((f32[8,512]{1,0:T(8,128)S(1)}, f32[8,512]{1,0:T(8,128)S(1)}, u32[]{:S(2)}, u32[]{:S(2)}) %collective-permute-start.5) | collective-permute-done | bytes 16416 | tf_op jit(solution)/shard_map/ppermute | solution.py:278
  21.2 1.2 %collective-permute-done.6.other = f32[8,512]{1,0:T(8,128)S(1)} collective-permute-done((f32[8,512]{1,0:T(8,128)S(1)}, f32[8,512]{1,0:T(8,128)S(1)}, u32[]{:S(2)}, u32[]{:S(2)}) %collective-permute-start.6) | collective-permute-done | bytes 16416 | tf_op jit(solution)/shard_map/ppermute | solution.py:303
  22.4 1.3 %shard_map.98 = f32[2,16]{1,0:T(2,128)} custom-call(s32[1]{0:T(128)} %bitcast.core_ref, f32[8,512]{1,0:T(8,128)S(1)} %fusion.own, f32[8,512]{1,0:T(8,128)S(1)} %collective-permute-done.6.other, f32[256,256]{1,0:T(8,128)S(1)} %copy-done.1, f32[256,256]{1,0:T(8,128)S(1)} %collective-permute-done.7.other_eigen, ...), custom_call_target="tpu_custom_call" | custom-call | tf_op jit(solution)/shard_map/pallas_call | solution.py:253
  (18 shorter events, 0.1 us)
Async XLA Ops:
  0.8 4.9 %copy-start = (bf16[3584,256]{1,0:T(8,128)(2,1)S(1)}, bf16[3584,256]{1,0:T(8,128)(2,1)}, u32[]{:S(2)}) copy-start(bf16[3584,256]{1,0:T(8,128)(2,1)} %out_basis.1) | copy-start | bytes 5505028
  0.8 4.9 %copy-start.2 = (bf16[3584,64]{0,1:T(8,128)(2,1)S(1)}, bf16[3584,64]{0,1:T(8,128)(2,1)}, u32[]{:S(2)}) copy-start(bf16[3584,64]{0,1:T(8,128)(2,1)} %param.9) | copy-start | bytes 1376260
  0.8 4.9 %copy-start.3 = (bf16[1024,128]{1,0:T(8,128)(2,1)S(1)}, bf16[1024,128]{1,0:T(8,128)(2,1)}, u32[]{:S(2)}) copy-start(bf16[1024,128]{1,0:T(8,128)(2,1)} %act_basis.1) | copy-start | bytes 786436
  0.8 4.9 %copy-start.4 = (bf16[1024,64]{0,1:T(8,128)(2,1)S(1)}, bf16[1024,64]{0,1:T(8,128)(2,1)}, u32[]{:S(2)}) copy-start(bf16[1024,64]{0,1:T(8,128)(2,1)} %param.10) | copy-start | bytes 393220
  0.8 12.8 %copy-start.1 = (f32[256,256]{1,0:T(8,128)S(1)}, f32[256,256]{1,0:T(8,128)}, u32[]{:S(2)}) copy-start(f32[256,256]{1,0:T(8,128)} %eigen.1) | copy-start | bytes 786436
  0.9 5.7 %collective-permute-start = (bf16[1,32,768]{2,1,0:T(8,128)(2,1)S(1)}, bf16[1,32,768]{2,1,0:T(8,128)(2,1)S(1)}, u32[]{:S(2)}, u32[]{:S(2)}) collective-permute-start(bf16[1,32,768]{2,1,0:T(8,128)(2,1)S(1)} %shard_map.93.first), channel_id=1, source_target_pairs={{0,9},{1,8},{2,11},{3,10},{4,13},{5,12},{6,15},{7,14},{8,1},{9,0},... | collective-permute-start | bytes 147464 | tf_op jit(solution)/shard_map/ppermute | solution.py:284
  6.6 5.8 %collective-permute-start.1 = (bf16[2,32,768]{2,1,0:T(8,128)(2,1)S(1)}, bf16[2,32,768]{2,1,0:T(8,128)(2,1)S(1)}, u32[]{:S(2)}, u32[]{:S(2)}) collective-permute-start(bf16[2,32,768]{2,1,0:T(8,128)(2,1)S(1)} %get-tuple-element.11.first), channel_id=1, source_target_pairs={{0,5},{1,4},{2,7},{3,6},{4,1},{5,0},{6,3},{7,2},{8,13},{9,12},{10,... | collective-permute-start | bytes 294920 | tf_op jit(solution)/shard_map/ppermute | solution.py:284
  8.8 5.4 %collective-permute-start.2 = (f32[2,8,512]{2,1,0:T(8,128)S(1)}, f32[2,8,512]{2,1,0:T(8,128)S(1)}, u32[]{:S(2)}, u32[]{:S(2)}) collective-permute-start(f32[2,8,512]{2,1,0:T(8,128)S(1)} %get-tuple-element.12), channel_id=1, source_target_pairs={{0,6},{2,4},{4,2},{6,0},{8,14},{10,12},{12,10},{14,8},{1,7},{3,5},... | collective-permute-start | bytes 98312 | tf_op jit(solution)/shard_map/ppermute | solution.py:278
  10.1 4.1 %collective-permute-start.3 = (f32[2,8,512]{2,1,0:T(8,128)S(1)}, f32[2,8,512]{2,1,0:T(8,128)S(1)}, u32[]{:S(2)}, u32[]{:S(2)}) collective-permute-start(f32[2,8,512]{2,1,0:T(8,128)S(1)} %get-tuple-element.13), channel_id=1, source_target_pairs={{0,4},{2,6},{4,0},{6,2},{8,12},{10,14},{12,8},{14,10},{1,5},{3,7},... | collective-permute-start | bytes 98312 | tf_op jit(solution)/shard_map/ppermute | solution.py:278
  11.8 4.2 %collective-permute-start.4 = (f32[2,8,512]{2,1,0:T(8,128)S(1)}, f32[2,8,512]{2,1,0:T(8,128)S(1)}, u32[]{:S(2)}, u32[]{:S(2)}) collective-permute-start(f32[2,8,512]{2,1,0:T(8,128)S(1)} %get-tuple-element.14), channel_id=1, source_target_pairs={{0,2},{2,0},{4,6},{6,4},{8,10},{10,8},{12,14},{14,12},{1,3},{3,1},... | collective-permute-start | bytes 98312 | tf_op jit(solution)/shard_map/ppermute | solution.py:278
  12.4 7.3 %collective-permute-start.8 = (bf16[4,32,768]{2,1,0:T(8,128)(2,1)S(1)}, bf16[4,32,768]{2,1,0:T(8,128)(2,1)S(1)}, u32[]{:S(2)}, u32[]{:S(2)}) collective-permute-start(bf16[4,32,768]{2,1,0:T(8,128)(2,1)S(1)} %shard_map.95.after.rest_0_), channel_id=1, source_target_pairs={{0,3},{1,2},{2,1},{3,0},{4,7},{5,6},{6,5},{7,4},{8,11},{9,10},{10,... | collective-permute-start | bytes 589832 | tf_op jit(solution)/shard_map/ppermute | solution.py:284
  13.7 8.7 %collective-permute-start.7 = (f32[256,256]{1,0:T(8,128)S(1)}, f32[256,256]{1,0:T(8,128)S(1)}, u32[]{:S(2)}, u32[]{:S(2)}) collective-permute-start(f32[256,256]{1,0:T(8,128)S(1)} %shard_map.97), channel_id=1, source_target_pairs={{0,1},{1,0},{2,3},{3,2},{4,5},{5,4},{6,7},{7,6},{8,9},{9,8},{10,11... | collective-permute-start | bytes 786440 | tf_op jit(solution)/shard_map/ppermute | solution.py:299
  16.1 5.1 %collective-permute-start.5 = (f32[8,512]{1,0:T(8,128)S(1)}, f32[8,512]{1,0:T(8,128)S(1)}, u32[]{:S(2)}, u32[]{:S(2)}) collective-permute-start(f32[8,512]{1,0:T(8,128)S(1)} %slice_bitcast_fusion), channel_id=1, source_target_pairs={{0,8},{2,10},{4,12},{6,14},{8,0},{10,2},{12,4},{14,6},{1,9},{3,11}... | collective-permute-start | bytes 49160 | tf_op jit(solution)/shard_map/ppermute | solution.py:278
  19.5 2.9 %collective-permute-start.9 = (bf16[4,32,768]{2,1,0:T(8,128)(2,1)S(1)}, bf16[4,32,768]{2,1,0:T(8,128)(2,1)S(1)}, u32[]{:S(2)}, u32[]{:S(2)}) collective-permute-start(bf16[4,32,768]{2,1,0:T(8,128)(2,1)S(1)} %shard_map.95.after.rest_0_), channel_id=1, source_target_pairs={{0,1},{1,0},{2,3},{3,2},{4,5},{5,4},{6,7},{7,6},{8,9},{9,8},{10,11... | collective-permute-start | bytes 589832 | tf_op jit(solution)/shard_map/ppermute | solution.py:300
  19.6 2.7 %collective-permute-start.10 = (bf16[4,32,768]{2,1,0:T(8,128)(2,1)S(1)}, bf16[4,32,768]{2,1,0:T(8,128)(2,1)S(1)}, u32[]{:S(2)}, u32[]{:S(2)}) collective-permute-start(bf16[4,32,768]{2,1,0:T(8,128)(2,1)S(1)} %collective-permute-done.8.rest_1_), channel_id=1, source_target_pairs={{0,1},{1,0},{2,3},{3,2},{4,5},{5,4},{6,7},{7,6},{8,9},{9,8},{10,11... | collective-permute-start | bytes 589832 | tf_op jit(solution)/shard_map/ppermute | solution.py:301
  21.2 1.2 %collective-permute-start.6 = (f32[8,512]{1,0:T(8,128)S(1)}, f32[8,512]{1,0:T(8,128)S(1)}, u32[]{:S(2)}, u32[]{:S(2)}) collective-permute-start(f32[8,512]{1,0:T(8,128)S(1)} %fusion.own), channel_id=1, source_target_pairs={{0,1},{1,0},{2,3},{3,2},{4,5},{5,4},{6,7},{7,6},{8,9},{9,8},{10,11... | collective-permute-start | bytes 49160 | tf_op jit(solution)/shard_map/ppermute | solution.py:303

commit v20 on v19

--- a/solution.py
+++ b/solution.py
@@ -158,7 +158,7 @@
 
 
 def spread_kernel(place_ref, tokens_ref, ids_ref, total, first, second, *rest):
-    pieces, joined = rest[:-1], rest[-1]
+    pieces, halves = rest[:-2], rest[-2:]
     groups = len(pieces)
     each, local_rows, _ = pieces[0].shape
     parts = groups * each
@@ -171,7 +171,10 @@
         piece = pieces[part % groups].at[part // groups]
         piece[:, :width] = total[pl.ds(start, local_rows), :]
         piece[:, width:] = jnp.where(row == doubling_slot(part, parts), facts, 0.0)
-    join_kernel(None, first, second, joined)
+    count, lanes = first.shape[0], halves[0].shape[2]
+    for i, joined in enumerate(halves):
+        joined[:count] = first[:, :, i * lanes : (i + 1) * lanes]
+        joined[count:] = second[:, :, i * lanes : (i + 1) * lanes]
 
 
 def spread(place, tokens, ids, total, first, second, parts, groups):
@@ -179,13 +182,13 @@
         (parts // groups, total.shape[0] // parts, total.shape[1] + LANES), jnp.float32
     )
     joined = jax.ShapeDtypeStruct(
-        (first.shape[0] + second.shape[0],) + first.shape[1:], first.dtype
+        (first.shape[0] + second.shape[0], first.shape[1], first.shape[2] // 2), first.dtype
     )
     return pl.pallas_call(
         spread_kernel,
-        out_shape=[piece] * groups + [joined],
+        out_shape=[piece] * groups + [joined] * 2,
         in_specs=[spec(pltpu.SMEM)] * 3 + [spec(pltpu.VMEM)] * 3,
-        out_specs=[spec(pltpu.VMEM)] * (groups + 1),
+        out_specs=[spec(pltpu.VMEM)] * (groups + 2),
         compiler_params=grant(4),
     )(place, tokens, ids, total, first, second)
 
@@ -202,8 +205,8 @@
     blocks, out = rest[:-1], rest[-1]
     first = core_ref[0] == 0
     half, ka = eigen.shape
-    factor_rows, width = blocks[0].shape[1:]
-    ks = width - ka
+    factor_rows, lanes = blocks[0].shape[1:]
+    ks = 2 * lanes - ka
     shared = own.shape[1] - LANES
     mine, theirs = own[...], other[...]
     coords = (jnp.where(first, mine, theirs), jnp.where(first, theirs, mine))
@@ -222,7 +225,14 @@
     facts = jnp.concatenate(
         [jnp.where(even, facts[0], facts[1]), jnp.where(even, facts[1], facts[0])], axis=0
     )
-    rows = jnp.concatenate([x[...] for x in blocks], axis=0)
+    each = blocks[0].shape[0] // 2
+    lefts, rights = [], []
+    for near, far in (blocks[:2], blocks[2:]):
+        lefts += [near[:each], far[:each]]
+        for cut in (slice(each, each + each // 2), slice(each + each // 2, 2 * each)):
+            rights += [near[cut], far[cut]]
+    halves = [jnp.concatenate(x, axis=0) for x in (lefts, rights)]
+    rows = jnp.concatenate(halves, axis=2)
     examples = rows.shape[0]
     lane = lax.broadcasted_iota(jnp.int32, (examples, LANES), 1).astype(jnp.float32)
     row = lax.broadcasted_iota(jnp.int32, (examples, factor_rows, ka), 1).astype(jnp.float32)
@@ -249,7 +259,7 @@
 
 
 def score(core, own, other, eigen, other_eigen, blocks):
-    examples = sum(x.shape[0] for x in blocks)
+    examples = sum(x.shape[0] for x in blocks) // 2
     return pl.pallas_call(
         score_kernel,
         out_shape=jax.ShapeDtypeStruct((own.shape[0] // RQ, examples), jnp.float32),
@@ -288,14 +298,16 @@
     block = relay(pack(train_out, train_act))
     arrived = crossed(block, 2)
     total = project(query_out.T, query_act.T, out_basis, act_basis)
-    *pieces, block = spread(
+    *pieces, left, right = spread(
         place, train_tokens, train_ids, total, block, arrived, parts, parts // 2
     )
-    near = join(pieces[0], block, crossed(block, 1))
+    near_left = join(pieces[0], left, crossed(left, 1))
+    near_right = join(pieces[0], right, crossed(right, 0))
+    near = join(pieces[0], near_left, near_right)
     far_first = reversed(range(1, len(pieces)))
     terms = [pieces[0]] + [apart(pieces[d], d) for d in far_first]
     sums = gather_sum(near, terms)
-    far = crossed(near, 0)
+    far = join(near, crossed(near_left, 0), crossed(near_right, 1))
     other_eigen = lax.ppermute(hold(near, eigenvalues), "fsdp", swap)
     other_near = lax.ppermute(near, "fsdp", swap)
     other_far = lax.ppermute(far, "fsdp", swap)

time: 24 us -> 24.4 us (1.017)
  starting transfers between devices: 14.8 us -> 15.3 us
    ppermute x3 -> x5, starting transfers between devices: 7.12 us -> 7.79 us  [crossed(): return lax.ppermute(x, ('blk', 'fsdp'), pairs)]
    ppermute x1, starting transfers between devices: 0.44 us -> 0.01 us  [direct(): other_eigen = lax.ppermute(hold(near, eigenvalues), 'fsdp', swap)]
  transfers between devices with their start and end apart: 11 -> 13, of which waited for: 6 -> 5; matrix products, arithmetic and copies ran while one was open for 0% -> 0% of each run, Pallas kernels for 2% -> 2%
where the time goes in v20:
time: 24.4 us; the launch traced here: 24.1 us
  starting transfers between devices  15.3 us (63%)
  waiting for transfers between devices  4.57 us (19%)
  Pallas kernels  2.7 us (11%)
  between operations  1.48 us (6%)
    ppermute x5, starting transfers between devices, crossed(): return lax.ppermute(x, ('blk', 'fsdp'), pairs)  7.79 us
    ppermute x4, starting transfers between devices, apart(): return lax.ppermute(x, 'blk', [(s, s ^ distance) for s in range(parts)])  6.97 us
    ppermute x4, waiting for transfers between devices, apart(): return lax.ppermute(x, 'blk', [(s, s ^ distance) for s in range(parts)])  3.08 us
    pallas_call x1, Pallas kernels, score(): pl.pallas_call(score_kernel, out_shape=jax.ShapeDtypeStruct((own.shape[0]...  1.34 us
    ppermute x1, waiting for transfers between devices, direct(): other = lax.ppermute(own, 'fsdp', swap)  1.17 us
    pallas_call x1, Pallas kernels, pack(): pl.pallas_call(pack_kernel, out_shape=jax.ShapeDtypeStruct(shape, train_o...  0.78 us
    ppermute x1, starting transfers between devices, direct(): other_far = lax.ppermute(far, 'fsdp', swap)  0.57 us
  transfers between devices with their start and end apart: 13, of which 5 were waited for; matrix products, arithmetic and copies ran while one was open for 0% of the time, Pallas kernels for 2%

profile of v20, /device:TPU:0, one launch (start us, length us, event | category | flops | bytes accessed | tf_op | source)
XLA Modules:
  0.0 24.1 jit_solution(3288160347503113060)
XLA Ops:
  0.0 0.8 %shard_map.92.source = bf16[1,32,768]{2,1,0:T(8,128)(2,1)S(1)} custom-call(bf16[1,32,512]{2,1,0:T(8,128)(2,1)} %train_out.1, bf16[1,32,256]{2,1,0:T(8,128)(2,1)} %train_act.1), custom_call_target="tpu_custom_call" | custom-call | tf_op jit(solution)/shard_map/pallas_call | solution.py:46
  0.8 0.0 copy-start
  0.8 0.0 copy-start.2
  0.8 0.0 copy-start.3
  0.8 0.0 copy-start.4
  0.8 3.5 %collective-permute-start = (bf16[1,32,768]{2,1,0:T(8,128)(2,1)S(1)}, bf16[1,32,768]{2,1,0:T(8,128)(2,1)S(1)}, u32[]{:S(2)}, u32[]{:S(2)}) collective-permute-start(bf16[1,32,768]{2,1,0:T(8,128)(2,1)S(1)} %shard_map.93.first), channel_id=1, source_target_pairs={{0,9},{1,8},{2,11},{3,10},{4,13},{5,12},{6,15},{7,14},{8,1},{9,0},... | collective-permute-start | bytes 147464 | tf_op jit(solution)/shard_map/ppermute | solution.py:294
  5.7 0.0 copy-start.1
  5.7 0.5 %shard_map.91.total = f32[64,384]{1,0:T(8,128)S(1)} custom-call(bf16[64,3584]{1,0:T(8,128)(2,1)S(1)} %bitcast.10, bf16[64,1024]{1,0:T(8,128)(2,1)S(1)} %bitcast.11, bf16[3584,256]{1,0:T(8,128)(2,1)S(1)} %copy-done, bf16[1024,128]{1,0:T(8,128)(2,1)S(1)} %copy-done.3), custom_call_target="tpu_custom_call" | custom-call | flops 134217728 | bytes 2686976 | tf_op jit(solution)/shard_map/pallas_call | solution.py:141
  6.2 0.3 %collective-permute-done.second = bf16[1,32,768]{2,1,0:T(8,128)(2,1)S(1)} collective-permute-done((bf16[1,32,768]{2,1,0:T(8,128)(2,1)S(1)}, bf16[1,32,768]{2,1,0:T(8,128)(2,1)S(1)}, u32[]{:S(2)}, u32[]{:S(2)}) %collective-permute-start) | collective-permute-done | bytes 49184 | tf_op jit(solution)/shard_map/ppermute | solution.py:294
  6.5 2.3 %collective-permute-start.1 = (bf16[2,32,384]{2,1,0:T(8,128)(2,1)S(1)}, bf16[2,32,384]{2,1,0:T(8,128)(2,1)S(1)}, u32[]{:S(2)}, u32[]{:S(2)}) collective-permute-start(bf16[2,32,384]{2,1,0:T(8,128)(2,1)S(1)} %get-tuple-element.12.first), channel_id=1, source_target_pairs={{0,5},{1,4},{2,7},{3,6},{4,1},{5,0},{6,3},{7,2},{8,13},{9,12},{10,... | collective-permute-start | bytes 147464 | tf_op jit(solution)/shard_map/ppermute | solution.py:294
  8.8 1.5 %collective-permute-start.2 = (bf16[2,32,384]{2,1,0:T(8,128)(2,1)S(1)}, bf16[2,32,384]{2,1,0:T(8,128)(2,1)S(1)}, u32[]{:S(2)}, u32[]{:S(2)}) collective-permute-start(bf16[2,32,384]{2,1,0:T(8,128)(2,1)S(1)} %get-tuple-element.13.first), channel_id=1, source_target_pairs={{0,3},{1,2},{2,1},{3,0},{4,7},{5,6},{6,5},{7,4},{8,11},{9,10},{10,... | collective-permute-start | bytes 147464 | tf_op jit(solution)/shard_map/ppermute | solution.py:294
  10.3 0.1 collective-permute-start.3
  10.4 1.9 %collective-permute-start.4 = (f32[2,8,512]{2,1,0:T(8,128)S(1)}, f32[2,8,512]{2,1,0:T(8,128)S(1)}, u32[]{:S(2)}, u32[]{:S(2)}) collective-permute-start(f32[2,8,512]{2,1,0:T(8,128)S(1)} %get-tuple-element.15), channel_id=1, source_target_pairs={{0,4},{2,6},{4,0},{6,2},{8,12},{10,14},{12,8},{14,10},{1,5},{3,7},... | collective-permute-start | bytes 98312 | tf_op jit(solution)/shard_map/ppermute | solution.py:288
  12.3 1.5 %collective-permute-start.5 = (f32[2,8,512]{2,1,0:T(8,128)S(1)}, f32[2,8,512]{2,1,0:T(8,128)S(1)}, u32[]{:S(2)}, u32[]{:S(2)}) collective-permute-start(f32[2,8,512]{2,1,0:T(8,128)S(1)} %get-tuple-element.16), channel_id=1, source_target_pairs={{0,2},{2,0},{4,6},{6,4},{8,10},{10,8},{12,14},{14,12},{1,3},{3,1},... | collective-permute-start | bytes 98312 | tf_op jit(solution)/shard_map/ppermute | solution.py:288
  13.8 0.0 collective-permute-done.1.second
  13.8 0.1 collective-permute-start.9
  14.0 0.4 %collective-permute-start.10 = (bf16[4,32,384]{2,1,0:T(8,128)(2,1)S(1)}, bf16[4,32,384]{2,1,0:T(8,128)(2,1)S(1)}, u32[]{:S(2)}, u32[]{:S(2)}) collective-permute-start(bf16[4,32,384]{2,1,0:T(8,128)(2,1)S(1)} %shard_map.96.second), channel_id=1, source_target_pairs={{0,5},{1,4},{2,7},{3,6},{4,1},{5,0},{6,3},{7,2},{8,13},{9,12},{10,... | collective-permute-start | bytes 294920 | tf_op jit(solution)/shard_map/ppermute | solution.py:294
  14.4 0.8 %collective-permute-done.3.refs_1_ = f32[2,8,512]{2,1,0:T(8,128)S(1)} collective-permute-done((f32[2,8,512]{2,1,0:T(8,128)S(1)}, f32[2,8,512]{2,1,0:T(8,128)S(1)}, u32[]{:S(2)}, u32[]{:S(2)}) %collective-permute-start.3) | collective-permute-done | bytes 32800 | tf_op jit(solution)/shard_map/ppermute | solution.py:288
  15.2 1.0 %collective-permute-done.5.refs_3_ = f32[2,8,512]{2,1,0:T(8,128)S(1)} collective-permute-done((f32[2,8,512]{2,1,0:T(8,128)S(1)}, f32[2,8,512]{2,1,0:T(8,128)S(1)}, u32[]{:S(2)}, u32[]{:S(2)}) %collective-permute-start.5) | collective-permute-done | bytes 32800 | tf_op jit(solution)/shard_map/ppermute | solution.py:288
  16.3 3.5 %collective-permute-start.6 = (f32[8,512]{1,0:T(8,128)S(1)}, f32[8,512]{1,0:T(8,128)S(1)}, u32[]{:S(2)}, u32[]{:S(2)}) collective-permute-start(f32[8,512]{1,0:T(8,128)S(1)} %slice_bitcast_fusion), channel_id=1, source_target_pairs={{0,8},{2,10},{4,12},{6,14},{8,0},{10,2},{12,4},{14,6},{1,9},{3,11}... | collective-permute-start | bytes 49160 | tf_op jit(solution)/shard_map/ppermute | solution.py:288
  19.8 0.6 %collective-permute-start.12 = (bf16[8,32,384]{2,1,0:T(8,128)(2,1)S(1)}, bf16[8,32,384]{2,1,0:T(8,128)(2,1)S(1)}, u32[]{:S(2)}, u32[]{:S(2)}) collective-permute-start(bf16[8,32,384]{2,1,0:T(8,128)(2,1)S(1)} %shard_map.100.rest_1_), channel_id=1, source_target_pairs={{0,1},{1,0},{2,3},{3,2},{4,5},{5,4},{6,7},{7,6},{8,9},{9,8},{10,11... | collective-permute-start | bytes 589832 | tf_op jit(solution)/shard_map/ppermute | solution.py:313
  20.3 1.2 %collective-permute-done.6 = f32[8,512]{1,0:T(8,128)S(1)} collective-permute-done((f32[8,512]{1,0:T(8,128)S(1)}, f32[8,512]{1,0:T(8,128)S(1)}, u32[]{:S(2)}, u32[]{:S(2)}) %collective-permute-start.6) | collective-permute-done | bytes 16416 | tf_op jit(solution)/shard_map/ppermute | solution.py:288
  21.6 1.2 %collective-permute-done.7.other = f32[8,512]{1,0:T(8,128)S(1)} collective-permute-done((f32[8,512]{1,0:T(8,128)S(1)}, f32[8,512]{1,0:T(8,128)S(1)}, u32[]{:S(2)}, u32[]{:S(2)}) %collective-permute-start.7) | collective-permute-done | bytes 16416 | tf_op jit(solution)/shard_map/ppermute | solution.py:315
  22.8 1.3 %shard_map.101 = f32[2,16]{1,0:T(2,128)} custom-call(s32[1]{0:T(128)} %bitcast.core_ref, f32[8,512]{1,0:T(8,128)S(1)} %fusion.own, f32[8,512]{1,0:T(8,128)S(1)} %collective-permute-done.7.other, f32[256,256]{1,0:T(8,128)S(1)} %copy-done.1, f32[256,256]{1,0:T(8,128)S(1)} %collective-permute-done.8.other_eigen, ...), custom_call_target="tpu_custom_call" | custom-call | tf_op jit(solution)/shard_map/pallas_call | solution.py:263
  (25 shorter events, 0.2 us)
Async XLA Ops:
  0.8 4.9 %copy-start = (bf16[3584,256]{1,0:T(8,128)(2,1)S(1)}, bf16[3584,256]{1,0:T(8,128)(2,1)}, u32[]{:S(2)}) copy-start(bf16[3584,256]{1,0:T(8,128)(2,1)} %out_basis.1) | copy-start | bytes 5505028
  0.8 4.9 %copy-start.2 = (bf16[3584,64]{0,1:T(8,128)(2,1)S(1)}, bf16[3584,64]{0,1:T(8,128)(2,1)}, u32[]{:S(2)}) copy-start(bf16[3584,64]{0,1:T(8,128)(2,1)} %param.9) | copy-start | bytes 1376260
  0.8 4.9 %copy-start.3 = (bf16[1024,128]{1,0:T(8,128)(2,1)S(1)}, bf16[1024,128]{1,0:T(8,128)(2,1)}, u32[]{:S(2)}) copy-start(bf16[1024,128]{1,0:T(8,128)(2,1)} %act_basis.1) | copy-start | bytes 786436
  0.8 4.9 %copy-start.4 = (bf16[1024,64]{0,1:T(8,128)(2,1)S(1)}, bf16[1024,64]{0,1:T(8,128)(2,1)}, u32[]{:S(2)}) copy-start(bf16[1024,64]{0,1:T(8,128)(2,1)} %param.10) | copy-start | bytes 393220
  0.8 5.7 %collective-permute-start = (bf16[1,32,768]{2,1,0:T(8,128)(2,1)S(1)}, bf16[1,32,768]{2,1,0:T(8,128)(2,1)S(1)}, u32[]{:S(2)}, u32[]{:S(2)}) collective-permute-start(bf16[1,32,768]{2,1,0:T(8,128)(2,1)S(1)} %shard_map.93.first), channel_id=1, source_target_pairs={{0,9},{1,8},{2,11},{3,10},{4,13},{5,12},{6,15},{7,14},{8,1},{9,0},... | collective-permute-start | bytes 147464 | tf_op jit(solution)/shard_map/ppermute | solution.py:294
  5.7 8.6 %copy-start.1 = (f32[256,256]{1,0:T(8,128)S(1)}, f32[256,256]{1,0:T(8,128)}, u32[]{:S(2)}) copy-start(f32[256,256]{1,0:T(8,128)} %eigen.1) | copy-start | bytes 786436
  6.5 7.3 %collective-permute-start.1 = (bf16[2,32,384]{2,1,0:T(8,128)(2,1)S(1)}, bf16[2,32,384]{2,1,0:T(8,128)(2,1)S(1)}, u32[]{:S(2)}, u32[]{:S(2)}) collective-permute-start(bf16[2,32,384]{2,1,0:T(8,128)(2,1)S(1)} %get-tuple-element.12.first), channel_id=1, source_target_pairs={{0,5},{1,4},{2,7},{3,6},{4,1},{5,0},{6,3},{7,2},{8,13},{9,12},{10,... | collective-permute-start | bytes 147464 | tf_op jit(solution)/shard_map/ppermute | solution.py:294
  8.8 5.1 %collective-permute-start.2 = (bf16[2,32,384]{2,1,0:T(8,128)(2,1)S(1)}, bf16[2,32,384]{2,1,0:T(8,128)(2,1)S(1)}, u32[]{:S(2)}, u32[]{:S(2)}) collective-permute-start(bf16[2,32,384]{2,1,0:T(8,128)(2,1)S(1)} %get-tuple-element.13.first), channel_id=1, source_target_pairs={{0,3},{1,2},{2,1},{3,0},{4,7},{5,6},{6,5},{7,4},{8,11},{9,10},{10,... | collective-permute-start | bytes 147464 | tf_op jit(solution)/shard_map/ppermute | solution.py:294
  10.3 4.9 %collective-permute-start.3 = (f32[2,8,512]{2,1,0:T(8,128)S(1)}, f32[2,8,512]{2,1,0:T(8,128)S(1)}, u32[]{:S(2)}, u32[]{:S(2)}) collective-permute-start(f32[2,8,512]{2,1,0:T(8,128)S(1)} %get-tuple-element.14), channel_id=1, source_target_pairs={{0,6},{2,4},{4,2},{6,0},{8,14},{10,12},{12,10},{14,8},{1,7},{3,5},... | collective-permute-start | bytes 98312 | tf_op jit(solution)/shard_map/ppermute | solution.py:288
  10.4 4.8 %collective-permute-start.4 = (f32[2,8,512]{2,1,0:T(8,128)S(1)}, f32[2,8,512]{2,1,0:T(8,128)S(1)}, u32[]{:S(2)}, u32[]{:S(2)}) collective-permute-start(f32[2,8,512]{2,1,0:T(8,128)S(1)} %get-tuple-element.15), channel_id=1, source_target_pairs={{0,4},{2,6},{4,0},{6,2},{8,12},{10,14},{12,8},{14,10},{1,5},{3,7},... | collective-permute-start | bytes 98312 | tf_op jit(solution)/shard_map/ppermute | solution.py:288
  12.3 3.9 %collective-permute-start.5 = (f32[2,8,512]{2,1,0:T(8,128)S(1)}, f32[2,8,512]{2,1,0:T(8,128)S(1)}, u32[]{:S(2)}, u32[]{:S(2)}) collective-permute-start(f32[2,8,512]{2,1,0:T(8,128)S(1)} %get-tuple-element.16), channel_id=1, source_target_pairs={{0,2},{2,0},{4,6},{6,4},{8,10},{10,8},{12,14},{14,12},{1,3},{3,1},... | collective-permute-start | bytes 98312 | tf_op jit(solution)/shard_map/ppermute | solution.py:288
  13.8 5.9 %collective-permute-start.9 = (bf16[4,32,384]{2,1,0:T(8,128)(2,1)S(1)}, bf16[4,32,384]{2,1,0:T(8,128)(2,1)S(1)}, u32[]{:S(2)}, u32[]{:S(2)}) collective-permute-start(bf16[4,32,384]{2,1,0:T(8,128)(2,1)S(1)} %shard_map.95.first), channel_id=1, source_target_pairs={{0,3},{1,2},{2,1},{3,0},{4,7},{5,6},{6,5},{7,4},{8,11},{9,10},{10,... | collective-permute-start | bytes 294920 | tf_op jit(solution)/shard_map/ppermute | solution.py:294
  14.0 5.8 %collective-permute-start.10 = (bf16[4,32,384]{2,1,0:T(8,128)(2,1)S(1)}, bf16[4,32,384]{2,1,0:T(8,128)(2,1)S(1)}, u32[]{:S(2)}, u32[]{:S(2)}) collective-permute-start(bf16[4,32,384]{2,1,0:T(8,128)(2,1)S(1)} %shard_map.96.second), channel_id=1, source_target_pairs={{0,5},{1,4},{2,7},{3,6},{4,1},{5,0},{6,3},{7,2},{8,13},{9,12},{10,... | collective-permute-start | bytes 294920 | tf_op jit(solution)/shard_map/ppermute | solution.py:294
  15.2 7.6 %collective-permute-start.8 = (f32[256,256]{1,0:T(8,128)S(1)}, f32[256,256]{1,0:T(8,128)S(1)}, u32[]{:S(2)}, u32[]{:S(2)}) collective-permute-start(f32[256,256]{1,0:T(8,128)S(1)} %shard_map.99), channel_id=1, source_target_pairs={{0,1},{1,0},{2,3},{3,2},{4,5},{5,4},{6,7},{7,6},{8,9},{9,8},{10,11... | collective-permute-start | bytes 786440 | tf_op jit(solution)/shard_map/ppermute | solution.py:311
  16.3 5.3 %collective-permute-start.6 = (f32[8,512]{1,0:T(8,128)S(1)}, f32[8,512]{1,0:T(8,128)S(1)}, u32[]{:S(2)}, u32[]{:S(2)}) collective-permute-start(f32[8,512]{1,0:T(8,128)S(1)} %slice_bitcast_fusion), channel_id=1, source_target_pairs={{0,8},{2,10},{4,12},{6,14},{8,0},{10,2},{12,4},{14,6},{1,9},{3,11}... | collective-permute-start | bytes 49160 | tf_op jit(solution)/shard_map/ppermute | solution.py:288
  19.7 3.0 %collective-permute-start.11 = (bf16[8,32,384]{2,1,0:T(8,128)(2,1)S(1)}, bf16[8,32,384]{2,1,0:T(8,128)(2,1)S(1)}, u32[]{:S(2)}, u32[]{:S(2)}) collective-permute-start(bf16[8,32,384]{2,1,0:T(8,128)(2,1)S(1)} %shard_map.97.after.rest_0_), channel_id=1, source_target_pairs={{0,1},{1,0},{2,3},{3,2},{4,5},{5,4},{6,7},{7,6},{8,9},{9,8},{10,11... | collective-permute-start | bytes 589832 | tf_op jit(solution)/shard_map/ppermute | solution.py:312
  19.8 3.0 %collective-permute-start.12 = (bf16[8,32,384]{2,1,0:T(8,128)(2,1)S(1)}, bf16[8,32,384]{2,1,0:T(8,128)(2,1)S(1)}, u32[]{:S(2)}, u32[]{:S(2)}) collective-permute-start(bf16[8,32,384]{2,1,0:T(8,128)(2,1)S(1)} %shard_map.100.rest_1_), channel_id=1, source_target_pairs={{0,1},{1,0},{2,3},{3,2},{4,5},{5,4},{6,7},{7,6},{8,9},{9,8},{10,11... | collective-permute-start | bytes 589832 | tf_op jit(solution)/shard_map/ppermute | solution.py:313
  21.6 1.2 %collective-permute-start.7 = (f32[8,512]{1,0:T(8,128)S(1)}, f32[8,512]{1,0:T(8,128)S(1)}, u32[]{:S(2)}, u32[]{:S(2)}) collective-permute-start(f32[8,512]{1,0:T(8,128)S(1)} %fusion.own), channel_id=1, source_target_pairs={{0,1},{1,0},{2,3},{3,2},{4,5},{5,4},{6,7},{7,6},{8,9},{9,8},{10,11... | collective-permute-start | bytes 49160 | tf_op jit(solution)/shard_map/ppermute | solution.py:315

commit v21 on v19

--- a/solution.py
+++ b/solution.py
@@ -10,6 +10,8 @@
 RQ = 4
 LANES = 128
 DIRECT_PARTS = 8
+DIRECT_STEPS = (0, 6, 4, 2)
+LAST_STEP = 1
 WAIT_FLOPS = 10**9
 
 
@@ -153,39 +155,38 @@
 
 
 def doubling_slot(distance, parts):
-    bits = parts.bit_length() - 1
-    return sum(1 << (bits - 1 - i) for i in range(bits) if distance >> i & 1)
+    steps = (parts // 2, 1, 2)
+    return sum(1 << i for i, step in enumerate(steps) if distance & step)
 
 
 def spread_kernel(place_ref, tokens_ref, ids_ref, total, first, second, *rest):
     pieces, joined = rest[:-1], rest[-1]
-    groups = len(pieces)
     each, local_rows, _ = pieces[0].shape
-    parts = groups * each
+    parts = each * len(pieces)
     width = total.shape[1]
     row = lax.broadcasted_iota(jnp.int32, (local_rows, LANES), 0)
     lane = lax.broadcasted_iota(jnp.int32, (local_rows, LANES), 1)
     facts = jnp.where(lane < LANES // 2, ids_ref[0], tokens_ref[0]).astype(jnp.float32)
     for part in range(parts):
         start = pl.multiple_of((place_ref[0] ^ part) * local_rows, local_rows)
-        piece = pieces[part % groups].at[part // groups]
+        piece = pieces[DIRECT_STEPS.index(part & DIRECT_STEPS[1])].at[int(part & LAST_STEP > 0)]
         piece[:, :width] = total[pl.ds(start, local_rows), :]
         piece[:, width:] = jnp.where(row == doubling_slot(part, parts), facts, 0.0)
     join_kernel(None, first, second, joined)
 
 
-def spread(place, tokens, ids, total, first, second, parts, groups):
+def spread(place, tokens, ids, total, first, second, parts):
     piece = jax.ShapeDtypeStruct(
-        (parts // groups, total.shape[0] // parts, total.shape[1] + LANES), jnp.float32
+        (parts // len(DIRECT_STEPS), total.shape[0] // parts, total.shape[1] + LANES), jnp.float32
     )
     joined = jax.ShapeDtypeStruct(
         (first.shape[0] + second.shape[0],) + first.shape[1:], first.dtype
     )
     return pl.pallas_call(
         spread_kernel,
-        out_shape=[piece] * groups + [joined],
+        out_shape=[piece] * len(DIRECT_STEPS) + [joined],
         in_specs=[spec(pltpu.SMEM)] * 3 + [spec(pltpu.VMEM)] * 3,
-        out_specs=[spec(pltpu.VMEM)] * (groups + 1),
+        out_specs=[spec(pltpu.VMEM)] * (len(DIRECT_STEPS) + 1),
         compiler_params=grant(4),
     )(place, tokens, ids, total, first, second)
 
@@ -289,17 +290,16 @@
     arrived = crossed(block, 2)
     total = project(query_out.T, query_act.T, out_basis, act_basis)
     *pieces, block = spread(
-        place, train_tokens, train_ids, total, block, arrived, parts, parts // 2
-    )
-    near = join(pieces[0], block, crossed(block, 1))
-    far_first = reversed(range(1, len(pieces)))
-    terms = [pieces[0]] + [apart(pieces[d], d) for d in far_first]
-    sums = gather_sum(near, terms)
-    far = crossed(near, 0)
+        place, train_tokens, train_ids, total, block, arrived, parts
+    )
+    near = join(pieces[0], block, crossed(block, 0))
+    terms = [apart(piece, step) for piece, step in zip(pieces[1:], DIRECT_STEPS[1:])]
+    sums = gather_sum(near, [pieces[0]] + terms)
+    far = crossed(near, 1)
     other_eigen = lax.ppermute(hold(near, eigenvalues), "fsdp", swap)
     other_near = lax.ppermute(near, "fsdp", swap)
     other_far = lax.ppermute(far, "fsdp", swap)
-    own = sums[0] + apart(sums[1], 4)
+    own = sums[0] + apart(sums[1], LAST_STEP)
     other = lax.ppermute(own, "fsdp", swap)
     return score(
         core, own, other, eigenvalues, other_eigen, (near, far, other_near, other_far)

time: 24 us -> 24.8 us (1.033)
  waiting for transfers between devices: 4.76 us -> 6.88 us
  starting transfers between devices: 14.8 us -> 13.6 us
    ppermute x3, waiting for transfers between devices: 0.48 us -> 3.34 us  [crossed(): return lax.ppermute(x, ('blk', 'fsdp'), pairs)]
    ppermute x4, starting transfers between devices: 6.93 us -> 5.95 us  [apart(): return lax.ppermute(x, 'blk', [(s, s ^ distance) for s in range(parts)])]
    ppermute x3, starting transfers between devices: 7.12 us -> 6.35 us  [crossed(): return lax.ppermute(x, ('blk', 'fsdp'), pairs)]
    ppermute x4, waiting for transfers between devices: 3.1 us -> 2.57 us  [apart(): return lax.ppermute(x, 'blk', [(s, s ^ distance) for s in range(parts)])]
    ppermute x1, starting transfers between devices: 0.01 us -> 0.29 us  [direct(): other = lax.ppermute(own, 'fsdp', swap)]
    ppermute x1, starting transfers between devices: 0.44 us -> 0.71 us  [direct(): other_eigen = lax.ppermute(hold(near, eigenvalues), 'fsdp', swap)]
  transfers between devices with their start and end apart: 11 -> 11, of which waited for: 6 -> 4; matrix products, arithmetic and copies ran while one was open for 0% -> 0% of each run, Pallas kernels for 2% -> 2%
where the time goes in v21:
time: 24.8 us; the launch traced here: 24.6 us
  starting transfers between devices  13.6 us (55%)
  waiting for transfers between devices  6.88 us (28%)
  Pallas kernels  2.66 us (11%)
  between operations  1.43 us (6%)
    ppermute x3, starting transfers between devices, crossed(): return lax.ppermute(x, ('blk', 'fsdp'), pairs)  6.35 us
    ppermute x4, starting transfers between devices, apart(): return lax.ppermute(x, 'blk', [(s, s ^ distance) for s in range(parts)])  5.95 us
    ppermute x3, waiting for transfers between devices, crossed(): return lax.ppermute(x, ('blk', 'fsdp'), pairs)  3.34 us
    ppermute x4, waiting for transfers between devices, apart(): return lax.ppermute(x, 'blk', [(s, s ^ distance) for s in range(parts)])  2.57 us
    pallas_call x1, Pallas kernels, score(): pl.pallas_call(score_kernel, out_shape=jax.ShapeDtypeStruct((own.shape[0]...  1.34 us
    ppermute x1, waiting for transfers between devices, direct(): other = lax.ppermute(own, 'fsdp', swap)  0.96 us
    pallas_call x1, Pallas kernels, pack(): pl.pallas_call(pack_kernel, out_shape=jax.ShapeDtypeStruct(shape, train_o...  0.78 us
    ppermute x1, starting transfers between devices, direct(): other_eigen = lax.ppermute(hold(near, eigenvalues), 'fsdp', swap)  0.71 us
  transfers between devices with their start and end apart: 11, of which 4 were waited for; matrix products, arithmetic and copies ran while one was open for 0% of the time, Pallas kernels for 2%

profile of v21, /device:TPU:0, one launch (start us, length us, event | category | flops | bytes accessed | tf_op | source)
XLA Modules:
  0.0 24.6 jit_solution(17888344046187485659)
XLA Ops:
  0.0 0.8 %shard_map.92.source = bf16[1,32,768]{2,1,0:T(8,128)(2,1)S(1)} custom-call(bf16[1,32,512]{2,1,0:T(8,128)(2,1)} %train_out.1, bf16[1,32,256]{2,1,0:T(8,128)(2,1)} %train_act.1), custom_call_target="tpu_custom_call" | custom-call | tf_op jit(solution)/shard_map/pallas_call | solution.py:48
  0.8 0.0 copy-start
  0.8 0.0 copy-start.2
  0.8 0.0 copy-start.3
  0.8 0.0 copy-start.4
  0.8 0.0 copy-start.1
  0.9 3.5 %collective-permute-start = (bf16[1,32,768]{2,1,0:T(8,128)(2,1)S(1)}, bf16[1,32,768]{2,1,0:T(8,128)(2,1)S(1)}, u32[]{:S(2)}, u32[]{:S(2)}) collective-permute-start(bf16[1,32,768]{2,1,0:T(8,128)(2,1)S(1)} %shard_map.93.first), channel_id=1, source_target_pairs={{0,9},{1,8},{2,11},{3,10},{4,13},{5,12},{6,15},{7,14},{8,1},{9,0},... | collective-permute-start | bytes 147464 | tf_op jit(solution)/shard_map/ppermute | solution.py:285
  5.7 0.5 %shard_map.91.total = f32[64,384]{1,0:T(8,128)S(1)} custom-call(bf16[64,3584]{1,0:T(8,128)(2,1)S(1)} %bitcast.10, bf16[64,1024]{1,0:T(8,128)(2,1)S(1)} %bitcast.11, bf16[3584,256]{1,0:T(8,128)(2,1)S(1)} %copy-done, bf16[1024,128]{1,0:T(8,128)(2,1)S(1)} %copy-done.3), custom_call_target="tpu_custom_call" | custom-call | flops 134217728 | bytes 2686976 | tf_op jit(solution)/shard_map/pallas_call | solution.py:143
  6.2 0.3 %collective-permute-done.second = bf16[1,32,768]{2,1,0:T(8,128)(2,1)S(1)} collective-permute-done((bf16[1,32,768]{2,1,0:T(8,128)(2,1)S(1)}, bf16[1,32,768]{2,1,0:T(8,128)(2,1)S(1)}, u32[]{:S(2)}, u32[]{:S(2)}) %collective-permute-start) | collective-permute-done | bytes 49184 | tf_op jit(solution)/shard_map/ppermute | solution.py:285
  6.6 1.8 %collective-permute-start.1 = (bf16[2,32,768]{2,1,0:T(8,128)(2,1)S(1)}, bf16[2,32,768]{2,1,0:T(8,128)(2,1)S(1)}, u32[]{:S(2)}, u32[]{:S(2)}) collective-permute-start(bf16[2,32,768]{2,1,0:T(8,128)(2,1)S(1)} %get-tuple-element.11.first), channel_id=1, source_target_pairs={{0,3},{1,2},{2,1},{3,0},{4,7},{5,6},{6,5},{7,4},{8,11},{9,10},{10,... | collective-permute-start | bytes 294920 | tf_op jit(solution)/shard_map/ppermute | solution.py:285
  8.4 4.8 %collective-permute-start.2 = (f32[2,8,512]{2,1,0:T(8,128)S(1)}, f32[2,8,512]{2,1,0:T(8,128)S(1)}, u32[]{:S(2)}, u32[]{:S(2)}) collective-permute-start(f32[2,8,512]{2,1,0:T(8,128)S(1)} %get-tuple-element.12), channel_id=1, source_target_pairs={{0,12},{2,14},{4,8},{6,10},{8,4},{10,6},{12,0},{14,2},{1,13},{3,15... | collective-permute-start | bytes 98312 | tf_op jit(solution)/shard_map/ppermute | solution.py:279
  13.1 0.0 collective-permute-start.3
  13.2 0.6 %collective-permute-start.4 = (f32[2,8,512]{2,1,0:T(8,128)S(1)}, f32[2,8,512]{2,1,0:T(8,128)S(1)}, u32[]{:S(2)}, u32[]{:S(2)}) collective-permute-start(f32[2,8,512]{2,1,0:T(8,128)S(1)} %get-tuple-element.14), channel_id=1, source_target_pairs={{0,4},{2,6},{4,0},{6,2},{8,12},{10,14},{12,8},{14,10},{1,5},{3,7},... | collective-permute-start | bytes 98312 | tf_op jit(solution)/shard_map/ppermute | solution.py:279
  13.7 1.0 %collective-permute-start.8 = (bf16[4,32,768]{2,1,0:T(8,128)(2,1)S(1)}, bf16[4,32,768]{2,1,0:T(8,128)(2,1)S(1)}, u32[]{:S(2)}, u32[]{:S(2)}) collective-permute-start(bf16[4,32,768]{2,1,0:T(8,128)(2,1)S(1)} %shard_map.95.after.rest_0_), channel_id=1, source_target_pairs={{0,5},{1,4},{2,7},{3,6},{4,1},{5,0},{6,3},{7,2},{8,13},{9,12},{10,... | collective-permute-start | bytes 589832 | tf_op jit(solution)/shard_map/ppermute | solution.py:285
  14.8 0.7 %collective-permute-start.7 = (f32[256,256]{1,0:T(8,128)S(1)}, f32[256,256]{1,0:T(8,128)S(1)}, u32[]{:S(2)}, u32[]{:S(2)}) collective-permute-start(f32[256,256]{1,0:T(8,128)S(1)} %shard_map.97), channel_id=1, source_target_pairs={{0,1},{1,0},{2,3},{3,2},{4,5},{5,4},{6,7},{7,6},{8,9},{9,8},{10,11... | collective-permute-start | bytes 786440 | tf_op jit(solution)/shard_map/ppermute | solution.py:299
  15.5 0.0 collective-permute-done.2.refs_1_
  15.5 2.5 %collective-permute-done.3.refs_2_ = f32[2,8,512]{2,1,0:T(8,128)S(1)} collective-permute-done((f32[2,8,512]{2,1,0:T(8,128)S(1)}, f32[2,8,512]{2,1,0:T(8,128)S(1)}, u32[]{:S(2)}, u32[]{:S(2)}) %collective-permute-start.3) | collective-permute-done | bytes 32800 | tf_op jit(solution)/shard_map/ppermute | solution.py:279
  18.0 0.0 collective-permute-done.4.refs_3_
  18.1 0.6 %collective-permute-start.5 = (f32[8,512]{1,0:T(8,128)S(1)}, f32[8,512]{1,0:T(8,128)S(1)}, u32[]{:S(2)}, u32[]{:S(2)}) collective-permute-start(f32[8,512]{1,0:T(8,128)S(1)} %slice_bitcast_fusion), channel_id=1, source_target_pairs={{0,2},{2,0},{4,6},{6,4},{8,10},{10,8},{12,14},{14,12},{1,3},{3,1},... | collective-permute-start | bytes 49160 | tf_op jit(solution)/shard_map/ppermute | solution.py:279
  18.7 3.0 %collective-permute-done.8.rest_1_ = bf16[4,32,768]{2,1,0:T(8,128)(2,1)S(1)} collective-permute-done((bf16[4,32,768]{2,1,0:T(8,128)(2,1)S(1)}, bf16[4,32,768]{2,1,0:T(8,128)(2,1)S(1)}, u32[]{:S(2)}, u32[]{:S(2)}) %collective-permute-start.8) | collective-permute-done | bytes 196640 | tf_op jit(solution)/shard_map/ppermute | solution.py:285
  21.7 0.3 %collective-permute-start.10 = (bf16[4,32,768]{2,1,0:T(8,128)(2,1)S(1)}, bf16[4,32,768]{2,1,0:T(8,128)(2,1)S(1)}, u32[]{:S(2)}, u32[]{:S(2)}) collective-permute-start(bf16[4,32,768]{2,1,0:T(8,128)(2,1)S(1)} %collective-permute-done.8.rest_1_), channel_id=1, source_target_pairs={{0,1},{1,0},{2,3},{3,2},{4,5},{5,4},{6,7},{7,6},{8,9},{9,8},{10,11... | collective-permute-start | bytes 589832 | tf_op jit(solution)/shard_map/ppermute | solution.py:301
  22.0 0.3 %collective-permute-start.6 = (f32[8,512]{1,0:T(8,128)S(1)}, f32[8,512]{1,0:T(8,128)S(1)}, u32[]{:S(2)}, u32[]{:S(2)}) collective-permute-start(f32[8,512]{1,0:T(8,128)S(1)} %fusion.own), channel_id=1, source_target_pairs={{0,1},{1,0},{2,3},{3,2},{4,5},{5,4},{6,7},{7,6},{8,9},{9,8},{10,11... | collective-permute-start | bytes 49160 | tf_op jit(solution)/shard_map/ppermute | solution.py:303
  22.3 1.0 %collective-permute-done.6.other = f32[8,512]{1,0:T(8,128)S(1)} collective-permute-done((f32[8,512]{1,0:T(8,128)S(1)}, f32[8,512]{1,0:T(8,128)S(1)}, u32[]{:S(2)}, u32[]{:S(2)}) %collective-permute-start.6) | collective-permute-done | bytes 16416 | tf_op jit(solution)/shard_map/ppermute | solution.py:303
  23.3 1.3 %shard_map.98 = f32[2,16]{1,0:T(2,128)} custom-call(s32[1]{0:T(128)} %bitcast.core_ref, f32[8,512]{1,0:T(8,128)S(1)} %fusion.own, f32[8,512]{1,0:T(8,128)S(1)} %collective-permute-done.6.other, f32[256,256]{1,0:T(8,128)S(1)} %copy-done.1, f32[256,256]{1,0:T(8,128)S(1)} %collective-permute-done.7.other_eigen, ...), custom_call_target="tpu_custom_call" | custom-call | tf_op jit(solution)/shard_map/pallas_call | solution.py:254
  (18 shorter events, 0.1 us)
Async XLA Ops:
  0.8 4.9 %copy-start = (bf16[3584,256]{1,0:T(8,128)(2,1)S(1)}, bf16[3584,256]{1,0:T(8,128)(2,1)}, u32[]{:S(2)}) copy-start(bf16[3584,256]{1,0:T(8,128)(2,1)} %out_basis.1) | copy-start | bytes 5505028
  0.8 4.9 %copy-start.2 = (bf16[3584,64]{0,1:T(8,128)(2,1)S(1)}, bf16[3584,64]{0,1:T(8,128)(2,1)}, u32[]{:S(2)}) copy-start(bf16[3584,64]{0,1:T(8,128)(2,1)} %param.9) | copy-start | bytes 1376260
  0.8 4.9 %copy-start.3 = (bf16[1024,128]{1,0:T(8,128)(2,1)S(1)}, bf16[1024,128]{1,0:T(8,128)(2,1)}, u32[]{:S(2)}) copy-start(bf16[1024,128]{1,0:T(8,128)(2,1)} %act_basis.1) | copy-start | bytes 786436
  0.8 4.9 %copy-start.4 = (bf16[1024,64]{0,1:T(8,128)(2,1)S(1)}, bf16[1024,64]{0,1:T(8,128)(2,1)}, u32[]{:S(2)}) copy-start(bf16[1024,64]{0,1:T(8,128)(2,1)} %param.10) | copy-start | bytes 393220
  0.8 13.9 %copy-start.1 = (f32[256,256]{1,0:T(8,128)S(1)}, f32[256,256]{1,0:T(8,128)}, u32[]{:S(2)}) copy-start(f32[256,256]{1,0:T(8,128)} %eigen.1) | copy-start | bytes 786436
  0.9 5.7 %collective-permute-start = (bf16[1,32,768]{2,1,0:T(8,128)(2,1)S(1)}, bf16[1,32,768]{2,1,0:T(8,128)(2,1)S(1)}, u32[]{:S(2)}, u32[]{:S(2)}) collective-permute-start(bf16[1,32,768]{2,1,0:T(8,128)(2,1)S(1)} %shard_map.93.first), channel_id=1, source_target_pairs={{0,9},{1,8},{2,11},{3,10},{4,13},{5,12},{6,15},{7,14},{8,1},{9,0},... | collective-permute-start | bytes 147464 | tf_op jit(solution)/shard_map/ppermute | solution.py:285
  6.6 7.2 %collective-permute-start.1 = (bf16[2,32,768]{2,1,0:T(8,128)(2,1)S(1)}, bf16[2,32,768]{2,1,0:T(8,128)(2,1)S(1)}, u32[]{:S(2)}, u32[]{:S(2)}) collective-permute-start(bf16[2,32,768]{2,1,0:T(8,128)(2,1)S(1)} %get-tuple-element.11.first), channel_id=1, source_target_pairs={{0,3},{1,2},{2,1},{3,0},{4,7},{5,6},{6,5},{7,4},{8,11},{9,10},{10,... | collective-permute-start | bytes 294920 | tf_op jit(solution)/shard_map/ppermute | solution.py:285
  8.4 7.1 %collective-permute-start.2 = (f32[2,8,512]{2,1,0:T(8,128)S(1)}, f32[2,8,512]{2,1,0:T(8,128)S(1)}, u32[]{:S(2)}, u32[]{:S(2)}) collective-permute-start(f32[2,8,512]{2,1,0:T(8,128)S(1)} %get-tuple-element.12), channel_id=1, source_target_pairs={{0,12},{2,14},{4,8},{6,10},{8,4},{10,6},{12,0},{14,2},{1,13},{3,15... | collective-permute-start | bytes 98312 | tf_op jit(solution)/shard_map/ppermute | solution.py:279
  13.1 4.9 %collective-permute-start.3 = (f32[2,8,512]{2,1,0:T(8,128)S(1)}, f32[2,8,512]{2,1,0:T(8,128)S(1)}, u32[]{:S(2)}, u32[]{:S(2)}) collective-permute-start(f32[2,8,512]{2,1,0:T(8,128)S(1)} %get-tuple-element.13), channel_id=1, source_target_pairs={{0,8},{2,10},{4,12},{6,14},{8,0},{10,2},{12,4},{14,6},{1,9},{3,11}... | collective-permute-start | bytes 98312 | tf_op jit(solution)/shard_map/ppermute | solution.py:279
  13.2 4.9 %collective-permute-start.4 = (f32[2,8,512]{2,1,0:T(8,128)S(1)}, f32[2,8,512]{2,1,0:T(8,128)S(1)}, u32[]{:S(2)}, u32[]{:S(2)}) collective-permute-start(f32[2,8,512]{2,1,0:T(8,128)S(1)} %get-tuple-element.14), channel_id=1, source_target_pairs={{0,4},{2,6},{4,0},{6,2},{8,12},{10,14},{12,8},{14,10},{1,5},{3,7},... | collective-permute-start | bytes 98312 | tf_op jit(solution)/shard_map/ppermute | solution.py:279
  13.7 8.0 %collective-permute-start.8 = (bf16[4,32,768]{2,1,0:T(8,128)(2,1)S(1)}, bf16[4,32,768]{2,1,0:T(8,128)(2,1)S(1)}, u32[]{:S(2)}, u32[]{:S(2)}) collective-permute-start(bf16[4,32,768]{2,1,0:T(8,128)(2,1)S(1)} %shard_map.95.after.rest_0_), channel_id=1, source_target_pairs={{0,5},{1,4},{2,7},{3,6},{4,1},{5,0},{6,3},{7,2},{8,13},{9,12},{10,... | collective-permute-start | bytes 589832 | tf_op jit(solution)/shard_map/ppermute | solution.py:285
  14.8 8.5 %collective-permute-start.7 = (f32[256,256]{1,0:T(8,128)S(1)}, f32[256,256]{1,0:T(8,128)S(1)}, u32[]{:S(2)}, u32[]{:S(2)}) collective-permute-start(f32[256,256]{1,0:T(8,128)S(1)} %shard_map.97), channel_id=1, source_target_pairs={{0,1},{1,0},{2,3},{3,2},{4,5},{5,4},{6,7},{7,6},{8,9},{9,8},{10,11... | collective-permute-start | bytes 786440 | tf_op jit(solution)/shard_map/ppermute | solution.py:299
  18.1 3.9 %collective-permute-start.5 = (f32[8,512]{1,0:T(8,128)S(1)}, f32[8,512]{1,0:T(8,128)S(1)}, u32[]{:S(2)}, u32[]{:S(2)}) collective-permute-start(f32[8,512]{1,0:T(8,128)S(1)} %slice_bitcast_fusion), channel_id=1, source_target_pairs={{0,2},{2,0},{4,6},{6,4},{8,10},{10,8},{12,14},{14,12},{1,3},{3,1},... | collective-permute-start | bytes 49160 | tf_op jit(solution)/shard_map/ppermute | solution.py:279
  18.7 4.6 %collective-permute-start.9 = (bf16[4,32,768]{2,1,0:T(8,128)(2,1)S(1)}, bf16[4,32,768]{2,1,0:T(8,128)(2,1)S(1)}, u32[]{:S(2)}, u32[]{:S(2)}) collective-permute-start(bf16[4,32,768]{2,1,0:T(8,128)(2,1)S(1)} %shard_map.95.after.rest_0_), channel_id=1, source_target_pairs={{0,1},{1,0},{2,3},{3,2},{4,5},{5,4},{6,7},{7,6},{8,9},{9,8},{10,11... | collective-permute-start | bytes 589832 | tf_op jit(solution)/shard_map/ppermute | solution.py:300
  21.7 1.5 %collective-permute-start.10 = (bf16[4,32,768]{2,1,0:T(8,128)(2,1)S(1)}, bf16[4,32,768]{2,1,0:T(8,128)(2,1)S(1)}, u32[]{:S(2)}, u32[]{:S(2)}) collective-permute-start(bf16[4,32,768]{2,1,0:T(8,128)(2,1)S(1)} %collective-permute-done.8.rest_1_), channel_id=1, source_target_pairs={{0,1},{1,0},{2,3},{3,2},{4,5},{5,4},{6,7},{7,6},{8,9},{9,8},{10,11... | collective-permute-start | bytes 589832 | tf_op jit(solution)/shard_map/ppermute | solution.py:301
  22.0 1.2 %collective-permute-start.6 = (f32[8,512]{1,0:T(8,128)S(1)}, f32[8,512]{1,0:T(8,128)S(1)}, u32[]{:S(2)}, u32[]{:S(2)}) collective-permute-start(f32[8,512]{1,0:T(8,128)S(1)} %fusion.own), channel_id=1, source_target_pairs={{0,1},{1,0},{2,3},{3,2},{4,5},{5,4},{6,7},{7,6},{8,9},{9,8},{10,11... | collective-permute-start | bytes 49160 | tf_op jit(solution)/shard_map/ppermute | solution.py:303

commit v22 on v16

--- a/solution.py
+++ b/solution.py
@@ -184,23 +184,37 @@
     return high, middle, low
 
 
-def score_kernel(core_ref, own, other, eigen, other_eigen, *rest):
+def scale_kernel(core_ref, after, eigen, other_eigen, scales):
+    del after
+    first = core_ref[0] == 0
+    half = eigen.shape[0]
+    scales[:half] = 1.0 / (jnp.where(first, eigen[...], other_eigen[...]) + damping)
+    scales[half:] = 1.0 / (jnp.where(first, other_eigen[...], eigen[...]) + damping)
+
+
+def invert(core, after, eigen, other_eigen):
+    half, ka = eigen.shape
+    return pl.pallas_call(
+        scale_kernel,
+        out_shape=jax.ShapeDtypeStruct((2 * half, ka), jnp.float32),
+        in_specs=[spec(pltpu.SMEM), spec(pl.ANY)] + [spec(pltpu.VMEM)] * 2,
+        out_specs=spec(pltpu.VMEM),
+        compiler_params=grant(4),
+    )(core, after, eigen, other_eigen)
+
+
+def score_kernel(core_ref, own, other, scales, *rest):
     blocks, out = rest[:-1], rest[-1]
     first = core_ref[0] == 0
-    half, ka = eigen.shape
+    half, ka = scales.shape[0] // 2, scales.shape[1]
     factor_rows, width = blocks[0].shape[1:]
     ks = width - ka
     shared = own.shape[1] - LANES
     mine, theirs = own[...], other[...]
     coords = (jnp.where(first, mine, theirs), jnp.where(first, theirs, mine))
-    eigens = (
-        jnp.where(first, eigen[...], other_eigen[...]),
-        jnp.where(first, other_eigen[...], eigen[...]),
-    )
-    scales = [1.0 / (e + damping) for e in eigens]
     act = jnp.concatenate([v[:, half:shared] for v in coords], axis=1)
     act_terms = split_three(act)
-    out_terms = [split_three(v[:, :half]) for v in coords]
+    out_terms = split_three(jnp.concatenate([v[:, :half] for v in coords], axis=1))
     order = ((0, 0), (0, 1), (1, 0), (1, 1), (0, 2), (2, 0))
     slot = lax.broadcasted_iota(jnp.int32, (mine.shape[0], LANES), 0)
     even = (slot // 4 + slot // 2 + slot) % 2 == 0
@@ -219,14 +233,11 @@
     for q in range(out.shape[0]):
         cut = slice(q * RQ, (q + 1) * RQ)
         right = jnp.concatenate([act_terms[b][cut] for _, b in order], axis=0)
-        precond = []
-        for part in range(2):
-            left = jnp.concatenate([out_terms[part][a][cut] for a, _ in order], axis=0)
-            numer = lax.dot_general(
-                left, right, (((0,), (0,)), ((), ())), preferred_element_type=jnp.float32
-            )
-            precond.append((numer * scales[part]).astype(jnp.bfloat16))
-        precond = jnp.concatenate(precond, axis=0)
+        left = jnp.concatenate([out_terms[a][cut] for a, _ in order], axis=0)
+        numer = lax.dot_general(
+            left, right, (((0,), (0,)), ((), ())), preferred_element_type=jnp.float32
+        )
+        precond = (numer * scales[...]).astype(jnp.bfloat16)
         projected = jnp.dot(flat, precond, preferred_element_type=jnp.float32)
         terms = projected.reshape(examples, factor_rows, ka) * weights
         per_example = jnp.sum(jnp.sum(terms, axis=1), axis=1, keepdims=True)
@@ -234,15 +245,15 @@
         out[q : q + 1, :] = scores[:, : out.shape[1]]
 
 
-def score(core, own, other, eigen, other_eigen, blocks):
+def score(core, own, other, scales, blocks):
     examples = sum(x.shape[0] for x in blocks)
     return pl.pallas_call(
         score_kernel,
         out_shape=jax.ShapeDtypeStruct((own.shape[0] // RQ, examples), jnp.float32),
-        in_specs=[spec(pltpu.SMEM)] + [spec(pltpu.VMEM)] * (4 + len(blocks)),
+        in_specs=[spec(pltpu.SMEM)] + [spec(pltpu.VMEM)] * (3 + len(blocks)),
         out_specs=spec(pltpu.VMEM),
         compiler_params=grant(12),
-    )(core, own, other, eigen, other_eigen, *blocks)
+    )(core, own, other, scales, *blocks)
 
 
 def direct(
@@ -287,9 +298,8 @@
     other_far = lax.ppermute(far, "fsdp", swap)
     own = sums[0] + apart(sums[1], 4)
     other = lax.ppermute(own, "fsdp", swap)
-    return score(
-        core, own, other, eigenvalues, other_eigen, (near, far, other_near, other_far)
-    )
+    scales = invert(core, near, eigenvalues, other_eigen)
+    return score(core, own, other, scales, (near, far, other_near, other_far))
 
 
 def score_block(precond, out_rows, act_rows, token_counts):

time: 24 us -> 24 us (level)
  transfers between devices with their start and end apart: 11 -> 11, of which waited for: 7 -> 7; matrix products, arithmetic and copies ran while one was open for 0% -> 0% of each run, Pallas kernels for 5% -> 6%
where the time goes in v22:
time: 24 us; the launch traced here: 23.8 us
  starting transfers between devices  15.7 us (65%)
  waiting for transfers between devices  3.85 us (16%)
  Pallas kernels  2.73 us (11%)
  between operations  1.44 us (6%)
    ppermute x3, starting transfers between devices, crossed(): return lax.ppermute(x, ('blk', 'fsdp'), pairs)  7.69 us
    ppermute x4, starting transfers between devices, apart(): return lax.ppermute(x, 'blk', [(s, s ^ distance) for s in range(parts)])  7.35 us
    ppermute x4, waiting for transfers between devices, apart(): return lax.ppermute(x, 'blk', [(s, s ^ distance) for s in range(parts)])  2.16 us
    pallas_call x1, Pallas kernels, score(): pl.pallas_call(score_kernel, out_shape=jax.ShapeDtypeStruct((own.shape[0]...  1.35 us
    ppermute x1, waiting for transfers between devices, direct(): other = lax.ppermute(own, 'fsdp', swap)  1.07 us
    pallas_call x1, Pallas kernels, pack(): pl.pallas_call(pack_kernel, out_shape=jax.ShapeDtypeStruct(shape, train_o...  0.78 us
    ppermute x3, waiting for transfers between devices, crossed(): return lax.ppermute(x, ('blk', 'fsdp'), pairs)  0.62 us
  transfers between devices with their start and end apart: 11, of which 7 were waited for; matrix products, arithmetic and copies ran while one was open for 0% of the time, Pallas kernels for 6%

profile of v22, /device:TPU:0, one launch (start us, length us, event | category | flops | bytes accessed | tf_op | source)
XLA Modules:
  0.0 23.8 jit_solution(16342327633488955133)
XLA Ops:
  0.0 0.5 %collective-permute-start = (f32[256,256]{1,0:T(8,128)}, f32[256,256]{1,0:T(8,128)S(1)}, u32[]{:S(2)}, u32[]{:S(2)}) collective-permute-start(f32[256,256]{1,0:T(8,128)} %eigen.1), channel_id=1, source_target_pairs={{0,1},{1,0},{2,3},{3,2},{4,5},{5,4},{6,7},{7,6},{8,9},{9,8},{10,11... | collective-permute-start | bytes 786440 | tf_op jit(solution)/shard_map/ppermute | solution.py:285
  0.5 0.8 %shard_map.92.source = bf16[1,32,768]{2,1,0:T(8,128)(2,1)S(1)} custom-call(bf16[1,32,512]{2,1,0:T(8,128)(2,1)} %train_out.1, bf16[1,32,256]{2,1,0:T(8,128)(2,1)} %train_act.1), custom_call_target="tpu_custom_call" | custom-call | tf_op jit(solution)/shard_map/pallas_call | solution.py:46
  1.2 0.0 copy-start
  1.2 0.0 copy-start.1
  1.3 0.0 copy-start.3
  1.3 0.0 copy-start.4
  1.3 3.8 %collective-permute-start.1 = (bf16[1,32,768]{2,1,0:T(8,128)(2,1)S(1)}, bf16[1,32,768]{2,1,0:T(8,128)(2,1)S(1)}, u32[]{:S(2)}, u32[]{:S(2)}) collective-permute-start(bf16[1,32,768]{2,1,0:T(8,128)(2,1)S(1)} %shard_map.93.first), channel_id=1, source_target_pairs={{0,9},{1,8},{2,11},{3,10},{4,13},{5,12},{6,15},{7,14},{8,1},{9,0},... | collective-permute-start | bytes 147464 | tf_op jit(solution)/shard_map/ppermute | solution.py:281
  6.4 0.5 %shard_map.91.total = f32[64,384]{1,0:T(8,128)S(1)} custom-call(bf16[64,3584]{1,0:T(8,128)(2,1)S(1)} %bitcast.10, bf16[64,1024]{1,0:T(8,128)(2,1)S(1)} %bitcast.11, bf16[3584,256]{1,0:T(8,128)(2,1)S(1)} %copy-done, bf16[1024,128]{1,0:T(8,128)(2,1)S(1)} %copy-done.3), custom_call_target="tpu_custom_call" | custom-call | flops 134217728 | bytes 2686976 | tf_op jit(solution)/shard_map/pallas_call | solution.py:126
  6.9 0.3 %collective-permute-done.1.second = bf16[1,32,768]{2,1,0:T(8,128)(2,1)S(1)} collective-permute-done((bf16[1,32,768]{2,1,0:T(8,128)(2,1)S(1)}, bf16[1,32,768]{2,1,0:T(8,128)(2,1)S(1)}, u32[]{:S(2)}, u32[]{:S(2)}) %collective-permute-start.1) | collective-permute-done | bytes 49184 | tf_op jit(solution)/shard_map/ppermute | solution.py:281
  7.2 1.4 %collective-permute-start.2 = (bf16[2,32,768]{2,1,0:T(8,128)(2,1)S(1)}, bf16[2,32,768]{2,1,0:T(8,128)(2,1)S(1)}, u32[]{:S(2)}, u32[]{:S(2)}) collective-permute-start(bf16[2,32,768]{2,1,0:T(8,128)(2,1)S(1)} %get-tuple-element.11.first), channel_id=1, source_target_pairs={{0,5},{1,4},{2,7},{3,6},{4,1},{5,0},{6,3},{7,2},{8,13},{9,12},{10,... | collective-permute-start | bytes 294920 | tf_op jit(solution)/shard_map/ppermute | solution.py:281
  8.6 2.4 %collective-permute-start.3 = (f32[2,8,512]{2,1,0:T(8,128)S(1)}, f32[2,8,512]{2,1,0:T(8,128)S(1)}, u32[]{:S(2)}, u32[]{:S(2)}) collective-permute-start(f32[2,8,512]{2,1,0:T(8,128)S(1)} %get-tuple-element.12), channel_id=1, source_target_pairs={{0,6},{2,4},{4,2},{6,0},{8,14},{10,12},{12,10},{14,8},{1,7},{3,5},... | collective-permute-start | bytes 98312 | tf_op jit(solution)/shard_map/ppermute | solution.py:275
  11.0 0.5 %collective-permute-start.4 = (f32[2,8,512]{2,1,0:T(8,128)S(1)}, f32[2,8,512]{2,1,0:T(8,128)S(1)}, u32[]{:S(2)}, u32[]{:S(2)}) collective-permute-start(f32[2,8,512]{2,1,0:T(8,128)S(1)} %get-tuple-element.13), channel_id=1, source_target_pairs={{0,4},{2,6},{4,0},{6,2},{8,12},{10,14},{12,8},{14,10},{1,5},{3,7},... | collective-permute-start | bytes 98312 | tf_op jit(solution)/shard_map/ppermute | solution.py:275
  11.5 0.5 %collective-permute-start.5 = (f32[2,8,512]{2,1,0:T(8,128)S(1)}, f32[2,8,512]{2,1,0:T(8,128)S(1)}, u32[]{:S(2)}, u32[]{:S(2)}) collective-permute-start(f32[2,8,512]{2,1,0:T(8,128)S(1)} %get-tuple-element.14), channel_id=1, source_target_pairs={{0,2},{2,0},{4,6},{6,4},{8,10},{10,8},{12,14},{14,12},{1,3},{3,1},... | collective-permute-start | bytes 98312 | tf_op jit(solution)/shard_map/ppermute | solution.py:275
  12.1 2.6 %collective-permute-start.8 = (bf16[4,32,768]{2,1,0:T(8,128)(2,1)S(1)}, bf16[4,32,768]{2,1,0:T(8,128)(2,1)S(1)}, u32[]{:S(2)}, u32[]{:S(2)}) collective-permute-start(bf16[4,32,768]{2,1,0:T(8,128)(2,1)S(1)} %shard_map.95.after.rest_0_), channel_id=1, source_target_pairs={{0,3},{1,2},{2,1},{3,0},{4,7},{5,6},{6,5},{7,4},{8,11},{9,10},{10,... | collective-permute-start | bytes 589832 | tf_op jit(solution)/shard_map/ppermute | solution.py:281
  14.6 0.1 collective-permute-done.3.refs_1_
  14.7 0.2 collective-permute-done.4.refs_2_
  14.9 0.5 %collective-permute-done.5.refs_3_ = f32[2,8,512]{2,1,0:T(8,128)S(1)} collective-permute-done((f32[2,8,512]{2,1,0:T(8,128)S(1)}, f32[2,8,512]{2,1,0:T(8,128)S(1)}, u32[]{:S(2)}, u32[]{:S(2)}) %collective-permute-start.5) | collective-permute-done | bytes 32800 | tf_op jit(solution)/shard_map/ppermute | solution.py:275
  15.5 3.9 %collective-permute-start.6 = (f32[8,512]{1,0:T(8,128)S(1)}, f32[8,512]{1,0:T(8,128)S(1)}, u32[]{:S(2)}, u32[]{:S(2)}) collective-permute-start(f32[8,512]{1,0:T(8,128)S(1)} %slice_bitcast_fusion), channel_id=1, source_target_pairs={{0,8},{2,10},{4,12},{6,14},{8,0},{10,2},{12,4},{14,6},{1,9},{3,11}... | collective-permute-start | bytes 49160 | tf_op jit(solution)/shard_map/ppermute | solution.py:275
  19.3 0.3 %collective-permute-done.8.rest_1_ = bf16[4,32,768]{2,1,0:T(8,128)(2,1)S(1)} collective-permute-done((bf16[4,32,768]{2,1,0:T(8,128)(2,1)S(1)}, bf16[4,32,768]{2,1,0:T(8,128)(2,1)S(1)}, u32[]{:S(2)}, u32[]{:S(2)}) %collective-permute-start.8) | collective-permute-done | bytes 196640 | tf_op jit(solution)/shard_map/ppermute | solution.py:281
  19.7 0.2 collective-permute-start.10
  19.8 1.4 %collective-permute-done.6 = f32[8,512]{1,0:T(8,128)S(1)} collective-permute-done((f32[8,512]{1,0:T(8,128)S(1)}, f32[8,512]{1,0:T(8,128)S(1)}, u32[]{:S(2)}, u32[]{:S(2)}) %collective-permute-start.6) | collective-permute-done | bytes 16416 | tf_op jit(solution)/shard_map/ppermute | solution.py:275
  21.2 0.1 shard_map.97.scales
  21.3 1.1 %collective-permute-done.7.other = f32[8,512]{1,0:T(8,128)S(1)} collective-permute-done((f32[8,512]{1,0:T(8,128)S(1)}, f32[8,512]{1,0:T(8,128)S(1)}, u32[]{:S(2)}, u32[]{:S(2)}) %collective-permute-start.7) | collective-permute-done | bytes 16416 | tf_op jit(solution)/shard_map/ppermute | solution.py:300
  22.4 1.3 %shard_map.98 = f32[2,16]{1,0:T(2,128)} custom-call(s32[1]{0:T(128)} %bitcast.core_ref, f32[8,512]{1,0:T(8,128)S(1)} %fusion.own, f32[8,512]{1,0:T(8,128)S(1)} %collective-permute-done.7.other, f32[512,256]{1,0:T(8,128)S(1)} %shard_map.97.scales, bf16[4,32,768]{2,1,0:T(8,128)(2,1)S(1)} %shard_map.95.after.rest_0_, ...), custom_call_target="tpu_custom_call" | custom-call | tf_op jit(solution)/shard_map/pallas_call | solution.py:250
  (18 shorter events, 0.1 us)
Async XLA Ops:
  0.0 7.2 %collective-permute-start = (f32[256,256]{1,0:T(8,128)}, f32[256,256]{1,0:T(8,128)S(1)}, u32[]{:S(2)}, u32[]{:S(2)}) collective-permute-start(f32[256,256]{1,0:T(8,128)} %eigen.1), channel_id=1, source_target_pairs={{0,1},{1,0},{2,3},{3,2},{4,5},{5,4},{6,7},{7,6},{8,9},{9,8},{10,11... | collective-permute-start | bytes 786440 | tf_op jit(solution)/shard_map/ppermute | solution.py:285
  1.2 5.1 %copy-start = (bf16[3584,256]{1,0:T(8,128)(2,1)S(1)}, bf16[3584,256]{1,0:T(8,128)(2,1)}, u32[]{:S(2)}) copy-start(bf16[3584,256]{1,0:T(8,128)(2,1)} %out_basis.1) | copy-start | bytes 5505028
  1.2 5.1 %copy-start.1 = (bf16[3584,64]{0,1:T(8,128)(2,1)S(1)}, bf16[3584,64]{0,1:T(8,128)(2,1)}, u32[]{:S(2)}) copy-start(bf16[3584,64]{0,1:T(8,128)(2,1)} %param.9) | copy-start | bytes 1376260
  1.3 5.1 %copy-start.3 = (bf16[1024,128]{1,0:T(8,128)(2,1)S(1)}, bf16[1024,128]{1,0:T(8,128)(2,1)}, u32[]{:S(2)}) copy-start(bf16[1024,128]{1,0:T(8,128)(2,1)} %act_basis.1) | copy-start | bytes 786436
  1.3 5.1 %copy-start.4 = (bf16[1024,64]{0,1:T(8,128)(2,1)S(1)}, bf16[1024,64]{0,1:T(8,128)(2,1)}, u32[]{:S(2)}) copy-start(bf16[1024,64]{0,1:T(8,128)(2,1)} %param.10) | copy-start | bytes 393220
  1.3 5.9 %collective-permute-start.1 = (bf16[1,32,768]{2,1,0:T(8,128)(2,1)S(1)}, bf16[1,32,768]{2,1,0:T(8,128)(2,1)S(1)}, u32[]{:S(2)}, u32[]{:S(2)}) collective-permute-start(bf16[1,32,768]{2,1,0:T(8,128)(2,1)S(1)} %shard_map.93.first), channel_id=1, source_target_pairs={{0,9},{1,8},{2,11},{3,10},{4,13},{5,12},{6,15},{7,14},{8,1},{9,0},... | collective-permute-start | bytes 147464 | tf_op jit(solution)/shard_map/ppermute | solution.py:281
  6.4 14.8 %copy-start.2 = (f32[256,256]{1,0:T(8,128)S(1)}, f32[256,256]{1,0:T(8,128)}, u32[]{:S(2)}) copy-start(f32[256,256]{1,0:T(8,128)} %eigen.1) | copy-start | bytes 786436
  7.2 4.8 %collective-permute-start.2 = (bf16[2,32,768]{2,1,0:T(8,128)(2,1)S(1)}, bf16[2,32,768]{2,1,0:T(8,128)(2,1)S(1)}, u32[]{:S(2)}, u32[]{:S(2)}) collective-permute-start(bf16[2,32,768]{2,1,0:T(8,128)(2,1)S(1)} %get-tuple-element.11.first), channel_id=1, source_target_pairs={{0,5},{1,4},{2,7},{3,6},{4,1},{5,0},{6,3},{7,2},{8,13},{9,12},{10,... | collective-permute-start | bytes 294920 | tf_op jit(solution)/shard_map/ppermute | solution.py:281
  8.6 6.2 %collective-permute-start.3 = (f32[2,8,512]{2,1,0:T(8,128)S(1)}, f32[2,8,512]{2,1,0:T(8,128)S(1)}, u32[]{:S(2)}, u32[]{:S(2)}) collective-permute-start(f32[2,8,512]{2,1,0:T(8,128)S(1)} %get-tuple-element.12), channel_id=1, source_target_pairs={{0,6},{2,4},{4,2},{6,0},{8,14},{10,12},{12,10},{14,8},{1,7},{3,5},... | collective-permute-start | bytes 98312 | tf_op jit(solution)/shard_map/ppermute | solution.py:275
  11.0 3.9 %collective-permute-start.4 = (f32[2,8,512]{2,1,0:T(8,128)S(1)}, f32[2,8,512]{2,1,0:T(8,128)S(1)}, u32[]{:S(2)}, u32[]{:S(2)}) collective-permute-start(f32[2,8,512]{2,1,0:T(8,128)S(1)} %get-tuple-element.13), channel_id=1, source_target_pairs={{0,4},{2,6},{4,0},{6,2},{8,12},{10,14},{12,8},{14,10},{1,5},{3,7},... | collective-permute-start | bytes 98312 | tf_op jit(solution)/shard_map/ppermute | solution.py:275
  11.5 3.9 %collective-permute-start.5 = (f32[2,8,512]{2,1,0:T(8,128)S(1)}, f32[2,8,512]{2,1,0:T(8,128)S(1)}, u32[]{:S(2)}, u32[]{:S(2)}) collective-permute-start(f32[2,8,512]{2,1,0:T(8,128)S(1)} %get-tuple-element.14), channel_id=1, source_target_pairs={{0,2},{2,0},{4,6},{6,4},{8,10},{10,8},{12,14},{14,12},{1,3},{3,1},... | collective-permute-start | bytes 98312 | tf_op jit(solution)/shard_map/ppermute | solution.py:275
  12.1 7.6 %collective-permute-start.8 = (bf16[4,32,768]{2,1,0:T(8,128)(2,1)S(1)}, bf16[4,32,768]{2,1,0:T(8,128)(2,1)S(1)}, u32[]{:S(2)}, u32[]{:S(2)}) collective-permute-start(bf16[4,32,768]{2,1,0:T(8,128)(2,1)S(1)} %shard_map.95.after.rest_0_), channel_id=1, source_target_pairs={{0,3},{1,2},{2,1},{3,0},{4,7},{5,6},{6,5},{7,4},{8,11},{9,10},{10,... | collective-permute-start | bytes 589832 | tf_op jit(solution)/shard_map/ppermute | solution.py:281
  15.5 5.8 %collective-permute-start.6 = (f32[8,512]{1,0:T(8,128)S(1)}, f32[8,512]{1,0:T(8,128)S(1)}, u32[]{:S(2)}, u32[]{:S(2)}) collective-permute-start(f32[8,512]{1,0:T(8,128)S(1)} %slice_bitcast_fusion), channel_id=1, source_target_pairs={{0,8},{2,10},{4,12},{6,14},{8,0},{10,2},{12,4},{14,6},{1,9},{3,11}... | collective-permute-start | bytes 49160 | tf_op jit(solution)/shard_map/ppermute | solution.py:275
  19.3 3.1 %collective-permute-start.9 = (bf16[4,32,768]{2,1,0:T(8,128)(2,1)S(1)}, bf16[4,32,768]{2,1,0:T(8,128)(2,1)S(1)}, u32[]{:S(2)}, u32[]{:S(2)}) collective-permute-start(bf16[4,32,768]{2,1,0:T(8,128)(2,1)S(1)} %shard_map.95.after.rest_0_), channel_id=1, source_target_pairs={{0,1},{1,0},{2,3},{3,2},{4,5},{5,4},{6,7},{7,6},{8,9},{9,8},{10,11... | collective-permute-start | bytes 589832 | tf_op jit(solution)/shard_map/ppermute | solution.py:297
  19.7 2.8 %collective-permute-start.10 = (bf16[4,32,768]{2,1,0:T(8,128)(2,1)S(1)}, bf16[4,32,768]{2,1,0:T(8,128)(2,1)S(1)}, u32[]{:S(2)}, u32[]{:S(2)}) collective-permute-start(bf16[4,32,768]{2,1,0:T(8,128)(2,1)S(1)} %collective-permute-done.8.rest_1_), channel_id=1, source_target_pairs={{0,1},{1,0},{2,3},{3,2},{4,5},{5,4},{6,7},{7,6},{8,9},{9,8},{10,11... | collective-permute-start | bytes 589832 | tf_op jit(solution)/shard_map/ppermute | solution.py:298
  21.2 1.2 %collective-permute-start.7 = (f32[8,512]{1,0:T(8,128)S(1)}, f32[8,512]{1,0:T(8,128)S(1)}, u32[]{:S(2)}, u32[]{:S(2)}) collective-permute-start(f32[8,512]{1,0:T(8,128)S(1)} %fusion.own), channel_id=1, source_target_pairs={{0,1},{1,0},{2,3},{3,2},{4,5},{5,4},{6,7},{7,6},{8,9},{9,8},{10,11... | collective-permute-start | bytes 49160 | tf_op jit(solution)/shard_map/ppermute | solution.py:300

commit v23 on v22

--- a/solution.py
+++ b/solution.py
@@ -230,16 +230,20 @@
     keep = row < facts[:, LANES // 2 : LANES // 2 + 1][:, :, None]
     weights = jnp.where(keep, rows[:, :, ks:].astype(jnp.float32), 0.0)
     flat = rows[:, :, :ks].reshape(examples * factor_rows, ks)
-    for q in range(out.shape[0]):
+    queries = out.shape[0]
+    preconds = []
+    for q in range(queries):
         cut = slice(q * RQ, (q + 1) * RQ)
         right = jnp.concatenate([act_terms[b][cut] for _, b in order], axis=0)
         left = jnp.concatenate([out_terms[a][cut] for a, _ in order], axis=0)
         numer = lax.dot_general(
             left, right, (((0,), (0,)), ((), ())), preferred_element_type=jnp.float32
         )
-        precond = (numer * scales[...]).astype(jnp.bfloat16)
-        projected = jnp.dot(flat, precond, preferred_element_type=jnp.float32)
-        terms = projected.reshape(examples, factor_rows, ka) * weights
+        preconds.append((numer * scales[...]).astype(jnp.bfloat16))
+    precond = jnp.concatenate(preconds, axis=1)
+    projected = jnp.dot(flat, precond, preferred_element_type=jnp.float32)
+    for q in range(queries):
+        terms = projected[:, q * ka : (q + 1) * ka].reshape(examples, factor_rows, ka) * weights
         per_example = jnp.sum(jnp.sum(terms, axis=1), axis=1, keepdims=True)
         scores = jnp.sum(jnp.where(hot, per_example, 0.0), axis=0, keepdims=True)
         out[q : q + 1, :] = scores[:, : out.shape[1]]

time: 24 us -> 24 us (level)
  no operation moved by 1% of the time
where the time goes in v23:
time: 24 us; the launch traced here: 23.8 us
  starting transfers between devices  15.7 us (65%)
  waiting for transfers between devices  3.85 us (16%)
  Pallas kernels  2.73 us (11%)
  between operations  1.44 us (6%)
    ppermute x3, starting transfers between devices, crossed(): return lax.ppermute(x, ('blk', 'fsdp'), pairs)  7.69 us
    ppermute x4, starting transfers between devices, apart(): return lax.ppermute(x, 'blk', [(s, s ^ distance) for s in range(parts)])  7.35 us
    ppermute x4, waiting for transfers between devices, apart(): return lax.ppermute(x, 'blk', [(s, s ^ distance) for s in range(parts)])  2.16 us
    pallas_call x1, Pallas kernels, score(): pl.pallas_call(score_kernel, out_shape=jax.ShapeDtypeStruct((own.shape[0]...  1.35 us
    ppermute x1, waiting for transfers between devices, direct(): other = lax.ppermute(own, 'fsdp', swap)  1.07 us
    pallas_call x1, Pallas kernels, pack(): pl.pallas_call(pack_kernel, out_shape=jax.ShapeDtypeStruct(shape, train_o...  0.78 us
    ppermute x3, waiting for transfers between devices, crossed(): return lax.ppermute(x, ('blk', 'fsdp'), pairs)  0.62 us
  transfers between devices with their start and end apart: 11, of which 7 were waited for; matrix products, arithmetic and copies ran while one was open for 0% of the time, Pallas kernels for 6%

profile of v23, /device:TPU:0, one launch (start us, length us, event | category | flops | bytes accessed | tf_op | source)
XLA Modules:
  0.0 23.8 jit_solution(11056233983654913854)
XLA Ops:
  0.0 0.5 %collective-permute-start = (f32[256,256]{1,0:T(8,128)}, f32[256,256]{1,0:T(8,128)S(1)}, u32[]{:S(2)}, u32[]{:S(2)}) collective-permute-start(f32[256,256]{1,0:T(8,128)} %eigen.1), channel_id=1, source_target_pairs={{0,1},{1,0},{2,3},{3,2},{4,5},{5,4},{6,7},{7,6},{8,9},{9,8},{10,11... | collective-permute-start | bytes 786440 | tf_op jit(solution)/shard_map/ppermute | solution.py:289
  0.5 0.8 %shard_map.92.source = bf16[1,32,768]{2,1,0:T(8,128)(2,1)S(1)} custom-call(bf16[1,32,512]{2,1,0:T(8,128)(2,1)} %train_out.1, bf16[1,32,256]{2,1,0:T(8,128)(2,1)} %train_act.1), custom_call_target="tpu_custom_call" | custom-call | tf_op jit(solution)/shard_map/pallas_call | solution.py:46
  1.2 0.0 copy-start
  1.2 0.0 copy-start.1
  1.3 0.0 copy-start.3
  1.3 0.0 copy-start.4
  1.3 3.8 %collective-permute-start.1 = (bf16[1,32,768]{2,1,0:T(8,128)(2,1)S(1)}, bf16[1,32,768]{2,1,0:T(8,128)(2,1)S(1)}, u32[]{:S(2)}, u32[]{:S(2)}) collective-permute-start(bf16[1,32,768]{2,1,0:T(8,128)(2,1)S(1)} %shard_map.93.first), channel_id=1, source_target_pairs={{0,9},{1,8},{2,11},{3,10},{4,13},{5,12},{6,15},{7,14},{8,1},{9,0},... | collective-permute-start | bytes 147464 | tf_op jit(solution)/shard_map/ppermute | solution.py:285
  6.4 0.5 %shard_map.91.total = f32[64,384]{1,0:T(8,128)S(1)} custom-call(bf16[64,3584]{1,0:T(8,128)(2,1)S(1)} %bitcast.10, bf16[64,1024]{1,0:T(8,128)(2,1)S(1)} %bitcast.11, bf16[3584,256]{1,0:T(8,128)(2,1)S(1)} %copy-done, bf16[1024,128]{1,0:T(8,128)(2,1)S(1)} %copy-done.3), custom_call_target="tpu_custom_call" | custom-call | flops 134217728 | bytes 2686976 | tf_op jit(solution)/shard_map/pallas_call | solution.py:126
  6.9 0.3 %collective-permute-done.1.second = bf16[1,32,768]{2,1,0:T(8,128)(2,1)S(1)} collective-permute-done((bf16[1,32,768]{2,1,0:T(8,128)(2,1)S(1)}, bf16[1,32,768]{2,1,0:T(8,128)(2,1)S(1)}, u32[]{:S(2)}, u32[]{:S(2)}) %collective-permute-start.1) | collective-permute-done | bytes 49184 | tf_op jit(solution)/shard_map/ppermute | solution.py:285
  7.2 1.4 %collective-permute-start.2 = (bf16[2,32,768]{2,1,0:T(8,128)(2,1)S(1)}, bf16[2,32,768]{2,1,0:T(8,128)(2,1)S(1)}, u32[]{:S(2)}, u32[]{:S(2)}) collective-permute-start(bf16[2,32,768]{2,1,0:T(8,128)(2,1)S(1)} %get-tuple-element.11.first), channel_id=1, source_target_pairs={{0,5},{1,4},{2,7},{3,6},{4,1},{5,0},{6,3},{7,2},{8,13},{9,12},{10,... | collective-permute-start | bytes 294920 | tf_op jit(solution)/shard_map/ppermute | solution.py:285
  8.6 2.4 %collective-permute-start.3 = (f32[2,8,512]{2,1,0:T(8,128)S(1)}, f32[2,8,512]{2,1,0:T(8,128)S(1)}, u32[]{:S(2)}, u32[]{:S(2)}) collective-permute-start(f32[2,8,512]{2,1,0:T(8,128)S(1)} %get-tuple-element.12), channel_id=1, source_target_pairs={{0,6},{2,4},{4,2},{6,0},{8,14},{10,12},{12,10},{14,8},{1,7},{3,5},... | collective-permute-start | bytes 98312 | tf_op jit(solution)/shard_map/ppermute | solution.py:279
  11.0 0.5 %collective-permute-start.4 = (f32[2,8,512]{2,1,0:T(8,128)S(1)}, f32[2,8,512]{2,1,0:T(8,128)S(1)}, u32[]{:S(2)}, u32[]{:S(2)}) collective-permute-start(f32[2,8,512]{2,1,0:T(8,128)S(1)} %get-tuple-element.13), channel_id=1, source_target_pairs={{0,4},{2,6},{4,0},{6,2},{8,12},{10,14},{12,8},{14,10},{1,5},{3,7},... | collective-permute-start | bytes 98312 | tf_op jit(solution)/shard_map/ppermute | solution.py:279
  11.5 0.5 %collective-permute-start.5 = (f32[2,8,512]{2,1,0:T(8,128)S(1)}, f32[2,8,512]{2,1,0:T(8,128)S(1)}, u32[]{:S(2)}, u32[]{:S(2)}) collective-permute-start(f32[2,8,512]{2,1,0:T(8,128)S(1)} %get-tuple-element.14), channel_id=1, source_target_pairs={{0,2},{2,0},{4,6},{6,4},{8,10},{10,8},{12,14},{14,12},{1,3},{3,1},... | collective-permute-start | bytes 98312 | tf_op jit(solution)/shard_map/ppermute | solution.py:279
  12.1 2.6 %collective-permute-start.8 = (bf16[4,32,768]{2,1,0:T(8,128)(2,1)S(1)}, bf16[4,32,768]{2,1,0:T(8,128)(2,1)S(1)}, u32[]{:S(2)}, u32[]{:S(2)}) collective-permute-start(bf16[4,32,768]{2,1,0:T(8,128)(2,1)S(1)} %shard_map.95.after.rest_0_), channel_id=1, source_target_pairs={{0,3},{1,2},{2,1},{3,0},{4,7},{5,6},{6,5},{7,4},{8,11},{9,10},{10,... | collective-permute-start | bytes 589832 | tf_op jit(solution)/shard_map/ppermute | solution.py:285
  14.6 0.1 collective-permute-done.3.refs_1_
  14.7 0.2 collective-permute-done.4.refs_2_
  14.9 0.5 %collective-permute-done.5.refs_3_ = f32[2,8,512]{2,1,0:T(8,128)S(1)} collective-permute-done((f32[2,8,512]{2,1,0:T(8,128)S(1)}, f32[2,8,512]{2,1,0:T(8,128)S(1)}, u32[]{:S(2)}, u32[]{:S(2)}) %collective-permute-start.5) | collective-permute-done | bytes 32800 | tf_op jit(solution)/shard_map/ppermute | solution.py:279
  15.5 3.9 %collective-permute-start.6 = (f32[8,512]{1,0:T(8,128)S(1)}, f32[8,512]{1,0:T(8,128)S(1)}, u32[]{:S(2)}, u32[]{:S(2)}) collective-permute-start(f32[8,512]{1,0:T(8,128)S(1)} %slice_bitcast_fusion), channel_id=1, source_target_pairs={{0,8},{2,10},{4,12},{6,14},{8,0},{10,2},{12,4},{14,6},{1,9},{3,11}... | collective-permute-start | bytes 49160 | tf_op jit(solution)/shard_map/ppermute | solution.py:279
  19.3 0.3 %collective-permute-done.8.rest_1_ = bf16[4,32,768]{2,1,0:T(8,128)(2,1)S(1)} collective-permute-done((bf16[4,32,768]{2,1,0:T(8,128)(2,1)S(1)}, bf16[4,32,768]{2,1,0:T(8,128)(2,1)S(1)}, u32[]{:S(2)}, u32[]{:S(2)}) %collective-permute-start.8) | collective-permute-done | bytes 196640 | tf_op jit(solution)/shard_map/ppermute | solution.py:285
  19.7 0.2 collective-permute-start.10
  19.8 1.4 %collective-permute-done.6 = f32[8,512]{1,0:T(8,128)S(1)} collective-permute-done((f32[8,512]{1,0:T(8,128)S(1)}, f32[8,512]{1,0:T(8,128)S(1)}, u32[]{:S(2)}, u32[]{:S(2)}) %collective-permute-start.6) | collective-permute-done | bytes 16416 | tf_op jit(solution)/shard_map/ppermute | solution.py:279
  21.2 0.1 shard_map.97.scales
  21.3 1.1 %collective-permute-done.7.other = f32[8,512]{1,0:T(8,128)S(1)} collective-permute-done((f32[8,512]{1,0:T(8,128)S(1)}, f32[8,512]{1,0:T(8,128)S(1)}, u32[]{:S(2)}, u32[]{:S(2)}) %collective-permute-start.7) | collective-permute-done | bytes 16416 | tf_op jit(solution)/shard_map/ppermute | solution.py:304
  22.4 1.3 %shard_map.98 = f32[2,16]{1,0:T(2,128)} custom-call(s32[1]{0:T(128)} %bitcast.core_ref, f32[8,512]{1,0:T(8,128)S(1)} %fusion.own, f32[8,512]{1,0:T(8,128)S(1)} %collective-permute-done.7.other, f32[512,256]{1,0:T(8,128)S(1)} %shard_map.97.scales, bf16[4,32,768]{2,1,0:T(8,128)(2,1)S(1)} %shard_map.95.after.rest_0_, ...), custom_call_target="tpu_custom_call" | custom-call | tf_op jit(solution)/shard_map/pallas_call | solution.py:254
  (18 shorter events, 0.1 us)
Async XLA Ops:
  0.0 7.2 %collective-permute-start = (f32[256,256]{1,0:T(8,128)}, f32[256,256]{1,0:T(8,128)S(1)}, u32[]{:S(2)}, u32[]{:S(2)}) collective-permute-start(f32[256,256]{1,0:T(8,128)} %eigen.1), channel_id=1, source_target_pairs={{0,1},{1,0},{2,3},{3,2},{4,5},{5,4},{6,7},{7,6},{8,9},{9,8},{10,11... | collective-permute-start | bytes 786440 | tf_op jit(solution)/shard_map/ppermute | solution.py:289
  1.2 5.1 %copy-start = (bf16[3584,256]{1,0:T(8,128)(2,1)S(1)}, bf16[3584,256]{1,0:T(8,128)(2,1)}, u32[]{:S(2)}) copy-start(bf16[3584,256]{1,0:T(8,128)(2,1)} %out_basis.1) | copy-start | bytes 5505028
  1.2 5.1 %copy-start.1 = (bf16[3584,64]{0,1:T(8,128)(2,1)S(1)}, bf16[3584,64]{0,1:T(8,128)(2,1)}, u32[]{:S(2)}) copy-start(bf16[3584,64]{0,1:T(8,128)(2,1)} %param.9) | copy-start | bytes 1376260
  1.3 5.1 %copy-start.3 = (bf16[1024,128]{1,0:T(8,128)(2,1)S(1)}, bf16[1024,128]{1,0:T(8,128)(2,1)}, u32[]{:S(2)}) copy-start(bf16[1024,128]{1,0:T(8,128)(2,1)} %act_basis.1) | copy-start | bytes 786436
  1.3 5.1 %copy-start.4 = (bf16[1024,64]{0,1:T(8,128)(2,1)S(1)}, bf16[1024,64]{0,1:T(8,128)(2,1)}, u32[]{:S(2)}) copy-start(bf16[1024,64]{0,1:T(8,128)(2,1)} %param.10) | copy-start | bytes 393220
  1.3 5.9 %collective-permute-start.1 = (bf16[1,32,768]{2,1,0:T(8,128)(2,1)S(1)}, bf16[1,32,768]{2,1,0:T(8,128)(2,1)S(1)}, u32[]{:S(2)}, u32[]{:S(2)}) collective-permute-start(bf16[1,32,768]{2,1,0:T(8,128)(2,1)S(1)} %shard_map.93.first), channel_id=1, source_target_pairs={{0,9},{1,8},{2,11},{3,10},{4,13},{5,12},{6,15},{7,14},{8,1},{9,0},... | collective-permute-start | bytes 147464 | tf_op jit(solution)/shard_map/ppermute | solution.py:285
  6.4 14.8 %copy-start.2 = (f32[256,256]{1,0:T(8,128)S(1)}, f32[256,256]{1,0:T(8,128)}, u32[]{:S(2)}) copy-start(f32[256,256]{1,0:T(8,128)} %eigen.1) | copy-start | bytes 786436
  7.2 4.8 %collective-permute-start.2 = (bf16[2,32,768]{2,1,0:T(8,128)(2,1)S(1)}, bf16[2,32,768]{2,1,0:T(8,128)(2,1)S(1)}, u32[]{:S(2)}, u32[]{:S(2)}) collective-permute-start(bf16[2,32,768]{2,1,0:T(8,128)(2,1)S(1)} %get-tuple-element.11.first), channel_id=1, source_target_pairs={{0,5},{1,4},{2,7},{3,6},{4,1},{5,0},{6,3},{7,2},{8,13},{9,12},{10,... | collective-permute-start | bytes 294920 | tf_op jit(solution)/shard_map/ppermute | solution.py:285
  8.6 6.2 %collective-permute-start.3 = (f32[2,8,512]{2,1,0:T(8,128)S(1)}, f32[2,8,512]{2,1,0:T(8,128)S(1)}, u32[]{:S(2)}, u32[]{:S(2)}) collective-permute-start(f32[2,8,512]{2,1,0:T(8,128)S(1)} %get-tuple-element.12), channel_id=1, source_target_pairs={{0,6},{2,4},{4,2},{6,0},{8,14},{10,12},{12,10},{14,8},{1,7},{3,5},... | collective-permute-start | bytes 98312 | tf_op jit(solution)/shard_map/ppermute | solution.py:279
  11.0 3.9 %collective-permute-start.4 = (f32[2,8,512]{2,1,0:T(8,128)S(1)}, f32[2,8,512]{2,1,0:T(8,128)S(1)}, u32[]{:S(2)}, u32[]{:S(2)}) collective-permute-start(f32[2,8,512]{2,1,0:T(8,128)S(1)} %get-tuple-element.13), channel_id=1, source_target_pairs={{0,4},{2,6},{4,0},{6,2},{8,12},{10,14},{12,8},{14,10},{1,5},{3,7},... | collective-permute-start | bytes 98312 | tf_op jit(solution)/shard_map/ppermute | solution.py:279
  11.5 3.9 %collective-permute-start.5 = (f32[2,8,512]{2,1,0:T(8,128)S(1)}, f32[2,8,512]{2,1,0:T(8,128)S(1)}, u32[]{:S(2)}, u32[]{:S(2)}) collective-permute-start(f32[2,8,512]{2,1,0:T(8,128)S(1)} %get-tuple-element.14), channel_id=1, source_target_pairs={{0,2},{2,0},{4,6},{6,4},{8,10},{10,8},{12,14},{14,12},{1,3},{3,1},... | collective-permute-start | bytes 98312 | tf_op jit(solution)/shard_map/ppermute | solution.py:279
  12.1 7.6 %collective-permute-start.8 = (bf16[4,32,768]{2,1,0:T(8,128)(2,1)S(1)}, bf16[4,32,768]{2,1,0:T(8,128)(2,1)S(1)}, u32[]{:S(2)}, u32[]{:S(2)}) collective-permute-start(bf16[4,32,768]{2,1,0:T(8,128)(2,1)S(1)} %shard_map.95.after.rest_0_), channel_id=1, source_target_pairs={{0,3},{1,2},{2,1},{3,0},{4,7},{5,6},{6,5},{7,4},{8,11},{9,10},{10,... | collective-permute-start | bytes 589832 | tf_op jit(solution)/shard_map/ppermute | solution.py:285
  15.5 5.8 %collective-permute-start.6 = (f32[8,512]{1,0:T(8,128)S(1)}, f32[8,512]{1,0:T(8,128)S(1)}, u32[]{:S(2)}, u32[]{:S(2)}) collective-permute-start(f32[8,512]{1,0:T(8,128)S(1)} %slice_bitcast_fusion), channel_id=1, source_target_pairs={{0,8},{2,10},{4,12},{6,14},{8,0},{10,2},{12,4},{14,6},{1,9},{3,11}... | collective-permute-start | bytes 49160 | tf_op jit(solution)/shard_map/ppermute | solution.py:279
  19.3 3.1 %collective-permute-start.9 = (bf16[4,32,768]{2,1,0:T(8,128)(2,1)S(1)}, bf16[4,32,768]{2,1,0:T(8,128)(2,1)S(1)}, u32[]{:S(2)}, u32[]{:S(2)}) collective-permute-start(bf16[4,32,768]{2,1,0:T(8,128)(2,1)S(1)} %shard_map.95.after.rest_0_), channel_id=1, source_target_pairs={{0,1},{1,0},{2,3},{3,2},{4,5},{5,4},{6,7},{7,6},{8,9},{9,8},{10,11... | collective-permute-start | bytes 589832 | tf_op jit(solution)/shard_map/ppermute | solution.py:301
  19.7 2.8 %collective-permute-start.10 = (bf16[4,32,768]{2,1,0:T(8,128)(2,1)S(1)}, bf16[4,32,768]{2,1,0:T(8,128)(2,1)S(1)}, u32[]{:S(2)}, u32[]{:S(2)}) collective-permute-start(bf16[4,32,768]{2,1,0:T(8,128)(2,1)S(1)} %collective-permute-done.8.rest_1_), channel_id=1, source_target_pairs={{0,1},{1,0},{2,3},{3,2},{4,5},{5,4},{6,7},{7,6},{8,9},{9,8},{10,11... | collective-permute-start | bytes 589832 | tf_op jit(solution)/shard_map/ppermute | solution.py:302
  21.2 1.2 %collective-permute-start.7 = (f32[8,512]{1,0:T(8,128)S(1)}, f32[8,512]{1,0:T(8,128)S(1)}, u32[]{:S(2)}, u32[]{:S(2)}) collective-permute-start(f32[8,512]{1,0:T(8,128)S(1)} %fusion.own), channel_id=1, source_target_pairs={{0,1},{1,0},{2,3},{3,2},{4,5},{5,4},{6,7},{7,6},{8,9},{9,8},{10,11... | collective-permute-start | bytes 49160 | tf_op jit(solution)/shard_map/ppermute | solution.py:304

commit v24 on v16

--- a/solution.py
+++ b/solution.py
@@ -279,7 +279,7 @@
         place, train_tokens, train_ids, other_eigen, total, block, arrived, parts, parts // 2
     )
     near = join(pieces[0], block, crossed(block, 1))
-    far_first = reversed(range(1, len(pieces)))
+    far_first = (len(pieces) - 1, *range(1, len(pieces) - 1))
     terms = [pieces[0]] + [apart(pieces[d], d) for d in far_first]
     sums = gather_sum(near, terms)
     far = crossed(near, 0)

time: 24 us -> 22.4 us (0.933)
  starting transfers between devices: 15.7 us -> 14.5 us
  waiting for transfers between devices: 3.96 us -> 3.62 us
    ppermute x4, waiting for transfers between devices: 2.16 us -> 0.96 us  [apart(): return lax.ppermute(x, 'blk', [(s, s ^ distance) for s in range(parts)])]
    ppermute x3, waiting for transfers between devices: 0.62 us -> 1.67 us  [crossed(): return lax.ppermute(x, ('blk', 'fsdp'), pairs)]
    ppermute x4, starting transfers between devices: 7.35 us -> 6.44 us  [apart(): return lax.ppermute(x, 'blk', [(s, s ^ distance) for s in range(parts)])]
    ppermute x3, starting transfers between devices: 7.69 us -> 7.05 us  [crossed(): return lax.ppermute(x, ('blk', 'fsdp'), pairs)]
  transfers between devices with their start and end apart: 11 -> 11, of which waited for: 7 -> 6; matrix products, arithmetic and copies ran while one was open for 0% -> 0% of each run, Pallas kernels for 5% -> 6%
where the time goes in v24:
time: 22.4 us; the launch traced here: 22.2 us
  starting transfers between devices  14.5 us (65%)
  waiting for transfers between devices  3.62 us (16%)
  Pallas kernels  2.64 us (12%)
  between operations  1.43 us (6%)
    ppermute x3, starting transfers between devices, crossed(): return lax.ppermute(x, ('blk', 'fsdp'), pairs)  7.05 us
    ppermute x4, starting transfers between devices, apart(): return lax.ppermute(x, 'blk', [(s, s ^ distance) for s in range(parts)])  6.44 us
    ppermute x3, waiting for transfers between devices, crossed(): return lax.ppermute(x, ('blk', 'fsdp'), pairs)  1.67 us
    pallas_call x1, Pallas kernels, score(): pl.pallas_call(score_kernel, out_shape=jax.ShapeDtypeStruct((own.shape[0]...  1.34 us
    ppermute x1, waiting for transfers between devices, direct(): other = lax.ppermute(own, 'fsdp', swap)  0.98 us
    ppermute x4, waiting for transfers between devices, apart(): return lax.ppermute(x, 'blk', [(s, s ^ distance) for s in range(parts)])  0.96 us
    pallas_call x1, Pallas kernels, pack(): pl.pallas_call(pack_kernel, out_shape=jax.ShapeDtypeStruct(shape, train_o...  0.78 us
    pallas_call x1, Pallas kernels, project(): pl.pallas_call(project_kernel, out_shape=jax.ShapeDtypeStruct((columns, w...  0.47 us
  transfers between devices with their start and end apart: 11, of which 6 were waited for; matrix products, arithmetic and copies ran while one was open for 0% of the time, Pallas kernels for 6%

profile of v24, /device:TPU:0, one launch (start us, length us, event | category | flops | bytes accessed | tf_op | source)
XLA Modules:
  0.0 22.2 jit_solution(2471327277639520168)
XLA Ops:
  0.0 0.5 %collective-permute-start = (f32[256,256]{1,0:T(8,128)}, f32[256,256]{1,0:T(8,128)S(1)}, u32[]{:S(2)}, u32[]{:S(2)}) collective-permute-start(f32[256,256]{1,0:T(8,128)} %eigen.1), channel_id=1, source_target_pairs={{0,1},{1,0},{2,3},{3,2},{4,5},{5,4},{6,7},{7,6},{8,9},{9,8},{10,11... | collective-permute-start | bytes 786440 | tf_op jit(solution)/shard_map/ppermute | solution.py:274
  0.5 0.8 %shard_map.92.source = bf16[1,32,768]{2,1,0:T(8,128)(2,1)S(1)} custom-call(bf16[1,32,512]{2,1,0:T(8,128)(2,1)} %train_out.1, bf16[1,32,256]{2,1,0:T(8,128)(2,1)} %train_act.1), custom_call_target="tpu_custom_call" | custom-call | tf_op jit(solution)/shard_map/pallas_call | solution.py:46
  1.2 0.0 copy-start
  1.2 0.0 copy-start.1
  1.3 0.0 copy-start.3
  1.3 0.0 copy-start.4
  1.3 3.8 %collective-permute-start.1 = (bf16[1,32,768]{2,1,0:T(8,128)(2,1)S(1)}, bf16[1,32,768]{2,1,0:T(8,128)(2,1)S(1)}, u32[]{:S(2)}, u32[]{:S(2)}) collective-permute-start(bf16[1,32,768]{2,1,0:T(8,128)(2,1)S(1)} %shard_map.93.first), channel_id=1, source_target_pairs={{0,9},{1,8},{2,11},{3,10},{4,13},{5,12},{6,15},{7,14},{8,1},{9,0},... | collective-permute-start | bytes 147464 | tf_op jit(solution)/shard_map/ppermute | solution.py:270
  6.4 0.0 copy-start.2
  6.4 0.5 %shard_map.91.total = f32[64,384]{1,0:T(8,128)S(1)} custom-call(bf16[64,3584]{1,0:T(8,128)(2,1)S(1)} %bitcast.10, bf16[64,1024]{1,0:T(8,128)(2,1)S(1)} %bitcast.11, bf16[3584,256]{1,0:T(8,128)(2,1)S(1)} %copy-done, bf16[1024,128]{1,0:T(8,128)(2,1)S(1)} %copy-done.3), custom_call_target="tpu_custom_call" | custom-call | flops 134217728 | bytes 2686976 | tf_op jit(solution)/shard_map/pallas_call | solution.py:126
  6.9 0.3 %collective-permute-done.1.second = bf16[1,32,768]{2,1,0:T(8,128)(2,1)S(1)} collective-permute-done((bf16[1,32,768]{2,1,0:T(8,128)(2,1)S(1)}, bf16[1,32,768]{2,1,0:T(8,128)(2,1)S(1)}, u32[]{:S(2)}, u32[]{:S(2)}) %collective-permute-start.1) | collective-permute-done | bytes 49184 | tf_op jit(solution)/shard_map/ppermute | solution.py:270
  7.2 0.0 collective-permute-done.after.other_eigen
  7.2 1.4 %collective-permute-start.2 = (bf16[2,32,768]{2,1,0:T(8,128)(2,1)S(1)}, bf16[2,32,768]{2,1,0:T(8,128)(2,1)S(1)}, u32[]{:S(2)}, u32[]{:S(2)}) collective-permute-start(bf16[2,32,768]{2,1,0:T(8,128)(2,1)S(1)} %get-tuple-element.11.first), channel_id=1, source_target_pairs={{0,5},{1,4},{2,7},{3,6},{4,1},{5,0},{6,3},{7,2},{8,13},{9,12},{10,... | collective-permute-start | bytes 294920 | tf_op jit(solution)/shard_map/ppermute | solution.py:270
  8.6 2.4 %collective-permute-start.3 = (f32[2,8,512]{2,1,0:T(8,128)S(1)}, f32[2,8,512]{2,1,0:T(8,128)S(1)}, u32[]{:S(2)}, u32[]{:S(2)}) collective-permute-start(f32[2,8,512]{2,1,0:T(8,128)S(1)} %get-tuple-element.12), channel_id=1, source_target_pairs={{0,6},{2,4},{4,2},{6,0},{8,14},{10,12},{12,10},{14,8},{1,7},{3,5},... | collective-permute-start | bytes 98312 | tf_op jit(solution)/shard_map/ppermute | solution.py:264
  11.0 1.1 %collective-permute-start.5 = (f32[2,8,512]{2,1,0:T(8,128)S(1)}, f32[2,8,512]{2,1,0:T(8,128)S(1)}, u32[]{:S(2)}, u32[]{:S(2)}) collective-permute-start(f32[2,8,512]{2,1,0:T(8,128)S(1)} %get-tuple-element.14), channel_id=1, source_target_pairs={{0,4},{2,6},{4,0},{6,2},{8,12},{10,14},{12,8},{14,10},{1,5},{3,7},... | collective-permute-start | bytes 98312 | tf_op jit(solution)/shard_map/ppermute | solution.py:264
  12.1 1.9 %collective-permute-start.8 = (bf16[4,32,768]{2,1,0:T(8,128)(2,1)S(1)}, bf16[4,32,768]{2,1,0:T(8,128)(2,1)S(1)}, u32[]{:S(2)}, u32[]{:S(2)}) collective-permute-start(bf16[4,32,768]{2,1,0:T(8,128)(2,1)S(1)} %shard_map.95.after.rest_0_), channel_id=1, source_target_pairs={{0,3},{1,2},{2,1},{3,0},{4,7},{5,6},{6,5},{7,4},{8,11},{9,10},{10,... | collective-permute-start | bytes 589832 | tf_op jit(solution)/shard_map/ppermute | solution.py:270
  14.0 0.5 %collective-permute-done.3.refs_1_ = f32[2,8,512]{2,1,0:T(8,128)S(1)} collective-permute-done((f32[2,8,512]{2,1,0:T(8,128)S(1)}, f32[2,8,512]{2,1,0:T(8,128)S(1)}, u32[]{:S(2)}, u32[]{:S(2)}) %collective-permute-start.3) | collective-permute-done | bytes 32800 | tf_op jit(solution)/shard_map/ppermute | solution.py:264
  14.5 0.4 %collective-permute-done.4.refs_2_ = f32[2,8,512]{2,1,0:T(8,128)S(1)} collective-permute-done((f32[2,8,512]{2,1,0:T(8,128)S(1)}, f32[2,8,512]{2,1,0:T(8,128)S(1)}, u32[]{:S(2)}, u32[]{:S(2)}) %collective-permute-start.4) | collective-permute-done | bytes 32800 | tf_op jit(solution)/shard_map/ppermute | solution.py:264
  14.9 3.0 %collective-permute-start.6 = (f32[8,512]{1,0:T(8,128)S(1)}, f32[8,512]{1,0:T(8,128)S(1)}, u32[]{:S(2)}, u32[]{:S(2)}) collective-permute-start(f32[8,512]{1,0:T(8,128)S(1)} %slice_bitcast_fusion), channel_id=1, source_target_pairs={{0,8},{2,10},{4,12},{6,14},{8,0},{10,2},{12,4},{14,6},{1,9},{3,11}... | collective-permute-start | bytes 49160 | tf_op jit(solution)/shard_map/ppermute | solution.py:264
  17.9 1.4 %collective-permute-done.8.rest_1_ = bf16[4,32,768]{2,1,0:T(8,128)(2,1)S(1)} collective-permute-done((bf16[4,32,768]{2,1,0:T(8,128)(2,1)S(1)}, bf16[4,32,768]{2,1,0:T(8,128)(2,1)S(1)}, u32[]{:S(2)}, u32[]{:S(2)}) %collective-permute-start.8) | collective-permute-done | bytes 196640 | tf_op jit(solution)/shard_map/ppermute | solution.py:270
  19.3 0.3 %collective-permute-start.10 = (bf16[4,32,768]{2,1,0:T(8,128)(2,1)S(1)}, bf16[4,32,768]{2,1,0:T(8,128)(2,1)S(1)}, u32[]{:S(2)}, u32[]{:S(2)}) collective-permute-start(bf16[4,32,768]{2,1,0:T(8,128)(2,1)S(1)} %collective-permute-done.8.rest_1_), channel_id=1, source_target_pairs={{0,1},{1,0},{2,3},{3,2},{4,5},{5,4},{6,7},{7,6},{8,9},{9,8},{10,11... | collective-permute-start | bytes 589832 | tf_op jit(solution)/shard_map/ppermute | solution.py:287
  19.6 0.1 collective-permute-done.6
  19.6 0.2 collective-permute-start.7
  19.9 1.0 %collective-permute-done.7.other = f32[8,512]{1,0:T(8,128)S(1)} collective-permute-done((f32[8,512]{1,0:T(8,128)S(1)}, f32[8,512]{1,0:T(8,128)S(1)}, u32[]{:S(2)}, u32[]{:S(2)}) %collective-permute-start.7) | collective-permute-done | bytes 16416 | tf_op jit(solution)/shard_map/ppermute | solution.py:289
  20.8 1.3 %shard_map.97 = f32[2,16]{1,0:T(2,128)} custom-call(s32[1]{0:T(128)} %bitcast.core_ref, f32[8,512]{1,0:T(8,128)S(1)} %fusion.own, f32[8,512]{1,0:T(8,128)S(1)} %collective-permute-done.7.other, f32[256,256]{1,0:T(8,128)S(1)} %copy-done.2, f32[256,256]{1,0:T(8,128)S(1)} %collective-permute-done.after.other_eigen, ...), custom_call_target="tpu_custom_call" | custom-call | tf_op jit(solution)/shard_map/pallas_call | solution.py:239
  (17 shorter events, 0.1 us)
Async XLA Ops:
  0.0 7.2 %collective-permute-start = (f32[256,256]{1,0:T(8,128)}, f32[256,256]{1,0:T(8,128)S(1)}, u32[]{:S(2)}, u32[]{:S(2)}) collective-permute-start(f32[256,256]{1,0:T(8,128)} %eigen.1), channel_id=1, source_target_pairs={{0,1},{1,0},{2,3},{3,2},{4,5},{5,4},{6,7},{7,6},{8,9},{9,8},{10,11... | collective-permute-start | bytes 786440 | tf_op jit(solution)/shard_map/ppermute | solution.py:274
  1.2 5.1 %copy-start = (bf16[3584,256]{1,0:T(8,128)(2,1)S(1)}, bf16[3584,256]{1,0:T(8,128)(2,1)}, u32[]{:S(2)}) copy-start(bf16[3584,256]{1,0:T(8,128)(2,1)} %out_basis.1) | copy-start | bytes 5505028
  1.2 5.1 %copy-start.1 = (bf16[3584,64]{0,1:T(8,128)(2,1)S(1)}, bf16[3584,64]{0,1:T(8,128)(2,1)}, u32[]{:S(2)}) copy-start(bf16[3584,64]{0,1:T(8,128)(2,1)} %param.9) | copy-start | bytes 1376260
  1.3 5.1 %copy-start.3 = (bf16[1024,128]{1,0:T(8,128)(2,1)S(1)}, bf16[1024,128]{1,0:T(8,128)(2,1)}, u32[]{:S(2)}) copy-start(bf16[1024,128]{1,0:T(8,128)(2,1)} %act_basis.1) | copy-start | bytes 786436
  1.3 5.1 %copy-start.4 = (bf16[1024,64]{0,1:T(8,128)(2,1)S(1)}, bf16[1024,64]{0,1:T(8,128)(2,1)}, u32[]{:S(2)}) copy-start(bf16[1024,64]{0,1:T(8,128)(2,1)} %param.10) | copy-start | bytes 393220
  1.3 5.9 %collective-permute-start.1 = (bf16[1,32,768]{2,1,0:T(8,128)(2,1)S(1)}, bf16[1,32,768]{2,1,0:T(8,128)(2,1)S(1)}, u32[]{:S(2)}, u32[]{:S(2)}) collective-permute-start(bf16[1,32,768]{2,1,0:T(8,128)(2,1)S(1)} %shard_map.93.first), channel_id=1, source_target_pairs={{0,9},{1,8},{2,11},{3,10},{4,13},{5,12},{6,15},{7,14},{8,1},{9,0},... | collective-permute-start | bytes 147464 | tf_op jit(solution)/shard_map/ppermute | solution.py:270
  6.4 14.4 %copy-start.2 = (f32[256,256]{1,0:T(8,128)S(1)}, f32[256,256]{1,0:T(8,128)}, u32[]{:S(2)}) copy-start(f32[256,256]{1,0:T(8,128)} %eigen.1) | copy-start | bytes 786436
  7.2 4.8 %collective-permute-start.2 = (bf16[2,32,768]{2,1,0:T(8,128)(2,1)S(1)}, bf16[2,32,768]{2,1,0:T(8,128)(2,1)S(1)}, u32[]{:S(2)}, u32[]{:S(2)}) collective-permute-start(bf16[2,32,768]{2,1,0:T(8,128)(2,1)S(1)} %get-tuple-element.11.first), channel_id=1, source_target_pairs={{0,5},{1,4},{2,7},{3,6},{4,1},{5,0},{6,3},{7,2},{8,13},{9,12},{10,... | collective-permute-start | bytes 294920 | tf_op jit(solution)/shard_map/ppermute | solution.py:270
  8.6 6.0 %collective-permute-start.3 = (f32[2,8,512]{2,1,0:T(8,128)S(1)}, f32[2,8,512]{2,1,0:T(8,128)S(1)}, u32[]{:S(2)}, u32[]{:S(2)}) collective-permute-start(f32[2,8,512]{2,1,0:T(8,128)S(1)} %get-tuple-element.12), channel_id=1, source_target_pairs={{0,6},{2,4},{4,2},{6,0},{8,14},{10,12},{12,10},{14,8},{1,7},{3,5},... | collective-permute-start | bytes 98312 | tf_op jit(solution)/shard_map/ppermute | solution.py:264
  11.0 3.9 %collective-permute-start.4 = (f32[2,8,512]{2,1,0:T(8,128)S(1)}, f32[2,8,512]{2,1,0:T(8,128)S(1)}, u32[]{:S(2)}, u32[]{:S(2)}) collective-permute-start(f32[2,8,512]{2,1,0:T(8,128)S(1)} %get-tuple-element.13), channel_id=1, source_target_pairs={{0,2},{2,0},{4,6},{6,4},{8,10},{10,8},{12,14},{14,12},{1,3},{3,1},... | collective-permute-start | bytes 98312 | tf_op jit(solution)/shard_map/ppermute | solution.py:264
  11.0 3.9 %collective-permute-start.5 = (f32[2,8,512]{2,1,0:T(8,128)S(1)}, f32[2,8,512]{2,1,0:T(8,128)S(1)}, u32[]{:S(2)}, u32[]{:S(2)}) collective-permute-start(f32[2,8,512]{2,1,0:T(8,128)S(1)} %get-tuple-element.14), channel_id=1, source_target_pairs={{0,4},{2,6},{4,0},{6,2},{8,12},{10,14},{12,8},{14,10},{1,5},{3,7},... | collective-permute-start | bytes 98312 | tf_op jit(solution)/shard_map/ppermute | solution.py:264
  12.1 7.2 %collective-permute-start.8 = (bf16[4,32,768]{2,1,0:T(8,128)(2,1)S(1)}, bf16[4,32,768]{2,1,0:T(8,128)(2,1)S(1)}, u32[]{:S(2)}, u32[]{:S(2)}) collective-permute-start(bf16[4,32,768]{2,1,0:T(8,128)(2,1)S(1)} %shard_map.95.after.rest_0_), channel_id=1, source_target_pairs={{0,3},{1,2},{2,1},{3,0},{4,7},{5,6},{6,5},{7,4},{8,11},{9,10},{10,... | collective-permute-start | bytes 589832 | tf_op jit(solution)/shard_map/ppermute | solution.py:270
  14.9 4.7 %collective-permute-start.6 = (f32[8,512]{1,0:T(8,128)S(1)}, f32[8,512]{1,0:T(8,128)S(1)}, u32[]{:S(2)}, u32[]{:S(2)}) collective-permute-start(f32[8,512]{1,0:T(8,128)S(1)} %slice_bitcast_fusion), channel_id=1, source_target_pairs={{0,8},{2,10},{4,12},{6,14},{8,0},{10,2},{12,4},{14,6},{1,9},{3,11}... | collective-permute-start | bytes 49160 | tf_op jit(solution)/shard_map/ppermute | solution.py:264
  17.9 3.0 %collective-permute-start.9 = (bf16[4,32,768]{2,1,0:T(8,128)(2,1)S(1)}, bf16[4,32,768]{2,1,0:T(8,128)(2,1)S(1)}, u32[]{:S(2)}, u32[]{:S(2)}) collective-permute-start(bf16[4,32,768]{2,1,0:T(8,128)(2,1)S(1)} %shard_map.95.after.rest_0_), channel_id=1, source_target_pairs={{0,1},{1,0},{2,3},{3,2},{4,5},{5,4},{6,7},{7,6},{8,9},{9,8},{10,11... | collective-permute-start | bytes 589832 | tf_op jit(solution)/shard_map/ppermute | solution.py:286
  19.3 1.6 %collective-permute-start.10 = (bf16[4,32,768]{2,1,0:T(8,128)(2,1)S(1)}, bf16[4,32,768]{2,1,0:T(8,128)(2,1)S(1)}, u32[]{:S(2)}, u32[]{:S(2)}) collective-permute-start(bf16[4,32,768]{2,1,0:T(8,128)(2,1)S(1)} %collective-permute-done.8.rest_1_), channel_id=1, source_target_pairs={{0,1},{1,0},{2,3},{3,2},{4,5},{5,4},{6,7},{7,6},{8,9},{9,8},{10,11... | collective-permute-start | bytes 589832 | tf_op jit(solution)/shard_map/ppermute | solution.py:287
  19.6 1.2 %collective-permute-start.7 = (f32[8,512]{1,0:T(8,128)S(1)}, f32[8,512]{1,0:T(8,128)S(1)}, u32[]{:S(2)}, u32[]{:S(2)}) collective-permute-start(f32[8,512]{1,0:T(8,128)S(1)} %fusion.own), channel_id=1, source_target_pairs={{0,1},{1,0},{2,3},{3,2},{4,5},{5,4},{6,7},{7,6},{8,9},{9,8},{10,11... | collective-permute-start | bytes 49160 | tf_op jit(solution)/shard_map/ppermute | solution.py:289

commit v25 on v19

--- a/solution.py
+++ b/solution.py
@@ -292,7 +292,7 @@
         place, train_tokens, train_ids, total, block, arrived, parts, parts // 2
     )
     near = join(pieces[0], block, crossed(block, 1))
-    far_first = reversed(range(1, len(pieces)))
+    far_first = (len(pieces) - 1, *range(1, len(pieces) - 1))
     terms = [pieces[0]] + [apart(pieces[d], d) for d in far_first]
     sums = gather_sum(near, terms)
     far = crossed(near, 0)

time: 24 us -> 22.7 us (0.946)
  waiting for transfers between devices: 4.76 us -> 3.19 us
  starting transfers between devices: 14.8 us -> 15.1 us
    ppermute x4, waiting for transfers between devices: 3.1 us -> 0.43 us  [apart(): return lax.ppermute(x, 'blk', [(s, s ^ distance) for s in range(parts)])]
    ppermute x3, waiting for transfers between devices: 0.48 us -> 1.86 us  [crossed(): return lax.ppermute(x, ('blk', 'fsdp'), pairs)]
    ppermute x1, starting transfers between devices: 0.01 us -> 0.41 us  [direct(): other = lax.ppermute(own, 'fsdp', swap)]
    ppermute x1, waiting for transfers between devices: 1.17 us -> 0.89 us  [direct(): other = lax.ppermute(own, 'fsdp', swap)]
  transfers between devices with their start and end apart: 11 -> 11, of which waited for: 6 -> 5; matrix products, arithmetic and copies ran while one was open for 0% -> 0% of each run, Pallas kernels for 2% -> 2%
where the time goes in v25:
time: 22.7 us; the launch traced here: 22.4 us
  starting transfers between devices  15.1 us (67%)
  waiting for transfers between devices  3.19 us (14%)
  Pallas kernels  2.66 us (12%)
  between operations  1.43 us (6%)
    ppermute x3, starting transfers between devices, crossed(): return lax.ppermute(x, ('blk', 'fsdp'), pairs)  7.05 us
    ppermute x4, starting transfers between devices, apart(): return lax.ppermute(x, 'blk', [(s, s ^ distance) for s in range(parts)])  6.97 us
    ppermute x3, waiting for transfers between devices, crossed(): return lax.ppermute(x, ('blk', 'fsdp'), pairs)  1.86 us
    pallas_call x1, Pallas kernels, score(): pl.pallas_call(score_kernel, out_shape=jax.ShapeDtypeStruct((own.shape[0]...  1.34 us
    ppermute x1, waiting for transfers between devices, direct(): other = lax.ppermute(own, 'fsdp', swap)  0.89 us
    pallas_call x1, Pallas kernels, pack(): pl.pallas_call(pack_kernel, out_shape=jax.ShapeDtypeStruct(shape, train_o...  0.78 us
    ppermute x1, starting transfers between devices, direct(): other_eigen = lax.ppermute(hold(near, eigenvalues), 'fsdp', swap)  0.52 us
    pallas_call x1, Pallas kernels, project(): pl.pallas_call(project_kernel, out_shape=jax.ShapeDtypeStruct((columns, w...  0.47 us
  transfers between devices with their start and end apart: 11, of which 5 were waited for; matrix products, arithmetic and copies ran while one was open for 0% of the time, Pallas kernels for 2%

profile of v25, /device:TPU:0, one launch (start us, length us, event | category | flops | bytes accessed | tf_op | source)
XLA Modules:
  0.0 22.4 jit_solution(14886123267064806294)
XLA Ops:
  0.0 0.8 %shard_map.92.source = bf16[1,32,768]{2,1,0:T(8,128)(2,1)S(1)} custom-call(bf16[1,32,512]{2,1,0:T(8,128)(2,1)} %train_out.1, bf16[1,32,256]{2,1,0:T(8,128)(2,1)} %train_act.1), custom_call_target="tpu_custom_call" | custom-call | tf_op jit(solution)/shard_map/pallas_call | solution.py:46
  0.8 0.0 copy-start
  0.8 0.0 copy-start.2
  0.8 0.0 copy-start.3
  0.8 0.0 copy-start.4
  0.8 0.0 copy-start.1
  0.9 3.5 %collective-permute-start = (bf16[1,32,768]{2,1,0:T(8,128)(2,1)S(1)}, bf16[1,32,768]{2,1,0:T(8,128)(2,1)S(1)}, u32[]{:S(2)}, u32[]{:S(2)}) collective-permute-start(bf16[1,32,768]{2,1,0:T(8,128)(2,1)S(1)} %shard_map.93.first), channel_id=1, source_target_pairs={{0,9},{1,8},{2,11},{3,10},{4,13},{5,12},{6,15},{7,14},{8,1},{9,0},... | collective-permute-start | bytes 147464 | tf_op jit(solution)/shard_map/ppermute | solution.py:284
  5.7 0.5 %shard_map.91.total = f32[64,384]{1,0:T(8,128)S(1)} custom-call(bf16[64,3584]{1,0:T(8,128)(2,1)S(1)} %bitcast.10, bf16[64,1024]{1,0:T(8,128)(2,1)S(1)} %bitcast.11, bf16[3584,256]{1,0:T(8,128)(2,1)S(1)} %copy-done, bf16[1024,128]{1,0:T(8,128)(2,1)S(1)} %copy-done.3), custom_call_target="tpu_custom_call" | custom-call | flops 134217728 | bytes 2686976 | tf_op jit(solution)/shard_map/pallas_call | solution.py:141
  6.2 0.3 %collective-permute-done.second = bf16[1,32,768]{2,1,0:T(8,128)(2,1)S(1)} collective-permute-done((bf16[1,32,768]{2,1,0:T(8,128)(2,1)S(1)}, bf16[1,32,768]{2,1,0:T(8,128)(2,1)S(1)}, u32[]{:S(2)}, u32[]{:S(2)}) %collective-permute-start) | collective-permute-done | bytes 49184 | tf_op jit(solution)/shard_map/ppermute | solution.py:284
  6.6 2.3 %collective-permute-start.1 = (bf16[2,32,768]{2,1,0:T(8,128)(2,1)S(1)}, bf16[2,32,768]{2,1,0:T(8,128)(2,1)S(1)}, u32[]{:S(2)}, u32[]{:S(2)}) collective-permute-start(bf16[2,32,768]{2,1,0:T(8,128)(2,1)S(1)} %get-tuple-element.11.first), channel_id=1, source_target_pairs={{0,5},{1,4},{2,7},{3,6},{4,1},{5,0},{6,3},{7,2},{8,13},{9,12},{10,... | collective-permute-start | bytes 294920 | tf_op jit(solution)/shard_map/ppermute | solution.py:284
  8.8 1.3 %collective-permute-start.2 = (f32[2,8,512]{2,1,0:T(8,128)S(1)}, f32[2,8,512]{2,1,0:T(8,128)S(1)}, u32[]{:S(2)}, u32[]{:S(2)}) collective-permute-start(f32[2,8,512]{2,1,0:T(8,128)S(1)} %get-tuple-element.12), channel_id=1, source_target_pairs={{0,6},{2,4},{4,2},{6,0},{8,14},{10,12},{12,10},{14,8},{1,7},{3,5},... | collective-permute-start | bytes 98312 | tf_op jit(solution)/shard_map/ppermute | solution.py:278
  10.1 0.5 %collective-permute-start.3 = (f32[2,8,512]{2,1,0:T(8,128)S(1)}, f32[2,8,512]{2,1,0:T(8,128)S(1)}, u32[]{:S(2)}, u32[]{:S(2)}) collective-permute-start(f32[2,8,512]{2,1,0:T(8,128)S(1)} %get-tuple-element.13), channel_id=1, source_target_pairs={{0,2},{2,0},{4,6},{6,4},{8,10},{10,8},{12,14},{14,12},{1,3},{3,1},... | collective-permute-start | bytes 98312 | tf_op jit(solution)/shard_map/ppermute | solution.py:278
  10.7 1.7 %collective-permute-start.4 = (f32[2,8,512]{2,1,0:T(8,128)S(1)}, f32[2,8,512]{2,1,0:T(8,128)S(1)}, u32[]{:S(2)}, u32[]{:S(2)}) collective-permute-start(f32[2,8,512]{2,1,0:T(8,128)S(1)} %get-tuple-element.14), channel_id=1, source_target_pairs={{0,4},{2,6},{4,0},{6,2},{8,12},{10,14},{12,8},{14,10},{1,5},{3,7},... | collective-permute-start | bytes 98312 | tf_op jit(solution)/shard_map/ppermute | solution.py:278
  12.4 0.0 collective-permute-done.1.second
  12.4 1.2 %collective-permute-start.8 = (bf16[4,32,768]{2,1,0:T(8,128)(2,1)S(1)}, bf16[4,32,768]{2,1,0:T(8,128)(2,1)S(1)}, u32[]{:S(2)}, u32[]{:S(2)}) collective-permute-start(bf16[4,32,768]{2,1,0:T(8,128)(2,1)S(1)} %shard_map.95.after.rest_0_), channel_id=1, source_target_pairs={{0,3},{1,2},{2,1},{3,0},{4,7},{5,6},{6,5},{7,4},{8,11},{9,10},{10,... | collective-permute-start | bytes 589832 | tf_op jit(solution)/shard_map/ppermute | solution.py:284
  13.6 0.5 %collective-permute-start.7 = (f32[256,256]{1,0:T(8,128)S(1)}, f32[256,256]{1,0:T(8,128)S(1)}, u32[]{:S(2)}, u32[]{:S(2)}) collective-permute-start(f32[256,256]{1,0:T(8,128)S(1)} %shard_map.97), channel_id=1, source_target_pairs={{0,1},{1,0},{2,3},{3,2},{4,5},{5,4},{6,7},{7,6},{8,9},{9,8},{10,11... | collective-permute-start | bytes 786440 | tf_op jit(solution)/shard_map/ppermute | solution.py:299
  14.1 0.1 collective-permute-done.3.refs_2_
  14.2 0.3 %collective-permute-done.4.refs_3_ = f32[2,8,512]{2,1,0:T(8,128)S(1)} collective-permute-done((f32[2,8,512]{2,1,0:T(8,128)S(1)}, f32[2,8,512]{2,1,0:T(8,128)S(1)}, u32[]{:S(2)}, u32[]{:S(2)}) %collective-permute-start.4) | collective-permute-done | bytes 32800 | tf_op jit(solution)/shard_map/ppermute | solution.py:278
  14.6 3.5 %collective-permute-start.5 = (f32[8,512]{1,0:T(8,128)S(1)}, f32[8,512]{1,0:T(8,128)S(1)}, u32[]{:S(2)}, u32[]{:S(2)}) collective-permute-start(f32[8,512]{1,0:T(8,128)S(1)} %slice_bitcast_fusion), channel_id=1, source_target_pairs={{0,8},{2,10},{4,12},{6,14},{8,0},{10,2},{12,4},{14,6},{1,9},{3,11}... | collective-permute-start | bytes 49160 | tf_op jit(solution)/shard_map/ppermute | solution.py:278
  18.1 1.5 %collective-permute-done.8.rest_1_ = bf16[4,32,768]{2,1,0:T(8,128)(2,1)S(1)} collective-permute-done((bf16[4,32,768]{2,1,0:T(8,128)(2,1)S(1)}, bf16[4,32,768]{2,1,0:T(8,128)(2,1)S(1)}, u32[]{:S(2)}, u32[]{:S(2)}) %collective-permute-start.8) | collective-permute-done | bytes 196640 | tf_op jit(solution)/shard_map/ppermute | solution.py:284
  19.6 0.2 collective-permute-start.10
  19.8 0.4 %collective-permute-start.6 = (f32[8,512]{1,0:T(8,128)S(1)}, f32[8,512]{1,0:T(8,128)S(1)}, u32[]{:S(2)}, u32[]{:S(2)}) collective-permute-start(f32[8,512]{1,0:T(8,128)S(1)} %fusion.own), channel_id=1, source_target_pairs={{0,1},{1,0},{2,3},{3,2},{4,5},{5,4},{6,7},{7,6},{8,9},{9,8},{10,11... | collective-permute-start | bytes 49160 | tf_op jit(solution)/shard_map/ppermute | solution.py:303
  20.2 0.9 %collective-permute-done.6.other = f32[8,512]{1,0:T(8,128)S(1)} collective-permute-done((f32[8,512]{1,0:T(8,128)S(1)}, f32[8,512]{1,0:T(8,128)S(1)}, u32[]{:S(2)}, u32[]{:S(2)}) %collective-permute-start.6) | collective-permute-done | bytes 16416 | tf_op jit(solution)/shard_map/ppermute | solution.py:303
  21.1 1.3 %shard_map.98 = f32[2,16]{1,0:T(2,128)} custom-call(s32[1]{0:T(128)} %bitcast.core_ref, f32[8,512]{1,0:T(8,128)S(1)} %fusion.own, f32[8,512]{1,0:T(8,128)S(1)} %collective-permute-done.6.other, f32[256,256]{1,0:T(8,128)S(1)} %copy-done.1, f32[256,256]{1,0:T(8,128)S(1)} %collective-permute-done.7.other_eigen, ...), custom_call_target="tpu_custom_call" | custom-call | tf_op jit(solution)/shard_map/pallas_call | solution.py:253
  (18 shorter events, 0.1 us)
Async XLA Ops:
  0.8 4.9 %copy-start = (bf16[3584,256]{1,0:T(8,128)(2,1)S(1)}, bf16[3584,256]{1,0:T(8,128)(2,1)}, u32[]{:S(2)}) copy-start(bf16[3584,256]{1,0:T(8,128)(2,1)} %out_basis.1) | copy-start | bytes 5505028
  0.8 4.9 %copy-start.2 = (bf16[3584,64]{0,1:T(8,128)(2,1)S(1)}, bf16[3584,64]{0,1:T(8,128)(2,1)}, u32[]{:S(2)}) copy-start(bf16[3584,64]{0,1:T(8,128)(2,1)} %param.9) | copy-start | bytes 1376260
  0.8 4.9 %copy-start.3 = (bf16[1024,128]{1,0:T(8,128)(2,1)S(1)}, bf16[1024,128]{1,0:T(8,128)(2,1)}, u32[]{:S(2)}) copy-start(bf16[1024,128]{1,0:T(8,128)(2,1)} %act_basis.1) | copy-start | bytes 786436
  0.8 4.9 %copy-start.4 = (bf16[1024,64]{0,1:T(8,128)(2,1)S(1)}, bf16[1024,64]{0,1:T(8,128)(2,1)}, u32[]{:S(2)}) copy-start(bf16[1024,64]{0,1:T(8,128)(2,1)} %param.10) | copy-start | bytes 393220
  0.8 12.8 %copy-start.1 = (f32[256,256]{1,0:T(8,128)S(1)}, f32[256,256]{1,0:T(8,128)}, u32[]{:S(2)}) copy-start(f32[256,256]{1,0:T(8,128)} %eigen.1) | copy-start | bytes 786436
  0.9 5.7 %collective-permute-start = (bf16[1,32,768]{2,1,0:T(8,128)(2,1)S(1)}, bf16[1,32,768]{2,1,0:T(8,128)(2,1)S(1)}, u32[]{:S(2)}, u32[]{:S(2)}) collective-permute-start(bf16[1,32,768]{2,1,0:T(8,128)(2,1)S(1)} %shard_map.93.first), channel_id=1, source_target_pairs={{0,9},{1,8},{2,11},{3,10},{4,13},{5,12},{6,15},{7,14},{8,1},{9,0},... | collective-permute-start | bytes 147464 | tf_op jit(solution)/shard_map/ppermute | solution.py:284
  6.6 5.8 %collective-permute-start.1 = (bf16[2,32,768]{2,1,0:T(8,128)(2,1)S(1)}, bf16[2,32,768]{2,1,0:T(8,128)(2,1)S(1)}, u32[]{:S(2)}, u32[]{:S(2)}) collective-permute-start(bf16[2,32,768]{2,1,0:T(8,128)(2,1)S(1)} %get-tuple-element.11.first), channel_id=1, source_target_pairs={{0,5},{1,4},{2,7},{3,6},{4,1},{5,0},{6,3},{7,2},{8,13},{9,12},{10,... | collective-permute-start | bytes 294920 | tf_op jit(solution)/shard_map/ppermute | solution.py:284
  8.8 5.3 %collective-permute-start.2 = (f32[2,8,512]{2,1,0:T(8,128)S(1)}, f32[2,8,512]{2,1,0:T(8,128)S(1)}, u32[]{:S(2)}, u32[]{:S(2)}) collective-permute-start(f32[2,8,512]{2,1,0:T(8,128)S(1)} %get-tuple-element.12), channel_id=1, source_target_pairs={{0,6},{2,4},{4,2},{6,0},{8,14},{10,12},{12,10},{14,8},{1,7},{3,5},... | collective-permute-start | bytes 98312 | tf_op jit(solution)/shard_map/ppermute | solution.py:278
  10.1 4.1 %collective-permute-start.3 = (f32[2,8,512]{2,1,0:T(8,128)S(1)}, f32[2,8,512]{2,1,0:T(8,128)S(1)}, u32[]{:S(2)}, u32[]{:S(2)}) collective-permute-start(f32[2,8,512]{2,1,0:T(8,128)S(1)} %get-tuple-element.13), channel_id=1, source_target_pairs={{0,2},{2,0},{4,6},{6,4},{8,10},{10,8},{12,14},{14,12},{1,3},{3,1},... | collective-permute-start | bytes 98312 | tf_op jit(solution)/shard_map/ppermute | solution.py:278
  10.7 3.9 %collective-permute-start.4 = (f32[2,8,512]{2,1,0:T(8,128)S(1)}, f32[2,8,512]{2,1,0:T(8,128)S(1)}, u32[]{:S(2)}, u32[]{:S(2)}) collective-permute-start(f32[2,8,512]{2,1,0:T(8,128)S(1)} %get-tuple-element.14), channel_id=1, source_target_pairs={{0,4},{2,6},{4,0},{6,2},{8,12},{10,14},{12,8},{14,10},{1,5},{3,7},... | collective-permute-start | bytes 98312 | tf_op jit(solution)/shard_map/ppermute | solution.py:278
  12.4 7.2 %collective-permute-start.8 = (bf16[4,32,768]{2,1,0:T(8,128)(2,1)S(1)}, bf16[4,32,768]{2,1,0:T(8,128)(2,1)S(1)}, u32[]{:S(2)}, u32[]{:S(2)}) collective-permute-start(bf16[4,32,768]{2,1,0:T(8,128)(2,1)S(1)} %shard_map.95.after.rest_0_), channel_id=1, source_target_pairs={{0,3},{1,2},{2,1},{3,0},{4,7},{5,6},{6,5},{7,4},{8,11},{9,10},{10,... | collective-permute-start | bytes 589832 | tf_op jit(solution)/shard_map/ppermute | solution.py:284
  13.6 7.5 %collective-permute-start.7 = (f32[256,256]{1,0:T(8,128)S(1)}, f32[256,256]{1,0:T(8,128)S(1)}, u32[]{:S(2)}, u32[]{:S(2)}) collective-permute-start(f32[256,256]{1,0:T(8,128)S(1)} %shard_map.97), channel_id=1, source_target_pairs={{0,1},{1,0},{2,3},{3,2},{4,5},{5,4},{6,7},{7,6},{8,9},{9,8},{10,11... | collective-permute-start | bytes 786440 | tf_op jit(solution)/shard_map/ppermute | solution.py:299
  14.6 5.2 %collective-permute-start.5 = (f32[8,512]{1,0:T(8,128)S(1)}, f32[8,512]{1,0:T(8,128)S(1)}, u32[]{:S(2)}, u32[]{:S(2)}) collective-permute-start(f32[8,512]{1,0:T(8,128)S(1)} %slice_bitcast_fusion), channel_id=1, source_target_pairs={{0,8},{2,10},{4,12},{6,14},{8,0},{10,2},{12,4},{14,6},{1,9},{3,11}... | collective-permute-start | bytes 49160 | tf_op jit(solution)/shard_map/ppermute | solution.py:278
  18.1 3.0 %collective-permute-start.9 = (bf16[4,32,768]{2,1,0:T(8,128)(2,1)S(1)}, bf16[4,32,768]{2,1,0:T(8,128)(2,1)S(1)}, u32[]{:S(2)}, u32[]{:S(2)}) collective-permute-start(bf16[4,32,768]{2,1,0:T(8,128)(2,1)S(1)} %shard_map.95.after.rest_0_), channel_id=1, source_target_pairs={{0,1},{1,0},{2,3},{3,2},{4,5},{5,4},{6,7},{7,6},{8,9},{9,8},{10,11... | collective-permute-start | bytes 589832 | tf_op jit(solution)/shard_map/ppermute | solution.py:300
  19.6 1.5 %collective-permute-start.10 = (bf16[4,32,768]{2,1,0:T(8,128)(2,1)S(1)}, bf16[4,32,768]{2,1,0:T(8,128)(2,1)S(1)}, u32[]{:S(2)}, u32[]{:S(2)}) collective-permute-start(bf16[4,32,768]{2,1,0:T(8,128)(2,1)S(1)} %collective-permute-done.8.rest_1_), channel_id=1, source_target_pairs={{0,1},{1,0},{2,3},{3,2},{4,5},{5,4},{6,7},{7,6},{8,9},{9,8},{10,11... | collective-permute-start | bytes 589832 | tf_op jit(solution)/shard_map/ppermute | solution.py:301
  19.8 1.3 %collective-permute-start.6 = (f32[8,512]{1,0:T(8,128)S(1)}, f32[8,512]{1,0:T(8,128)S(1)}, u32[]{:S(2)}, u32[]{:S(2)}) collective-permute-start(f32[8,512]{1,0:T(8,128)S(1)} %fusion.own), channel_id=1, source_target_pairs={{0,1},{1,0},{2,3},{3,2},{4,5},{5,4},{6,7},{7,6},{8,9},{9,8},{10,11... | collective-permute-start | bytes 49160 | tf_op jit(solution)/shard_map/ppermute | solution.py:303

commit v26 on v24

--- a/solution.py
+++ b/solution.py
@@ -279,7 +279,7 @@
         place, train_tokens, train_ids, other_eigen, total, block, arrived, parts, parts // 2
     )
     near = join(pieces[0], block, crossed(block, 1))
-    far_first = (len(pieces) - 1, *range(1, len(pieces) - 1))
+    far_first = (1, *range(len(pieces) - 1, 1, -1))
     terms = [pieces[0]] + [apart(pieces[d], d) for d in far_first]
     sums = gather_sum(near, terms)
     far = crossed(near, 0)

time: 22.4 us -> 23 us (1.027)
  waiting for transfers between devices: 3.62 us -> 3.99 us
    ppermute x4, waiting for transfers between devices: 0.96 us -> 2.22 us  [apart(): return lax.ppermute(x, 'blk', [(s, s ^ distance) for s in range(parts)])]
    ppermute x3, waiting for transfers between devices: 1.67 us -> 0.59 us  [crossed(): return lax.ppermute(x, ('blk', 'fsdp'), pairs)]
    ppermute x4, starting transfers between devices: 6.44 us -> 6.89 us  [apart(): return lax.ppermute(x, 'blk', [(s, s ^ distance) for s in range(parts)])]
  transfers between devices with their start and end apart: 11 -> 11, of which waited for: 6 -> 5; matrix products, arithmetic and copies ran while one was open for 0% -> 0% of each run, Pallas kernels for 6% -> 6%
where the time goes in v26:
time: 23 us; the launch traced here: 22.7 us
  starting transfers between devices  14.6 us (63%)
  waiting for transfers between devices  3.99 us (17%)
  Pallas kernels  2.64 us (11%)
  between operations  1.44 us (6%)
    ppermute x4, starting transfers between devices, apart(): return lax.ppermute(x, 'blk', [(s, s ^ distance) for s in range(parts)])  6.89 us
    ppermute x3, starting transfers between devices, crossed(): return lax.ppermute(x, ('blk', 'fsdp'), pairs)  6.87 us
    ppermute x4, waiting for transfers between devices, apart(): return lax.ppermute(x, 'blk', [(s, s ^ distance) for s in range(parts)])  2.22 us
    pallas_call x1, Pallas kernels, score(): pl.pallas_call(score_kernel, out_shape=jax.ShapeDtypeStruct((own.shape[0]...  1.34 us
    ppermute x1, waiting for transfers between devices, direct(): other = lax.ppermute(own, 'fsdp', swap)  1.17 us
    pallas_call x1, Pallas kernels, pack(): pl.pallas_call(pack_kernel, out_shape=jax.ShapeDtypeStruct(shape, train_o...  0.78 us
    ppermute x3, waiting for transfers between devices, crossed(): return lax.ppermute(x, ('blk', 'fsdp'), pairs)  0.59 us
    pallas_call x1, Pallas kernels, project(): pl.pallas_call(project_kernel, out_shape=jax.ShapeDtypeStruct((columns, w...  0.47 us
  transfers between devices with their start and end apart: 11, of which 5 were waited for; matrix products, arithmetic and copies ran while one was open for 0% of the time, Pallas kernels for 6%

profile of v26, /device:TPU:0, one launch (start us, length us, event | category | flops | bytes accessed | tf_op | source)
XLA Modules:
  0.0 22.7 jit_solution(14242028293232847095)
XLA Ops:
  0.0 0.5 %collective-permute-start = (f32[256,256]{1,0:T(8,128)}, f32[256,256]{1,0:T(8,128)S(1)}, u32[]{:S(2)}, u32[]{:S(2)}) collective-permute-start(f32[256,256]{1,0:T(8,128)} %eigen.1), channel_id=1, source_target_pairs={{0,1},{1,0},{2,3},{3,2},{4,5},{5,4},{6,7},{7,6},{8,9},{9,8},{10,11... | collective-permute-start | bytes 786440 | tf_op jit(solution)/shard_map/ppermute | solution.py:274
  0.5 0.8 %shard_map.92.source = bf16[1,32,768]{2,1,0:T(8,128)(2,1)S(1)} custom-call(bf16[1,32,512]{2,1,0:T(8,128)(2,1)} %train_out.1, bf16[1,32,256]{2,1,0:T(8,128)(2,1)} %train_act.1), custom_call_target="tpu_custom_call" | custom-call | tf_op jit(solution)/shard_map/pallas_call | solution.py:46
  1.2 0.0 copy-start
  1.2 0.0 copy-start.1
  1.3 0.0 copy-start.3
  1.3 0.0 copy-start.4
  1.3 3.8 %collective-permute-start.1 = (bf16[1,32,768]{2,1,0:T(8,128)(2,1)S(1)}, bf16[1,32,768]{2,1,0:T(8,128)(2,1)S(1)}, u32[]{:S(2)}, u32[]{:S(2)}) collective-permute-start(bf16[1,32,768]{2,1,0:T(8,128)(2,1)S(1)} %shard_map.93.first), channel_id=1, source_target_pairs={{0,9},{1,8},{2,11},{3,10},{4,13},{5,12},{6,15},{7,14},{8,1},{9,0},... | collective-permute-start | bytes 147464 | tf_op jit(solution)/shard_map/ppermute | solution.py:270
  6.4 0.0 copy-start.2
  6.4 0.5 %shard_map.91.total = f32[64,384]{1,0:T(8,128)S(1)} custom-call(bf16[64,3584]{1,0:T(8,128)(2,1)S(1)} %bitcast.10, bf16[64,1024]{1,0:T(8,128)(2,1)S(1)} %bitcast.11, bf16[3584,256]{1,0:T(8,128)(2,1)S(1)} %copy-done, bf16[1024,128]{1,0:T(8,128)(2,1)S(1)} %copy-done.3), custom_call_target="tpu_custom_call" | custom-call | flops 134217728 | bytes 2686976 | tf_op jit(solution)/shard_map/pallas_call | solution.py:126
  6.9 0.3 %collective-permute-done.1.second = bf16[1,32,768]{2,1,0:T(8,128)(2,1)S(1)} collective-permute-done((bf16[1,32,768]{2,1,0:T(8,128)(2,1)S(1)}, bf16[1,32,768]{2,1,0:T(8,128)(2,1)S(1)}, u32[]{:S(2)}, u32[]{:S(2)}) %collective-permute-start.1) | collective-permute-done | bytes 49184 | tf_op jit(solution)/shard_map/ppermute | solution.py:270
  7.2 0.0 collective-permute-done.after.other_eigen
  7.2 1.4 %collective-permute-start.2 = (bf16[2,32,768]{2,1,0:T(8,128)(2,1)S(1)}, bf16[2,32,768]{2,1,0:T(8,128)(2,1)S(1)}, u32[]{:S(2)}, u32[]{:S(2)}) collective-permute-start(bf16[2,32,768]{2,1,0:T(8,128)(2,1)S(1)} %get-tuple-element.11.first), channel_id=1, source_target_pairs={{0,5},{1,4},{2,7},{3,6},{4,1},{5,0},{6,3},{7,2},{8,13},{9,12},{10,... | collective-permute-start | bytes 294920 | tf_op jit(solution)/shard_map/ppermute | solution.py:270
  8.6 1.5 %collective-permute-start.3 = (f32[2,8,512]{2,1,0:T(8,128)S(1)}, f32[2,8,512]{2,1,0:T(8,128)S(1)}, u32[]{:S(2)}, u32[]{:S(2)}) collective-permute-start(f32[2,8,512]{2,1,0:T(8,128)S(1)} %get-tuple-element.12), channel_id=1, source_target_pairs={{0,2},{2,0},{4,6},{6,4},{8,10},{10,8},{12,14},{14,12},{1,3},{3,1},... | collective-permute-start | bytes 98312 | tf_op jit(solution)/shard_map/ppermute | solution.py:264
  10.1 0.9 %collective-permute-start.4 = (f32[2,8,512]{2,1,0:T(8,128)S(1)}, f32[2,8,512]{2,1,0:T(8,128)S(1)}, u32[]{:S(2)}, u32[]{:S(2)}) collective-permute-start(f32[2,8,512]{2,1,0:T(8,128)S(1)} %get-tuple-element.13), channel_id=1, source_target_pairs={{0,6},{2,4},{4,2},{6,0},{8,14},{10,12},{12,10},{14,8},{1,7},{3,5},... | collective-permute-start | bytes 98312 | tf_op jit(solution)/shard_map/ppermute | solution.py:264
  11.0 1.1 %collective-permute-start.5 = (f32[2,8,512]{2,1,0:T(8,128)S(1)}, f32[2,8,512]{2,1,0:T(8,128)S(1)}, u32[]{:S(2)}, u32[]{:S(2)}) collective-permute-start(f32[2,8,512]{2,1,0:T(8,128)S(1)} %get-tuple-element.14), channel_id=1, source_target_pairs={{0,4},{2,6},{4,0},{6,2},{8,12},{10,14},{12,8},{14,10},{1,5},{3,7},... | collective-permute-start | bytes 98312 | tf_op jit(solution)/shard_map/ppermute | solution.py:264
  12.1 1.8 %collective-permute-start.8 = (bf16[4,32,768]{2,1,0:T(8,128)(2,1)S(1)}, bf16[4,32,768]{2,1,0:T(8,128)(2,1)S(1)}, u32[]{:S(2)}, u32[]{:S(2)}) collective-permute-start(bf16[4,32,768]{2,1,0:T(8,128)(2,1)S(1)} %shard_map.95.after.rest_0_), channel_id=1, source_target_pairs={{0,3},{1,2},{2,1},{3,0},{4,7},{5,6},{6,5},{7,4},{8,11},{9,10},{10,... | collective-permute-start | bytes 589832 | tf_op jit(solution)/shard_map/ppermute | solution.py:270
  13.8 0.0 collective-permute-done.3.refs_1_
  13.8 1.2 %collective-permute-done.4.refs_2_ = f32[2,8,512]{2,1,0:T(8,128)S(1)} collective-permute-done((f32[2,8,512]{2,1,0:T(8,128)S(1)}, f32[2,8,512]{2,1,0:T(8,128)S(1)}, u32[]{:S(2)}, u32[]{:S(2)}) %collective-permute-start.4) | collective-permute-done | bytes 32800 | tf_op jit(solution)/shard_map/ppermute | solution.py:264
  15.1 3.4 %collective-permute-start.6 = (f32[8,512]{1,0:T(8,128)S(1)}, f32[8,512]{1,0:T(8,128)S(1)}, u32[]{:S(2)}, u32[]{:S(2)}) collective-permute-start(f32[8,512]{1,0:T(8,128)S(1)} %slice_bitcast_fusion), channel_id=1, source_target_pairs={{0,8},{2,10},{4,12},{6,14},{8,0},{10,2},{12,4},{14,6},{1,9},{3,11}... | collective-permute-start | bytes 49160 | tf_op jit(solution)/shard_map/ppermute | solution.py:264
  18.5 0.3 %collective-permute-done.8.rest_1_ = bf16[4,32,768]{2,1,0:T(8,128)(2,1)S(1)} collective-permute-done((bf16[4,32,768]{2,1,0:T(8,128)(2,1)S(1)}, bf16[4,32,768]{2,1,0:T(8,128)(2,1)S(1)}, u32[]{:S(2)}, u32[]{:S(2)}) %collective-permute-start.8) | collective-permute-done | bytes 196640 | tf_op jit(solution)/shard_map/ppermute | solution.py:270
  18.8 0.4 %collective-permute-start.10 = (bf16[4,32,768]{2,1,0:T(8,128)(2,1)S(1)}, bf16[4,32,768]{2,1,0:T(8,128)(2,1)S(1)}, u32[]{:S(2)}, u32[]{:S(2)}) collective-permute-start(bf16[4,32,768]{2,1,0:T(8,128)(2,1)S(1)} %collective-permute-done.8.rest_1_), channel_id=1, source_target_pairs={{0,1},{1,0},{2,3},{3,2},{4,5},{5,4},{6,7},{7,6},{8,9},{9,8},{10,11... | collective-permute-start | bytes 589832 | tf_op jit(solution)/shard_map/ppermute | solution.py:287
  19.2 1.0 %collective-permute-done.6 = f32[8,512]{1,0:T(8,128)S(1)} collective-permute-done((f32[8,512]{1,0:T(8,128)S(1)}, f32[8,512]{1,0:T(8,128)S(1)}, u32[]{:S(2)}, u32[]{:S(2)}) %collective-permute-start.6) | collective-permute-done | bytes 16416 | tf_op jit(solution)/shard_map/ppermute | solution.py:264
  20.2 1.2 %collective-permute-done.7.other = f32[8,512]{1,0:T(8,128)S(1)} collective-permute-done((f32[8,512]{1,0:T(8,128)S(1)}, f32[8,512]{1,0:T(8,128)S(1)}, u32[]{:S(2)}, u32[]{:S(2)}) %collective-permute-start.7) | collective-permute-done | bytes 16416 | tf_op jit(solution)/shard_map/ppermute | solution.py:289
  21.4 1.3 %shard_map.97 = f32[2,16]{1,0:T(2,128)} custom-call(s32[1]{0:T(128)} %bitcast.core_ref, f32[8,512]{1,0:T(8,128)S(1)} %fusion.own, f32[8,512]{1,0:T(8,128)S(1)} %collective-permute-done.7.other, f32[256,256]{1,0:T(8,128)S(1)} %copy-done.2, f32[256,256]{1,0:T(8,128)S(1)} %collective-permute-done.after.other_eigen, ...), custom_call_target="tpu_custom_call" | custom-call | tf_op jit(solution)/shard_map/pallas_call | solution.py:239
  (17 shorter events, 0.1 us)
Async XLA Ops:
  0.0 7.2 %collective-permute-start = (f32[256,256]{1,0:T(8,128)}, f32[256,256]{1,0:T(8,128)S(1)}, u32[]{:S(2)}, u32[]{:S(2)}) collective-permute-start(f32[256,256]{1,0:T(8,128)} %eigen.1), channel_id=1, source_target_pairs={{0,1},{1,0},{2,3},{3,2},{4,5},{5,4},{6,7},{7,6},{8,9},{9,8},{10,11... | collective-permute-start | bytes 786440 | tf_op jit(solution)/shard_map/ppermute | solution.py:274
  1.2 5.1 %copy-start = (bf16[3584,256]{1,0:T(8,128)(2,1)S(1)}, bf16[3584,256]{1,0:T(8,128)(2,1)}, u32[]{:S(2)}) copy-start(bf16[3584,256]{1,0:T(8,128)(2,1)} %out_basis.1) | copy-start | bytes 5505028
  1.2 5.1 %copy-start.1 = (bf16[3584,64]{0,1:T(8,128)(2,1)S(1)}, bf16[3584,64]{0,1:T(8,128)(2,1)}, u32[]{:S(2)}) copy-start(bf16[3584,64]{0,1:T(8,128)(2,1)} %param.9) | copy-start | bytes 1376260
  1.3 5.1 %copy-start.3 = (bf16[1024,128]{1,0:T(8,128)(2,1)S(1)}, bf16[1024,128]{1,0:T(8,128)(2,1)}, u32[]{:S(2)}) copy-start(bf16[1024,128]{1,0:T(8,128)(2,1)} %act_basis.1) | copy-start | bytes 786436
  1.3 5.1 %copy-start.4 = (bf16[1024,64]{0,1:T(8,128)(2,1)S(1)}, bf16[1024,64]{0,1:T(8,128)(2,1)}, u32[]{:S(2)}) copy-start(bf16[1024,64]{0,1:T(8,128)(2,1)} %param.10) | copy-start | bytes 393220
  1.3 5.9 %collective-permute-start.1 = (bf16[1,32,768]{2,1,0:T(8,128)(2,1)S(1)}, bf16[1,32,768]{2,1,0:T(8,128)(2,1)S(1)}, u32[]{:S(2)}, u32[]{:S(2)}) collective-permute-start(bf16[1,32,768]{2,1,0:T(8,128)(2,1)S(1)} %shard_map.93.first), channel_id=1, source_target_pairs={{0,9},{1,8},{2,11},{3,10},{4,13},{5,12},{6,15},{7,14},{8,1},{9,0},... | collective-permute-start | bytes 147464 | tf_op jit(solution)/shard_map/ppermute | solution.py:270
  6.4 15.0 %copy-start.2 = (f32[256,256]{1,0:T(8,128)S(1)}, f32[256,256]{1,0:T(8,128)}, u32[]{:S(2)}) copy-start(f32[256,256]{1,0:T(8,128)} %eigen.1) | copy-start | bytes 786436
  7.2 4.8 %collective-permute-start.2 = (bf16[2,32,768]{2,1,0:T(8,128)(2,1)S(1)}, bf16[2,32,768]{2,1,0:T(8,128)(2,1)S(1)}, u32[]{:S(2)}, u32[]{:S(2)}) collective-permute-start(bf16[2,32,768]{2,1,0:T(8,128)(2,1)S(1)} %get-tuple-element.11.first), channel_id=1, source_target_pairs={{0,5},{1,4},{2,7},{3,6},{4,1},{5,0},{6,3},{7,2},{8,13},{9,12},{10,... | collective-permute-start | bytes 294920 | tf_op jit(solution)/shard_map/ppermute | solution.py:270
  8.6 5.3 %collective-permute-start.3 = (f32[2,8,512]{2,1,0:T(8,128)S(1)}, f32[2,8,512]{2,1,0:T(8,128)S(1)}, u32[]{:S(2)}, u32[]{:S(2)}) collective-permute-start(f32[2,8,512]{2,1,0:T(8,128)S(1)} %get-tuple-element.12), channel_id=1, source_target_pairs={{0,2},{2,0},{4,6},{6,4},{8,10},{10,8},{12,14},{14,12},{1,3},{3,1},... | collective-permute-start | bytes 98312 | tf_op jit(solution)/shard_map/ppermute | solution.py:264
  10.1 5.0 %collective-permute-start.4 = (f32[2,8,512]{2,1,0:T(8,128)S(1)}, f32[2,8,512]{2,1,0:T(8,128)S(1)}, u32[]{:S(2)}, u32[]{:S(2)}) collective-permute-start(f32[2,8,512]{2,1,0:T(8,128)S(1)} %get-tuple-element.13), channel_id=1, source_target_pairs={{0,6},{2,4},{4,2},{6,0},{8,14},{10,12},{12,10},{14,8},{1,7},{3,5},... | collective-permute-start | bytes 98312 | tf_op jit(solution)/shard_map/ppermute | solution.py:264
  11.0 4.0 %collective-permute-start.5 = (f32[2,8,512]{2,1,0:T(8,128)S(1)}, f32[2,8,512]{2,1,0:T(8,128)S(1)}, u32[]{:S(2)}, u32[]{:S(2)}) collective-permute-start(f32[2,8,512]{2,1,0:T(8,128)S(1)} %get-tuple-element.14), channel_id=1, source_target_pairs={{0,4},{2,6},{4,0},{6,2},{8,12},{10,14},{12,8},{14,10},{1,5},{3,7},... | collective-permute-start | bytes 98312 | tf_op jit(solution)/shard_map/ppermute | solution.py:264
  12.1 6.7 %collective-permute-start.8 = (bf16[4,32,768]{2,1,0:T(8,128)(2,1)S(1)}, bf16[4,32,768]{2,1,0:T(8,128)(2,1)S(1)}, u32[]{:S(2)}, u32[]{:S(2)}) collective-permute-start(bf16[4,32,768]{2,1,0:T(8,128)(2,1)S(1)} %shard_map.95.after.rest_0_), channel_id=1, source_target_pairs={{0,3},{1,2},{2,1},{3,0},{4,7},{5,6},{6,5},{7,4},{8,11},{9,10},{10,... | collective-permute-start | bytes 589832 | tf_op jit(solution)/shard_map/ppermute | solution.py:270
  15.1 5.1 %collective-permute-start.6 = (f32[8,512]{1,0:T(8,128)S(1)}, f32[8,512]{1,0:T(8,128)S(1)}, u32[]{:S(2)}, u32[]{:S(2)}) collective-permute-start(f32[8,512]{1,0:T(8,128)S(1)} %slice_bitcast_fusion), channel_id=1, source_target_pairs={{0,8},{2,10},{4,12},{6,14},{8,0},{10,2},{12,4},{14,6},{1,9},{3,11}... | collective-permute-start | bytes 49160 | tf_op jit(solution)/shard_map/ppermute | solution.py:264
  18.5 2.9 %collective-permute-start.9 = (bf16[4,32,768]{2,1,0:T(8,128)(2,1)S(1)}, bf16[4,32,768]{2,1,0:T(8,128)(2,1)S(1)}, u32[]{:S(2)}, u32[]{:S(2)}) collective-permute-start(bf16[4,32,768]{2,1,0:T(8,128)(2,1)S(1)} %shard_map.95.after.rest_0_), channel_id=1, source_target_pairs={{0,1},{1,0},{2,3},{3,2},{4,5},{5,4},{6,7},{7,6},{8,9},{9,8},{10,11... | collective-permute-start | bytes 589832 | tf_op jit(solution)/shard_map/ppermute | solution.py:286
  18.8 2.6 %collective-permute-start.10 = (bf16[4,32,768]{2,1,0:T(8,128)(2,1)S(1)}, bf16[4,32,768]{2,1,0:T(8,128)(2,1)S(1)}, u32[]{:S(2)}, u32[]{:S(2)}) collective-permute-start(bf16[4,32,768]{2,1,0:T(8,128)(2,1)S(1)} %collective-permute-done.8.rest_1_), channel_id=1, source_target_pairs={{0,1},{1,0},{2,3},{3,2},{4,5},{5,4},{6,7},{7,6},{8,9},{9,8},{10,11... | collective-permute-start | bytes 589832 | tf_op jit(solution)/shard_map/ppermute | solution.py:287
  20.2 1.2 %collective-permute-start.7 = (f32[8,512]{1,0:T(8,128)S(1)}, f32[8,512]{1,0:T(8,128)S(1)}, u32[]{:S(2)}, u32[]{:S(2)}) collective-permute-start(f32[8,512]{1,0:T(8,128)S(1)} %fusion.own), channel_id=1, source_target_pairs={{0,1},{1,0},{2,3},{3,2},{4,5},{5,4},{6,7},{7,6},{8,9},{9,8},{10,11... | collective-permute-start | bytes 49160 | tf_op jit(solution)/shard_map/ppermute | solution.py:289
